TPU v7x, 32 devices: a whole 2x2x4 slice. The times are simulated.
32 devices in a mesh: group: 4 (over z), dp: 2 (over x), tensor: 4 (over y, core).
Axes of the slice: x: 2, y: 2, z: 4, core: 2. Of those that a mesh axis runs over, the one named last changes fastest.
Arguments:
- block_input: bfloat16 [20480, 2048], P(('group', 'dp', 'tensor')), may hold values from -6 to 6
- cotangent: bfloat16 [20480, 2048], P(('group', 'dp', 'tensor')), may hold values from -6 to 6
- lengths: int32 [8, 8], P(('group', 'dp')), may hold values from 0 to 2560, as said below
- weight_heads: float32 [2048, 8192], P(('dp', 'group'), 'tensor')
- weight_hidden: float32 [2, 2048, 8192], P(None, ('dp', 'group'), 'tensor')
- norm_gains: float32 [2, 2048], P(None, 'group'), may hold values from 0.5 to 1.5
- momentum_heads: float32 [2048, 8192], P(('dp', 'group'), 'tensor'), may hold values from -0.15625 to 0.15625
- momentum_hidden: float32 [2, 2048, 8192], P(None, ('dp', 'group'), 'tensor'), may hold values from -0.15625 to 0.15625
- momentum_gains: float32 [2, 2048], P(None, 'group'), may hold values from -3 to 3
- average_heads: float32 [2048, 8192], P(('dp', 'group'), 'tensor'), may hold values from -0.125 to 0.125
- average_hidden: float32 [2, 2048, 8192], P(None, ('dp', 'group'), 'tensor'), may hold values from -0.125 to 0.125
- average_gains: float32 [2, 2048], P(None, 'group'), may hold values from 0.5 to 1.5
- first_heads: float32 [4, 2048, 8192], P('group', 'dp', 'tensor'), may hold values from -24 to 24
- first_hidden: float32 [4, 2, 2048, 8192], P('group', None, 'dp', 'tensor'), may hold values from -24 to 24
- first_gains: float32 [4, 2, 2048], P('group'), may hold values from -48 to 48
- second_heads: float32 [4, 2048, 8192], P('group', 'dp', 'tensor'), may hold values from 66.56 to 271.36
- second_hidden: float32 [4, 2, 2048, 8192], P('group', None, 'dp', 'tensor'), may hold values from 66.56 to 271.36
- second_gains: float32 [4, 2, 2048], P('group'), may hold values from 256 to 1024
Outputs:
- block_output: bfloat16 [20480, 2048], P(('group', 'dp', 'tensor'))
- input_grad: float32 [20480, 2048], P(('group', 'dp', 'tensor'))
- moment_heads: float32 [4, 2048, 8192], P('group', 'dp', 'tensor')
- moment_hidden: float32 [4, 2, 2048, 8192], P('group', None, 'dp', 'tensor')
- moment_gains: float32 [4, 2, 2048], P('group')
- square_heads: float32 [4, 2048, 8192], P('group', 'dp', 'tensor')
- square_hidden: float32 [4, 2, 2048, 8192], P('group', None, 'dp', 'tensor')
- square_gains: float32 [4, 2, 2048], P('group')
- change_heads: float32 [2048, 8192], P(('dp', 'group'), 'tensor')
- change_hidden: float32 [2, 2048, 8192], P(None, ('dp', 'group'), 'tensor')
- change_gains: float32 [2, 2048], P(None, 'group')
- velocity_heads: float32 [2048, 8192], P(('dp', 'group'), 'tensor')
- velocity_hidden: float32 [2, 2048, 8192], P(None, ('dp', 'group'), 'tensor')
- velocity_gains: float32 [2, 2048], P(None, 'group')
- trail_heads: float32 [2048, 8192], P(('dp', 'group'), 'tensor')
- trail_hidden: float32 [2, 2048, 8192], P(None, ('dp', 'group'), 'tensor')
- trail_gains: float32 [2, 2048], P(None, 'group')
- master_heads: float32 [2048, 8192], P(('dp', 'group'), 'tensor')
- master_hidden: float32 [2, 2048, 8192], P(None, ('dp', 'group'), 'tensor')
- master_gains: float32 [2, 2048], P(None, 'group')
- copy_heads: bfloat16 [2048, 8192], P(('dp', 'group'), 'tensor')
- copy_hidden: bfloat16 [2, 2048, 8192], P(None, ('dp', 'group'), 'tensor')
Inputs may be any that keep to these rules, and one draw needn't show every extreme that they name: `lengths`: each row sums to 2560; items may be empty. In every draw one row is a single item of 2560 tokens, and every other row holds one item of 640 to 1280 tokens beside others.
All inputs are finite; a program needn't handle non-finite values.
Results may differ from a plain program's by a relative error of at most 0.028.
Values may be sent and summed in bfloat16 or wider, within the bound.
No kernel may reach another device: no remote copies, remote signals or barrier semaphores. Data moves between devices by JAX's collectives and lax.ppermute only.
A program may use at most 448 MiB of HBM per device.

v0:
```python
import jax
import jax.numpy as jnp
from jax import lax
from jax.sharding import PartitionSpec as P

HEAD_DIM = 128
STEP = 8


NORM_EPS = 1e-05
INNER_RATE = 0.02
GAIN_RATE = 0.5
BETA_ONE = 0.9
BETA_TWO = 0.95
ADAM_EPS = 1e-08
WEIGHT_DECAY = 0.1
OUTER_RATE = 0.7
OUTER_MOMENTUM = 0.9
EMA_KEEP = 0.5


def layer_norm(rows, gain):
    mean = jnp.mean(rows, axis=-1, keepdims=True)
    centred = rows - mean
    var = jnp.mean(centred * centred, axis=-1, keepdims=True)
    return centred * lax.rsqrt(var + NORM_EPS) * gain


def item_ids(lengths, total):
    ends = jnp.cumsum(lengths)
    places = jnp.arange(total, dtype=jnp.int32)
    return jnp.sum((places[:, None] >= ends[None, :]).astype(jnp.int32), axis=1)


def adam_step(weight, grad, first, second, rate, decay):
    first = BETA_ONE * first + (1.0 - BETA_ONE) * grad
    second = BETA_TWO * second + (1.0 - BETA_TWO) * grad * grad
    scaled_first = first / (1.0 - BETA_ONE**STEP)
    scaled_second = second / (1.0 - BETA_TWO**STEP)
    update = scaled_first / (jnp.sqrt(scaled_second) + ADAM_EPS) + decay * weight
    return (first, second, rate * update)


def outer_step(weight, change, momentum, average):
    velocity = OUTER_MOMENTUM * momentum + change
    master = weight - OUTER_RATE * (change + OUTER_MOMENTUM * velocity)
    trail = EMA_KEEP * average + (1.0 - EMA_KEEP) * master
    return (velocity, trail, master)


def reduce_hidden(grad_hidden):
    return lax.psum_scatter(
        grad_hidden.astype(jnp.bfloat16), "dp", scatter_dimension=1, tiled=True
    ).astype(jnp.float32)


def contract_last(left, right):
    return lax.dot_general(
        left, right, (((1,), (1,)), ((), ())), preferred_element_type=jnp.float32
    )


def contract_first(left, right):
    return lax.dot_general(
        left, right, (((0,), (0,)), ((), ())), preferred_element_type=jnp.float32
    )


def local(
    block_input,
    cotangent,
    lengths,
    weight_heads,
    weight_hidden,
    norm_gains,
    momentum_heads,
    momentum_hidden,
    momentum_gains,
    average_heads,
    average_hidden,
    average_gains,
    first_heads,
    first_hidden,
    first_gains,
    second_heads,
    second_hidden,
    second_gains,
):
    inner_heads, inner_hidden, inner_gains = (
        lax.all_gather(weight_heads.astype(jnp.bfloat16), "group", axis=0, tiled=True).astype(
            weight_heads.dtype
        ),
        lax.all_gather(weight_hidden.astype(jnp.bfloat16), "group", axis=1, tiled=True).astype(
            weight_hidden.dtype
        ),
        lax.all_gather(norm_gains.astype(jnp.bfloat16), "group", axis=1, tiled=True).astype(
            norm_gains.dtype
        ),
    )
    whole_heads, whole_hidden = (
        lax.all_gather(inner_heads.astype(jnp.bfloat16), "dp", axis=0, tiled=True),
        lax.all_gather(inner_hidden.astype(jnp.bfloat16), "dp", axis=1, tiled=True),
    )
    width = whole_heads.shape[0]
    heads = whole_heads.shape[1] // (4 * HEAD_DIM)
    split_heads = whole_heads.reshape(width, heads, 4, HEAD_DIM)
    inward_heads = split_heads[:, :, :3, :].reshape(width, heads * 3 * HEAD_DIM)
    outward_heads = split_heads[:, :, 3, :].reshape(width, heads * HEAD_DIM)
    raise_hidden = whole_hidden[0]
    lower_hidden = whole_hidden[1]
    rows = block_input.astype(jnp.float32)
    gain_one = inner_gains[0]
    gain_two = inner_gains[1]
    first_norm = layer_norm(rows, gain_one)
    gathered_one = lax.all_gather(first_norm.astype(jnp.bfloat16), "tensor", axis=0, tiled=True)
    total = gathered_one.shape[0]
    triple = jnp.dot(gathered_one, inward_heads, preferred_element_type=jnp.float32).astype(
        jnp.bfloat16
    )
    triple = triple.reshape(total, heads, 3, HEAD_DIM)
    queries = triple[:, :, 0, :]
    keys_all = triple[:, :, 1, :]
    values = triple[:, :, 2, :]
    items = item_ids(lengths[0], total)
    block = min(512, total)
    blocks = total // block
    scale = HEAD_DIM ** (-0.5)
    places = jnp.arange(block, dtype=jnp.int32)

    def lowest_block():
        return jnp.int32(0)

    def block_scores(query_block, key_block):
        q_rows = lax.dynamic_slice_in_dim(queries, query_block * block, block, 0)
        k_rows = lax.dynamic_slice_in_dim(keys_all, key_block * block, block, 0)
        logits = (
            jnp.einsum("qhe,khe->hqk", q_rows, k_rows, preferred_element_type=jnp.float32) * scale
        )
        q_items = lax.dynamic_slice_in_dim(items, query_block * block, block, 0)
        k_items = lax.dynamic_slice_in_dim(items, key_block * block, block, 0)
        causal = query_block * block + places[:, None] >= key_block * block + places[None, :]
        live = (causal & (q_items[:, None] == k_items[None, :]))[None]
        return (jnp.where(live, logits, -1e30), live)

    def forward_block(query_block):
        lower = lowest_block()

        def find_top(key_block, state):
            top, weight_sum = state
            logits, live = block_scores(query_block, key_block)
            new_top = jnp.maximum(top, jnp.max(logits, axis=-1))
            weights = jnp.where(live, jnp.exp(logits - new_top[..., None]), 0.0)
            return (new_top, weight_sum * jnp.exp(top - new_top) + jnp.sum(weights, axis=-1))

        start_state = (
            jnp.full((heads, block), -1e30, jnp.float32),
            jnp.zeros((heads, block), jnp.float32),
        )
        top, weight_sum = lax.fori_loop(lower, query_block + 1, find_top, start_state)
        log_total = top + jnp.log(weight_sum)

        def add_values(key_block, mixed_part):
            logits, live = block_scores(query_block, key_block)
            probs = jnp.where(live, jnp.exp(logits - log_total[..., None]), 0.0)
            v_rows = lax.dynamic_slice_in_dim(values, key_block * block, block, 0)
            return mixed_part + jnp.einsum(
                "hqk,khe->qhe",
                probs.astype(jnp.bfloat16),
                v_rows,
                preferred_element_type=jnp.float32,
            )

        empty = jnp.zeros((block, heads, HEAD_DIM), jnp.float32)
        mixed_part = lax.fori_loop(lower, query_block + 1, add_values, empty)
        return (mixed_part, log_total)

    mixed_blocks, log_totals = lax.map(forward_block, jnp.arange(blocks, dtype=jnp.int32))
    mixed_full = mixed_blocks.reshape(total, heads, HEAD_DIM)
    mixed_low = mixed_blocks.reshape(total, heads * HEAD_DIM).astype(jnp.bfloat16)
    middle = rows + lax.psum_scatter(
        contract_last(mixed_low, outward_heads).astype(jnp.bfloat16),
        "tensor",
        scatter_dimension=0,
        tiled=True,
    ).astype(jnp.float32)
    second_norm = layer_norm(middle, gain_two)
    gathered_two = lax.all_gather(second_norm.astype(jnp.bfloat16), "tensor", axis=0, tiled=True)
    before = jnp.dot(gathered_two, raise_hidden, preferred_element_type=jnp.float32)
    hidden = jax.nn.gelu(before, approximate=False).astype(jnp.bfloat16)
    output = middle + lax.psum_scatter(
        contract_last(hidden, lower_hidden).astype(jnp.bfloat16),
        "tensor",
        scatter_dimension=0,
        tiled=True,
    ).astype(jnp.float32)
    block_output = output.astype(jnp.bfloat16)
    back_all = lax.all_gather(cotangent, "tensor", axis=0, tiled=True)
    grad_lower = contract_first(back_all, hidden)
    back_hidden = jnp.dot(back_all, lower_hidden, preferred_element_type=jnp.float32)
    gelu_back = jax.vjp(lambda value: jax.nn.gelu(value, approximate=False), before)[1]
    back_before = gelu_back(back_hidden)[0].astype(jnp.bfloat16)
    grad_raise = contract_first(gathered_two, back_before)
    grad_hidden = jnp.stack([grad_raise, grad_lower])
    back_second = lax.psum_scatter(
        contract_last(back_before, raise_hidden).astype(jnp.bfloat16),
        "tensor",
        scatter_dimension=0,
        tiled=True,
    ).astype(jnp.float32)
    middle_ln, grad_gain_two = jax.vjp(layer_norm, middle, gain_two)[1](back_second)
    back_middle = cotangent.astype(jnp.float32) + middle_ln
    middle_all = lax.all_gather(back_middle.astype(jnp.bfloat16), "tensor", axis=0, tiled=True)
    grad_outward = contract_first(middle_all, mixed_low)
    back_mixed = jnp.dot(middle_all, outward_heads, preferred_element_type=jnp.float32).astype(
        jnp.bfloat16
    )
    back_mixed = back_mixed.reshape(total, heads, HEAD_DIM)
    row_terms = jnp.sum(back_mixed.astype(jnp.float32) * mixed_full, axis=-1)
    row_terms = row_terms.reshape(blocks, block, heads).transpose(0, 2, 1)

    def backward_block(carry, query_block):
        grad_keys, grad_values = carry
        lower = lowest_block()
        q_rows = lax.dynamic_slice_in_dim(queries, query_block * block, block, 0)
        back_rows = lax.dynamic_slice_in_dim(back_mixed, query_block * block, block, 0)
        log_total = log_totals[query_block]
        row_term = row_terms[query_block]

        def step(key_block, state):
            grad_query, grad_keys, grad_values = state
            logits, live = block_scores(query_block, key_block)
            k_rows = lax.dynamic_slice_in_dim(keys_all, key_block * block, block, 0)
            v_rows = lax.dynamic_slice_in_dim(values, key_block * block, block, 0)
            probs = jnp.where(live, jnp.exp(logits - log_total[..., None]), 0.0)
            back_probs = jnp.einsum(
                "qhe,khe->hqk", back_rows, v_rows, preferred_element_type=jnp.float32
            )
            back_scores = (probs * (back_probs - row_term[..., None])).astype(jnp.bfloat16)
            grad_query = (
                grad_query
                + jnp.einsum(
                    "hqk,khe->qhe", back_scores, k_rows, preferred_element_type=jnp.float32
                )
                * scale
            )
            key_add = (
                jnp.einsum("hqk,qhe->khe", back_scores, q_rows, preferred_element_type=jnp.float32)
                * scale
            )
            value_add = jnp.einsum(
                "hqk,qhe->khe",
                probs.astype(jnp.bfloat16),
                back_rows,
                preferred_element_type=jnp.float32,
            )
            offset = key_block * block
            grad_keys = lax.dynamic_update_slice_in_dim(
                grad_keys,
                lax.dynamic_slice_in_dim(grad_keys, offset, block, 0) + key_add,
                offset,
                0,
            )
            grad_values = lax.dynamic_update_slice_in_dim(
                grad_values,
                lax.dynamic_slice_in_dim(grad_values, offset, block, 0) + value_add,
                offset,
                0,
            )
            return (grad_query, grad_keys, grad_values)

        start_query = jnp.zeros((block, heads, HEAD_DIM), jnp.float32)
        grad_query, grad_keys, grad_values = lax.fori_loop(
            lower, query_block + 1, step, (start_query, grad_keys, grad_values)
        )
        return ((grad_keys, grad_values), grad_query)

    zero_rows = jnp.zeros((total, heads, HEAD_DIM), jnp.float32)
    (grad_keys, grad_values), grad_queries = lax.scan(
        backward_block, (zero_rows, zero_rows), jnp.arange(blocks, dtype=jnp.int32)
    )
    grad_queries = grad_queries.reshape(total, heads, HEAD_DIM)
    back_triple = jnp.stack([grad_queries, grad_keys, grad_values], axis=2).astype(jnp.bfloat16)
    back_triple = back_triple.reshape(total, heads * 3 * HEAD_DIM)
    grad_inward = contract_first(gathered_one, back_triple)
    grad_heads = jnp.concatenate(
        [
            grad_inward.reshape(width, heads, 3, HEAD_DIM),
            grad_outward.reshape(width, heads, 1, HEAD_DIM),
        ],
        axis=2,
    )
    grad_heads = grad_heads.reshape(width, heads * 4 * HEAD_DIM)
    back_first = lax.psum_scatter(
        contract_last(back_triple, inward_heads).astype(jnp.bfloat16),
        "tensor",
        scatter_dimension=0,
        tiled=True,
    ).astype(jnp.float32)
    rows_ln, grad_gain_one = jax.vjp(layer_norm, rows, gain_one)[1](back_first)
    input_grad = back_middle + rows_ln
    gain_grad = lax.psum(jnp.stack([grad_gain_one, grad_gain_two]), ("dp", "tensor"))
    hidden_shard = reduce_hidden(grad_hidden)
    heads_shard = lax.psum_scatter(
        grad_heads.astype(jnp.bfloat16), "dp", scatter_dimension=0, tiled=True
    ).astype(jnp.float32)
    moment_heads, square_heads, delta_heads = adam_step(
        inner_heads, heads_shard, first_heads[0], second_heads[0], INNER_RATE, WEIGHT_DECAY
    )
    moment_hidden, square_hidden, delta_hidden = adam_step(
        inner_hidden, hidden_shard, first_hidden[0], second_hidden[0], INNER_RATE, WEIGHT_DECAY
    )
    moment_gains, square_gains, delta_gains = adam_step(
        inner_gains, gain_grad, first_gains[0], second_gains[0], GAIN_RATE, 0.0
    )
    groups = lax.axis_size("group")
    summed_heads, summed_hidden, summed_gains = (
        lax.psum_scatter(
            delta_heads.astype(jnp.bfloat16), "group", scatter_dimension=0, tiled=True
        ).astype(jnp.float32),
        lax.psum_scatter(
            delta_hidden.astype(jnp.bfloat16), "group", scatter_dimension=1, tiled=True
        ).astype(jnp.float32),
        lax.psum_scatter(
            delta_gains.astype(jnp.bfloat16), "group", scatter_dimension=1, tiled=True
        ).astype(jnp.float32),
    )
    change_heads = summed_heads / groups
    change_hidden = summed_hidden / groups
    change_gains = summed_gains / groups
    velocity_heads, trail_heads, master_heads = outer_step(
        weight_heads, change_heads, momentum_heads, average_heads
    )
    velocity_hidden, trail_hidden, master_hidden = outer_step(
        weight_hidden, change_hidden, momentum_hidden, average_hidden
    )
    velocity_gains, trail_gains, master_gains = outer_step(
        norm_gains, change_gains, momentum_gains, average_gains
    )
    return (
        block_output,
        input_grad,
        moment_heads[None],
        moment_hidden[None],
        moment_gains[None],
        square_heads[None],
        square_hidden[None],
        square_gains[None],
        change_heads,
        change_hidden,
        change_gains,
        velocity_heads,
        velocity_hidden,
        velocity_gains,
        trail_heads,
        trail_hidden,
        trail_gains,
        master_heads,
        master_hidden,
        master_gains,
        master_heads.astype(jnp.bfloat16),
        master_hidden.astype(jnp.bfloat16),
    )


def solution(mesh):
    in_specs = (
        P(("group", "dp", "tensor"), None),
        P(("group", "dp", "tensor"), None),
        P(("group", "dp"), None),
        P(("dp", "group"), "tensor"),
        P(None, ("dp", "group"), "tensor"),
        P(None, "group"),
        P(("dp", "group"), "tensor"),
        P(None, ("dp", "group"), "tensor"),
        P(None, "group"),
        P(("dp", "group"), "tensor"),
        P(None, ("dp", "group"), "tensor"),
        P(None, "group"),
        P("group", "dp", "tensor"),
        P("group", None, "dp", "tensor"),
        P("group", None, None),
        P("group", "dp", "tensor"),
        P("group", None, "dp", "tensor"),
        P("group", None, None),
    )
    out_specs = (
        P(("group", "dp", "tensor"), None),
        P(("group", "dp", "tensor"), None),
        P("group", "dp", "tensor"),
        P("group", None, "dp", "tensor"),
        P("group", None, None),
        P("group", "dp", "tensor"),
        P("group", None, "dp", "tensor"),
        P("group", None, None),
        P(("dp", "group"), "tensor"),
        P(None, ("dp", "group"), "tensor"),
        P(None, "group"),
        P(("dp", "group"), "tensor"),
        P(None, ("dp", "group"), "tensor"),
        P(None, "group"),
        P(("dp", "group"), "tensor"),
        P(None, ("dp", "group"), "tensor"),
        P(None, "group"),
        P(("dp", "group"), "tensor"),
        P(None, ("dp", "group"), "tensor"),
        P(None, "group"),
        P(("dp", "group"), "tensor"),
        P(None, ("dp", "group"), "tensor"),
    )
    return jax.shard_map(local, mesh=mesh, in_specs=in_specs, out_specs=out_specs, check_vma=False)
```

profile of v0, /device:TPU:24, one launch (start us, length us, event | category | flops | bytes accessed | tf_op | source)
XLA Modules:
  0.0 1997.0 jit_solution(13127402955272047553)
XLA Ops:
  13.0 78.8 %all-gather.11.cloned.1.call-done = bf16[1024,2048]{0,1:T(8,128)(2,1)} async-done(((bf16[256,2048]{0,1:T(8,128)(2,1)}), bf16[1024,2048]{0,1:T(8,128)(2,1)}) %all-gather.11.cloned.1.call-update) | async-done | bytes 4194320 | tf_op jit(solution)/shard_map/all_gather | solution.py:90
  91.9 11.2 all_gather.27
  112.6 85.8 %all-gather.13.cloned.1.call-done = bf16[2048,2048]{0,1:T(8,128)(2,1)} async-done(((bf16[1024,2048]{0,1:T(8,128)(2,1)}), bf16[2048,2048]{0,1:T(8,128)(2,1)}) %all-gather.13.cloned.1.call-update) | async-done | bytes 8388624 | tf_op jit(solution)/shard_map/all_gather | solution.py:101
  208.2 62.6 %all-gather.9.cloned.1.call-done = bf16[2560,2048]{1,0:T(8,128)(2,1)} async-done(((bf16[640,2048]{1,0:T(8,128)(2,1)}), bf16[2560,2048]{1,0:T(8,128)(2,1)}) %all-gather.9.cloned.1.call-update) | async-done | bytes 10485776 | tf_op jit(solution)/shard_map/all_gather | solution.py:115
  270.8 21.0 %convolution_convert_fusion.2 = bf16[2560,1536]{0,1:T(8,128)(2,1)S(1)} fusion(bf16[2560,2048]{1,0:T(8,128)(2,1)} %all-gather.9.cloned.1.call-done, bf16[2048,1536]{0,1:T(8,128)(2,1)} %bitcast.294), kind=kOutput, calls=%fused_computation.98 | convolution fusion | flops 16110059520 | bytes 24641536 | tf_op jit(solution)/shard_map/dot_general | solution.py:117
  301.0 137.7 %while.84 = (s32[]{:T(128)}, f32[5,512,4,128]{1,3,2,0:T(8,128)}, f32[5,4,512]{2,1,0:T(4,128)}, s32[5]{0:T(128)S(1)}, s32[2560]{0:T(1024)S(1)}, /*index=5*/bf16[2...) while((s32[]{:T(128)}, f32[5,512,4,128]{1,3,2,0:T(8,128)}, ...), condition=%wide.region_11.12_spmd.clone.clone, body=%wide.region_4.11_spmd.clone.clone.sunk | while | flops 820781056 | bytes 18822056 | solution.py:177
  324.5 8.9 while.88
  347.6 13.3 while.88
  366.3 9.5 while.87
  377.5 17.7 while.88
  400.6 11.9 while.87
  414.3 22.2 %while.88 = (s32[]{:T(128)}, f32[512,4,128]{0,2,1:T(8,128)}, s32[]{:T(128)}, bf16[2560,4,128]{0,2,1:T(8,128)(2,1)}, s32[]{:T(128)}, /*index=5*/s32[512]{0:T(512)...) while((s32[]{:T(128)}, f32[512,4,128]{0,2,1:T(8,128)}, ...), condition=%wide.region_10.10_spmd.clone, body=%wide.region_9.9_spmd.clone.sunk | while | flops 543163392 | bytes 4222151 | solution.py:174
  449.3 10.2 convolution_convert_fusion.3
  460.2 84.8 %reduce-scatter.12.cloned.1.call-done = bf16[640,2048]{1,0:T(8,128)(2,1)} async-done(((bf16[2560,2048]{1,0:T(8,128)(2,1)}), bf16[640,2048]{1,0:T(8,128)(2,1)}) %reduce-scatter.12.cloned.1.call-update) | async-done | bytes 2621456 | tf_op jit(solution)/shard_map/reduce_scatter | solution.py:180
  553.4 191.9 %all-gather.19.cloned.1.call-done = bf16[2,2048,2048]{2,1,0:T(8,128)(2,1)} async-done(((bf16[2,1024,2048]{2,1,0:T(8,128)(2,1)}), bf16[2,2048,2048]{2,1,0:T(8,128)(2,1)}) %all-gather.19.cloned.1.call-update) | async-done | bytes 16777232 | tf_op jit(solution)/shard_map/all_gather | solution.py:102
  745.3 72.4 %all-gather.15.cloned.1.call-done = bf16[2560,2048]{1,0:T(8,128)(2,1)} async-done(((bf16[640,2048]{1,0:T(8,128)(2,1)}), bf16[2560,2048]{1,0:T(8,128)(2,1)}) %all-gather.15.cloned.1.call-update) | async-done | bytes 10485776 | tf_op jit(solution)/shard_map/all_gather | solution.py:187
  817.6 73.7 %multiply_convert_fusion = (bf16[2560,2048]{1,0:T(8,128)(2,1)}, f32[2560,2048]{1,0:T(8,128)}, f32[2560,2048]{1,0:T(8,128)}) fusion(bf16[2560,2048]{1,0:T(8,128)(2,1)} %all-gather.15.cloned.1.call-done, bf16[2,2048,2048]{2,1,0:T(8,128)(2,1)} %all-gather.19.cloned.1.call-done), kind=kOutput, calls=%fused_computation.76 | convolution fusion | flops 21815623680 | bytes 71303168 | tf_op jit(solution)/shard_map/dot_general | solution.py:188
  891.4 38.2 %add_convert_fusion = bf16[2560,2048]{1,0:T(8,128)(2,1)} fusion(f32[2560,2048]{1,0:T(8,128)} %get-tuple-element.1136, f32[2560,2048]{1,0:T(8,128)} %get-tuple-element.1165, bf16[2560,2048]{1,0:T(8,128)(2,1)} %all-gather.21.cloned.1.call-done, bf16[2,2048,2048]{2,1,0:T(8,128)(2,1)} %all-gather.19.cloned.1.call-done), kind=kOutput, calls=%fused_computation.75 | convolution fusion | flops 21548236800 | bytes 71303168 | tf_op jit(solution)/shard_map/dot_general | solution.py:199
  929.6 28.0 %convolution_convert_fusion = bf16[2560,2048]{1,0:T(8,128)(2,1)} fusion(bf16[2560,2048]{1,0:T(8,128)(2,1)} %add_convert_fusion, bf16[2,2048,2048]{2,1,0:T(8,128)(2,1)} %all-gather.19.cloned.1.call-done), kind=kOutput, calls=%fused_computation.96 | convolution fusion | flops 21480079360 | bytes 29360128 | tf_op jit(solution)/shard_map/dot_general | solution.py:58
  957.7 28.0 %convolution_convert_fusion.1 = bf16[2560,2048]{1,0:T(8,128)(2,1)} fusion(bf16[2560,2048]{1,0:T(8,128)(2,1)} %get-tuple-element.1135, bf16[2,2048,2048]{2,1,0:T(8,128)(2,1)} %all-gather.19.cloned.1.call-done), kind=kOutput, calls=%fused_computation.97 | convolution fusion | flops 21480079360 | bytes 29360128 | tf_op jit(solution)/shard_map/dot_general | solution.py:58
  985.9 57.3 %reduce-scatter.16.cloned.1.call-done = bf16[640,2048]{1,0:T(8,128)(2,1)} async-done(((bf16[2560,2048]{1,0:T(8,128)(2,1)}), bf16[640,2048]{1,0:T(8,128)(2,1)}) %reduce-scatter.16.cloned.1.call-update) | async-done | bytes 2621456 | tf_op jit(solution)/shard_map/reduce_scatter | solution.py:204
  1048.5 82.4 %reduce-scatter.14.cloned.1.call-done = bf16[640,2048]{1,0:T(8,128)(2,1)} async-done(((bf16[2560,2048]{1,0:T(8,128)(2,1)}), bf16[640,2048]{1,0:T(8,128)(2,1)}) %reduce-scatter.14.cloned.1.call-update) | async-done | bytes 2621456 | tf_op jit(solution)/shard_map/reduce_scatter | solution.py:190
  1141.4 7.5 copy.131
  1151.6 29.3 %convert_bitcast_fusion.1 = bf16[1,2048,2048]{2,1,0:T(8,128)(2,1)S(1)} fusion(bf16[2560,2048]{1,0:T(8,128)(2,1)} %all-gather.15.cloned.1.call-done, bf16[2560,2048]{1,0:T(8,128)(2,1)} %add_convert_fusion), kind=kOutput, calls=%fused_computation.114 | convolution fusion | flops 21479030784 | bytes 29360128 | tf_op jit(solution)/shard_map/dot_general | solution.py:64
  1180.9 27.7 %convert_bitcast_fusion = bf16[1,2048,2048]{2,1,0:T(8,128)(2,1)S(1)} fusion(bf16[2560,2048]{1,0:T(8,128)(2,1)} %get-tuple-element.1135, bf16[2560,2048]{1,0:T(8,128)(2,1)} %all-gather.21.cloned.1.call-done), kind=kOutput, calls=%fused_computation.113 | convolution fusion | flops 21479030784 | bytes 29360128 | tf_op jit(solution)/shard_map/dot_general | solution.py:64
  1217.0 11.3 convolution_convert_fusion.4
  1233.3 7.2 reshape.393
  1253.5 253.3 %while.86 = (s32[]{:T(128)}, f32[2560,4,128]{2,0,1:T(8,128)}, f32[2560,4,128]{2,0,1:T(8,128)}, bf16[5,512,4,128]{3,1,0,2:T(8,128)(2,1)}, s32[5]{0:T(128)S(1)}, /...) while((s32[]{:T(128)}, f32[2560,4,128]{2,0,1:T(8,128)}, ...), condition=%wide.region_23.24_spmd.clone.clone, body=%wide.region_20.23_spmd.clone.clone.sunk | while | flops 1356858368 | bytes 36521180 | solution.py:278
  1261.6 14.0 while.89
  1284.6 27.7 %while.89 = (s32[]{:T(128)}, f32[512,4,128]{0,2,1:T(8,128)S(1)}, f32[2560,4,128]{2,0,1:T(8,128)}, f32[2560,4,128]{2,0,1:T(8,128)}, s32[]{:T(128)}, /*index=5*/bf...) while((s32[]{:T(128)}, f32[512,4,128]{0,2,1:T(8,128)S(1)}, ...), condition=%wide.region_22.22_spmd.clone, body=%wide.region_21.21_spmd.clone.sunk | while | flops 1356858368 | bytes 29665532 | solution.py:272
  1321.4 41.6 %while.89 = (s32[]{:T(128)}, f32[512,4,128]{0,2,1:T(8,128)S(1)}, f32[2560,4,128]{2,0,1:T(8,128)}, f32[2560,4,128]{2,0,1:T(8,128)}, s32[]{:T(128)}, /*index=5*/bf...) while((s32[]{:T(128)}, f32[512,4,128]{0,2,1:T(8,128)S(1)}, ...), condition=%wide.region_22.22_spmd.clone, body=%wide.region_21.21_spmd.clone.sunk | while | flops 1356858368 | bytes 29665532 | solution.py:272
  1372.0 55.3 %while.89 = (s32[]{:T(128)}, f32[512,4,128]{0,2,1:T(8,128)S(1)}, f32[2560,4,128]{2,0,1:T(8,128)}, f32[2560,4,128]{2,0,1:T(8,128)}, s32[]{:T(128)}, /*index=5*/bf...) while((s32[]{:T(128)}, f32[512,4,128]{0,2,1:T(8,128)S(1)}, ...), condition=%wide.region_22.22_spmd.clone, body=%wide.region_21.21_spmd.clone.sunk | while | flops 1356858368 | bytes 29665532 | solution.py:272
  1436.4 69.1 %while.89 = (s32[]{:T(128)}, f32[512,4,128]{0,2,1:T(8,128)S(1)}, f32[2560,4,128]{2,0,1:T(8,128)}, f32[2560,4,128]{2,0,1:T(8,128)}, s32[]{:T(128)}, /*index=5*/bf...) while((s32[]{:T(128)}, f32[512,4,128]{0,2,1:T(8,128)S(1)}, ...), condition=%wide.region_22.22_spmd.clone, body=%wide.region_21.21_spmd.clone.sunk | while | flops 1356858368 | bytes 29665532 | solution.py:272
  1515.9 18.6 bitcast_convert_fusion
  1542.0 11.3 copy.136
  1553.3 10.9 fusion.102
  1564.2 19.0 fusion.91
  1589.0 31.6 %multiply_convert_fusion.1 = (bf16[2,1024,2048]{2,1,0:T(8,128)(2,1)}, f32[1,2,1024,2048]{3,2,1,0:T(8,128)}, f32[1,2,1024,2048]{3,2,1,0:T(8,128)}) fusion(bf16[2,1024,2048]{2,1,0:T(8,128)(2,1)} %all-gather.17.cloned.1.call-done, bf16[2,1024,2048]{2,1,0:T(8,128)(2,1)} %reduce-scatter.22.cloned.1.call-done, f32[1,2,1024,2048]{3,2,1,0:T(8,128)} %param.41, ...), kind=kLoop, calls=%fused_computation.93 | loop fusion | flops 71303168 | bytes 92274688 | tf_op jit(solution)/shard_map/convert_element_type | solution.py:321
  1620.6 9.3 copy.135
  1629.9 9.5 copy.139
  1645.0 24.4 %psum.7 = f32[2,2048]{1,0:T(2,128)S(1)} all-reduce(f32[2,2048]{1,0:T(2,128)S(1)} %pad_maximum_fusion.2), channel_id=1, replica_groups=mesh['group'=4,'dp'=2,'tensor'=4] {'dp','tensor'}, use_global_device_ids=true, to_apply=%region_31.32 | all-reduce | flops 4096 | bytes 32768 | tf_op jit(solution)/shard_map/psum | solution.py:301
  1671.2 51.4 %reduce-scatter.20.cloned.1.call-done = bf16[1024,2048]{0,1:T(8,128)(2,1)} async-done(((bf16[2048,2048]{0,1:T(8,128)(2,1)}), bf16[1024,2048]{0,1:T(8,128)(2,1)}) %reduce-scatter.20.cloned.1.call-update) | async-done | bytes 4194320 | tf_op jit(solution)/shard_map/reduce_scatter | solution.py:303
  1722.6 18.0 multiply_convert_fusion.2
  1746.4 122.5 %reduce-scatter.26.cloned.1.call-done = bf16[2,256,2048]{2,1,0:T(8,128)(2,1)} async-done(((bf16[2,1024,2048]{2,1,0:T(8,128)(2,1)}), bf16[2,256,2048]{2,1,0:T(8,128)(2,1)}) %reduce-scatter.26.cloned.1.call-update) | async-done | bytes 2097168 | tf_op jit(solution)/shard_map/reduce_scatter | solution.py:320
  1868.9 10.9 fusion.113
  1886.6 9.1 copy.143
  1895.7 9.2 copy.144
  1913.3 57.7 %reduce-scatter.24.cloned.1.call-done = bf16[256,2048]{0,1:T(8,128)(2,1)} async-done(((bf16[1024,2048]{0,1:T(8,128)(2,1)}), bf16[256,2048]{0,1:T(8,128)(2,1)}) %reduce-scatter.24.cloned.1.call-update) | async-done | bytes 1048592 | tf_op jit(solution)/shard_map/reduce_scatter | solution.py:317
  (594 shorter events, 552.9 us)
Async XLA Ops:
  7.2 84.6 %all-gather.11.cloned.1.call-start = ((), (), s32[]{:S(2)}) async-start(), calls=%async_computation.10 | async-start | bytes 5242880 | tf_op jit(solution)/shard_map/all_gather | solution.py:90
  10.1 81.8 %copy-start.38 = (f32[2,512]{1,0:T(2,128)S(1)}, f32[2,512]{1,0:T(2,128)}, u32[]{:S(2)}) copy-start(f32[2,512]{1,0:T(2,128)} %param.33) | copy-start | bytes 12292
  10.1 93.0 %copy-start.1 = (bf16[640,2048]{1,0:T(8,128)(2,1)S(1)}, bf16[640,2048]{1,0:T(8,128)(2,1)}, u32[]{:S(2)}) copy-start(bf16[640,2048]{1,0:T(8,128)(2,1)} %param.28) | copy-start | bytes 7864324
  13.0 185.5 %all-gather.13.cloned.1.call-start = ((), (), s32[]{:S(2)}) async-start(), calls=%async_computation.11 | async-start | bytes 12582912 | tf_op jit(solution)/shard_map/all_gather | solution.py:101
  91.8 179.0 %all-gather.9.cloned.1.call-start = ((), (), s32[]{:S(2)}) async-start(), calls=%async_computation.9 | async-start | bytes 13107200 | tf_op jit(solution)/shard_map/all_gather | solution.py:115
  108.0 4.3 copy-start.44
  108.0 351.6 %all-gather.17.cloned.1.call-start = ((), (), s32[]{:S(2)}) async-start(), calls=%async_computation.14 | async-start | bytes 10485760 | tf_op jit(solution)/shard_map/all_gather | solution.py:93
  112.2 432.8 %reduce-scatter.12.cloned.1.call-start = ((), (), s32[]{:S(2)}) async-start(), calls=%async_computation.12 | async-start | bytes 13107200 | tf_op jit(solution)/shard_map/reduce_scatter | solution.py:180
  438.7 10.6 copy-start
  438.7 10.6 copy-start.15
  459.5 85.5 %copy-start.2 = (bf16[640,2048]{1,0:T(8,128)(2,1)S(1)}, bf16[640,2048]{1,0:T(8,128)(2,1)}, u32[]{:S(2)}) copy-start(bf16[640,2048]{1,0:T(8,128)(2,1)} %param.28) | copy-start | bytes 7864324
  459.5 285.8 %all-gather.19.cloned.1.call-start = ((), (), s32[]{:S(2)}) async-start(), calls=%async_computation.15 | async-start | bytes 25165824 | tf_op jit(solution)/shard_map/all_gather | solution.py:102
  460.1 89.9 %copy-start.21 = (f32[1,2048]{1,0:T(1,128)S(1)}, f32[1,2048]{1,0:T(1,128)}, u32[]{:S(2)}) copy-start(f32[1,2048]{1,0:T(1,128)} %get-tuple-element.1163) | copy-start | bytes 24580
  460.1 357.5 %all-gather.15.cloned.1.call-start = ((), (), s32[]{:S(2)}) async-start(), calls=%async_computation.13 | async-start | bytes 13107200 | tf_op jit(solution)/shard_map/all_gather | solution.py:187
  552.6 338.8 %all-gather.21.cloned.1.call-start = ((), (), s32[]{:S(2)}) async-start(), calls=%async_computation.17 | async-start | bytes 13107200 | tf_op jit(solution)/shard_map/all_gather | solution.py:197
  553.4 489.8 %reduce-scatter.16.cloned.1.call-start = ((), (), s32[]{:S(2)}) async-start(), calls=%async_computation.18 | async-start | bytes 13107200 | tf_op jit(solution)/shard_map/reduce_scatter | solution.py:204
  957.7 173.3 %reduce-scatter.14.cloned.1.call-start = ((), (), s32[]{:S(2)}) async-start(), calls=%async_computation.16 | async-start | bytes 13107200 | tf_op jit(solution)/shard_map/reduce_scatter | solution.py:190
  985.8 57.4 %copy-start.3 = (bf16[640,2048]{1,0:T(8,128)(2,1)S(1)}, bf16[640,2048]{1,0:T(8,128)(2,1)}, u32[]{:S(2)}) copy-start(bf16[640,2048]{1,0:T(8,128)(2,1)} %param.28) | copy-start | bytes 7864324
  985.8 57.4 %copy-start.22 = (f32[1,2048]{1,0:T(1,128)S(1)}, f32[1,2048]{1,0:T(1,128)}, u32[]{:S(2)}) copy-start(f32[1,2048]{1,0:T(1,128)} %get-tuple-element.1163) | copy-start | bytes 24580
  985.8 57.4 %copy-start.26 = (f32[640]{0:T(1024)S(1)}, f32[640]{0:T(1024)}, u32[]{:S(2)}) copy-start(f32[640]{0:T(1024)} %copy-done.25) | copy-start | bytes 7684
  985.8 57.4 %copy-start.28 = (f32[640]{0:T(1024)S(1)}, f32[640]{0:T(1024)}, u32[]{:S(2)}) copy-start(f32[640]{0:T(1024)} %copy-done.27) | copy-start | bytes 7684
  985.8 62.7 %copy-start.34 = (f32[640]{0:T(1024)S(1)}, f32[640]{0:T(1024)}, u32[]{:S(2)}) copy-start(f32[640]{0:T(1024)} %copy-done.33) | copy-start | bytes 7684
  985.8 229.7 %all-gather.23.cloned.1.call-start = ((), (), s32[]{:S(2)}) async-start(), calls=%async_computation.19 | async-start | bytes 13107200 | tf_op jit(solution)/shard_map/all_gather | solution.py:212
  1130.9 8.2 copy-start.9
  1141.3 447.7 %reduce-scatter.22.cloned.1.call-start = ((), (), s32[]{:S(2)}) async-start(), calls=%async_computation.22 | async-start | bytes 25165824 | tf_op jit(solution)/shard_map/reduce_scatter | solution.py:52
  1141.4 7.5 copy-start.10
  1215.4 424.0 %reduce-scatter.18.cloned.1.call-start = ((), (), s32[]{:S(2)}) async-start(), calls=%async_computation.20 | async-start | bytes 13107200 | tf_op jit(solution)/shard_map/reduce_scatter | solution.py:293
  1506.8 9.2 copy-start.12
  1512.7 3.2 copy-start.7
  1534.6 188.0 %reduce-scatter.20.cloned.1.call-start = ((), (), s32[]{:S(2)}) async-start(), calls=%async_computation.21 | async-start | bytes 12582912 | tf_op jit(solution)/shard_map/reduce_scatter | solution.py:303
  1553.3 10.9 copy-start.14
  1588.9 280.0 %reduce-scatter.26.cloned.1.call-start = ((), (), s32[]{:S(2)}) async-start(), calls=%async_computation.24 | async-start | bytes 10485760 | tf_op jit(solution)/shard_map/reduce_scatter | solution.py:320
  1620.6 291.1 %reduce-scatter.28.cloned.1.call-start = ((), (), s32[]{:S(2)}) async-start(), calls=%async_computation.25 | async-start | bytes 655360
  1629.9 9.5 copy-start.4
  1629.9 9.6 copy-start.18
  1629.9 9.6 copy-start.20
  1639.4 3.1 copy-start.32
  1639.4 3.2 copy-start.30
  1639.4 5.6 copy-start.37
  1639.4 30.0 %copy-start.24 = (bf16[2,2048]{1,0:T(2,128)(2,1)S(1)}, bf16[2,2048]{1,0:T(2,128)(2,1)}, u32[]{:S(2)}) copy-start(bf16[2,2048]{1,0:T(2,128)(2,1)} %copy-done.23) | copy-start | bytes 24580
  1639.4 30.0 %copy-start.40 = (f32[1,2,2048]{2,1,0:T(2,128)S(1)}, f32[1,2,2048]{2,1,0:T(2,128)}, u32[]{:S(2)}) copy-start(f32[1,2,2048]{2,1,0:T(2,128)} %param.42) | copy-start | bytes 49156
  1639.4 30.0 %copy-start.41 = (f32[1,2,2048]{2,1,0:T(2,128)S(1)}, f32[1,2,2048]{2,1,0:T(2,128)}, u32[]{:S(2)}) copy-start(f32[1,2,2048]{2,1,0:T(2,128)} %param.45) | copy-start | bytes 49156
  1671.1 299.8 %reduce-scatter.24.cloned.1.call-start = ((), (), s32[]{:S(2)}) async-start(), calls=%async_computation.23 | async-start | bytes 5242880 | tf_op jit(solution)/shard_map/reduce_scatter | solution.py:317
  1895.7 9.2 copy-start.36
  1904.9 7.8 copy-start.39
  1904.9 7.8 copy-start.42
  1904.9 7.8 copy-start.43
  1981.1 5.9 copy-start.13
  (14 other events, 21.2 us)
Sparse Core Ops, SparseCore 0:
  13.1 78.6 all-gather.10
  93.3 105.0 all-gather.12
  200.6 70.1 all-gather.8
  272.8 146.5 all-gather.16
  459.6 85.2 reduce-scatter.11
  546.4 198.8 all-gather.18
  747.4 70.1 all-gather.14
  819.2 70.1 all-gather.20
  957.8 85.3 reduce-scatter.15
  1045.6 85.2 reduce-scatter.13
  1141.4 70.1 all-gather.22
  1215.5 189.4 reduce-scatter.21
  1534.7 85.4 reduce-scatter.17
  1623.1 99.4 reduce-scatter.19
  1724.8 144.0 reduce-scatter.25
  1871.6 19.9 reduce-scatter.27
  1893.7 77.2 reduce-scatter.23
where the time goes:
time: 2010 us; the launch traced here: 2000 us
  waiting for transfers between devices  949 us (47%)
  matrix products  582 us (29%)
  local copies, waits for them, and re-layouts  208 us (10%)
  other arithmetic  182 us (9%)
  blocking collectives  35.6 us (2%)
  loops' own time  25.3 us (1%)
    all_gather x1, waiting for transfers between devices, local(): lax.all_gather(inner_hidden.astype(jnp.bfloat16), 'dp', axis=1, tiled=True)  192 us
    reduce_scatter x1, waiting for transfers between devices, local(): lax.psum_scatter(delta_hidden.astype(jnp.bfloat16), 'group', scatter_dime...  123 us
    dot_general x4, matrix products, contract_first(): lax.dot_general(left, right, (((0,), (0,)), ((), ())), preferred_element_...  86.9 us
    unnamed x110, local copies, waits for them, and re-layouts  86.7 us
    all_gather x1, waiting for transfers between devices, local(): lax.all_gather(inner_heads.astype(jnp.bfloat16), 'dp', axis=0, tiled=True)  85.8 us
    dot_general x4, matrix products, contract_last(): lax.dot_general(left, right, (((1,), (1,)), ((), ())), preferred_element_...  84.9 us
    reduce_scatter x1, waiting for transfers between devices, local(): lax.psum_scatter(contract_last(mixed_low, outward_heads).astype(jnp.bfloa...  84.8 us
    reduce_scatter x1, waiting for transfers between devices, local(): lax.psum_scatter(contract_last(hidden, lower_hidden).astype(jnp.bfloat16)...  82.4 us
  transfers between devices with their start and end apart: 17, of which 11 were waited for; matrix products, arithmetic and copies ran while one was open for 43% of the time, Pallas kernels for 0%

commit v1 on v0

v1 whole, which is shorter than its diff:
```python
import functools
import math

import jax
import jax.numpy as jnp
from jax import lax
from jax.experimental import pallas as pl
from jax.experimental.pallas import tpu as pltpu
from jax.sharding import PartitionSpec as P

HEAD_DIM = 128
STEP = 8

NORM_EPS = 1e-05
INNER_RATE = 0.02
GAIN_RATE = 0.5
BETA_ONE = 0.9
BETA_TWO = 0.95
ADAM_EPS = 1e-08
WEIGHT_DECAY = 0.1
OUTER_RATE = 0.7
OUTER_MOMENTUM = 0.9
EMA_KEEP = 0.5

BF16 = jnp.bfloat16
F32 = jnp.float32
SCALE = HEAD_DIM ** (-0.5)
LOG2E = math.log2(math.e)
SCALE_LOG2 = SCALE * LOG2E
NEGATIVE = -1e30


def swap(value, axis, bit, size):
    return lax.ppermute(value, axis, [(i, i ^ bit) for i in range(size)])


ANYWHERE = pl.BlockSpec(memory_space=pl.ANY)
LIMIT = 60 * 2**20
line = []


def run(kernel, name, grid, meta, ins, outs, scratch=(), after=(), alias=None):
    arrays = [a for a, _ in ins]
    extra = [a for a in line + list(after) if all(a is not b for b in arrays)]
    count, skip = len(ins), len(extra)

    def body(*refs):
        kernel(*refs[: 1 + count], *refs[1 + count + skip :])

    result = pl.pallas_call(
        body,
        grid_spec=pltpu.PrefetchScalarGridSpec(
            num_scalar_prefetch=1,
            grid=grid,
            in_specs=[s for _, s in ins] + [ANYWHERE] * skip,
            out_specs=[s for _, _, s in outs],
            scratch_shapes=list(scratch),
        ),
        out_shape=[jax.ShapeDtypeStruct(s, d) for s, d, _ in outs],
        input_output_aliases={1 + a: b for a, b in (alias or {}).items()},
        compiler_params=pltpu.CompilerParams(vmem_limit_bytes=LIMIT),
        cost_estimate=pl.CostEstimate(flops=10**12, bytes_accessed=1, transcendentals=0),
        name=name,
    )(meta, *arrays, *extra)
    line[:] = [result[0]]
    return result


def dot_last(left, right):
    return lax.dot_general(
        left, right, (((1,), (1,)), ((), ())), preferred_element_type=F32
    )


def dot_first(left, right):
    return lax.dot_general(
        left, right, (((0,), (0,)), ((), ())), preferred_element_type=F32
    )


def dot(left, right):
    return jnp.dot(left, right, preferred_element_type=F32)


def normalize(rows):
    mean = jnp.mean(rows, axis=-1, keepdims=True)
    centred = rows - mean
    var = jnp.mean(centred * centred, axis=-1, keepdims=True)
    inverse = lax.rsqrt(var + NORM_EPS)
    return centred * inverse, inverse


def normalize_back(back, normed, inverse, gain):
    scaled = back * gain
    first = jnp.mean(scaled, axis=-1, keepdims=True)
    second = jnp.mean(scaled * normed, axis=-1, keepdims=True)
    terms = (back * normed).reshape(-1, 8, back.shape[-1])
    return inverse * (scaled - first - normed * second), jnp.sum(terms, axis=0)


def gelu_parts(u):
    size = jnp.abs(u) * (0.5**0.5)
    t = 1.0 / (1.0 + 0.3275911 * size)
    poly = t * (
        0.254829592
        + t * (-0.284496736 + t * (1.421413741 + t * (-1.453152027 + t * 1.061405429)))
    )
    bell = jnp.exp(-0.5 * u * u)
    tail = 0.5 * poly * bell
    below = jnp.where(u >= 0.0, 1.0 - tail, tail)
    return below, bell * (1.0 / math.sqrt(2.0 * math.pi))


def item_start(places, meta, items):
    start = jnp.zeros_like(places)
    for k in range(items):
        start = jnp.where(places >= meta[k], meta[k], start)
    return start


def copy_in(meta, items, source, target, rows, step, total):
    for s in range(total // step):
        owner, offset = (s * step) // rows, (s * step) % rows
        local = pl.multiple_of((owner ^ meta[items]) * rows + offset, step)
        target[s * step : (s + 1) * step, :] = source[pl.ds(local, step), :]


def local_row(meta, items, chunk, rows, step):
    per = rows // step
    owner, offset = chunk // per, chunk % per
    return pl.multiple_of((owner ^ meta[items]) * rows + offset * step, step)


def attend_kernel(items, rows, step, block, meta, qkv, mixed, logs, nat, acc, top, weight):
    total = qkv.shape[0]
    index = pl.program_id(1)

    @pl.when(index == 0)
    def _():
        copy_in(meta, items, qkv, nat, rows, step, total)

    first_row = index * block
    q = nat[pl.ds(pl.multiple_of(first_row, block), block), 0:HEAD_DIM]
    acc[...] = jnp.zeros_like(acc)
    top[...] = jnp.full_like(top, NEGATIVE)
    weight[...] = jnp.zeros_like(weight)
    low_start = item_start(first_row, meta, items)
    high_start = item_start(first_row + block - 1, meta, items)

    def tile(j, masked):
        at = pl.ds(pl.multiple_of(j * block, block), block)
        k = nat[at, HEAD_DIM : 2 * HEAD_DIM]
        v = nat[at, 2 * HEAD_DIM : 3 * HEAD_DIM]
        s = dot_last(q, k)
        if masked:
            q_place = first_row + lax.broadcasted_iota(jnp.int32, (block, 1), 0)
            k_place = j * block + lax.broadcasted_iota(jnp.int32, (1, block), 1)
            live = (k_place <= q_place) & (k_place >= item_start(q_place, meta, items))
            s = jnp.where(live, s, NEGATIVE)
        old = top[:, 0:1]
        new = jnp.maximum(old, jnp.max(s, axis=1, keepdims=True))
        p = jnp.exp2((s - new) * SCALE_LOG2)
        keep = jnp.exp2((old - new) * SCALE_LOG2)
        top[...] = jnp.broadcast_to(new, top.shape)
        weight[...] = weight[...] * keep + jnp.sum(p, axis=1, keepdims=True)
        acc[...] = acc[...] * keep + dot(p.astype(BF16), v)

    @pl.loop(low_start // block, index)
    def _(j):
        whole = high_start <= j * block

        @pl.when(whole)
        def _():
            tile(j, False)

        @pl.when(jnp.logical_not(whole))
        def _():
            tile(j, True)

    tile(index, True)
    out = (acc[...] / weight[...]).astype(BF16)
    per = block // step
    for c in range(per):
        at = local_row(meta, items, index * per + c, rows, step)
        mixed[pl.ds(at, step), :] = out[c * step : (c + 1) * step, :]
    log = top[...] * SCALE_LOG2 + jnp.log(weight[...]) * LOG2E
    logs[0, 0] = log.T[0:8, :]


def attend(meta, qkv, items, rows, heads, after=()):
    total = qkv.shape[0]
    block = min(512, total)
    step = math.gcd(rows, block)
    count = total // block
    return run(
        functools.partial(attend_kernel, items, rows, step, block),
        "attend",
        (heads, count),
        meta,
        [(qkv, pl.BlockSpec((total, 3 * HEAD_DIM), lambda h, i, m: (0, h)))],
        [
            ((total, heads * HEAD_DIM), BF16, pl.BlockSpec((total, HEAD_DIM), lambda h, i, m: (0, h))),
            ((heads, count, 8, block), F32, pl.BlockSpec((1, 1, 8, block), lambda h, i, m: (h, i, 0, 0))),
        ],
        [
            pltpu.VMEM((total, 3 * HEAD_DIM), BF16),
            pltpu.VMEM((block, HEAD_DIM), F32),
            pltpu.VMEM((block, HEAD_DIM), F32),
            pltpu.VMEM((block, HEAD_DIM), F32),
        ],
        after,
    )


def attend_back_kernel(
    items, rows, step, block, meta, qkv, mixed, back, logs, grads, nat, nat_mixed, nat_back, dq, dk, dv
):
    total = qkv.shape[0]
    index = pl.program_id(1)

    @pl.when(index == 0)
    def _():
        copy_in(meta, items, qkv, nat, rows, step, total)
        copy_in(meta, items, mixed, nat_mixed, rows, step, total)
        copy_in(meta, items, back, nat_back, rows, step, total)
        dk[...] = jnp.zeros_like(dk)
        dv[...] = jnp.zeros_like(dv)

    first_row = index * block
    here = pl.ds(pl.multiple_of(first_row, block), block)
    q = nat[here, 0:HEAD_DIM]
    g = nat_back[here, :]
    product = g.astype(F32) * nat_mixed[here, :].astype(F32)
    row_term = jnp.sum(product.T, axis=0, keepdims=True)
    log = logs[0, 0, 0:1, :]
    dq[...] = jnp.zeros_like(dq)
    low_start = item_start(first_row, meta, items)
    high_start = item_start(first_row + block - 1, meta, items)

    def tile(j, masked):
        at = pl.ds(pl.multiple_of(j * block, block), block)
        k = nat[at, HEAD_DIM : 2 * HEAD_DIM]
        v = nat[at, 2 * HEAD_DIM : 3 * HEAD_DIM]
        p = jnp.exp2(dot_last(k, q) * SCALE_LOG2 - log)
        if masked:
            k_place = j * block + lax.broadcasted_iota(jnp.int32, (block, 1), 0)
            q_place = first_row + lax.broadcasted_iota(jnp.int32, (1, block), 1)
            live = (k_place <= q_place) & (k_place >= item_start(q_place, meta, items))
            p = jnp.where(live, p, 0.0)
        s = (p * (dot_last(v, g) - row_term)).astype(BF16)
        dv[at, :] += dot(p.astype(BF16), g)
        dk[at, :] += dot(s, q)
        dq[...] += dot_first(s, k)

    @pl.loop(low_start // block, index)
    def _(j):
        whole = high_start <= j * block

        @pl.when(whole)
        def _():
            tile(j, False)

        @pl.when(jnp.logical_not(whole))
        def _():
            tile(j, True)

    tile(index, True)
    out = (dq[...] * SCALE).astype(BF16)
    per = block // step
    for c in range(per):
        to = local_row(meta, items, index * per + c, rows, step)
        grads[pl.ds(to, step), 0:HEAD_DIM] = out[c * step : (c + 1) * step, :]

    @pl.when(index == pl.num_programs(1) - 1)
    def _():
        for s in range(total // step):
            to = local_row(meta, items, s, rows, step)
            part = slice(s * step, (s + 1) * step)
            grads[pl.ds(to, step), HEAD_DIM : 2 * HEAD_DIM] = (dk[part, :] * SCALE).astype(BF16)
            grads[pl.ds(to, step), 2 * HEAD_DIM : 3 * HEAD_DIM] = dv[part, :].astype(BF16)


def attend_back(meta, qkv, mixed, back, logs, items, rows, heads, after=()):
    total = qkv.shape[0]
    block = logs.shape[-1]
    step = math.gcd(rows, block)
    count = total // block
    wide = pl.BlockSpec((total, 3 * HEAD_DIM), lambda h, i, m: (0, h))
    narrow = pl.BlockSpec((total, HEAD_DIM), lambda h, i, m: (0, h))
    return run(
        functools.partial(attend_back_kernel, items, rows, step, block),
        "attend_back",
        (heads, count),
        meta,
        [
            (qkv, wide),
            (mixed, narrow),
            (back, narrow),
            (logs, pl.BlockSpec((1, 1, 8, block), lambda h, i, m: (h, i, 0, 0))),
        ],
        [(qkv.shape, BF16, wide)],
        [
            pltpu.VMEM((total, 3 * HEAD_DIM), BF16),
            pltpu.VMEM((total, HEAD_DIM), BF16),
            pltpu.VMEM((total, HEAD_DIM), BF16),
            pltpu.VMEM((block, HEAD_DIM), F32),
            pltpu.VMEM((total, HEAD_DIM), F32),
            pltpu.VMEM((total, HEAD_DIM), F32),
        ],
        after,
    )[0]


def copies(refs, places, meta, target, sems):
    out = []
    for n, (ref, (row, column)) in enumerate(zip(refs, places)):
        tall, wide = ref.shape
        at = pl.multiple_of(row(meta), tall)
        out.append(
            pltpu.make_async_copy(ref, target.at[pl.ds(at, tall), pl.ds(column, wide)], sems.at[n])
        )
    return out


def rows_kernel(count, places, saved, finish, meta, *refs):
    parts = len(places)
    pieces, strips, refs = refs[:count], refs[count : count + parts], refs[count + parts :]
    blocks, (slots, weight, piece_sems, weight_sems) = refs[:-4], refs[-4:]
    i = pl.program_id(0)

    def fetch(n):
        return pltpu.make_async_copy(pieces[n], slots.at[n % 2], piece_sems.at[n % 2])

    @pl.when(i == 0)
    def _():
        for copy in copies(strips, places, meta, weight, weight_sems):
            copy.start()
        fetch(0).start()

    for n in range(1, count):

        @pl.when(i + 1 == n)
        def _(n=n):
            fetch(n).start()

    @pl.when(i == 0)
    def _():
        for copy in copies(strips, places, meta, weight, weight_sems):
            copy.wait()

    for n in range(count):

        @pl.when(i == n)
        def _(n=n):
            fetch(n).wait()

    if saved:
        blocks, kept = blocks[:-1], blocks[-1]
        kept[...] = weight[pl.ds(pl.multiple_of(i * kept.shape[0], kept.shape[0]), kept.shape[0]), :]
    wide = min(512, weight.shape[1])

    @pl.loop(0, weight.shape[1] // wide)
    def _(n):
        at = pl.ds(pl.multiple_of(n * wide, wide), wide)
        finish(dot(slots[i % 2], weight[:, at]), at, *blocks)


def rows_matmul(name, meta, pieces, weight, finish, extra, outs, saved=0, after=()):
    strips, places = weight
    tall, depth = pieces[0].shape
    wide = max(column + a.shape[1] for a, (_, column) in zip(strips, places))
    count, parts = len(pieces), len(strips)
    block = lambda index: pl.BlockSpec((tall, wide), lambda i, m: (index(i), 0))
    more = [((saved, wide), BF16, pl.BlockSpec((saved // count, wide), lambda i, m: (i, 0)))] if saved else []
    return run(
        functools.partial(rows_kernel, count, places, saved, finish),
        name,
        (count,),
        meta,
        [(p, ANYWHERE) for p in pieces] + [(p, ANYWHERE) for p in strips] + [(a, block(f)) for a, f in extra],
        [((count * tall, wide), d, block(f)) for d, f in outs] + more,
        [
            pltpu.VMEM((2, tall, depth), BF16),
            pltpu.VMEM((depth, wide), BF16),
            pltpu.SemaphoreType.DMA((2,)),
            pltpu.SemaphoreType.DMA((parts,)),
        ],
        after,
    )


def store_rounded(value, at, out):
    out[:, at] = value.astype(BF16)


def store_gelu(value, at, back, hidden, back_before):
    below, density = gelu_parts(value)
    hidden[:, at] = (value * below).astype(BF16)
    back_before[:, at] = (back[:, at].astype(F32) * (below + value * density)).astype(BF16)


def same(i):
    return i


def term_kernel(places, half, far, meta, x, *refs):
    strips, refs = refs[: len(places)], refs[len(places) :]
    weight, sems = refs[-2:]
    i = pl.program_id(0)

    @pl.when(i == 0)
    def _():
        for copy in copies(strips, places, meta, weight, sems):
            copy.start()
        for copy in copies(strips, places, meta, weight, sems):
            copy.wait()

    wide = min(512, weight.shape[0])

    @pl.loop(0, weight.shape[0] // wide)
    def _(n):
        at = pl.ds(pl.multiple_of(n * wide, wide), wide)
        value = dot_last(x[...], weight[at, :])
        if far:
            refs[0][:, at] = value.astype(BF16)
        else:
            received, send, keep = refs[:3]
            value = (value + received[:, at].astype(F32)).astype(BF16)

            @pl.when(i < half)
            def _():
                send[:, at] = value

            @pl.when(i >= half)
            def _():
                keep[:, at] = value


def term(name, meta, x, weight, width, part, ranks, index, received=None, after=()):
    n = x.shape[1]
    strips, places = weight
    many = ranks // 2
    half = many // 2
    wide = lambda f: pl.BlockSpec((part, width), lambda i, m: (f(i), 0))
    turn = lambda i: jnp.where(i < half, 2 * i + 1, 2 * (i - half))
    if received is None:
        owner = lambda i: 2 * i + 1
        more, outs = [], [((many * part, width), BF16, wide(same))]
    else:
        owner = lambda i: 2 * turn(i)
        more = [(received, wide(turn))]
        outs = [
            ((half * part, width), BF16, wide(lambda i: jnp.minimum(i, half - 1))),
            ((half * part, width), BF16, wide(lambda i: jnp.maximum(i - half, 0))),
        ]
    return run(
        functools.partial(term_kernel, places, half, received is None),
        name,
        (many,),
        meta,
        [(x, pl.BlockSpec((part, n), lambda i, m: (index(owner(i)), 0)))] + [(s, ANYWHERE) for s in strips] + more,
        outs,
        [pltpu.VMEM((width, n), BF16), pltpu.SemaphoreType.DMA((len(strips),))],
        after,
    )


def finish_sum(send, keep, part, ranks):
    bit = 2
    while True:
        received = swap(send, "tensor", bit, ranks)
        if keep.shape[0] == part:
            return keep, received
        total = (keep.astype(F32) + received.astype(F32)).astype(BF16).reshape(-1, 2, part, keep.shape[1])
        keep, send = (total[:, n].reshape(-1, keep.shape[1]) for n in (0, 1))
        bit *= 2


def weight_grad_kernel(rows_a, rows_b, first, meta, *refs):
    count, many = len(rows_a), len(rows_b)
    left, right, refs = refs[:count], refs[count : count + many], refs[count + many :]
    out, slots, held, left_sems, right_sems = refs
    i = pl.program_id(0)
    steps = pl.num_programs(0)
    wide = slots.shape[2]

    def fetch(step, slot):
        at = pl.ds(pl.multiple_of(first + step * wide, wide), wide)
        return [
            pltpu.make_async_copy(ref.at[:, at], slots.at[slot, pl.ds(row, ref.shape[0])], left_sems.at[slot, n])
            for n, (ref, row) in enumerate(zip(left, rows_a))
        ]

    def fetch_right():
        return [
            pltpu.make_async_copy(right[n].at[pl.ds(source, tall)], held.at[pl.ds(row, tall)], right_sems.at[n])
            for n, (source, row, tall) in enumerate(rows_b)
        ]

    @pl.when(i == 0)
    def _():
        for copy in fetch(0, 0) + fetch_right():
            copy.start()

    @pl.when(i + 1 < steps)
    def _():
        for copy in fetch(i + 1, (i + 1) % 2):
            copy.start()

    @pl.when(i == 0)
    def _():
        for copy in fetch_right():
            copy.wait()

    for copy in fetch(i, i % 2):
        copy.wait()

    tile = min(512, held.shape[1])

    @pl.loop(0, held.shape[1] // tile)
    def _(n):
        at = pl.ds(pl.multiple_of(n * tile, tile), tile)
        out[:, at] = dot_first(slots[i % 2], held[:, at]).astype(BF16)


def weight_grad(name, meta, left, right, first, half, total, after=()):
    wide = min(512, half)
    n = right[0][0].shape[1]
    return run(
        functools.partial(weight_grad_kernel, [r for _, r in left], [r[1:] for r in right], first),
        name,
        (half // wide,),
        meta,
        [(a, ANYWHERE) for a, _ in left] + [(r[0], ANYWHERE) for r in right],
        [((half, n), BF16, pl.BlockSpec((wide, n), lambda i, m: (i, 0)))],
        [
            pltpu.VMEM((2, total, wide), BF16),
            pltpu.VMEM((total, n), BF16),
            pltpu.SemaphoreType.DMA((2, len(left))),
            pltpu.SemaphoreType.DMA((len(right),)),
        ],
        after,
    )[0]


def strip_at(p, place, strip):
    return pl.ds(pl.multiple_of((p ^ place) * strip, strip), strip)


def turned(ref, place, strip):
    return jnp.concatenate([ref[:, strip_at(p, place, strip)] for p in range(ref.shape[1] // strip)], axis=1)


def store_turned(ref, value, place, strip):
    for p in range(value.shape[1] // strip):
        ref[:, strip_at(p, place, strip)] = value[:, p * strip : (p + 1) * strip].astype(ref.dtype)


def gains_kernel(items, strip, meta, *refs):
    pieces, (turned_out, plain, stack) = refs[:-3], refs[-3:]
    groups, short = len(pieces), pieces[0].shape[1]
    for k in range(groups):
        stack[k] = pieces[k][...]
    for j in range(groups):
        plain[:, j * short : (j + 1) * short] = stack[j ^ meta[items + 1]]
    turned_out[...] = turned(plain, meta[items + 2], strip)


def cast_heads_kernel(meta, weight, inward, outward):
    inward[...] = weight[:, : 3 * HEAD_DIM].astype(BF16)
    outward[...] = weight[:, 3 * HEAD_DIM :].astype(BF16)


def cast_hidden_kernel(meta, weight, *outs):
    wide = outs[0].shape[1]
    for n, out in enumerate(outs):
        at = n % 2 * wide
        out[...] = weight[n // 2, :, at : at + wide].astype(BF16)


def first_norm_kernel(items, strip, meta, rows, gains, *outs):
    normed, _ = normalize(turned(rows, meta[items + 2], strip).astype(F32))
    for out in outs:
        out[...] = (normed * gains[0:1, :]).astype(BF16)


def turn_kernel(items, strip, meta, rows, *outs):
    for out in outs:
        out[...] = turned(rows, meta[items + 2], strip)


def add_kernel(meta, left, right, out):
    out[...] = left[...] + right[...]


def second_norm_kernel(items, strip, meta, rows, keep, received, gains, middle_out, *outs):
    middle = turned(rows, meta[items + 2], strip).astype(F32) + (
        keep[...].astype(F32) + received[...].astype(F32)
    )
    normed, _ = normalize(middle)
    middle_out[...] = middle
    for out in outs:
        out[...] = (normed * gains[1:2, :]).astype(BF16)


def second_back_kernel(middle, keep, received, back, gains, out, gain_out, *lows):
    normed, inverse = normalize(middle[...])
    given = keep[...].astype(F32) + received[...].astype(F32)
    grad, gain_part = normalize_back(given, normed, inverse, gains[1:2, :])
    grad = grad + back[...].astype(F32)
    out[...] = grad
    for low in lows:
        low[...] = grad.astype(BF16)

    @pl.when(pl.program_id(0) == 0)
    def _():
        gain_out[...] = jnp.zeros_like(gain_out)

    gain_out[...] += gain_part


def first_back_kernel(items, strip, meta, rows, gains, back, keep, received, out, gain_out):
    place = meta[items + 2]

    @pl.when(pl.program_id(0) == 0)
    def _():
        gain_out[...] = jnp.zeros_like(gain_out)

    normed, inverse = normalize(turned(rows, place, strip).astype(F32))
    given = keep[...].astype(F32) + received[...].astype(F32)
    grad, gain_part = normalize_back(given, normed, inverse, gains[0:1, :])
    gain_out[...] += gain_part
    store_turned(out, grad + back[...], place, strip)


def output_kernel(items, strip, meta, middle, keep, received, out):
    value = middle[...] + (keep[...].astype(F32) + received[...].astype(F32))
    store_turned(out, value, meta[items + 2], strip)


def gain_total_kernel(items, strip, meta, first, second, out):
    both = [jnp.sum(v, axis=0, keepdims=True) for v in (first[...], second[...])]
    store_turned(out, jnp.concatenate(both, axis=0), meta[items + 2], strip)


def adam_math(weight, grad, first, second, rate, decay):
    first = BETA_ONE * first + (1.0 - BETA_ONE) * grad
    second = BETA_TWO * second + (1.0 - BETA_TWO) * grad * grad
    scaled_first = first * (1.0 / (1.0 - BETA_ONE**STEP))
    scaled_second = second * (1.0 / (1.0 - BETA_TWO**STEP))
    update = scaled_first / (jnp.sqrt(scaled_second) + ADAM_EPS) + decay * weight
    return first, second, rate * update


def adam_kernel(join, counts, meta, *refs):
    parts, at = [], 0
    for count in counts:
        parts.append(join([r[...].astype(F32) for r in refs[at : at + count]]))
        at += count
    own, far, weight = parts
    first, second = refs[at : at + 2]
    moment, square, delta = refs[-3:]
    moment[...], square[...], change = adam_math(
        weight, own + far, first[...], second[...], INNER_RATE, WEIGHT_DECAY
    )
    delta[...] = change.astype(BF16)


def side_by_side(parts):
    return parts[0] if len(parts) == 1 else jnp.concatenate(parts, axis=1)


def by_head(parts):
    inward, outward = parts
    out = []
    for h in range(outward.shape[1] // HEAD_DIM):
        out += [
            inward[:, h * 3 * HEAD_DIM : (h + 1) * 3 * HEAD_DIM],
            outward[:, h * HEAD_DIM : (h + 1) * HEAD_DIM],
        ]
    return jnp.concatenate(out, axis=1)


def adam(name, meta, join, own, far, weight, first, second, part, filled=(), after=()):
    rows, wide = first.shape[2:]
    tall = min(64, rows)
    state = pl.BlockSpec((None, None, tall, wide), lambda i, m: (0, part, i, 0))
    ins = [(v, pl.BlockSpec((tall, v.shape[1]), lambda i, m: (i, 0))) for v in own + far + weight]
    ins += [(first, state), (second, state)]
    alias = {len(ins) + n: n for n in range(len(filled))}
    ins += [(v, ANYWHERE) for v in filled]
    return run(
        functools.partial(adam_kernel, join, [len(v) for v in (own, far, weight)]),
        name,
        (rows // tall,),
        meta,
        ins,
        [(first.shape, F32, state)] * 2
        + [((rows, wide), BF16, pl.BlockSpec((tall, wide), lambda i, m: (i, 0)))],
        (),
        after,
        alias,
    )


def outer_math(weight, change, momentum, average):
    velocity = OUTER_MOMENTUM * momentum + change
    master = weight - OUTER_RATE * (change + OUTER_MOMENTUM * velocity)
    trail = EMA_KEEP * average + (1.0 - EMA_KEEP) * master
    return velocity, trail, master


def outer_kernel(groups, meta, total, weight, momentum, average, *refs):
    change_out, velocity_out, trail_out, master_out, copy_out = refs[-5:]
    change = total[...].astype(F32) * (1.0 / groups)
    velocity, trail, master = outer_math(weight[...], change, momentum[...], average[...])
    change_out[...] = change
    velocity_out[...] = velocity
    trail_out[...] = trail
    master_out[...] = master
    copy_out[...] = master.astype(BF16)


def outer(name, meta, groups, total, weight, momentum, average, part, filled=(), after=()):
    tall, wide = min(64, weight.shape[1]), weight.shape[2]
    spec = pl.BlockSpec((tall, wide), lambda i, m: (i, 0))
    state = pl.BlockSpec((None, tall, wide), lambda i, m: (part, i, 0))
    ins = [(total, spec)] + [(v, state) for v in (weight, momentum, average)]
    alias = {len(ins) + n: n for n in range(len(filled))}
    return run(
        functools.partial(outer_kernel, groups),
        name,
        (weight.shape[1] // tall,),
        meta,
        ins + [(v, ANYWHERE) for v in filled],
        [(weight.shape, F32, state)] * 4 + [(weight.shape, BF16, state)],
        (),
        after,
        alias,
    )


def pause_kernel(meta, *refs):
    refs[-1][0] = 0


def pause(meta, *values, after=()):
    token = ((1,), jnp.int32, pl.BlockSpec(memory_space=pltpu.SMEM))
    out = run(
        pause_kernel, "pause", (1,), meta, [(v, ANYWHERE) for v in values],
        [(v.shape, v.dtype, ANYWHERE) for v in values] + [token], (), after, {n: n for n in range(len(values))},
    )
    line[:] = [out[-1]]
    return out[:-1]


def local(
    block_input,
    cotangent,
    lengths,
    weight_heads,
    weight_hidden,
    norm_gains,
    momentum_heads,
    momentum_hidden,
    momentum_gains,
    average_heads,
    average_hidden,
    average_gains,
    first_heads,
    first_hidden,
    first_gains,
    second_heads,
    second_hidden,
    second_gains,
):
    line.clear()
    groups, ranks = lax.axis_size("group"), lax.axis_size("tensor")
    group = lax.axis_index("group").astype(jnp.int32)
    shard = lax.axis_index("dp").astype(jnp.int32)
    rank = lax.axis_index("tensor").astype(jnp.int32)
    rows_here, width = block_input.shape
    total = rows_here * ranks
    strip = weight_heads.shape[0]
    half = width // 2
    heads = weight_heads.shape[1] // (4 * HEAD_DIM)
    units = weight_hidden.shape[2]
    quarter = units // 2
    items = lengths.shape[1]
    ends = jnp.cumsum(lengths[0]).astype(jnp.int32)
    meta = jnp.concatenate([ends, jnp.stack([rank, group, shard])])
    tall = math.gcd(rows_here, 64)
    steps = rows_here // tall
    order = range(groups)
    wait = functools.partial(pause, meta)
    whole = lambda a: pl.BlockSpec(a.shape, lambda *i: (0,) * a.ndim)
    both = pl.BlockSpec((2, width), lambda *i: (0, 0))
    row_block = pl.BlockSpec((tall, width), lambda i, m: (i, 0))
    row_shape = (rows_here, width)
    gain_block = pl.BlockSpec((8, width), lambda i, m: (0, 0))

    def near(value):
        return swap(value, "tensor", 1, ranks)

    def across(value):
        return swap(value, "dp", 1, 2)

    def gather_far(value):
        pieces = {0: value}
        bit = ranks // 2
        while bit > 1:
            pieces |= {k | bit: swap(v, "tensor", bit, ranks) for k, v in pieces.items()}
            bit //= 2
        return [pieces[k] for k in range(0, ranks, 2)]

    def ordered(even, odd):
        return [v for pair in zip(even, odd) for v in pair]

    gain_pieces = [norm_gains] + [swap(norm_gains, "group", k, groups) for k in order[1:]]
    strip_block = lambda w: pl.BlockSpec((strip // 2, w), lambda i, m: (i, 0))
    shards = run(
        cast_hidden_kernel, "cast_hidden", (2,), meta,
        [(weight_hidden, pl.BlockSpec((2, strip // 2, units), lambda i, m: (0, i, 0)))],
        [((strip, quarter), BF16, strip_block(quarter))] * 4,
    )
    gains, plain_gains = run(
        functools.partial(gains_kernel, items, half), "gains", (1,), meta,
        [(v, whole(v)) for v in gain_pieces],
        [((2, width), F32, both)] * 2,
        [pltpu.VMEM((groups, 2, width // groups), F32)],
    )
    column = lambda n: pl.BlockSpec((strip, n * HEAD_DIM), lambda h, m: (0, h))
    inward, outward = run(
        cast_heads_kernel, "cast_heads", (heads,), meta,
        [(weight_heads, column(4))],
        [((strip, heads * 3 * HEAD_DIM), BF16, column(3)), ((strip, heads * HEAD_DIM), BF16, column(1))],
    )
    strips = [inward] + [swap(inward, "group", k, groups) for k in order[1:]]
    crossed = [across(inward)]

    def along(value):
        return lax.all_gather(value, "group", axis=0, tiled=True)

    out_own = along(outward)
    lower_own = [along(v) for v in shards[2:]]
    raise_own = [along(v) for v in shards[:2]]

    def gather_near(even, copy):
        return [near(v) for v in even[1:]], near(copy)

    first_norm, copy = run(
        functools.partial(first_norm_kernel, items, half), "first_norm", (steps,), meta,
        [(block_input, row_block), (gains, both)],
        [(row_shape, BF16, row_block)] * 2,
    )
    even_one = gather_far(first_norm)
    wait()
    odd_first = near(wait(copy, after=crossed)[0])
    for k in order[1:]:
        wait()
        strips[k] = wait(strips[k], after=[odd_first] if k == 1 else [])[0]
        crossed.append(across(strips[k]))
    wait()
    even_one[1:] = wait(*even_one[1:], after=crossed[1:2])
    odd_one = [odd_first] + [near(v) for v in even_one[1:]]
    back_low, copy = run(
        functools.partial(turn_kernel, items, half), "turn", (steps,), meta,
        [(cotangent, row_block)], [(row_shape, BF16, row_block)] * 2,
    )
    even_back = gather_far(back_low)
    wait()
    out_own = wait(out_own, after=odd_one[1:] + crossed[2:3])[0]
    out_far = across(out_own)
    all_one = ordered(even_one, odd_one)
    rows_of = lambda off: [(lambda m, k=k: (m[items + 1] ^ k) * strip + off, 0) for k in order]
    inward_w = (strips + crossed, rows_of(0) + rows_of(half))

    def pair(own, far):
        parts, places, at = [], [], 0
        for a, b in zip(own, far):
            parts += [a, b]
            places += [(lambda m: 0, at), (lambda m: half, at)]
            at += a.shape[1]
        return parts, places

    triple, inward_own = rows_matmul(
        "qkv", meta, all_one, inward_w, store_rounded, [], [(BF16, same)], half
    )
    lower_own[0] = wait(lower_own[0])[0]
    lower_far = [across(lower_own[0])]
    mixed, logs = attend(meta, triple, items, rows_here, heads)
    lower_own[1], copy, *even_back[1:] = wait(lower_own[1], copy, *even_back[1:], after=[out_far])
    lower_far.append(across(lower_own[1]))
    odd_back = [near(copy)] + [near(v) for v in even_back[1:]]
    outward_w = pair([out_own], [out_far])

    def scatter(name, x, weight, after=()):
        far = near(term(name + "_far", meta, x, weight, width, rows_here, ranks, same)[0])
        wait(after=after)
        send, keep = term(name, meta, x, weight, width, rows_here, ranks, same, far)
        return finish_sum(send, keep, rows_here, ranks)

    keep, received = scatter("project", mixed, outward_w, odd_back)
    raise_own[0] = wait(raise_own[0])[0]
    raise_far = [across(raise_own[0])]
    lower_w = pair(lower_own, lower_far)
    all_back = ordered(even_back, odd_back)
    back_hidden = rows_matmul("back_hidden", meta, all_back, lower_w, store_rounded, [], [(BF16, same)])[0]
    raise_own[1] = wait(raise_own[1])[0]
    raise_far.append(across(raise_own[1]))
    raise_w = pair(raise_own, raise_far)
    middle, second_norm, copy = run(
        functools.partial(second_norm_kernel, items, half), "second_norm", (steps,), meta,
        [(block_input, row_block), (keep, row_block), (received, row_block), (gains, both)],
        [(row_shape, F32, row_block)] + [(row_shape, BF16, row_block)] * 2,
    )
    even_two = gather_far(second_norm)
    odd_first = near(copy)
    wait()
    wait(after=[odd_first])
    even_two[1:] = wait(*even_two[1:])
    odd_two = [odd_first] + [near(v) for v in even_two[1:]]
    wait()
    all_two = ordered(even_two, odd_two)

    hidden, back_before = rows_matmul(
        "raise", meta, all_two, raise_w, store_gelu, [(back_hidden, same)], [(BF16, same)] * 2
    )
    pieces = lambda values: [(v, k * rows_here) for k, v in enumerate(values)]

    def grad(name, left, right, first):
        return weight_grad(name, meta, pieces(left), [(right, 0, 0, total)], first, half, total)

    grad_lower_far = across(grad("lower_far", all_back, hidden, half))
    keep, received = scatter("back_second", back_before, raise_w)
    grad_raise_far = across(grad("raise_far", all_two, back_before, half))
    grad_lower = grad("lower_own", all_back, hidden, 0)
    grad_raise = grad("raise_own", all_two, back_before, 0)
    back_middle, gain_second, back_low_middle, copy = run(
        lambda meta, *refs: second_back_kernel(*refs), "second_back", (steps,), meta,
        [(v, row_block) for v in (middle, keep, received, back_low)] + [(gains, both)],
        [(row_shape, F32, row_block), ((8, width), F32, gain_block)] + [(row_shape, BF16, row_block)] * 2,
    )
    even_middle = gather_far(back_low_middle)
    odd_middle = [near(copy)]
    out_keep, out_received = scatter("lower", hidden, lower_w, odd_middle)

    def summed(delta):
        return lax.psum_scatter(delta, "group", scatter_dimension=0, tiled=True)

    moment_hidden, square_hidden, delta = adam(
        "adam_lower", meta, side_by_side, [grad_lower], [grad_lower_far], lower_own, first_hidden, second_hidden, 1
    )
    lower_delta = summed(delta)
    even_middle[1:] = wait(*even_middle[1:])
    odd_middle += [near(v) for v in even_middle[1:]]
    moment_hidden, square_hidden, delta = adam(
        "adam_raise", meta, side_by_side, [grad_raise], [grad_raise_far], raise_own, first_hidden, second_hidden, 0,
        (moment_hidden, square_hidden),
    )
    raise_delta = summed(delta)

    all_middle = ordered(even_middle, odd_middle)
    back_mixed = rows_matmul("back_mixed", meta, all_middle, outward_w, store_rounded, [], [(BF16, same)])[0]
    grad_out_far = across(grad("out_far", all_middle, mixed, half))
    back_triple = attend_back(meta, triple, mixed, back_mixed, logs, items, rows_here, heads)
    grad_in_far = across(grad("in_far", all_one, back_triple, half))
    keep, received = scatter("back_first", back_triple, inward_w)
    grad_in = grad("in_own", all_one, back_triple, 0)
    grad_out = grad("out_own", all_middle, mixed, 0)
    block_output = run(
        functools.partial(output_kernel, items, half), "output", (steps,), meta,
        [(v, row_block) for v in (middle, out_keep, out_received)],
        [(row_shape, BF16, row_block)],
    )[0]
    hidden_out = outer(
        "outer_lower", meta, groups, lower_delta, weight_hidden, momentum_hidden, average_hidden, 1
    )
    moment_heads, square_heads, delta = adam(
        "adam_heads", meta, by_head, [grad_in, grad_out], [grad_in_far, grad_out_far], [inward_own, out_own],
        first_heads[:, None], second_heads[:, None], 0,
    )
    heads_delta = summed(delta)
    input_grad, gain_first = run(
        functools.partial(first_back_kernel, items, half), "first_back", (steps,), meta,
        [(block_input, row_block), (gains, both)] + [(v, row_block) for v in (back_middle, keep, received)],
        [(row_shape, F32, row_block), ((8, width), F32, gain_block)],
    )
    gain_grad = run(
        functools.partial(gain_total_kernel, items, half), "gain_total", (1,), meta,
        [(v, whole(v)) for v in (gain_first, gain_second)],
        [((2, width), F32, both)],
    )[0]

    def added(value, other):
        wait()
        return run(
            add_kernel, "add", (1,), meta, [(value, whole(value)), (other, whole(other))],
            [(value.shape, F32, whole(value))],
        )[0]

    gain_grad = added(gain_grad, across(gain_grad))
    bit = 1
    while bit < ranks:
        gain_grad = added(gain_grad, swap(gain_grad, "tensor", bit, ranks))
        bit *= 2
    moment_gains, square_gains, delta_gains = adam_math(
        plain_gains, gain_grad, first_gains[0], second_gains[0], GAIN_RATE, 0.0
    )
    short = width // groups

    def gain_part(k):
        return lax.dynamic_slice_in_dim(delta_gains, (group ^ k) * short, short, 1)

    change_gains = gain_part(0)
    for k in order[1:]:
        change_gains = change_gains + swap(gain_part(k), "group", k, groups)
    change_gains = change_gains / groups
    velocity_gains, trail_gains, master_gains = outer_math(
        norm_gains, change_gains, momentum_gains, average_gains
    )
    change_hidden, velocity_hidden, trail_hidden, master_hidden, copy_hidden = outer(
        "outer_raise", meta, groups, raise_delta, weight_hidden, momentum_hidden, average_hidden, 0, hidden_out
    )
    change_heads, velocity_heads, trail_heads, master_heads, copy_heads = (
        v[0]
        for v in outer(
            "outer_heads", meta, groups, heads_delta, weight_heads[None], momentum_heads[None],
            average_heads[None], 0,
        )
    )
    return (
        block_output,
        input_grad,
        moment_heads[:, 0],
        moment_hidden,
        moment_gains[None],
        square_heads[:, 0],
        square_hidden,
        square_gains[None],
        change_heads,
        change_hidden,
        change_gains,
        velocity_heads,
        velocity_hidden,
        velocity_gains,
        trail_heads,
        trail_hidden,
        trail_gains,
        master_heads,
        master_hidden,
        master_gains,
        copy_heads,
        copy_hidden,
    )


def solution(mesh):
    rows = P(("group", "dp", "tensor"), None)
    heads, hidden, gains = P(("dp", "group"), "tensor"), P(None, ("dp", "group"), "tensor"), P(None, "group")
    states = (P("group", "dp", "tensor"), P("group", None, "dp", "tensor"), P("group", None, None))
    in_specs = (rows, rows, P(("group", "dp"), None)) + (heads, hidden, gains) * 3 + states * 2
    out_specs = (rows, rows) + states * 2 + (heads, hidden, gains) * 4 + (heads, hidden)
    return jax.shard_map(local, mesh=mesh, in_specs=in_specs, out_specs=out_specs, check_vma=False)
```

time: 2010 us -> 1070 us (0.53)
  Pallas kernels: 0 us -> 726 us
  waiting for transfers between devices: 949 us -> 223 us
  matrix products: 582 us -> 0 us
  local copies, waits for them, and re-layouts: 208 us -> 1.23 us
  other arithmetic: 182 us -> 4.2 us
  starting transfers between devices: 0.69 us -> 90.8 us
  blocking collectives: 35.6 us -> 0 us
  loops' own time: 25.3 us -> 0 us
    pallas_call x0 -> x69, Pallas kernels: none -> 726 us  [run(): pl.pallas_call(body, grid_spec=pltpu.PrefetchScalarGridSpec(num_scalar_pr...]
    dot_general x117 -> x0, matrix products: 582 us -> none  [the longest x4 86.9 us: contract_first(): lax.dot_general(left, right, (((0,), (0,)), ((), ())), preferred_element_...]
    all_gather x8 -> x5, waiting for transfers between devices: 492 us -> 0.05 us  [along(): return lax.all_gather(value, 'group', axis=0, tiled=True)]
    reduce_scatter x8 -> x3, waiting for transfers between devices: 456 us -> 28.9 us  [summed(): return lax.psum_scatter(delta, 'group', scatter_dimension=0, tiled=True)]
    ppermute x0 -> x45, waiting for transfers between devices: none -> 191 us  [swap(): return lax.ppermute(value, axis, [(i, i ^ bit) for i in range(size)])]
    convert_element_type x13 -> x0, other arithmetic: 91.6 us -> none  [the longest x1 31.6 us: local(): delta_hidden.astype(jnp.bfloat16)]
    ppermute x0 -> x45, starting transfers between devices: none -> 90.4 us  [swap(): return lax.ppermute(value, axis, [(i, i ^ bit) for i in range(size)])]
    unnamed x110 -> x14, local copies, waits for them, and re-layouts: 86.7 us -> 0.63 us
  transfers between devices with their start and end apart: 17 -> 53, of which waited for: 11 -> 18; matrix products, arithmetic and copies ran while one was open for 43% -> 0% of each run, Pallas kernels for 0% -> 60%
where the time goes in v1:
time: 1070 us; the launch traced here: 1060 us
  Pallas kernels  726 us (68%)
  waiting for transfers between devices  223 us (21%)
  starting transfers between devices  90.8 us (8%)
  between operations  15 us (1%)
    pallas_call x69, Pallas kernels, run(): pl.pallas_call(body, grid_spec=pltpu.PrefetchScalarGridSpec(num_scalar_pr...  726 us
    ppermute x45, waiting for transfers between devices, swap(): return lax.ppermute(value, axis, [(i, i ^ bit) for i in range(size)])  191 us
    ppermute x45, starting transfers between devices, swap(): return lax.ppermute(value, axis, [(i, i ^ bit) for i in range(size)])  90.4 us
    reduce_scatter x3, waiting for transfers between devices, summed(): return lax.psum_scatter(delta, 'group', scatter_dimension=0, tiled=True)  28.9 us
  transfers between devices with their start and end apart: 53, of which 18 were waited for; matrix products, arithmetic and copies ran while one was open for 0% of the time, Pallas kernels for 60%

profile of v1, /device:TPU:24, one launch (start us, length us, event | category | flops | bytes accessed | tf_op | source)
XLA Modules:
  0.0 1059.8 jit_solution(16008950653946290607)
XLA Ops:
  32.1 9.0 first_norm.1
  52.3 25.2 %collective-permute-done.8.refs_1_ = bf16[256,1536]{1,0:T(8,128)(2,1)} collective-permute-done((bf16[256,1536]{1,0:T(8,128)(2,1)}, bf16[256,1536]{1,0:T(8,128)(2,1)}, u32[]{:S(2)}, u32[]{:S(2)}) %collective-permute-start.8) | collective-permute-done | bytes 786464 | tf_op jit(solution)/shard_map/ppermute | solution.py:34
  81.1 27.7 %collective-permute-done.7.refs_1_ = bf16[256,1536]{1,0:T(8,128)(2,1)} collective-permute-done((bf16[256,1536]{1,0:T(8,128)(2,1)}, bf16[256,1536]{1,0:T(8,128)(2,1)}, u32[]{:S(2)}, u32[]{:S(2)}) %collective-permute-start.7) | collective-permute-done | bytes 786464 | tf_op jit(solution)/shard_map/ppermute | solution.py:34
  119.8 13.5 %collective-permute-done.9.refs_3_.refs_10_.refs_7_ = bf16[256,1536]{1,0:T(8,128)(2,1)} collective-permute-done((bf16[256,1536]{1,0:T(8,128)(2,1)}, bf16[256,1536]{1,0:T(8,128)(2,1)}, u32[]{:S(2)}, u32[]{:S(2)}) %collective-permute-start.9) | collective-permute-done | bytes 786464 | tf_op jit(solution)/shard_map/ppermute | solution.py:34
  135.2 8.5 turn.1
  146.5 5.4 collective-permute-done.11.refs_4_.refs_11_.refs_8_
  154.9 26.1 %qkv.1 = (bf16[2560,1536]{1,0:T(8,128)(2,1)}, bf16[1024,1536]{1,0:T(8,128)(2,1)}) custom-call(s32[11]{0:T(128)} %pad_add_fusion.refs_0_, bf16[640,2048]{1,0:T(8,128)(2,1)} %get-tuple-element.110.refs_1_, bf16[640,2048]{1,0:T(8,128)(2,1)} %collective-permute-done.4.refs_3_.refs_2_, bf16[640,2048]{1,0:T(8,128)(2,1)} %get-tuple-element.118.refs_3_, ...), custom_call_target="tpu_custom_call" | custom-call | flops 999999995904 | bytes 1 | tf_op jit(solution)/shard_map/qkv/pallas_call | solution.py:50
  183.3 55.1 %attend.1 = (bf16[2560,512]{1,0:T(8,128)(2,1)}, f32[4,5,8,512]{3,2,1,0:T(8,128)}) custom-call(s32[11]{0:T(128)} %pad_add_fusion.refs_0_, bf16[2560,1536]{1,0:T(8,128)(2,1)} %get-tuple-element.125.refs_2_.refs_1_, s32[1]{0:T(128)} %get-tuple-element.127.refs_2_), custom_call_target="tpu_custom_call" | custom-call | flops 999999995904 | bytes 1 | tf_op jit(solution)/shard_map/attend/pallas_call | solution.py:50
  239.7 27.8 %collective-permute-start.20 = (bf16[1024,1024]{1,0:T(8,128)(2,1)}, bf16[1024,1024]{1,0:T(8,128)(2,1)}, u32[]{:S(2)}, u32[]{:S(2)}) collective-permute-start(bf16[1024,1024]{1,0:T(8,128)(2,1)} %get-tuple-element.139.refs_7_.refs_4_), channel_id=1, source_target_pairs={{0,4},{4,0},{1,5},{5,1},{2,6},{6,2},{3,7},{7,3},{8,12},{12,8},{9,1... | collective-permute-start | bytes 6291464 | tf_op jit(solution)/shard_map/ppermute | solution.py:34
  267.9 9.8 project_far.1.refs_1_
  279.1 7.8 collective-permute-done.15.refs_4_
  286.9 12.3 %project.1 = (bf16[640,2048]{1,0:T(8,128)(2,1)}, bf16[640,2048]{1,0:T(8,128)(2,1)}) custom-call(s32[11]{0:T(128)} %pad_add_fusion.refs_0_, bf16[2560,512]{1,0:T(8,128)(2,1)} %get-tuple-element.128.refs_4_.refs_1_.refs_5_.refs_2_, bf16[1024,512]{1,0:T(8,128)(2,1)} %get-tuple-element.129.refs_2_.refs_5_.refs_6_, ...), custom_call_target="tpu_custom_call" | custom-call | flops 999999995904 | bytes 1 | tf_op jit(solution)/shard_map/project/pallas_call | solution.py:50
  303.0 7.8 collective-permute-done.20.refs_8_.refs_5_
  310.8 32.3 %back_hidden.1.refs_2_.refs_9_ = bf16[2560,2048]{1,0:T(8,128)(2,1)} custom-call(s32[11]{0:T(128)} %pad_add_fusion.refs_0_, bf16[640,2048]{1,0:T(8,128)(2,1)} %get-tuple-element.123.refs_1_.refs_4_, bf16[640,2048]{1,0:T(8,128)(2,1)} %collective-permute-done.16.refs_2_, bf16[640,2048]{1,0:T(8,128)(2,1)} %get-tuple-element.134.refs_3_, ...), custom_call_target="tpu_custom_call" | custom-call | flops 999999995904 | bytes 1 | tf_op jit(solution)/shard_map/back_hidden/pallas_call | solution.py:50
  346.9 12.2 %collective-permute-done.18.refs_3_ = bf16[640,2048]{1,0:T(8,128)(2,1)} collective-permute-done((bf16[640,2048]{1,0:T(8,128)(2,1)}, bf16[640,2048]{1,0:T(8,128)(2,1)}, u32[]{:S(2)}, u32[]{:S(2)}) %collective-permute-start.18) | collective-permute-done | bytes 2621472 | tf_op jit(solution)/shard_map/ppermute | solution.py:34
  359.1 12.0 %second_norm.1 = (f32[640,2048]{1,0:T(8,128)}, bf16[640,2048]{1,0:T(8,128)(2,1)}, bf16[640,2048]{1,0:T(8,128)(2,1)}) custom-call(s32[11]{0:T(128)} %pad_add_fusion.refs_0_, bf16[640,2048]{1,0:T(8,128)(2,1)} %refs_1_.13, bf16[640,2048]{1,0:T(8,128)(2,1)} %get-tuple-element.135.refs_2_, bf16[640,2048]{1,0:T(8,128)(2,1)} %collective-permute-done.18.refs_3_, ...), custom_call_target="tpu_custom_call" | custom-call | flops 999999995904 | bytes 1 | tf_op jit(solution)/shard_map/second_norm/pallas_call | solution.py:50
  378.1 53.8 %collective-permute-done.22.refs_1_ = bf16[640,2048]{1,0:T(8,128)(2,1)} collective-permute-done((bf16[640,2048]{1,0:T(8,128)(2,1)}, bf16[640,2048]{1,0:T(8,128)(2,1)}, u32[]{:S(2)}, u32[]{:S(2)}) %collective-permute-start.22) | collective-permute-done | bytes 2621472 | tf_op jit(solution)/shard_map/ppermute | solution.py:34
  439.1 52.8 %raise.1 = (bf16[2560,2048]{1,0:T(8,128)(2,1)}, bf16[2560,2048]{1,0:T(8,128)(2,1)}) custom-call(s32[11]{0:T(128)} %pad_add_fusion.refs_0_, bf16[640,2048]{1,0:T(8,128)(2,1)} %get-tuple-element.143.refs_1_, bf16[640,2048]{1,0:T(8,128)(2,1)} %collective-permute-done.21.refs_2_, bf16[640,2048]{1,0:T(8,128)(2,1)} %get-tuple-element.145.refs_3_, ...), custom_call_target="tpu_custom_call" | custom-call | flops 999999995904 | bytes 1 | tf_op jit(solution)/shard_map/raise/pallas_call | solution.py:50
  491.8 19.9 %lower_far.2.refs_6_ = bf16[1024,2048]{1,0:T(8,128)(2,1)} custom-call(s32[11]{0:T(128)} %pad_add_fusion.refs_0_, bf16[640,2048]{1,0:T(8,128)(2,1)} %get-tuple-element.123.refs_1_.refs_4_, bf16[640,2048]{1,0:T(8,128)(2,1)} %collective-permute-done.16.refs_2_, bf16[640,2048]{1,0:T(8,128)(2,1)} %get-tuple-element.134.refs_3_, ...), custom_call_target="tpu_custom_call" | custom-call | flops 999999995904 | bytes 1 | tf_op jit(solution)/shard_map/lower_far/pallas_call | solution.py:50
  511.9 20.3 %back_second_far.1.refs_1_ = bf16[1280,2048]{1,0:T(8,128)(2,1)} custom-call(s32[11]{0:T(128)} %pad_add_fusion.refs_0_, bf16[2560,2048]{1,0:T(8,128)(2,1)} %get-tuple-element.150.refs_1_.refs_5_, bf16[1024,1024]{1,0:T(8,128)(2,1)} %get-tuple-element.146.refs_5_.refs_2_.refs_3_, bf16[1024,1024]{1,0:T(8,128)(2,1)} %collective-permute-done.24.refs_6_.refs_3_, ...), custom_call_target="tpu_custom_call" | custom-call | flops 999999995904 | bytes 1 | tf_op jit(solution)/shard_map/back_second_far/pallas_call | solution.py:50
  533.5 7.7 collective-permute-done.26.refs_6_
  541.2 23.4 %back_second.1 = (bf16[640,2048]{1,0:T(8,128)(2,1)}, bf16[640,2048]{1,0:T(8,128)(2,1)}) custom-call(s32[11]{0:T(128)} %pad_add_fusion.refs_0_, bf16[2560,2048]{1,0:T(8,128)(2,1)} %get-tuple-element.150.refs_1_.refs_5_, bf16[1024,1024]{1,0:T(8,128)(2,1)} %get-tuple-element.146.refs_5_.refs_2_.refs_3_, ...), custom_call_target="tpu_custom_call" | custom-call | flops 999999995904 | bytes 1 | tf_op jit(solution)/shard_map/back_second/pallas_call | solution.py:50
  566.5 19.9 %raise_far.1.refs_6_ = bf16[1024,2048]{1,0:T(8,128)(2,1)} custom-call(s32[11]{0:T(128)} %pad_add_fusion.refs_0_, bf16[640,2048]{1,0:T(8,128)(2,1)} %get-tuple-element.143.refs_1_, bf16[640,2048]{1,0:T(8,128)(2,1)} %collective-permute-done.21.refs_2_, bf16[640,2048]{1,0:T(8,128)(2,1)} %get-tuple-element.145.refs_3_, ...), custom_call_target="tpu_custom_call" | custom-call | flops 999999995904 | bytes 1 | tf_op jit(solution)/shard_map/raise_far/pallas_call | solution.py:50
  588.4 19.9 %lower_own.1.refs_6_.refs_1_ = bf16[1024,2048]{1,0:T(8,128)(2,1)} custom-call(s32[11]{0:T(128)} %pad_add_fusion.refs_0_, bf16[640,2048]{1,0:T(8,128)(2,1)} %get-tuple-element.123.refs_1_.refs_4_, bf16[640,2048]{1,0:T(8,128)(2,1)} %collective-permute-done.16.refs_2_, bf16[640,2048]{1,0:T(8,128)(2,1)} %get-tuple-element.134.refs_3_, ...), custom_call_target="tpu_custom_call" | custom-call | flops 999999995904 | bytes 1 | tf_op jit(solution)/shard_map/lower_own/pallas_call | solution.py:50
  608.3 19.9 %raise_own.1.refs_6_.refs_1_ = bf16[1024,2048]{1,0:T(8,128)(2,1)} custom-call(s32[11]{0:T(128)} %pad_add_fusion.refs_0_, bf16[640,2048]{1,0:T(8,128)(2,1)} %get-tuple-element.143.refs_1_, bf16[640,2048]{1,0:T(8,128)(2,1)} %collective-permute-done.21.refs_2_, bf16[640,2048]{1,0:T(8,128)(2,1)} %get-tuple-element.145.refs_3_, ...), custom_call_target="tpu_custom_call" | custom-call | flops 999999995904 | bytes 1 | tf_op jit(solution)/shard_map/raise_own/pallas_call | solution.py:50
  628.3 14.1 %second_back.1 = (f32[640,2048]{1,0:T(8,128)}, f32[8,2048]{1,0:T(8,128)}, bf16[640,2048]{1,0:T(8,128)(2,1)}, bf16[640,2048]{1,0:T(8,128)(2,1)}) custom-call(s32[11]{0:T(128)} %pad_add_fusion.refs_0_, f32[640,2048]{1,0:T(8,128)} %get-tuple-element.142.refs_1_, bf16[640,2048]{1,0:T(8,128)(2,1)} %get-tuple-element.151.refs_2_, ...), custom_call_target="tpu_custom_call" | custom-call | flops 999999995904 | bytes 1 | tf_op jit(solution)/shard_map/second_back/pallas_call | solution.py:50
  642.8 20.0 %lower_far.3.refs_1_ = bf16[1280,2048]{1,0:T(8,128)(2,1)} custom-call(s32[11]{0:T(128)} %pad_add_fusion.refs_0_, bf16[2560,2048]{1,0:T(8,128)(2,1)} %get-tuple-element.149.refs_5_.refs_1_, bf16[1024,1024]{1,0:T(8,128)(2,1)} %get-tuple-element.138.refs_5_.refs_2_.refs_3_, bf16[1024,1024]{1,0:T(8,128)(2,1)} %collective-permute-done.19.refs_6_.refs_3_, ...), custom_call_target="tpu_custom_call" | custom-call | flops 999999995904 | bytes 1 | tf_op jit(solution)/shard_map/lower_far/pallas_call | solution.py:50
  664.2 7.6 collective-permute-done.28.refs_6_
  671.8 23.3 %lower.1 = (bf16[640,2048]{1,0:T(8,128)(2,1)}, bf16[640,2048]{1,0:T(8,128)(2,1)}) custom-call(s32[11]{0:T(128)} %pad_add_fusion.refs_0_, bf16[2560,2048]{1,0:T(8,128)(2,1)} %get-tuple-element.149.refs_5_.refs_1_, bf16[1024,1024]{1,0:T(8,128)(2,1)} %get-tuple-element.138.refs_5_.refs_2_.refs_3_, bf16[1024,1024]{1,0:T(8,128)(2,1)} %collective-permute-done.19.refs_6_.refs_3_, ...), custom_call_target="tpu_custom_call" | custom-call | flops 999999995904 | bytes 1 | tf_op jit(solution)/shard_map/lower/pallas_call | solution.py:50
  697.0 23.0 %adam_lower.1 = (f32[1,2,1024,2048]{3,2,1,0:T(8,128)}, f32[1,2,1024,2048]{3,2,1,0:T(8,128)}, bf16[1024,2048]{1,0:T(8,128)(2,1)}) custom-call(s32[11]{0:T(128)} %pad_add_fusion.refs_0_, bf16[1024,2048]{1,0:T(8,128)(2,1)} %lower_own.1.refs_6_.refs_1_, bf16[1024,2048]{1,0:T(8,128)(2,1)} %collective-permute-done.32.refs_2_, ...), custom_call_target="tpu_custom_call" | custom-call | flops 999999995904 | bytes 1 | tf_op jit(solution)/shard_map/adam_lower/pallas_call | solution.py:50
  721.4 23.9 %adam_raise.1 = (f32[1,2,1024,2048]{3,2,1,0:T(8,128)}, f32[1,2,1024,2048]{3,2,1,0:T(8,128)}, bf16[1024,2048]{1,0:T(8,128)(2,1)}) custom-call(s32[11]{0:T(128)} %pad_add_fusion.refs_0_, bf16[1024,2048]{1,0:T(8,128)(2,1)} %raise_own.1.refs_6_.refs_1_, ...), custom_call_target="tpu_custom_call", output_to_operand_aliasing={{0}: (7, {}), {1}: (8, {})} | custom-call | flops 999999995904 | bytes 1 | tf_op jit(solution)/shard_map/adam_raise/pallas_call | solution.py:50
  745.4 21.3 %back_mixed.1.refs_6_.refs_3_ = bf16[2560,512]{1,0:T(8,128)(2,1)} custom-call(s32[11]{0:T(128)} %pad_add_fusion.refs_0_, bf16[640,2048]{1,0:T(8,128)(2,1)} %get-tuple-element.157.refs_1_, bf16[640,2048]{1,0:T(8,128)(2,1)} %collective-permute-done.29.refs_2_, bf16[640,2048]{1,0:T(8,128)(2,1)} %get-tuple-element.159.refs_3_, ...), custom_call_target="tpu_custom_call" | custom-call | flops 999999995904 | bytes 1 | tf_op jit(solution)/shard_map/back_mixed/pallas_call | solution.py:50
  766.7 7.9 out_far.1.refs_5_
  775.0 45.2 %attend_back.1.refs_5_.refs_1_ = bf16[2560,1536]{1,0:T(8,128)(2,1)} custom-call(s32[11]{0:T(128)} %pad_add_fusion.refs_0_, bf16[2560,1536]{1,0:T(8,128)(2,1)} %get-tuple-element.125.refs_2_.refs_1_, bf16[2560,512]{1,0:T(8,128)(2,1)} %get-tuple-element.128.refs_4_.refs_1_.refs_5_.refs_2_, bf16[2560,512]{1,0:T(8,128)(2,1)} %back_mixed.1.refs_6_.refs_3_, ...), custom_call_target="tpu_custom_call" | custom-call | flops 999999995904 | bytes 1 | tf_op jit(solution)/shard_map/attend_back/pallas_call | solution.py:50
  820.2 15.9 %in_far.1.refs_10_ = bf16[1024,1536]{1,0:T(8,128)(2,1)} custom-call(s32[11]{0:T(128)} %pad_add_fusion.refs_0_, bf16[640,2048]{1,0:T(8,128)(2,1)} %get-tuple-element.110.refs_1_, bf16[640,2048]{1,0:T(8,128)(2,1)} %collective-permute-done.4.refs_3_.refs_2_, bf16[640,2048]{1,0:T(8,128)(2,1)} %get-tuple-element.118.refs_3_, ...), custom_call_target="tpu_custom_call" | custom-call | flops 999999995904 | bytes 1 | tf_op jit(solution)/shard_map/in_far/pallas_call | solution.py:50
  836.1 21.1 %collective-permute-start.37 = (bf16[1024,1536]{1,0:T(8,128)(2,1)}, bf16[1024,1536]{1,0:T(8,128)(2,1)}, u32[]{:S(2)}, u32[]{:S(2)}) collective-permute-start(bf16[1024,1536]{1,0:T(8,128)(2,1)} %in_far.1.refs_10_), channel_id=1, source_target_pairs={{0,4},{4,0},{1,5},{5,1},{2,6},{6,2},{3,7},{7,3},{8,12},{12,8},{9,1... | collective-permute-start | bytes 9437192 | tf_op jit(solution)/shard_map/ppermute | solution.py:34
  857.2 16.5 %back_first_far.1.refs_1_ = bf16[1280,2048]{1,0:T(8,128)(2,1)} custom-call(s32[11]{0:T(128)} %pad_add_fusion.refs_0_, bf16[2560,1536]{1,0:T(8,128)(2,1)} %attend_back.1.refs_5_.refs_1_, bf16[256,1536]{1,0:T(8,128)(2,1)} %get-tuple-element.109.refs_3_.refs_5_.refs_2_, bf16[256,1536]{1,0:T(8,128)(2,1)} %get-tuple-element.117.refs_6_.refs_3_, ...), custom_call_target="tpu_custom_call" | custom-call | flops 999999995904 | bytes 1 | tf_op jit(solution)/shard_map/back_first_far/pallas_call | solution.py:50
  875.0 7.8 collective-permute-done.35.refs_10_
  882.8 19.7 %back_first.1 = (bf16[640,2048]{1,0:T(8,128)(2,1)}, bf16[640,2048]{1,0:T(8,128)(2,1)}) custom-call(s32[11]{0:T(128)} %pad_add_fusion.refs_0_, bf16[2560,1536]{1,0:T(8,128)(2,1)} %attend_back.1.refs_5_.refs_1_, bf16[256,1536]{1,0:T(8,128)(2,1)} %get-tuple-element.109.refs_3_.refs_5_.refs_2_, bf16[256,1536]{1,0:T(8,128)(2,1)} %get-tuple-element.117.refs_6_.refs_3_, ...), custom_call_target="tpu_custom_call" | custom-call | flops 999999995904 | bytes 1 | tf_op jit(solution)/shard_map/back_first/pallas_call | solution.py:50
  903.0 15.9 %in_own.1.refs_6_.refs_1_ = bf16[1024,1536]{1,0:T(8,128)(2,1)} custom-call(s32[11]{0:T(128)} %pad_add_fusion.refs_0_, bf16[640,2048]{1,0:T(8,128)(2,1)} %get-tuple-element.110.refs_1_, bf16[640,2048]{1,0:T(8,128)(2,1)} %collective-permute-done.4.refs_3_.refs_2_, bf16[640,2048]{1,0:T(8,128)(2,1)} %get-tuple-element.118.refs_3_, ...), custom_call_target="tpu_custom_call" | custom-call | flops 999999995904 | bytes 1 | tf_op jit(solution)/shard_map/in_own/pallas_call | solution.py:50
  918.9 7.9 out_own.1.refs_4_.refs_2_
  926.8 9.1 output.1.refs_5_
  935.9 7.6 outer_lower.1
  943.5 23.4 %adam_heads.1 = (f32[1,1,1024,2048]{3,2,1,0:T(8,128)}, f32[1,1,1024,2048]{3,2,1,0:T(8,128)}, bf16[1024,2048]{1,0:T(8,128)(2,1)}) custom-call(s32[11]{0:T(128)} %pad_add_fusion.refs_0_, bf16[1024,1536]{1,0:T(8,128)(2,1)} %in_own.1.refs_6_.refs_1_, bf16[1024,512]{1,0:T(8,128)(2,1)} %out_own.1.refs_4_.refs_2_, ...), custom_call_target="tpu_custom_call" | custom-call | flops 999999995904 | bytes 1 | tf_op jit(solution)/shard_map/adam_heads/pallas_call | solution.py:50
  967.0 12.7 %first_back.1 = (f32[640,2048]{1,0:T(8,128)}, f32[8,2048]{1,0:T(8,128)}) custom-call(s32[11]{0:T(128)} %pad_add_fusion.refs_0_, bf16[640,2048]{1,0:T(8,128)(2,1)} %refs_1_.13, f32[2,2048]{1,0:T(2,128)} %get-tuple-element.108.refs_2_.refs_4_.refs_5_, f32[640,2048]{1,0:T(8,128)} %get-tuple-element.153.refs_6_.refs_3_, ...), custom_call_target="tpu_custom_call" | custom-call | flops 999999995904 | bytes 1 | tf_op jit(solution)/shard_map/first_back/pallas_call | solution.py:50
  1007.1 7.8 outer_raise.1
  1016.3 28.9 %reduce-scatter.6.cloned.1.call-done.refs_1_ = bf16[256,2048]{1,0:T(8,128)(2,1)} async-done(((bf16[1024,2048]{1,0:T(8,128)(2,1)}), bf16[256,2048]{1,0:T(8,128)(2,1)}) %reduce-scatter.6.cloned.1.call-update) | async-done | bytes 1048592 | tf_op jit(solution)/shard_map/reduce_scatter | solution.py:949
  1045.2 7.6 outer_heads.1
  (154 shorter events, 126.4 us)
Async XLA Ops:
  7.2 139.3 %all-gather.6.cloned.1.call-start = ((), (), s32[]{:S(2)}) async-start(), calls=%async_computation.3 | async-start | bytes 1310720 | tf_op jit(solution)/shard_map/all_gather | solution.py:842
  7.2 9.9 collective-permute-start.2
  7.3 9.9 collective-permute-start.1
  9.2 8.0 collective-permute-start
  23.5 157.6 %all-gather.8.cloned.1.call-start = ((), (), s32[]{:S(2)}) async-start(), calls=%async_computation.4 | async-start | bytes 2621440 | tf_op jit(solution)/shard_map/all_gather | solution.py:842
  24.2 214.2 %all-gather.10.cloned.1.call-start = ((), (), s32[]{:S(2)}) async-start(), calls=%async_computation.5 | async-start | bytes 2621440 | tf_op jit(solution)/shard_map/all_gather | solution.py:842
  25.0 276.7 %all-gather.14.cloned.1.call-start = ((), (), s32[]{:S(2)}) async-start(), calls=%async_computation.7 | async-start | bytes 2621440 | tf_op jit(solution)/shard_map/all_gather | solution.py:842
  25.5 317.6 %all-gather.12.cloned.1.call-start = ((), (), s32[]{:S(2)}) async-start(), calls=%async_computation.6 | async-start | bytes 2621440 | tf_op jit(solution)/shard_map/all_gather | solution.py:842
  26.1 909.8 %reduce-scatter.4.cloned.1.call-start = ((), (), s32[]{:S(2)}) async-start(), calls=%async_computation.8 | async-start | bytes 5242880 | tf_op jit(solution)/shard_map/reduce_scatter | solution.py:949
  26.2 51.3 %collective-permute-start.8 = (bf16[256,1536]{1,0:T(8,128)(2,1)}, bf16[256,1536]{1,0:T(8,128)(2,1)}, u32[]{:S(2)}, u32[]{:S(2)}) collective-permute-start(bf16[256,1536]{1,0:T(8,128)(2,1)} %get-tuple-element.109.refs_3_.refs_5_.refs_2_), channel_id=1, source_target_pairs={{0,8},{8,0},{16,24},{24,16},{1,9},{9,1},{17,25},{25,17},{2,10},{10... | collective-permute-start | bytes 2359304 | tf_op jit(solution)/shard_map/ppermute | solution.py:34
  26.3 82.5 %collective-permute-start.7 = (bf16[256,1536]{1,0:T(8,128)(2,1)}, bf16[256,1536]{1,0:T(8,128)(2,1)}, u32[]{:S(2)}, u32[]{:S(2)}) collective-permute-start(bf16[256,1536]{1,0:T(8,128)(2,1)} %get-tuple-element.109.refs_3_.refs_5_.refs_2_), channel_id=1, source_target_pairs={{0,16},{8,24},{16,0},{24,8},{1,17},{9,25},{17,1},{25,9},{2,18},{10... | collective-permute-start | bytes 2359304 | tf_op jit(solution)/shard_map/ppermute | solution.py:34
  26.9 87.1 %collective-permute-start.6 = (bf16[256,1536]{1,0:T(8,128)(2,1)}, bf16[256,1536]{1,0:T(8,128)(2,1)}, u32[]{:S(2)}, u32[]{:S(2)}) collective-permute-start(bf16[256,1536]{1,0:T(8,128)(2,1)} %get-tuple-element.109.refs_3_.refs_5_.refs_2_), channel_id=1, source_target_pairs={{0,24},{8,16},{16,8},{24,0},{1,25},{9,17},{17,9},{25,1},{2,26},{10... | collective-permute-start | bytes 2359304 | tf_op jit(solution)/shard_map/ppermute | solution.py:34
  30.6 17.9 %collective-permute-start.3 = (bf16[256,1536]{1,0:T(8,128)(2,1)}, bf16[256,1536]{1,0:T(8,128)(2,1)}, u32[]{:S(2)}, u32[]{:S(2)}) collective-permute-start(bf16[256,1536]{1,0:T(8,128)(2,1)} %get-tuple-element.109.refs_3_.refs_5_.refs_2_), channel_id=1, source_target_pairs={{0,4},{4,0},{1,5},{5,1},{2,6},{6,2},{3,7},{7,3},{8,12},{12,8},{9,1... | collective-permute-start | bytes 2359304 | tf_op jit(solution)/shard_map/ppermute | solution.py:34
  42.3 77.4 %collective-permute-start.5 = (bf16[640,2048]{1,0:T(8,128)(2,1)}, bf16[640,2048]{1,0:T(8,128)(2,1)}, u32[]{:S(2)}, u32[]{:S(2)}) collective-permute-start(bf16[640,2048]{1,0:T(8,128)(2,1)} %get-tuple-element.110.refs_1_), channel_id=1, source_target_pairs={{0,2},{1,3},{2,0},{3,1},{4,6},{5,7},{6,4},{7,5},{8,10},{9,11},{10,... | collective-permute-start | bytes 7864328 | tf_op jit(solution)/shard_map/ppermute | solution.py:34
  50.4 27.1 %collective-permute-start.4 = (bf16[640,2048]{1,0:T(8,128)(2,1)}, bf16[640,2048]{1,0:T(8,128)(2,1)}, u32[]{:S(2)}, u32[]{:S(2)}) collective-permute-start(bf16[640,2048]{1,0:T(8,128)(2,1)} %get-tuple-element.112), channel_id=1, source_target_pairs={{0,1},{1,0},{2,3},{3,2},{4,5},{5,4},{6,7},{7,6},{8,9},{9,8},{10,11... | collective-permute-start | bytes 7864328 | tf_op jit(solution)/shard_map/ppermute | solution.py:34
  112.5 20.9 %collective-permute-start.9 = (bf16[256,1536]{1,0:T(8,128)(2,1)}, bf16[256,1536]{1,0:T(8,128)(2,1)}, u32[]{:S(2)}, u32[]{:S(2)}) collective-permute-start(bf16[256,1536]{1,0:T(8,128)(2,1)} %get-tuple-element.117.refs_6_.refs_3_), channel_id=1, source_target_pairs={{0,4},{4,0},{1,5},{5,1},{2,6},{6,2},{3,7},{7,3},{8,12},{12,8},{9,1... | collective-permute-start | bytes 2359304 | tf_op jit(solution)/shard_map/ppermute | solution.py:34
  117.7 37.2 %collective-permute-start.12 = (bf16[256,1536]{1,0:T(8,128)(2,1)}, bf16[256,1536]{1,0:T(8,128)(2,1)}, u32[]{:S(2)}, u32[]{:S(2)}) collective-permute-start(bf16[256,1536]{1,0:T(8,128)(2,1)} %get-tuple-element.120.refs_8_.refs_5_), channel_id=1, source_target_pairs={{0,4},{4,0},{1,5},{5,1},{2,6},{6,2},{3,7},{7,3},{8,12},{12,8},{9,1... | collective-permute-start | bytes 2359304 | tf_op jit(solution)/shard_map/ppermute | solution.py:34
  118.3 33.6 %collective-permute-start.11 = (bf16[256,1536]{1,0:T(8,128)(2,1)}, bf16[256,1536]{1,0:T(8,128)(2,1)}, u32[]{:S(2)}, u32[]{:S(2)}) collective-permute-start(bf16[256,1536]{1,0:T(8,128)(2,1)} %get-tuple-element.119.refs_7_.refs_4_), channel_id=1, source_target_pairs={{0,4},{4,0},{1,5},{5,1},{2,6},{6,2},{3,7},{7,3},{8,12},{12,8},{9,1... | collective-permute-start | bytes 2359304 | tf_op jit(solution)/shard_map/ppermute | solution.py:34
  135.1 16.8 %collective-permute-start.10 = (bf16[640,2048]{1,0:T(8,128)(2,1)}, bf16[640,2048]{1,0:T(8,128)(2,1)}, u32[]{:S(2)}, u32[]{:S(2)}) collective-permute-start(bf16[640,2048]{1,0:T(8,128)(2,1)} %get-tuple-element.118.refs_3_), channel_id=1, source_target_pairs={{0,1},{1,0},{2,3},{3,2},{4,5},{5,4},{6,7},{7,6},{8,9},{9,8},{10,11... | collective-permute-start | bytes 7864328 | tf_op jit(solution)/shard_map/ppermute | solution.py:34
  144.9 93.6 %collective-permute-start.14 = (bf16[640,2048]{1,0:T(8,128)(2,1)}, bf16[640,2048]{1,0:T(8,128)(2,1)}, u32[]{:S(2)}, u32[]{:S(2)}) collective-permute-start(bf16[640,2048]{1,0:T(8,128)(2,1)} %get-tuple-element.123.refs_1_.refs_4_), channel_id=1, source_target_pairs={{0,2},{1,3},{2,0},{3,1},{4,6},{5,7},{6,4},{7,5},{8,10},{9,11},{10,... | collective-permute-start | bytes 7864328 | tf_op jit(solution)/shard_map/ppermute | solution.py:34
  153.7 84.7 %collective-permute-start.13 = (bf16[1024,512]{1,0:T(8,128)(2,1)}, bf16[1024,512]{1,0:T(8,128)(2,1)}, u32[]{:S(2)}, u32[]{:S(2)}) collective-permute-start(bf16[1024,512]{1,0:T(8,128)(2,1)} %get-tuple-element.129.refs_2_.refs_5_.refs_6_), channel_id=1, source_target_pairs={{0,4},{4,0},{1,5},{5,1},{2,6},{6,2},{3,7},{7,3},{8,12},{12,8},{9,1... | collective-permute-start | bytes 3145736 | tf_op jit(solution)/shard_map/ppermute | solution.py:34
  182.2 120.7 %collective-permute-start.19 = (bf16[1024,1024]{1,0:T(8,128)(2,1)}, bf16[1024,1024]{1,0:T(8,128)(2,1)}, u32[]{:S(2)}, u32[]{:S(2)}) collective-permute-start(bf16[1024,1024]{1,0:T(8,128)(2,1)} %get-tuple-element.138.refs_5_.refs_2_.refs_3_), channel_id=1, source_target_pairs={{0,4},{4,0},{1,5},{5,1},{2,6},{6,2},{3,7},{7,3},{8,12},{12,8},{9,1... | collective-permute-start | bytes 6291464 | tf_op jit(solution)/shard_map/ppermute | solution.py:34
  239.7 71.1 %collective-permute-start.20 = (bf16[1024,1024]{1,0:T(8,128)(2,1)}, bf16[1024,1024]{1,0:T(8,128)(2,1)}, u32[]{:S(2)}, u32[]{:S(2)}) collective-permute-start(bf16[1024,1024]{1,0:T(8,128)(2,1)} %get-tuple-element.139.refs_7_.refs_4_), channel_id=1, source_target_pairs={{0,4},{4,0},{1,5},{5,1},{2,6},{6,2},{3,7},{7,3},{8,12},{12,8},{9,1... | collective-permute-start | bytes 6291464 | tf_op jit(solution)/shard_map/ppermute | solution.py:34
  267.4 10.5 collective-permute-start.16
  267.4 10.5 collective-permute-start.17
  277.8 9.1 collective-permute-start.15
  299.1 60.0 %collective-permute-start.18 = (bf16[640,2048]{1,0:T(8,128)(2,1)}, bf16[640,2048]{1,0:T(8,128)(2,1)}, u32[]{:S(2)}, u32[]{:S(2)}) collective-permute-start(bf16[640,2048]{1,0:T(8,128)(2,1)} %get-tuple-element.136.refs_2_), channel_id=1, source_target_pairs={{0,2},{1,3},{2,0},{3,1},{4,6},{5,7},{6,4},{7,5},{8,10},{9,11},{10,... | collective-permute-start | bytes 7864328 | tf_op jit(solution)/shard_map/ppermute | solution.py:34
  302.8 132.8 %collective-permute-start.24 = (bf16[1024,1024]{1,0:T(8,128)(2,1)}, bf16[1024,1024]{1,0:T(8,128)(2,1)}, u32[]{:S(2)}, u32[]{:S(2)}) collective-permute-start(bf16[1024,1024]{1,0:T(8,128)(2,1)} %get-tuple-element.146.refs_5_.refs_2_.refs_3_), channel_id=1, source_target_pairs={{0,4},{4,0},{1,5},{5,1},{2,6},{6,2},{3,7},{7,3},{8,12},{12,8},{9,1... | collective-permute-start | bytes 6291464 | tf_op jit(solution)/shard_map/ppermute | solution.py:34
  344.3 91.3 %collective-permute-start.25 = (bf16[1024,1024]{1,0:T(8,128)(2,1)}, bf16[1024,1024]{1,0:T(8,128)(2,1)}, u32[]{:S(2)}, u32[]{:S(2)}) collective-permute-start(bf16[1024,1024]{1,0:T(8,128)(2,1)} %get-tuple-element.147.refs_7_.refs_4_), channel_id=1, source_target_pairs={{0,4},{4,0},{1,5},{5,1},{2,6},{6,2},{3,7},{7,3},{8,12},{12,8},{9,1... | collective-permute-start | bytes 6291464 | tf_op jit(solution)/shard_map/ppermute | solution.py:34
  372.2 59.7 %collective-permute-start.22 = (bf16[640,2048]{1,0:T(8,128)(2,1)}, bf16[640,2048]{1,0:T(8,128)(2,1)}, u32[]{:S(2)}, u32[]{:S(2)}) collective-permute-start(bf16[640,2048]{1,0:T(8,128)(2,1)} %get-tuple-element.143.refs_1_), channel_id=1, source_target_pairs={{0,2},{1,3},{2,0},{3,1},{4,6},{5,7},{6,4},{7,5},{8,10},{9,11},{10,... | collective-permute-start | bytes 7864328 | tf_op jit(solution)/shard_map/ppermute | solution.py:34
  511.8 185.2 %collective-permute-start.32 = (bf16[1024,2048]{1,0:T(8,128)(2,1)}, bf16[1024,2048]{1,0:T(8,128)(2,1)}, u32[]{:S(2)}, u32[]{:S(2)}) collective-permute-start(bf16[1024,2048]{1,0:T(8,128)(2,1)} %lower_far.2.refs_6_), channel_id=1, source_target_pairs={{0,4},{4,0},{1,5},{5,1},{2,6},{6,2},{3,7},{7,3},{8,12},{12,8},{9,1... | collective-permute-start | bytes 12582920 | tf_op jit(solution)/shard_map/ppermute | solution.py:34
  532.2 9.1 collective-permute-start.26
  564.6 63.6 %collective-permute-start.27 = (bf16[640,2048]{1,0:T(8,128)(2,1)}, bf16[640,2048]{1,0:T(8,128)(2,1)}, u32[]{:S(2)}, u32[]{:S(2)}) collective-permute-start(bf16[640,2048]{1,0:T(8,128)(2,1)} %get-tuple-element.152.refs_6_), channel_id=1, source_target_pairs={{0,2},{1,3},{2,0},{3,1},{4,6},{5,7},{6,4},{7,5},{8,10},{9,11},{10,... | collective-permute-start | bytes 7864328 | tf_op jit(solution)/shard_map/ppermute | solution.py:34
  586.4 135.0 %collective-permute-start.34 = (bf16[1024,2048]{1,0:T(8,128)(2,1)}, bf16[1024,2048]{1,0:T(8,128)(2,1)}, u32[]{:S(2)}, u32[]{:S(2)}) collective-permute-start(bf16[1024,2048]{1,0:T(8,128)(2,1)} %raise_far.1.refs_6_), channel_id=1, source_target_pairs={{0,4},{4,0},{1,5},{5,1},{2,6},{6,2},{3,7},{7,3},{8,12},{12,8},{9,1... | collective-permute-start | bytes 12582920 | tf_op jit(solution)/shard_map/ppermute | solution.py:34
  642.3 20.7 %collective-permute-start.29 = (bf16[640,2048]{1,0:T(8,128)(2,1)}, bf16[640,2048]{1,0:T(8,128)(2,1)}, u32[]{:S(2)}, u32[]{:S(2)}) collective-permute-start(bf16[640,2048]{1,0:T(8,128)(2,1)} %get-tuple-element.154), channel_id=1, source_target_pairs={{0,1},{1,0},{2,3},{3,2},{4,5},{5,4},{6,7},{7,6},{8,9},{9,8},{10,11... | collective-permute-start | bytes 7864328 | tf_op jit(solution)/shard_map/ppermute | solution.py:34
  642.4 77.6 %collective-permute-start.31 = (bf16[640,2048]{1,0:T(8,128)(2,1)}, bf16[640,2048]{1,0:T(8,128)(2,1)}, u32[]{:S(2)}, u32[]{:S(2)}) collective-permute-start(bf16[640,2048]{1,0:T(8,128)(2,1)} %get-tuple-element.157.refs_1_), channel_id=1, source_target_pairs={{0,2},{1,3},{2,0},{3,1},{4,6},{5,7},{6,4},{7,5},{8,10},{9,11},{10,... | collective-permute-start | bytes 7864328 | tf_op jit(solution)/shard_map/ppermute | solution.py:34
  662.8 9.1 collective-permute-start.28
  695.1 231.6 %collective-permute-start.30 = (bf16[640,2048]{1,0:T(8,128)(2,1)}, bf16[640,2048]{1,0:T(8,128)(2,1)}, u32[]{:S(2)}, u32[]{:S(2)}) collective-permute-start(bf16[640,2048]{1,0:T(8,128)(2,1)} %get-tuple-element.156.refs_7_), channel_id=1, source_target_pairs={{0,2},{1,3},{2,0},{3,1},{4,6},{5,7},{6,4},{7,5},{8,10},{9,11},{10,... | collective-permute-start | bytes 7864328 | tf_op jit(solution)/shard_map/ppermute | solution.py:34
  720.0 287.1 %reduce-scatter.8.cloned.1.call-start = ((), (), s32[]{:S(2)}) async-start(), calls=%async_computation.10 | async-start | bytes 5242880 | tf_op jit(solution)/shard_map/reduce_scatter | solution.py:949
  721.3 24.1 %collective-permute-start.33 = (bf16[640,2048]{1,0:T(8,128)(2,1)}, bf16[640,2048]{1,0:T(8,128)(2,1)}, u32[]{:S(2)}, u32[]{:S(2)}) collective-permute-start(bf16[640,2048]{1,0:T(8,128)(2,1)} %get-tuple-element.159.refs_3_), channel_id=1, source_target_pairs={{0,1},{1,0},{2,3},{3,2},{4,5},{5,4},{6,7},{7,6},{8,9},{9,8},{10,11... | collective-permute-start | bytes 7864328 | tf_op jit(solution)/shard_map/ppermute | solution.py:34
  745.3 299.9 %reduce-scatter.6.cloned.1.call-start = ((), (), s32[]{:S(2)}) async-start(), calls=%async_computation.9 | async-start | bytes 5242880 | tf_op jit(solution)/shard_map/reduce_scatter | solution.py:949
  774.6 168.9 %collective-permute-start.38 = (bf16[1024,512]{1,0:T(8,128)(2,1)}, bf16[1024,512]{1,0:T(8,128)(2,1)}, u32[]{:S(2)}, u32[]{:S(2)}) collective-permute-start(bf16[1024,512]{1,0:T(8,128)(2,1)} %out_far.1.refs_5_), channel_id=1, source_target_pairs={{0,4},{4,0},{1,5},{5,1},{2,6},{6,2},{3,7},{7,3},{8,12},{12,8},{9,1... | collective-permute-start | bytes 3145736 | tf_op jit(solution)/shard_map/ppermute | solution.py:34
  836.1 107.4 %collective-permute-start.37 = (bf16[1024,1536]{1,0:T(8,128)(2,1)}, bf16[1024,1536]{1,0:T(8,128)(2,1)}, u32[]{:S(2)}, u32[]{:S(2)}) collective-permute-start(bf16[1024,1536]{1,0:T(8,128)(2,1)} %in_far.1.refs_10_), channel_id=1, source_target_pairs={{0,4},{4,0},{1,5},{5,1},{2,6},{6,2},{3,7},{7,3},{8,12},{12,8},{9,1... | collective-permute-start | bytes 9437192 | tf_op jit(solution)/shard_map/ppermute | solution.py:34
  873.7 9.1 collective-permute-start.35
  902.5 64.4 %collective-permute-start.36 = (bf16[640,2048]{1,0:T(8,128)(2,1)}, bf16[640,2048]{1,0:T(8,128)(2,1)}, u32[]{:S(2)}, u32[]{:S(2)}) collective-permute-start(bf16[640,2048]{1,0:T(8,128)(2,1)} %get-tuple-element.164.refs_6_), channel_id=1, source_target_pairs={{0,2},{1,3},{2,0},{3,1},{4,6},{5,7},{6,4},{7,5},{8,10},{9,11},{10,... | collective-permute-start | bytes 7864328 | tf_op jit(solution)/shard_map/ppermute | solution.py:34
  1002.0 12.9 %collective-permute-start.42 = (f32[2,512]{1,0:T(2,128)}, f32[2,512]{1,0:T(2,128)}, u32[]{:S(2)}, u32[]{:S(2)}) collective-permute-start(f32[2,512]{1,0:T(2,128)} %get-tuple-element.199), channel_id=1, source_target_pairs={{0,8},{8,0},{16,24},{24,16},{1,9},{9,1},{17,25},{25,17},{2,10},{10... | collective-permute-start | bytes 12296 | tf_op jit(solution)/shard_map/ppermute | solution.py:34
  1002.0 12.9 %collective-permute-start.44 = (f32[2,512]{1,0:T(2,128)}, f32[2,512]{1,0:T(2,128)}, u32[]{:S(2)}, u32[]{:S(2)}) collective-permute-start(f32[2,512]{1,0:T(2,128)} %get-tuple-element.200), channel_id=1, source_target_pairs={{0,24},{8,16},{16,8},{24,0},{1,25},{9,17},{17,9},{25,1},{2,26},{10... | collective-permute-start | bytes 12296 | tf_op jit(solution)/shard_map/ppermute | solution.py:34
  1007.1 7.8 collective-permute-start.43
  (12 other events, 52.4 us)
Sparse Core Ops, SparseCore 0:
  23.6 47.9 all-gather.5
  73.8 72.0 all-gather.7
  148.0 44.6 all-gather.9
  194.7 44.6 all-gather.13
  241.4 44.7 all-gather.11
  720.1 87.7 reduce-scatter.3
  810.4 77.2 reduce-scatter.7
  967.1 78.0 reduce-scatter.5

commit v2 on v1

v2 whole, which is shorter than its diff:
```python
import functools
import math

import jax
import jax.numpy as jnp
from jax import lax
from jax.experimental import pallas as pl
from jax.experimental.pallas import tpu as pltpu
from jax.sharding import PartitionSpec as P

HEAD_DIM = 128
STEP = 8

NORM_EPS = 1e-05
INNER_RATE = 0.02
GAIN_RATE = 0.5
BETA_ONE = 0.9
BETA_TWO = 0.95
ADAM_EPS = 1e-08
WEIGHT_DECAY = 0.1
OUTER_RATE = 0.7
OUTER_MOMENTUM = 0.9
EMA_KEEP = 0.5

BF16 = jnp.bfloat16
F32 = jnp.float32
SCALE = HEAD_DIM ** (-0.5)
LOG2E = math.log2(math.e)
SCALE_LOG2 = SCALE * LOG2E
NEGATIVE = -1e30


def swap(value, axis, bit, size):
    return lax.ppermute(value, axis, [(i, i ^ bit) for i in range(size)])


ANYWHERE = pl.BlockSpec(memory_space=pl.ANY)
LIMIT = 60 * 2**20
line = []


def run(kernel, name, grid, meta, ins, outs, scratch=(), after=(), alias=None):
    arrays = [a for a, _ in ins]
    extra = [a for a in line + list(after) if all(a is not b for b in arrays)]
    count, skip = len(ins), len(extra)

    def body(*refs):
        kernel(*refs[: 1 + count], *refs[1 + count + skip :])

    result = pl.pallas_call(
        body,
        grid_spec=pltpu.PrefetchScalarGridSpec(
            num_scalar_prefetch=1,
            grid=grid,
            in_specs=[s for _, s in ins] + [ANYWHERE] * skip,
            out_specs=[s for _, _, s in outs],
            scratch_shapes=list(scratch),
        ),
        out_shape=[jax.ShapeDtypeStruct(s, d) for s, d, _ in outs],
        input_output_aliases={1 + a: b for a, b in (alias or {}).items()},
        compiler_params=pltpu.CompilerParams(vmem_limit_bytes=LIMIT),
        cost_estimate=pl.CostEstimate(flops=10**12, bytes_accessed=1, transcendentals=0),
        name=name,
    )(meta, *arrays, *extra)
    line[:] = [result[0]]
    return result


def dot_last(left, right):
    return lax.dot_general(
        left, right, (((1,), (1,)), ((), ())), preferred_element_type=F32
    )


def dot_first(left, right):
    return lax.dot_general(
        left, right, (((0,), (0,)), ((), ())), preferred_element_type=F32
    )


def dot(left, right):
    return jnp.dot(left, right, preferred_element_type=F32)


def normalize(rows):
    mean = jnp.mean(rows, axis=-1, keepdims=True)
    centred = rows - mean
    var = jnp.mean(centred * centred, axis=-1, keepdims=True)
    inverse = lax.rsqrt(var + NORM_EPS)
    return centred * inverse, inverse


def normalize_back(back, normed, inverse, gain):
    scaled = back * gain
    first = jnp.mean(scaled, axis=-1, keepdims=True)
    second = jnp.mean(scaled * normed, axis=-1, keepdims=True)
    terms = (back * normed).reshape(-1, 8, back.shape[-1])
    return inverse * (scaled - first - normed * second), jnp.sum(terms, axis=0)


def gelu_parts(u):
    size = jnp.abs(u) * (0.5**0.5)
    t = 1.0 / (1.0 + 0.3275911 * size)
    poly = t * (
        0.254829592
        + t * (-0.284496736 + t * (1.421413741 + t * (-1.453152027 + t * 1.061405429)))
    )
    bell = jnp.exp(-0.5 * u * u)
    tail = 0.5 * poly * bell
    below = jnp.where(u >= 0.0, 1.0 - tail, tail)
    return below, bell * (1.0 / math.sqrt(2.0 * math.pi))


def item_start(places, meta, items):
    start = jnp.zeros_like(places)
    for k in range(items):
        start = jnp.where(places >= meta[k], meta[k], start)
    return start


def copy_in(meta, items, source, target, rows, step, total):
    for s in range(total // step):
        owner, offset = (s * step) // rows, (s * step) % rows
        local = pl.multiple_of((owner ^ meta[items]) * rows + offset, step)
        target[s * step : (s + 1) * step, :] = source[pl.ds(local, step), :]


def local_row(meta, items, chunk, rows, step):
    per = rows // step
    owner, offset = chunk // per, chunk % per
    return pl.multiple_of((owner ^ meta[items]) * rows + offset * step, step)


def head_columns(n, c):
    return slice((3 * n + c) * HEAD_DIM, (3 * n + c + 1) * HEAD_DIM)


def attend_kernel(items, rows, step, block, pairs, meta, qkv, *refs):
    mixed, logs, nat, values, acc, top = refs[-6:]
    total = qkv.shape[0]
    index = pl.program_id(0)

    @pl.when(index == 0)
    def _():
        copy_in(meta, items, qkv, nat, rows, step, total)
        for n in range(pairs):
            values[n, :, 0:HEAD_DIM] = nat[:, head_columns(n, 2)]
            values[n, :, HEAD_DIM:] = jnp.ones((total, HEAD_DIM), BF16)

    first_row = index * block
    here = pl.ds(pl.multiple_of(first_row, block), block)
    acc[...] = jnp.zeros_like(acc)
    top[...] = jnp.full_like(top, NEGATIVE)
    low_start = item_start(first_row, meta, items)
    high_start = item_start(first_row + block - 1, meta, items)

    def tile(j, masked):
        at = pl.ds(pl.multiple_of(j * block, block), block)
        if masked:
            q_place = first_row + lax.broadcasted_iota(jnp.int32, (block, 1), 0)
            k_place = j * block + lax.broadcasted_iota(jnp.int32, (1, block), 1)
            live = (k_place <= q_place) & (k_place >= item_start(q_place, meta, items))
        scores = [dot_last(nat[here, head_columns(n, 0)], nat[at, head_columns(n, 1)]) for n in range(pairs)]
        for n in range(pairs):
            s = jnp.where(live, scores[n], NEGATIVE) if masked else scores[n]
            old = top[n]
            new = jnp.maximum(old, jnp.max(s, axis=1, keepdims=True))
            p = jnp.exp2((s - jnp.concatenate([new] * (block // HEAD_DIM), axis=1)) * SCALE_LOG2)
            keep = jnp.exp2((old - new) * SCALE_LOG2)
            top[n] = new
            acc[n] = acc[n] * jnp.concatenate([keep, keep], axis=1) + dot(p.astype(BF16), values[n, at, :])

    @pl.loop(low_start // block, index)
    def _(j):
        whole = high_start <= j * block

        @pl.when(whole)
        def _():
            tile(j, False)

        @pl.when(jnp.logical_not(whole))
        def _():
            tile(j, True)

    tile(index, True)
    per = block // step
    for n in range(pairs):
        weight = acc[n, :, HEAD_DIM:]
        out = (acc[n, :, 0:HEAD_DIM] / weight).astype(BF16)
        for c in range(per):
            at = local_row(meta, items, index * per + c, rows, step)
            mixed[pl.ds(at, step), n * HEAD_DIM : (n + 1) * HEAD_DIM] = out[c * step : (c + 1) * step, :]
        log = top[n] * SCALE_LOG2 + jnp.log(weight) * LOG2E
        logs[n, 0] = log.T[0:8, :]


def attend(meta, qkv, items, rows, heads, pairs, call, filled=(), after=()):
    total = qkv.shape[0]
    block = min(512, total)
    step = math.gcd(rows, block)
    count = total // block
    return run(
        functools.partial(attend_kernel, items, rows, step, block, pairs),
        "attend",
        (count,),
        meta,
        [(qkv, pl.BlockSpec((total, pairs * 3 * HEAD_DIM), lambda i, m: (0, call)))]
        + [(v, ANYWHERE) for v in filled],
        [
            ((total, heads * HEAD_DIM), BF16, pl.BlockSpec((total, pairs * HEAD_DIM), lambda i, m: (0, call))),
            ((heads, count, 8, block), F32, pl.BlockSpec((pairs, 1, 8, block), lambda i, m: (call, i, 0, 0))),
        ],
        [
            pltpu.VMEM((total, pairs * 3 * HEAD_DIM), BF16),
            pltpu.VMEM((pairs, total, 2 * HEAD_DIM), BF16),
            pltpu.VMEM((pairs, block, 2 * HEAD_DIM), F32),
            pltpu.VMEM((pairs, block, HEAD_DIM), F32),
        ],
        after,
        {1 + n: n for n in range(len(filled))},
    )


def attend_back_kernel(
    items, rows, step, block, pairs, meta, qkv, mixed, back, logs, grads, nat, nat_mixed, nat_back, dq, dk, dv
):
    total = qkv.shape[0]
    index = pl.program_id(0)
    own = [slice(n * HEAD_DIM, (n + 1) * HEAD_DIM) for n in range(pairs)]

    @pl.when(index == 0)
    def _():
        copy_in(meta, items, qkv, nat, rows, step, total)
        copy_in(meta, items, mixed, nat_mixed, rows, step, total)
        copy_in(meta, items, back, nat_back, rows, step, total)
        dk[...] = jnp.zeros_like(dk)
        dv[...] = jnp.zeros_like(dv)

    first_row = index * block
    here = pl.ds(pl.multiple_of(first_row, block), block)
    row_terms = []
    for n in range(pairs):
        product = nat_back[here, own[n]].astype(F32) * nat_mixed[here, own[n]].astype(F32)
        row_terms.append(jnp.sum(product.T, axis=0, keepdims=True))
    dq[...] = jnp.zeros_like(dq)
    low_start = item_start(first_row, meta, items)
    high_start = item_start(first_row + block - 1, meta, items)

    def tile(j, masked):
        at = pl.ds(pl.multiple_of(j * block, block), block)
        if masked:
            k_place = j * block + lax.broadcasted_iota(jnp.int32, (block, 1), 0)
            q_place = first_row + lax.broadcasted_iota(jnp.int32, (1, block), 1)
            live = (k_place <= q_place) & (k_place >= item_start(q_place, meta, items))
        scores = [dot_last(nat[at, head_columns(n, 1)], nat[here, head_columns(n, 0)]) for n in range(pairs)]
        backs = [dot_last(nat[at, head_columns(n, 2)], nat_back[here, own[n]]) for n in range(pairs)]
        for n in range(pairs):
            p = jnp.exp2(scores[n] * SCALE_LOG2 - logs[n, 0, 0:1, :])
            if masked:
                p = jnp.where(live, p, 0.0)
            s = (p * (backs[n] - row_terms[n])).astype(BF16)
            dv[at, own[n]] += dot(p.astype(BF16), nat_back[here, own[n]])
            dk[at, own[n]] += dot(s, nat[here, head_columns(n, 0)])
            dq[:, own[n]] += dot_first(s, nat[at, head_columns(n, 1)])

    @pl.loop(low_start // block, index)
    def _(j):
        whole = high_start <= j * block

        @pl.when(whole)
        def _():
            tile(j, False)

        @pl.when(jnp.logical_not(whole))
        def _():
            tile(j, True)

    tile(index, True)
    per = block // step
    for n in range(pairs):
        out = (dq[:, own[n]] * SCALE).astype(BF16)
        for c in range(per):
            to = local_row(meta, items, index * per + c, rows, step)
            grads[pl.ds(to, step), head_columns(n, 0)] = out[c * step : (c + 1) * step, :]

    @pl.when(index == pl.num_programs(0) - 1)
    def _():
        for s in range(total // step):
            to = local_row(meta, items, s, rows, step)
            part = slice(s * step, (s + 1) * step)
            for n in range(pairs):
                grads[pl.ds(to, step), head_columns(n, 1)] = (dk[part, own[n]] * SCALE).astype(BF16)
                grads[pl.ds(to, step), head_columns(n, 2)] = dv[part, own[n]].astype(BF16)


def attend_back(meta, qkv, mixed, back, logs, items, rows, heads, pairs, call, after=()):
    total = qkv.shape[0]
    block = logs.shape[-1]
    step = math.gcd(rows, block)
    count = total // block
    wide = pl.BlockSpec((total, pairs * 3 * HEAD_DIM), lambda i, m: (0, call))
    narrow = pl.BlockSpec((total, pairs * HEAD_DIM), lambda i, m: (0, call))
    return run(
        functools.partial(attend_back_kernel, items, rows, step, block, pairs),
        "attend_back",
        (count,),
        meta,
        [
            (qkv, wide),
            (mixed, narrow),
            (back, narrow),
            (logs, pl.BlockSpec((pairs, 1, 8, block), lambda i, m: (call, i, 0, 0))),
        ],
        [((total, pairs * 3 * HEAD_DIM), BF16, pl.BlockSpec((total, pairs * 3 * HEAD_DIM), lambda i, m: (0, 0)))],
        [
            pltpu.VMEM((total, pairs * 3 * HEAD_DIM), BF16),
            pltpu.VMEM((total, pairs * HEAD_DIM), BF16),
            pltpu.VMEM((total, pairs * HEAD_DIM), BF16),
            pltpu.VMEM((block, pairs * HEAD_DIM), F32),
            pltpu.VMEM((total, pairs * HEAD_DIM), F32),
            pltpu.VMEM((total, pairs * HEAD_DIM), F32),
        ],
        after,
    )[0]


TILE = 512


def tile_of(size):
    return next(tile for tile in (min(TILE, size), 384, 256, 128) if size % tile == 0)


def part_of(array, row=lambda m: 0, column=0, source_row=0, rows=None, source_column=0, columns=None):
    rows, columns = rows or array.shape[0] - source_row, columns or array.shape[1] - source_column
    return array, (row, column, source_row, rows, source_column, columns)


class Pieces:
    def __init__(self, refs, places, dim, target, sems, meta):
        self.refs, self.places, self.dim, self.target, self.sems, self.meta = refs, places, dim, target, sems, meta
        self.tile = tile_of(target.shape[dim])

    def span(self, p):
        row, column, _, rows, _, columns = self.places[p]
        first, size = (column, columns) if self.dim else (row(None), rows)
        return first // self.tile, size // self.tile

    def copy(self, p, n):
        row, column, source_row, rows, source_column, columns = self.places[p]
        tile = self.tile
        at = (n - self.span(p)[0]) * tile + (source_column if self.dim else source_row)
        at = pl.ds(pl.multiple_of(at, math.gcd(tile, source_column if self.dim else source_row)), tile)
        to = pl.ds(pl.multiple_of(n * tile, tile), tile)
        if self.dim:
            source = self.refs[p].at[pl.ds(source_row, rows), at]
            target = self.target.at[pl.ds(pl.multiple_of(row(self.meta), math.gcd(rows, TILE)), rows), to]
        else:
            source = self.refs[p].at[at, pl.ds(source_column, columns)]
            target = self.target.at[to, pl.ds(column, columns)]
        return pltpu.make_async_copy(source, target, self.sems.at[p, n])

    def start(self):
        for n in range(self.target.shape[self.dim] // self.tile):
            for p in range(len(self.refs)):
                first, count = self.span(p)
                if first <= n < first + count:
                    self.copy(p, n).start()

    def wait(self, n):
        for p in range(len(self.refs)):
            first, count = self.span(p)
            if isinstance(n, int):
                if first <= n < first + count:
                    self.copy(p, n).wait()
            elif first == 0 and count == self.target.shape[self.dim] // self.tile:
                self.copy(p, n).wait()
            else:

                @pl.when((n >= first) & (n < first + count))
                def _(p=p):
                    self.copy(p, n).wait()


def tiles_of(size):
    return size // tile_of(size)


def rows_kernel(count, places, use, saved, finish, staged, filled, meta, *refs):
    parts = len(places)
    pieces, strips, refs = refs[:count], refs[count : count + parts], refs[count + parts :]
    stages = refs[len(refs) - staged :]
    refs = refs[: len(refs) - staged]
    blocks, (slots, weight, piece_sems, weight_sems) = refs[:-4], refs[-4:]
    i = pl.program_id(0)
    parts = Pieces(strips, places, 1, weight, weight_sems, meta)

    def fetch(n):
        return pltpu.make_async_copy(pieces[n], slots.at[n % 2], piece_sems.at[n % 2])

    @pl.when(i == 0)
    def _():
        fetch(0).start()
        parts.start()

    for n in range(1, count):

        @pl.when(i + 1 == n)
        def _(n=n):
            fetch(n).start()

    for n in range(count):

        @pl.when(i == n)
        def _(n=n):
            fetch(n).wait()

    wide = tile_of(use)
    many, loaded = use // wide, weight.shape[1] // parts.tile
    early = wide != parts.tile
    if early or staged:

        @pl.when(i == 0)
        def _():
            for n in range(loaded):
                parts.wait(n)

    if staged:
        blocks = blocks[: len(blocks) - 2 - saved - filled] + blocks[len(blocks) - 2 - saved :]
        x = slots[i % 2]
        for n in range(many + 1):
            if n < many:
                stages[n % 2][...] = dot(x, weight[:, n * wide : (n + 1) * wide])
            if n:
                finish(
                    stages[(n - 1) % 2][...], slice((n - 1) * wide, n * wide), *blocks[: len(blocks) - saved]
                )
    else:

        @pl.loop(0, many)
        def _(n):
            if not early:

                @pl.when(i == 0)
                def _():
                    parts.wait(n)

            at = pl.ds(pl.multiple_of(n * wide, wide), wide)
            finish(dot(slots[i % 2], weight[:, at]), at, *blocks[: len(blocks) - saved])

        if not early and loaded > many:

            @pl.when(i == 0)
            def _():
                for n in range(many, loaded):
                    parts.wait(n)

    if saved:
        kept = blocks[-1]
        kept[...] = weight[pl.ds(pl.multiple_of(i * kept.shape[0], kept.shape[0]), kept.shape[0]), :]


def rows_matmul(
    name, meta, pieces, weight, finish, extra, outs, use=None, rows=None, saved=False, staged=False, filled=(),
    after=()
):
    strips, places = zip(*weight)
    tall, depth = pieces[0].shape
    wide = max(place[1] + place[5] for place in places)
    use = use or wide
    count, parts = len(pieces), len(strips)
    block = lambda index: pl.BlockSpec((tall, use), lambda i, m: (index(i), 0))
    more = [((depth, wide), BF16, pl.BlockSpec((depth // count, wide), lambda i, m: (i, 0)))] if saved else []
    ins = [(p, ANYWHERE) for p in pieces] + [(p, ANYWHERE) for p in strips] + [(a, block(f)) for a, f in extra]
    return run(
        functools.partial(rows_kernel, count, places, use, saved, finish, 2 * staged, len(filled)),
        name,
        (count,),
        meta,
        ins + [(v, ANYWHERE) for v in filled],
        [((rows or count * tall, use), d, block(f)) for d, f in outs] + more,
        [
            pltpu.VMEM((2, tall, depth), BF16),
            pltpu.VMEM((depth, wide), BF16),
            pltpu.SemaphoreType.DMA((2,)),
            pltpu.SemaphoreType.DMA((parts, tiles_of(wide))),
        ]
        + [pltpu.VMEM((tall, tile_of(use)), F32)] * (2 * staged),
        after,
        {len(ins) + n: n for n in range(len(filled))},
    )


def store_rounded(value, at, out):
    out[:, at] = value.astype(BF16)


def store_gelu(value, at, back, hidden, back_before):
    below, density = gelu_parts(value)
    hidden[:, at] = (value * below).astype(BF16)
    back_before[:, at] = (back[:, at].astype(F32) * (below + value * density)).astype(BF16)


def same(i):
    return i


def term_kernel(count, places, offset, part, meta, *refs):
    x, strips, refs = refs[:count], refs[count : count + len(places)], refs[count + len(places) :]
    received = refs[0] if len(refs) == 11 else None
    out, held, extra, tiles, weight, x_sems, extra_sems, tile_sems, sems, _ = refs[-10:]
    i = pl.program_id(0)
    parts = Pieces(strips, places, 0, weight, sems, meta)
    wide = parts.tile
    many = weight.shape[0] // wide
    own_rows = pl.ds(pl.multiple_of((4 * i + offset) * part, part), part)
    out_rows = pl.ds(pl.multiple_of(i * part, part), part)

    def load_x(n):
        at = sum(v.shape[1] for v in x[:n])
        to = held.at[:, at : at + x[n].shape[1]]
        return pltpu.make_async_copy(x[n].at[own_rows, :], to, x_sems.at[n])

    def load_extra(n):
        at = pl.ds(pl.multiple_of(n * wide, wide), wide)
        return pltpu.make_async_copy(received.at[out_rows, at], extra.at[n], extra_sems.at[n])

    def put(n):
        at = pl.ds(pl.multiple_of(n * wide, wide), wide)
        return pltpu.make_async_copy(tiles.at[n % 2], out.at[out_rows, at], tile_sems.at[n % 2])

    for n in range(count):
        load_x(n).start()

    @pl.when(i == 0)
    def _():
        parts.start()

    if received is not None:
        for n in range(many):
            load_extra(n).start()
    for n in range(count):
        load_x(n).wait()

    @pl.loop(0, many)
    def _(n):
        @pl.when(i == 0)
        def _():
            parts.wait(n)

        if received is not None:
            load_extra(n).wait()

        @pl.when(n > 1)
        def _():
            put(n - 2).wait()

        at = pl.ds(pl.multiple_of(n * wide, wide), wide)
        value = dot_last(held[...], weight[at, :])
        if received is not None:
            value = value + extra[n].astype(F32)
        tiles[n % 2] = value.astype(BF16)
        put(n).start()

    for n in range(max(many - 2, 0), many):
        put(n).wait()


def term(name, meta, x, weight, part, ranks, offset, received=None, after=()):
    strips, places = zip(*weight)
    n = sum(v.shape[1] for v in x)
    width = max(place[0](None) + place[3] for place in places)
    many, wide = tiles_of(width), tile_of(width)
    rows = ranks // 4 * part
    return run(
        functools.partial(term_kernel, len(x), places, offset, part),
        name,
        (ranks // 4,),
        meta,
        [(v, ANYWHERE) for v in x]
        + [(s, ANYWHERE) for s in strips]
        + ([] if received is None else [(received, ANYWHERE)]),
        [((rows, width), BF16, ANYWHERE)],
        [
            pltpu.VMEM((part, n), BF16),
            pltpu.VMEM((many, part, wide), BF16),
            pltpu.VMEM((2, part, wide), BF16),
            pltpu.VMEM((width, n), BF16),
            pltpu.SemaphoreType.DMA((len(x),)),
            pltpu.SemaphoreType.DMA((many,)),
            pltpu.SemaphoreType.DMA((2,)),
            pltpu.SemaphoreType.DMA((len(strips), many)),
            pltpu.SMEM((1,), jnp.int32),
        ],
        after,
    )[0]


def finish_sum(send, keep, part, ranks):
    bit = 2
    while True:
        received = swap(send, "tensor", bit, ranks)
        if keep.shape[0] == part:
            return keep, received
        total = (keep.astype(F32) + received.astype(F32)).astype(BF16).reshape(-1, 2, part, keep.shape[1])
        keep, send = (total[:, n].reshape(-1, keep.shape[1]) for n in (0, 1))
        bit *= 2


def weight_grad_kernel(rows_a, first, meta, *refs):
    count = len(rows_a)
    left, (right, out, slots, held, left_sems, right_sems) = refs[:count], refs[count:]
    i = pl.program_id(0)
    steps = pl.num_programs(0)
    wide = slots.shape[2]
    parts = Pieces([right], [part_of(right)[1]], 1, held, right_sems, meta)
    tile = parts.tile

    def fetch(step, slot):
        at = pl.ds(pl.multiple_of(first + step * wide, wide), wide)
        return [
            pltpu.make_async_copy(ref.at[:, at], slots.at[slot, pl.ds(row, ref.shape[0])], left_sems.at[slot, n])
            for n, (ref, row) in enumerate(zip(left, rows_a))
        ]

    @pl.when(i == 0)
    def _():
        for copy in fetch(0, 0):
            copy.start()
        parts.start()

    @pl.when(i + 1 < steps)
    def _():
        for copy in fetch(i + 1, (i + 1) % 2):
            copy.start()

    for copy in fetch(i, i % 2):
        copy.wait()

    @pl.loop(0, held.shape[1] // tile)
    def _(n):
        @pl.when(i == 0)
        def _():
            parts.wait(n)

        at = pl.ds(pl.multiple_of(n * tile, tile), tile)
        out[:, at] = dot_first(slots[i % 2], held[:, at]).astype(BF16)


def weight_grad(name, meta, left, right, first, half, after=()):
    wide = min(512, half)
    total, n = right.shape
    return run(
        functools.partial(weight_grad_kernel, [r for _, r in left], first),
        name,
        (half // wide,),
        meta,
        [(a, ANYWHERE) for a, _ in left] + [(right, ANYWHERE)],
        [((half, n), BF16, pl.BlockSpec((wide, n), lambda i, m: (i, 0)))],
        [
            pltpu.VMEM((2, total, wide), BF16),
            pltpu.VMEM((total, n), BF16),
            pltpu.SemaphoreType.DMA((2, len(left))),
            pltpu.SemaphoreType.DMA((1, tiles_of(n))),
        ],
        after,
    )[0]


def strip_at(p, place, strip):
    return pl.ds(pl.multiple_of((p ^ place) * strip, strip), strip)


def turned(ref, place, strip):
    return jnp.concatenate([ref[:, strip_at(p, place, strip)] for p in range(ref.shape[1] // strip)], axis=1)


def store_turned(ref, value, place, strip):
    for p in range(value.shape[1] // strip):
        ref[:, strip_at(p, place, strip)] = value[:, p * strip : (p + 1) * strip].astype(ref.dtype)


def gains_kernel(items, strip, meta, *refs):
    pieces, (turned_out, plain, stack) = refs[:-3], refs[-3:]
    groups, short = len(pieces), pieces[0].shape[1]
    for k in range(groups):
        stack[k] = pieces[k][...]
    for j in range(groups):
        plain[:, j * short : (j + 1) * short] = stack[j ^ meta[items + 1]]
    turned_out[...] = turned(plain, meta[items + 2], strip)


def cast_heads_kernel(meta, weight, *outs):
    heads = weight.shape[1] // (4 * HEAD_DIM)
    for out in outs:
        for h in range(heads):
            at, near, far = 4 * h * HEAD_DIM, 3 * h * HEAD_DIM, (3 * heads + h) * HEAD_DIM
            out[:, near : near + 3 * HEAD_DIM] = weight[:, at : at + 3 * HEAD_DIM].astype(BF16)
            out[:, far : far + HEAD_DIM] = weight[:, at + 3 * HEAD_DIM : at + 4 * HEAD_DIM].astype(BF16)


def cast_hidden_kernel(meta, weight, *outs):
    for n, out in enumerate(outs):
        wide = out.shape[1]
        out[...] = weight[int(n < 2), :, n % 2 * wide : (n % 2 + 1) * wide].astype(BF16)


def first_norm_kernel(items, strip, meta, rows, gains, *outs):
    normed, _ = normalize(turned(rows, meta[items + 2], strip).astype(F32))
    for out in outs:
        out[...] = (normed * gains[0:1, :]).astype(BF16)


def turn_kernel(items, strip, meta, rows, *outs):
    for out in outs:
        out[...] = turned(rows, meta[items + 2], strip)


def add_kernel(meta, left, right, out):
    out[...] = left[...] + right[...]


def second_norm_kernel(items, strip, meta, rows, keep, received, gains, middle_out, *outs):
    middle = turned(rows, meta[items + 2], strip).astype(F32) + (
        keep[...].astype(F32) + received[...].astype(F32)
    )
    normed, _ = normalize(middle)
    middle_out[...] = middle
    for out in outs:
        out[...] = (normed * gains[1:2, :]).astype(BF16)


def second_back_kernel(middle, keep, received, back, gains, out, gain_out, *lows):
    normed, inverse = normalize(middle[...])
    given = keep[...].astype(F32) + received[...].astype(F32)
    grad, gain_part = normalize_back(given, normed, inverse, gains[1:2, :])
    grad = grad + back[...].astype(F32)
    out[...] = grad
    for low in lows:
        low[...] = grad.astype(BF16)

    @pl.when(pl.program_id(0) == 0)
    def _():
        gain_out[...] = jnp.zeros_like(gain_out)

    gain_out[...] += gain_part


def first_back_kernel(items, strip, meta, rows, gains, back, keep, received, out, gain_out):
    place = meta[items + 2]

    @pl.when(pl.program_id(0) == 0)
    def _():
        gain_out[...] = jnp.zeros_like(gain_out)

    normed, inverse = normalize(turned(rows, place, strip).astype(F32))
    given = keep[...].astype(F32) + received[...].astype(F32)
    grad, gain_part = normalize_back(given, normed, inverse, gains[0:1, :])
    gain_out[...] += gain_part
    store_turned(out, grad + back[...], place, strip)


def output_kernel(items, strip, meta, middle, keep, received, out):
    value = middle[...] + (keep[...].astype(F32) + received[...].astype(F32))
    store_turned(out, value, meta[items + 2], strip)


def gain_total_kernel(items, strip, meta, first, second, out):
    both = [jnp.sum(v, axis=0, keepdims=True) for v in (first[...], second[...])]
    store_turned(out, jnp.concatenate(both, axis=0), meta[items + 2], strip)


def adam_math(weight, grad, first, second, rate, decay):
    first = BETA_ONE * first + (1.0 - BETA_ONE) * grad
    second = BETA_TWO * second + (1.0 - BETA_TWO) * grad * grad
    scaled_first = first * (1.0 / (1.0 - BETA_ONE**STEP))
    scaled_second = second * (1.0 / (1.0 - BETA_TWO**STEP))
    update = scaled_first / (jnp.sqrt(scaled_second) + ADAM_EPS) + decay * weight
    return first, second, rate * update


def adam_kernel(join, counts, groups, per, items, meta, *refs):
    parts, at = [], 0
    for count in counts:
        parts.append(join([r[...].astype(F32) for r in refs[at : at + count]]))
        at += count
    own, far, weight = parts
    first, second = refs[at : at + 2]
    moment, square, *deltas = refs[-2 - groups :]
    moment[...], square[...], change = adam_math(
        weight, own + far, first[...], second[...], INNER_RATE, WEIGHT_DECAY
    )
    change = change.astype(BF16)
    if groups == 1:
        deltas[0][...] = change
    else:
        step = lax.rem(pl.program_id(0) // per + groups - meta[items + 1], groups)
        for k in range(groups):

            @pl.when(step == k)
            def _(k=k):
                deltas[k][...] = change


def side_by_side(parts):
    return parts[0] if len(parts) == 1 else jnp.concatenate(parts, axis=1)


def by_head(parts):
    *inward, outward = parts
    out, h = [], 0
    for part in inward:
        for n in range(part.shape[1] // (3 * HEAD_DIM)):
            out += [
                part[:, n * 3 * HEAD_DIM : (n + 1) * 3 * HEAD_DIM],
                outward[:, h * HEAD_DIM : (h + 1) * HEAD_DIM],
            ]
            h += 1
    return jnp.concatenate(out, axis=1)


def adam(name, meta, items, join, own, far, weight, first, second, part, groups=1, filled=(), after=()):
    rows, columns = first.shape[2:]
    tall = min(128, rows // groups)
    per = rows // groups // tall
    state = pl.BlockSpec((None, None, tall, columns), lambda i, m: (0, part, i, 0))

    def delta_block(k):
        def index(i, m):
            return (i if groups == 1 else jnp.clip(i - lax.rem(m[items + 1] + k, groups) * per, 0, per - 1), 0)

        return ((rows // groups, columns), BF16, pl.BlockSpec((tall, columns), index))

    ins = [
        (v, pl.BlockSpec((tall, wide), lambda i, m, at=at: (i, at))) for v, wide, at in own + far + weight
    ]
    ins += [(first, state), (second, state)]
    alias = {len(ins) + n: n for n in range(len(filled))}
    ins += [(v, ANYWHERE) for v in filled]
    return run(
        functools.partial(adam_kernel, join, [len(v) for v in (own, far, weight)], groups, per, items),
        name,
        (rows // tall,),
        meta,
        ins,
        [(first.shape, F32, state)] * 2 + [delta_block(k) for k in range(groups)],
        (),
        after,
        alias,
    )


def outer_math(weight, change, momentum, average):
    velocity = OUTER_MOMENTUM * momentum + change
    master = weight - OUTER_RATE * (change + OUTER_MOMENTUM * velocity)
    trail = EMA_KEEP * average + (1.0 - EMA_KEEP) * master
    return velocity, trail, master


def outer_kernel(groups, count, meta, *refs):
    totals, (weight, momentum, average) = refs[:count], refs[count : count + 3]
    change_out, velocity_out, trail_out, master_out, copy_out = refs[-5:]
    total = totals[0][...].astype(F32)
    for other in totals[1:]:
        total = total + other[...].astype(F32)
    change = total * (1.0 / groups)
    velocity, trail, master = outer_math(weight[...], change, momentum[...], average[...])
    change_out[...] = change
    velocity_out[...] = velocity
    trail_out[...] = trail
    master_out[...] = master
    copy_out[...] = master.astype(BF16)


def outer(name, meta, groups, totals, weight, momentum, average, part, filled=(), after=()):
    tall, wide = min(64, weight.shape[1]), weight.shape[2]
    spec = pl.BlockSpec((tall, wide), lambda i, m: (i, 0))
    state = pl.BlockSpec((None, tall, wide), lambda i, m: (part, i, 0))
    ins = [(v, spec) for v in totals] + [(v, state) for v in (weight, momentum, average)]
    alias = {len(ins) + n: n for n in range(len(filled))}
    return run(
        functools.partial(outer_kernel, groups, len(totals)),
        name,
        (weight.shape[1] // tall,),
        meta,
        ins + [(v, ANYWHERE) for v in filled],
        [(weight.shape, F32, state)] * 4 + [(weight.shape, BF16, state)],
        (),
        after,
        alias,
    )


def pause_kernel(meta, *refs):
    refs[-1][0] = 0


def pause(meta, *values, after=()):
    token = ((1,), jnp.int32, pl.BlockSpec(memory_space=pltpu.SMEM))
    out = run(
        pause_kernel, "pause", (1,), meta, [(v, ANYWHERE) for v in values],
        [(v.shape, v.dtype, ANYWHERE) for v in values] + [token], (), after, {n: n for n in range(len(values))},
    )
    line[:] = [out[-1]]
    return out[:-1]


def local(
    block_input,
    cotangent,
    lengths,
    weight_heads,
    weight_hidden,
    norm_gains,
    momentum_heads,
    momentum_hidden,
    momentum_gains,
    average_heads,
    average_hidden,
    average_gains,
    first_heads,
    first_hidden,
    first_gains,
    second_heads,
    second_hidden,
    second_gains,
):
    line.clear()
    groups, ranks = lax.axis_size("group"), lax.axis_size("tensor")
    group = lax.axis_index("group").astype(jnp.int32)
    shard = lax.axis_index("dp").astype(jnp.int32)
    rank = lax.axis_index("tensor").astype(jnp.int32)
    rows_here, width = block_input.shape
    total = rows_here * ranks
    strip = weight_heads.shape[0]
    half = width // 2
    heads = weight_heads.shape[1] // (4 * HEAD_DIM)
    units = weight_hidden.shape[2]
    items = lengths.shape[1]
    ends = jnp.cumsum(lengths[0]).astype(jnp.int32)
    meta = jnp.concatenate([ends, jnp.stack([rank, group, shard])])
    tall = math.gcd(rows_here, 160)
    steps = rows_here // tall
    wait = functools.partial(pause, meta)
    whole = lambda a: pl.BlockSpec(a.shape, lambda *i: (0,) * a.ndim)
    both = pl.BlockSpec((2, width), lambda *i: (0, 0))
    row_block = pl.BlockSpec((tall, width), lambda i, m: (i, 0))
    row_shape = (rows_here, width)
    gain_block = pl.BlockSpec((8, width), lambda i, m: (0, 0))

    def near(value):
        return swap(value, "tensor", 1, ranks)

    def across(value):
        return swap(value, "dp", 1, 2)

    def gather_far(value):
        pieces = {0: value}
        bit = ranks // 2
        while bit > 1:
            pieces |= {k | bit: swap(v, "tensor", bit, ranks) for k, v in pieces.items()}
            bit //= 2
        return [pieces[k] for k in range(0, ranks, 2)]

    def ordered(even, odd):
        return [v for pair in zip(even, odd) for v in pair]

    def gather_near(even, copy):
        return [near(copy)] + [near(v) for v in even[1:]]

    def scatter(name, x, weight):
        product = lambda n, received=None: term(
            f"{name}_{n}", meta, x, weight, rows_here, ranks, n, received
        )
        far_send = near(product(3))
        far_keep = near(product(1))
        send = product(2, far_send)
        keep = product(0, far_keep)
        return finish_sum(send, keep, rows_here, ranks)

    def along(value):
        return lax.ppermute(value, "group", [(i, (i + 1) % groups) for i in range(groups)])

    def row_parts(own, far):
        return [
            part_of(v, lambda m, k=k, at=at: lax.rem(m[items + 1] + groups - k, groups) * strip + at)
            for k, both_halves in enumerate(zip(own, far)) for at, v in zip((0, half), both_halves)
        ]

    gain_pieces = [norm_gains] + [swap(norm_gains, "group", k, groups) for k in range(1, groups)]
    tall_strip = pl.BlockSpec((strip // 2, heads * 4 * HEAD_DIM), lambda i, m: (i, 0))
    strips = list(run(
        cast_heads_kernel, "cast_heads", (2,), meta, [(weight_heads, tall_strip)],
        [((strip, heads * 4 * HEAD_DIM), BF16, tall_strip)],
    ))
    strips.append(along(strips[0]))
    crossed = [across(strips[0])]
    gains, plain_gains = run(
        functools.partial(gains_kernel, items, half), "gains", (1,), meta,
        [(v, whole(v)) for v in gain_pieces],
        [((2, width), F32, both)] * 2,
        [pltpu.VMEM((groups, 2, width // groups), F32)],
    )
    first_norm, copy = run(
        functools.partial(first_norm_kernel, items, half), "first_norm", (steps,), meta,
        [(block_input, row_block), (gains, both)],
        [(row_shape, BF16, row_block)] * 2,
    )
    even_one = gather_far(first_norm)
    quarter = units // 2
    strip_block = pl.BlockSpec((strip // 2, quarter), lambda i, m: (i, 0))
    shards = run(
        cast_hidden_kernel, "cast_hidden", (2,), meta,
        [(weight_hidden, pl.BlockSpec((2, strip // 2, units), lambda i, m: (0, i, 0)))],
        [((strip, quarter), BF16, strip_block)] * 4,
    )
    odd_first = near(wait(copy, after=crossed)[0])
    back_low, back_copy = run(
        functools.partial(turn_kernel, items, half), "turn", (steps,), meta,
        [(cotangent, row_block)], [(row_shape, BF16, row_block)] * 2,
    )
    strips[1] = wait(strips[1], after=[odd_first])[0]
    strips.append(along(strips[1]))
    crossed.append(across(strips[1]))
    wait()
    strips[2] = wait(strips[2], after=crossed[1:])[0]
    strips.append(along(strips[2]))
    crossed.append(across(strips[2]))
    wait()
    even_one[1:] = wait(*even_one[1:], after=crossed[2:])
    odd_one = [odd_first] + [near(v) for v in even_one[1:]]
    strips[3] = wait(strips[3])[0]
    crossed.append(across(strips[3]))
    def gathered(shard, after=()):
        return lax.all_gather(wait(shard, after=after)[0], "group", axis=0, tiled=True)

    def columns(own, far):
        return [
            part_of(v, lambda m, at=at: at, n * quarter)
            for n in range(2) for at, v in ((0, own[n]), (half, far[n]))
        ]

    lower_own = [gathered(shards[0], odd_one[1:])]
    back_low = wait(back_low)[0]
    even_back = gather_far(back_low)
    all_one = ordered(even_one, odd_one)
    triple, heads_all = rows_matmul(
        "qkv", meta, all_one, row_parts(strips, crossed), store_rounded, [], [(BF16, same)],
        use=heads * 3 * HEAD_DIM, saved=True,
    )
    inward_w = [part_of(heads_all, columns=heads * 3 * HEAD_DIM)]
    outward_w = [part_of(heads_all, source_column=heads * 3 * HEAD_DIM)]
    lower_own.append(gathered(shards[1]))
    lower_own[0] = wait(lower_own[0])[0]
    lower_far = [across(lower_own[0])]
    pairs = 2 if heads % 2 == 0 else 1
    calls = heads // pairs
    mixed, logs = attend(meta, triple, items, rows_here, heads, pairs, 0)
    raise_own = [gathered(shards[2])]
    for n in range(1, calls):
        mixed, logs = attend(meta, triple, items, rows_here, heads, pairs, n, (mixed, logs))
    lower_own[1] = wait(lower_own[1], after=lower_far)[0]
    lower_far.append(across(lower_own[1]))
    back_copy, *even_back[1:] = wait(back_copy, *even_back[1:])
    odd_back = gather_near(even_back, back_copy)
    raise_own.append(gathered(shards[3]))
    wait(after=odd_back)
    keep, received = scatter("project", [mixed], outward_w)
    raise_own[0] = wait(raise_own[0])[0]
    raise_far = [across(raise_own[0])]
    middle, second_norm = run(
        functools.partial(second_norm_kernel, items, half), "second_norm", (steps,), meta,
        [(block_input, row_block), (keep, row_block), (received, row_block), (gains, both)],
        [(row_shape, F32, row_block), (row_shape, BF16, row_block)],
    )
    even_two = gather_far(second_norm)
    odd_first = near(second_norm)
    raise_own[1] = wait(raise_own[1])[0]
    raise_far.append(across(raise_own[1]))
    raise_w = columns(raise_own, raise_far)
    all_back = ordered(even_back, odd_back)
    back_hidden, lower_all = rows_matmul(
        "back_hidden", meta, all_back, columns(lower_own, lower_far), store_rounded, [], [(BF16, same)], saved=True
    )
    lower_w = [part_of(lower_all)]
    wait(after=[odd_first])

    def feed(pieces, first, filled=()):
        return rows_matmul(
            "raise", meta, pieces, raise_w, store_gelu, [(back_hidden, lambda i: i + first)],
            [(BF16, lambda i: i + first)] * 2, rows=total, staged=True, filled=filled,
        )

    filled = feed([even_two[0], odd_first], 0)
    even_two[1:] = wait(*even_two[1:])
    odd_two = [odd_first] + [near(v) for v in even_two[1:]]
    wait()
    all_two = ordered(even_two, odd_two)
    hidden, back_before = feed(all_two[2:], 2, filled)
    pieces = lambda values: [(v, k * rows_here) for k, v in enumerate(values)]

    def grad(name, left, right, first):
        return weight_grad(name, meta, pieces(left), right, first, half)

    grad_lower_far = across(grad("lower_far", all_back, hidden, half))
    keep, received = scatter("back_second", [back_before], raise_w)
    grad_raise_far = across(grad("raise_far", all_two, back_before, half))
    grad_lower = grad("lower_own", all_back, hidden, 0)
    back_middle, gain_second, back_low_middle = run(
        lambda meta, *refs: second_back_kernel(*refs), "second_back", (steps,), meta,
        [(v, row_block) for v in (middle, keep, received, back_low)] + [(gains, both)],
        [(row_shape, F32, row_block), ((8, width), F32, gain_block), (row_shape, BF16, row_block)],
    )
    even_middle = gather_far(back_low_middle)
    odd_first = near(back_low_middle)
    grad_raise = grad("raise_own", all_two, back_before, 0)
    wait(after=[odd_first])
    out_keep, out_received = scatter("lower", [hidden], lower_w)

    def summed(delta):
        return lax.psum_scatter(delta, "group", scatter_dimension=0, tiled=True)

    def adam_hidden(name, own, far, weight, part, filled=()):
        moment, square, delta = adam(
            name, meta, items, side_by_side, [(own, units, 0)], [(far, units, 0)],
            [(v, v.shape[1], 0) for v in weight],
            first_hidden, second_hidden, part, filled=filled,
        )
        return moment, square, summed(delta)

    *states, lower_delta = adam_hidden("adam_lower", grad_lower, grad_lower_far, [lower_all], 1)
    even_middle[1:] = wait(*even_middle[1:])
    odd_middle = [odd_first] + [near(v) for v in even_middle[1:]]
    wait()

    all_middle = ordered(even_middle, odd_middle)
    back_mixed = rows_matmul("back_mixed", meta, all_middle, outward_w, store_rounded, [], [(BF16, same)])[0]
    grad_out_far = across(grad("out_far", all_middle, mixed, half))
    moment_hidden, square_hidden, raise_delta = adam_hidden(
        "adam_raise", grad_raise, grad_raise_far, raise_own, 0, tuple(states)
    )
    back_triples, grad_in_fars = [], []
    for n in range(calls):
        back_triples.append(
            attend_back(meta, triple, mixed, back_mixed, logs, items, rows_here, heads, pairs, n)
        )
        grad_in_fars.append(across(grad("in_far", all_one, back_triples[n], half)))
        if n == 0:
            grad_out = grad("out_own", all_middle, mixed, 0)
            block_output = run(
                functools.partial(output_kernel, items, half), "output", (steps,), meta,
                [(v, row_block) for v in (middle, out_keep, out_received)],
                [(row_shape, BF16, row_block)],
            )[0]
            hidden_out = outer(
                "outer_lower", meta, groups, [lower_delta], weight_hidden, momentum_hidden, average_hidden, 1
            )
    product = lambda n, received=None: term(
        f"back_first_{n}", meta, back_triples, inward_w, rows_here, ranks, n, received
    )
    far_send = near(product(3))
    far_keep = near(product(1))
    grad_ins = [grad("in_own", all_one, back_triples[0], 0)]
    send = product(2, far_send)
    grad_ins += [grad("in_own", all_one, v, 0) for v in back_triples[1:]]
    in_wide, out_wide = pairs * 3 * HEAD_DIM, heads * HEAD_DIM
    moment_heads, square_heads, *deltas = adam(
        "adam_heads", meta, items, by_head,
        [(v, in_wide, 0) for v in grad_ins] + [(grad_out, out_wide, 0)],
        [(v, in_wide, 0) for v in grad_in_fars] + [(grad_out_far, out_wide, 0)],
        [(heads_all, in_wide, n) for n in range(calls)] + [(heads_all, out_wide, 3)],
        first_heads[:, None], second_heads[:, None], 0, groups,
    )
    heads_deltas = [deltas[0]] + [
        lax.ppermute(deltas[k], "group", [(i, (i + k) % groups) for i in range(groups)])
        for k in range(1, groups)
    ]
    keep = product(0, far_keep)
    keep, received = finish_sum(send, keep, rows_here, ranks)
    input_grad, gain_first = run(
        functools.partial(first_back_kernel, items, half), "first_back", (steps,), meta,
        [(block_input, row_block), (gains, both)] + [(v, row_block) for v in (back_middle, keep, received)],
        [(row_shape, F32, row_block), ((8, width), F32, gain_block)],
    )
    gain_grad = run(
        functools.partial(gain_total_kernel, items, half), "gain_total", (1,), meta,
        [(v, whole(v)) for v in (gain_first, gain_second)],
        [((2, width), F32, both)],
    )[0]

    def added(value, other):
        return run(
            add_kernel, "add", (1,), meta, [(value, whole(value)), (other, whole(other))],
            [(value.shape, F32, whole(value))],
        )[0]

    far_gain = across(gain_grad)
    wait()
    gain_grad = added(gain_grad, far_gain)
    bit = 1
    while bit < ranks:
        far_gain = swap(gain_grad, "tensor", bit, ranks)
        wait()
        gain_grad = added(gain_grad, far_gain)
        bit *= 2
    moment_gains, square_gains, delta_gains = adam_math(
        plain_gains, gain_grad, first_gains[0], second_gains[0], GAIN_RATE, 0.0
    )
    short = width // groups

    def gain_part(k):
        return lax.dynamic_slice_in_dim(delta_gains, (group ^ k) * short, short, 1)

    change_gains = gain_part(0)
    for k in range(1, groups):
        change_gains = change_gains + swap(gain_part(k), "group", k, groups)
    change_gains = change_gains / groups
    velocity_gains, trail_gains, master_gains = outer_math(
        norm_gains, change_gains, momentum_gains, average_gains
    )
    change_hidden, velocity_hidden, trail_hidden, master_hidden, copy_hidden = outer(
        "outer_raise", meta, groups, [raise_delta], weight_hidden, momentum_hidden, average_hidden, 0,
        filled=hidden_out,
    )
    change_heads, velocity_heads, trail_heads, master_heads, copy_heads = (
        v[0]
        for v in outer(
            "outer_heads", meta, groups, heads_deltas, weight_heads[None], momentum_heads[None],
            average_heads[None], 0,
        )
    )
    return (
        block_output,
        input_grad,
        moment_heads[:, 0],
        moment_hidden,
        moment_gains[None],
        square_heads[:, 0],
        square_hidden,
        square_gains[None],
        change_heads,
        change_hidden,
        change_gains,
        velocity_heads,
        velocity_hidden,
        velocity_gains,
        trail_heads,
        trail_hidden,
        trail_gains,
        master_heads,
        master_hidden,
        master_gains,
        copy_heads,
        copy_hidden,
    )


def solution(mesh):
    rows = P(("group", "dp", "tensor"), None)
    heads, hidden, gains = P(("dp", "group"), "tensor"), P(None, ("dp", "group"), "tensor"), P(None, "group")
    states = (P("group", "dp", "tensor"), P("group", None, "dp", "tensor"), P("group", None, None))
    in_specs = (rows, rows, P(("group", "dp"), None)) + (heads, hidden, gains) * 3 + states * 2
    out_specs = (rows, rows) + states * 2 + (heads, hidden, gains) * 4 + (heads, hidden)
    return jax.shard_map(local, mesh=mesh, in_specs=in_specs, out_specs=out_specs, check_vma=False)
```

time: 1070 us -> 996 us (0.931)
  Pallas kernels: 726 us -> 698 us
  starting transfers between devices: 90.8 us -> 66.2 us
  waiting for transfers between devices: 223 us -> 200 us
    ppermute x45 -> x46, starting transfers between devices: 90.4 us -> 46.7 us  [swap(): return lax.ppermute(value, axis, [(i, i ^ bit) for i in range(size)])]
    reduce_scatter x3 -> x2, waiting for transfers between devices: 28.9 us -> 0.01 us  [summed(): return lax.psum_scatter(delta, 'group', scatter_dimension=0, tiled=True)]
    pallas_call x69 -> x81, Pallas kernels: 726 us -> 698 us  [run(): pl.pallas_call(body, grid_spec=pltpu.PrefetchScalarGridSpec(num_scalar_pr...]
    ppermute x0 -> x6, waiting for transfers between devices: none -> 24.3 us  [the longest x3 23 us: local(): lax.ppermute(deltas[k], 'group', [(i, (i + k) % groups) for i in range(gr...]
    ppermute x45 -> x46, waiting for transfers between devices: 191 us -> 170 us  [swap(): return lax.ppermute(value, axis, [(i, i ^ bit) for i in range(size)])]
    ppermute x0 -> x6, starting transfers between devices: none -> 19.1 us  [the longest x3 14.4 us: local(): lax.ppermute(deltas[k], 'group', [(i, (i + k) % groups) for i in range(gr...]
  transfers between devices with their start and end apart: 53 -> 58, of which waited for: 18 -> 21; matrix products, arithmetic and copies ran while one was open for 0% -> 0% of each run, Pallas kernels for 60% -> 66%
where the time goes in v2:
time: 996 us; the launch traced here: 986 us
  Pallas kernels  698 us (70%)
  waiting for transfers between devices  200 us (20%)
  starting transfers between devices  66.2 us (7%)
  between operations  15.1 us (2%)
    pallas_call x81, Pallas kernels, run(): pl.pallas_call(body, grid_spec=pltpu.PrefetchScalarGridSpec(num_scalar_pr...  698 us
    ppermute x46, waiting for transfers between devices, swap(): return lax.ppermute(value, axis, [(i, i ^ bit) for i in range(size)])  170 us
    ppermute x46, starting transfers between devices, swap(): return lax.ppermute(value, axis, [(i, i ^ bit) for i in range(size)])  46.7 us
    ppermute x3, waiting for transfers between devices, local(): lax.ppermute(deltas[k], 'group', [(i, (i + k) % groups) for i in range(gr...  23 us
  transfers between devices with their start and end apart: 58, of which 21 were waited for; matrix products, arithmetic and copies ran while one was open for 0% of the time, Pallas kernels for 66%

profile of v2, /device:TPU:24, one launch (start us, length us, event | category | flops | bytes accessed | tf_op | source)
XLA Modules:
  0.0 985.5 jit_solution(2437154715343156240)
XLA Ops:
  31.4 9.3 collective-permute-done.3.refs_3_.refs_6_
  53.8 21.2 %collective-permute-done.8.refs_3_.refs_8_ = bf16[256,2048]{1,0:T(8,128)(2,1)} collective-permute-done((bf16[256,2048]{1,0:T(8,128)(2,1)}, bf16[256,2048]{1,0:T(8,128)(2,1)}, u32[]{:S(2)}, u32[]{:S(2)}) %collective-permute-start.8) | collective-permute-done | bytes 1048608 | tf_op jit(solution)/shard_map/ppermute | solution.py:34
  83.6 22.1 %collective-permute-done.9.refs_3_.refs_10_ = bf16[256,2048]{1,0:T(8,128)(2,1)} collective-permute-done((bf16[256,2048]{1,0:T(8,128)(2,1)}, bf16[256,2048]{1,0:T(8,128)(2,1)}, u32[]{:S(2)}, u32[]{:S(2)}) %collective-permute-start.9) | collective-permute-done | bytes 1048608 | tf_op jit(solution)/shard_map/ppermute | solution.py:34
  118.2 17.2 %collective-permute-done.12.refs_12_ = bf16[256,2048]{1,0:T(8,128)(2,1)} collective-permute-done((bf16[256,2048]{1,0:T(8,128)(2,1)}, bf16[256,2048]{1,0:T(8,128)(2,1)}, u32[]{:S(2)}, u32[]{:S(2)}) %collective-permute-start.12) | collective-permute-done | bytes 1048608 | tf_op jit(solution)/shard_map/ppermute | solution.py:34
  135.4 27.0 %qkv.1 = (bf16[2560,1536]{1,0:T(8,128)(2,1)}, bf16[2048,2048]{1,0:T(8,128)(2,1)}) custom-call(s32[11]{0:T(128)} %pad_add_fusion.refs_0_, bf16[640,2048]{1,0:T(8,128)(2,1)} %get-tuple-element.114.refs_2_.refs_1_, bf16[640,2048]{1,0:T(8,128)(2,1)} %collective-permute-done.4.refs_3_.refs_2_, bf16[640,2048]{1,0:T(8,128)(2,1)} %get-tuple-element.124.refs_3_, ...), custom_call_target="tpu_custom_call" | custom-call | flops 999999995904 | bytes 1 | tf_op jit(solution)/shard_map/qkv/pallas_call | solution.py:50
  166.1 17.1 %attend.2 = (bf16[2560,512]{1,0:T(8,128)(2,1)}, f32[4,5,8,512]{3,2,1,0:T(8,128)}) custom-call(s32[11]{0:T(128)} %pad_add_fusion.refs_0_, bf16[2560,1536]{1,0:T(8,128)(2,1)} %get-tuple-element.130.refs_2_.refs_1_, s32[1]{0:T(128)} %get-tuple-element.134.refs_2_), custom_call_target="tpu_custom_call" | custom-call | flops 999999995904 | bytes 1 | tf_op jit(solution)/shard_map/attend/pallas_call | solution.py:50
  184.4 17.1 %attend.3 = (bf16[2560,512]{1,0:T(8,128)(2,1)}, f32[4,5,8,512]{3,2,1,0:T(8,128)}) custom-call(s32[11]{0:T(128)} %pad_add_fusion.refs_0_, bf16[2560,1536]{1,0:T(8,128)(2,1)} %get-tuple-element.130.refs_2_.refs_1_, bf16[2560,512]{1,0:T(8,128)(2,1)} %get-tuple-element.135.refs_2_, ...), custom_call_target="tpu_custom_call", output_to_operand_aliasing={{0}: (2, {}), {1}: (3, {})} | custom-call | flops 999999995904 | bytes 1 | tf_op jit(solution)/shard_map/attend/pallas_call | solution.py:50
  257.4 48.4 %collective-permute-done.19.refs_3_ = bf16[640,2048]{1,0:T(8,128)(2,1)} collective-permute-done((bf16[640,2048]{1,0:T(8,128)(2,1)}, bf16[640,2048]{1,0:T(8,128)(2,1)}, u32[]{:S(2)}, u32[]{:S(2)}) %collective-permute-start.19) | collective-permute-done | bytes 2621472 | tf_op jit(solution)/shard_map/ppermute | solution.py:34
  305.8 8.4 second_norm.1
  318.4 31.8 %back_hidden.1 = (bf16[2560,2048]{1,0:T(8,128)(2,1)}, bf16[2048,2048]{1,0:T(8,128)(2,1)}) custom-call(s32[11]{0:T(128)} %pad_add_fusion.refs_0_, bf16[640,2048]{1,0:T(8,128)(2,1)} %get-tuple-element.143.refs_1_.refs_4_, bf16[640,2048]{1,0:T(8,128)(2,1)} %collective-permute-done.15.refs_2_, bf16[640,2048]{1,0:T(8,128)(2,1)} %get-tuple-element.150.refs_3_, ...), custom_call_target="tpu_custom_call" | custom-call | flops 999999995904 | bytes 1 | tf_op jit(solution)/shard_map/back_hidden/pallas_call | solution.py:50
  351.5 13.6 %collective-permute-done.23.refs_6_.refs_5_ = bf16[1024,1024]{1,0:T(8,128)(2,1)} collective-permute-done((bf16[1024,1024]{1,0:T(8,128)(2,1)}, bf16[1024,1024]{1,0:T(8,128)(2,1)}, u32[]{:S(2)}, u32[]{:S(2)}) %collective-permute-start.23) | collective-permute-done | bytes 2097184 | tf_op jit(solution)/shard_map/ppermute | solution.py:34
  365.0 29.9 %raise.2 = (bf16[2560,2048]{1,0:T(8,128)(2,1)}, bf16[2560,2048]{1,0:T(8,128)(2,1)}) custom-call(s32[11]{0:T(128)} %pad_add_fusion.refs_0_, bf16[640,2048]{1,0:T(8,128)(2,1)} %get-tuple-element.154.refs_1_, bf16[640,2048]{1,0:T(8,128)(2,1)} %collective-permute-done.21.refs_2_, bf16[1024,1024]{1,0:T(8,128)(2,1)} %get-tuple-element.155.refs_3_.refs_2_, ...), custom_call_target="tpu_custom_call" | custom-call | flops 999999995904 | bytes 1 | tf_op jit(solution)/shard_map/raise/pallas_call | solution.py:50
  401.5 30.3 %raise.3 = (bf16[2560,2048]{1,0:T(8,128)(2,1)}, bf16[2560,2048]{1,0:T(8,128)(2,1)}) custom-call(s32[11]{0:T(128)} %pad_add_fusion.refs_0_, bf16[640,2048]{1,0:T(8,128)(2,1)} %get-tuple-element.162.refs_1_.refs_3_, bf16[640,2048]{1,0:T(8,128)(2,1)} %collective-permute-done.25.refs_2_.refs_4_, ...), custom_call_target="tpu_custom_call", output_to_operand_aliasing={{0}: (8, {}), {1}: (9, {})} | custom-call | flops 999999995904 | bytes 1 | tf_op jit(solution)/shard_map/raise/pallas_call | solution.py:50
  431.8 17.1 %lower_far.1.refs_6_ = bf16[1024,2048]{1,0:T(8,128)(2,1)} custom-call(s32[11]{0:T(128)} %pad_add_fusion.refs_0_, bf16[640,2048]{1,0:T(8,128)(2,1)} %get-tuple-element.143.refs_1_.refs_4_, bf16[640,2048]{1,0:T(8,128)(2,1)} %collective-permute-done.15.refs_2_, bf16[640,2048]{1,0:T(8,128)(2,1)} %get-tuple-element.150.refs_3_, ...), custom_call_target="tpu_custom_call" | custom-call | flops 999999995904 | bytes 1 | tf_op jit(solution)/shard_map/lower_far/pallas_call | solution.py:50
  450.4 11.9 %back_second_3.1.refs_6_ = bf16[640,2048]{1,0:T(8,128)(2,1)} custom-call(s32[11]{0:T(128)} %pad_add_fusion.refs_0_, bf16[2560,2048]{1,0:T(8,128)(2,1)} %get-tuple-element.167.refs_1_.refs_5_, bf16[1024,1024]{1,0:T(8,128)(2,1)} %get-tuple-element.155.refs_3_.refs_2_, bf16[1024,1024]{1,0:T(8,128)(2,1)} %collective-permute-done.22.refs_4_.refs_3_, ...), custom_call_target="tpu_custom_call" | custom-call | flops 999999995904 | bytes 1 | tf_op jit(solution)/shard_map/back_second_3/pallas_call | solution.py:50
  462.4 12.0 %back_second_1.1.refs_7_ = bf16[640,2048]{1,0:T(8,128)(2,1)} custom-call(s32[11]{0:T(128)} %pad_add_fusion.refs_0_, bf16[2560,2048]{1,0:T(8,128)(2,1)} %get-tuple-element.167.refs_1_.refs_5_, bf16[1024,1024]{1,0:T(8,128)(2,1)} %get-tuple-element.155.refs_3_.refs_2_, bf16[1024,1024]{1,0:T(8,128)(2,1)} %collective-permute-done.22.refs_4_.refs_3_, ...), custom_call_target="tpu_custom_call" | custom-call | flops 999999995904 | bytes 1 | tf_op jit(solution)/shard_map/back_second_1/pallas_call | solution.py:50
  475.0 12.5 %back_second_2.1.refs_7_ = bf16[640,2048]{1,0:T(8,128)(2,1)} custom-call(s32[11]{0:T(128)} %pad_add_fusion.refs_0_, bf16[2560,2048]{1,0:T(8,128)(2,1)} %get-tuple-element.167.refs_1_.refs_5_, bf16[1024,1024]{1,0:T(8,128)(2,1)} %get-tuple-element.155.refs_3_.refs_2_, bf16[1024,1024]{1,0:T(8,128)(2,1)} %collective-permute-done.22.refs_4_.refs_3_, ...), custom_call_target="tpu_custom_call" | custom-call | flops 999999995904 | bytes 1 | tf_op jit(solution)/shard_map/back_second_2/pallas_call | solution.py:50
  488.1 12.5 %back_second_0.1.refs_6_.refs_2_ = bf16[640,2048]{1,0:T(8,128)(2,1)} custom-call(s32[11]{0:T(128)} %pad_add_fusion.refs_0_, bf16[2560,2048]{1,0:T(8,128)(2,1)} %get-tuple-element.167.refs_1_.refs_5_, bf16[1024,1024]{1,0:T(8,128)(2,1)} %get-tuple-element.155.refs_3_.refs_2_, bf16[1024,1024]{1,0:T(8,128)(2,1)} %collective-permute-done.22.refs_4_.refs_3_, ...), custom_call_target="tpu_custom_call" | custom-call | flops 999999995904 | bytes 1 | tf_op jit(solution)/shard_map/back_second_0/pallas_call | solution.py:50
  500.6 17.1 %raise_far.1.refs_6_ = bf16[1024,2048]{1,0:T(8,128)(2,1)} custom-call(s32[11]{0:T(128)} %pad_add_fusion.refs_0_, bf16[640,2048]{1,0:T(8,128)(2,1)} %get-tuple-element.154.refs_1_, bf16[640,2048]{1,0:T(8,128)(2,1)} %collective-permute-done.21.refs_2_, bf16[640,2048]{1,0:T(8,128)(2,1)} %get-tuple-element.162.refs_1_.refs_3_, ...), custom_call_target="tpu_custom_call" | custom-call | flops 999999995904 | bytes 1 | tf_op jit(solution)/shard_map/raise_far/pallas_call | solution.py:50
  518.3 17.1 %lower_own.1.refs_6_.refs_1_ = bf16[1024,2048]{1,0:T(8,128)(2,1)} custom-call(s32[11]{0:T(128)} %pad_add_fusion.refs_0_, bf16[640,2048]{1,0:T(8,128)(2,1)} %get-tuple-element.143.refs_1_.refs_4_, bf16[640,2048]{1,0:T(8,128)(2,1)} %collective-permute-done.15.refs_2_, bf16[640,2048]{1,0:T(8,128)(2,1)} %get-tuple-element.150.refs_3_, ...), custom_call_target="tpu_custom_call" | custom-call | flops 999999995904 | bytes 1 | tf_op jit(solution)/shard_map/lower_own/pallas_call | solution.py:50
  535.4 11.2 %collective-permute-done.28.refs_3_ = bf16[640,2048]{1,0:T(8,128)(2,1)} collective-permute-done((bf16[640,2048]{1,0:T(8,128)(2,1)}, bf16[640,2048]{1,0:T(8,128)(2,1)}, u32[]{:S(2)}, u32[]{:S(2)}) %collective-permute-start.28) | collective-permute-done | bytes 2621472 | tf_op jit(solution)/shard_map/ppermute | solution.py:34
  546.6 11.0 %second_back.1 = (f32[640,2048]{1,0:T(8,128)}, f32[8,2048]{1,0:T(8,128)}, bf16[640,2048]{1,0:T(8,128)(2,1)}) custom-call(s32[11]{0:T(128)} %pad_add_fusion.refs_0_, f32[640,2048]{1,0:T(8,128)} %get-tuple-element.153.refs_2_.refs_1_, bf16[640,2048]{1,0:T(8,128)(2,1)} %back_second_0.1.refs_6_.refs_2_, bf16[640,2048]{1,0:T(8,128)(2,1)} %collective-permute-done.28.refs_3_, ...), custom_call_target="tpu_custom_call" | custom-call | flops 999999995904 | bytes 1 | tf_op jit(solution)/shard_map/second_back/pallas_call | solution.py:50
  558.3 17.1 %raise_own.1.refs_1_ = bf16[1024,2048]{1,0:T(8,128)(2,1)} custom-call(s32[11]{0:T(128)} %pad_add_fusion.refs_0_, bf16[640,2048]{1,0:T(8,128)(2,1)} %get-tuple-element.154.refs_1_, bf16[640,2048]{1,0:T(8,128)(2,1)} %collective-permute-done.21.refs_2_, bf16[640,2048]{1,0:T(8,128)(2,1)} %get-tuple-element.162.refs_1_.refs_3_, ...), custom_call_target="tpu_custom_call" | custom-call | flops 999999995904 | bytes 1 | tf_op jit(solution)/shard_map/raise_own/pallas_call | solution.py:50
  576.6 12.1 %lower_3.1.refs_3_ = bf16[640,2048]{1,0:T(8,128)(2,1)} custom-call(s32[11]{0:T(128)} %pad_add_fusion.refs_0_, bf16[2560,2048]{1,0:T(8,128)(2,1)} %get-tuple-element.165.refs_5_.refs_1_, bf16[2048,2048]{1,0:T(8,128)(2,1)} %get-tuple-element.166.refs_2_.refs_3_, s32[1]{0:T(128)} %pause.48.refs_3_), custom_call_target="tpu_custom_call" | custom-call | flops 999999995904 | bytes 1 | tf_op jit(solution)/shard_map/lower_3/pallas_call | solution.py:50
  589.2 11.4 %lower_1.1.refs_4_ = bf16[640,2048]{1,0:T(8,128)(2,1)} custom-call(s32[11]{0:T(128)} %pad_add_fusion.refs_0_, bf16[2560,2048]{1,0:T(8,128)(2,1)} %get-tuple-element.165.refs_5_.refs_1_, bf16[2048,2048]{1,0:T(8,128)(2,1)} %get-tuple-element.166.refs_2_.refs_3_, bf16[640,2048]{1,0:T(8,128)(2,1)} %lower_3.1.refs_3_), custom_call_target="tpu_custom_call" | custom-call | flops 999999995904 | bytes 1 | tf_op jit(solution)/shard_map/lower_1/pallas_call | solution.py:50
  600.8 12.0 %lower_2.1.refs_4_ = bf16[640,2048]{1,0:T(8,128)(2,1)} custom-call(s32[11]{0:T(128)} %pad_add_fusion.refs_0_, bf16[2560,2048]{1,0:T(8,128)(2,1)} %get-tuple-element.165.refs_5_.refs_1_, bf16[2048,2048]{1,0:T(8,128)(2,1)} %get-tuple-element.166.refs_2_.refs_3_, bf16[640,2048]{1,0:T(8,128)(2,1)} %collective-permute-done.31.refs_3_, ...), custom_call_target="tpu_custom_call" | custom-call | flops 999999995904 | bytes 1 | tf_op jit(solution)/shard_map/lower_2/pallas_call | solution.py:50
  614.3 12.1 %lower_0.1.refs_6_.refs_2_ = bf16[640,2048]{1,0:T(8,128)(2,1)} custom-call(s32[11]{0:T(128)} %pad_add_fusion.refs_0_, bf16[2560,2048]{1,0:T(8,128)(2,1)} %get-tuple-element.165.refs_5_.refs_1_, bf16[2048,2048]{1,0:T(8,128)(2,1)} %get-tuple-element.166.refs_2_.refs_3_, bf16[640,2048]{1,0:T(8,128)(2,1)} %collective-permute-done.30.refs_3_, ...), custom_call_target="tpu_custom_call" | custom-call | flops 999999995904 | bytes 1 | tf_op jit(solution)/shard_map/lower_0/pallas_call | solution.py:50
  626.4 19.5 %adam_lower.1 = (f32[1,2,1024,2048]{3,2,1,0:T(8,128)}, f32[1,2,1024,2048]{3,2,1,0:T(8,128)}, bf16[1024,2048]{1,0:T(8,128)(2,1)}) custom-call(s32[11]{0:T(128)} %pad_add_fusion.refs_0_, bf16[1024,2048]{1,0:T(8,128)(2,1)} %lower_own.1.refs_6_.refs_1_, bf16[1024,2048]{1,0:T(8,128)(2,1)} %collective-permute-done.34.refs_2_, ...), custom_call_target="tpu_custom_call" | custom-call | flops 999999995904 | bytes 1 | tf_op jit(solution)/shard_map/adam_lower/pallas_call | solution.py:50
  652.5 12.4 %back_mixed.1.refs_6_.refs_3_ = bf16[2560,512]{1,0:T(8,128)(2,1)} custom-call(s32[11]{0:T(128)} %pad_add_fusion.refs_0_, bf16[640,2048]{1,0:T(8,128)(2,1)} %get-tuple-element.169.refs_1_, bf16[640,2048]{1,0:T(8,128)(2,1)} %collective-permute-done.29.refs_2_, bf16[640,2048]{1,0:T(8,128)(2,1)} %get-tuple-element.171.refs_3_, ...), custom_call_target="tpu_custom_call" | custom-call | flops 999999995904 | bytes 1 | tf_op jit(solution)/shard_map/back_mixed/pallas_call | solution.py:50
  673.5 19.6 %adam_raise.1 = (f32[1,2,1024,2048]{3,2,1,0:T(8,128)}, f32[1,2,1024,2048]{3,2,1,0:T(8,128)}, bf16[1024,2048]{1,0:T(8,128)(2,1)}) custom-call(s32[11]{0:T(128)} %pad_add_fusion.refs_0_, bf16[1024,2048]{1,0:T(8,128)(2,1)} %raise_own.1.refs_1_, bf16[1024,2048]{1,0:T(8,128)(2,1)} %collective-permute-done.36.refs_2_, ...), custom_call_target="tpu_custom_call", output_to_operand_aliasing={{0}: (7, {}), {1}: (8, {})} | custom-call | flops 999999995904 | bytes 1 | tf_op jit(solution)/shard_map/adam_raise/pallas_call | solution.py:50
  693.1 26.0 %attend_back.2.refs_5_.refs_1_ = bf16[2560,768]{1,0:T(8,128)(2,1)} custom-call(s32[11]{0:T(128)} %pad_add_fusion.refs_0_, bf16[2560,1536]{1,0:T(8,128)(2,1)} %get-tuple-element.130.refs_2_.refs_1_, bf16[2560,512]{1,0:T(8,128)(2,1)} %get-tuple-element.139.refs_2_.refs_1_.refs_5_, bf16[2560,512]{1,0:T(8,128)(2,1)} %back_mixed.1.refs_6_.refs_3_, ...), custom_call_target="tpu_custom_call" | custom-call | flops 999999995904 | bytes 1 | tf_op jit(solution)/shard_map/attend_back/pallas_call | solution.py:50
  719.1 10.8 %in_far.2.refs_6_ = bf16[1024,768]{1,0:T(8,128)(2,1)} custom-call(s32[11]{0:T(128)} %pad_add_fusion.refs_0_, bf16[640,2048]{1,0:T(8,128)(2,1)} %get-tuple-element.114.refs_2_.refs_1_, bf16[640,2048]{1,0:T(8,128)(2,1)} %collective-permute-done.4.refs_3_.refs_2_, bf16[640,2048]{1,0:T(8,128)(2,1)} %get-tuple-element.124.refs_3_, ...), custom_call_target="tpu_custom_call" | custom-call | flops 999999995904 | bytes 1 | tf_op jit(solution)/shard_map/in_far/pallas_call | solution.py:50
  731.1 7.9 out_own.1.refs_4_.refs_3_
  739.0 7.9 output.1.refs_5_
  754.5 26.0 %attend_back.3.refs_5_.refs_2_ = bf16[2560,768]{1,0:T(8,128)(2,1)} custom-call(s32[11]{0:T(128)} %pad_add_fusion.refs_0_, bf16[2560,1536]{1,0:T(8,128)(2,1)} %get-tuple-element.130.refs_2_.refs_1_, bf16[2560,512]{1,0:T(8,128)(2,1)} %get-tuple-element.139.refs_2_.refs_1_.refs_5_, bf16[2560,512]{1,0:T(8,128)(2,1)} %back_mixed.1.refs_6_.refs_3_, ...), custom_call_target="tpu_custom_call" | custom-call | flops 999999995904 | bytes 1 | tf_op jit(solution)/shard_map/attend_back/pallas_call | solution.py:50
  780.5 10.7 %in_far.3.refs_4_ = bf16[1024,768]{1,0:T(8,128)(2,1)} custom-call(s32[11]{0:T(128)} %pad_add_fusion.refs_0_, bf16[640,2048]{1,0:T(8,128)(2,1)} %get-tuple-element.114.refs_2_.refs_1_, bf16[640,2048]{1,0:T(8,128)(2,1)} %collective-permute-done.4.refs_3_.refs_2_, bf16[640,2048]{1,0:T(8,128)(2,1)} %get-tuple-element.124.refs_3_, ...), custom_call_target="tpu_custom_call" | custom-call | flops 999999995904 | bytes 1 | tf_op jit(solution)/shard_map/in_far/pallas_call | solution.py:50
  791.4 9.5 back_first_3.1.refs_4_
  800.9 9.4 back_first_1.1.refs_6_
  810.9 10.7 %in_own.2.refs_5_.refs_1_ = bf16[1024,768]{1,0:T(8,128)(2,1)} custom-call(s32[11]{0:T(128)} %pad_add_fusion.refs_0_, bf16[640,2048]{1,0:T(8,128)(2,1)} %get-tuple-element.114.refs_2_.refs_1_, bf16[640,2048]{1,0:T(8,128)(2,1)} %collective-permute-done.4.refs_3_.refs_2_, bf16[640,2048]{1,0:T(8,128)(2,1)} %get-tuple-element.124.refs_3_, ...), custom_call_target="tpu_custom_call" | custom-call | flops 999999995904 | bytes 1 | tf_op jit(solution)/shard_map/in_own/pallas_call | solution.py:50
  821.6 10.0 %back_first_2.1.refs_6_ = bf16[640,2048]{1,0:T(8,128)(2,1)} custom-call(s32[11]{0:T(128)} %pad_add_fusion.refs_0_, bf16[2560,768]{1,0:T(8,128)(2,1)} %attend_back.2.refs_5_.refs_1_, bf16[2560,768]{1,0:T(8,128)(2,1)} %attend_back.3.refs_5_.refs_2_, bf16[2048,2048]{1,0:T(8,128)(2,1)} %get-tuple-element.140.refs_2_.refs_5_.refs_3_.refs_7_.refs_8_.refs_9_, ...), custom_call_target="tpu_custom_call" | custom-call | flops 999999995904 | bytes 1 | tf_op jit(solution)/shard_map/back_first_2/pallas_call | solution.py:50
  832.2 10.9 %in_own.3.refs_2_ = bf16[1024,768]{1,0:T(8,128)(2,1)} custom-call(s32[11]{0:T(128)} %pad_add_fusion.refs_0_, bf16[640,2048]{1,0:T(8,128)(2,1)} %get-tuple-element.114.refs_2_.refs_1_, bf16[640,2048]{1,0:T(8,128)(2,1)} %collective-permute-done.4.refs_3_.refs_2_, bf16[640,2048]{1,0:T(8,128)(2,1)} %get-tuple-element.124.refs_3_, ...), custom_call_target="tpu_custom_call" | custom-call | flops 999999995904 | bytes 1 | tf_op jit(solution)/shard_map/in_own/pallas_call | solution.py:50
  843.1 21.7 %adam_heads.1 = (f32[1,1,1024,2048]{3,2,1,0:T(8,128)}, f32[1,1,1024,2048]{3,2,1,0:T(8,128)}, bf16[256,2048]{1,0:T(8,128)(2,1)}, bf16[256,2048]{1,0:T(8,128)(2,1)...) custom-call(s32[11]{0:T(128)} %pad_add_fusion.refs_0_, bf16[1024,768]{1,0:T(8,128)(2,1)} %in_own.2.refs_5_.refs_1_, ...), custom_call_target="tpu_custom_call" | custom-call | flops 999999995904 | bytes 1 | tf_op jit(solution)/shard_map/adam_heads/pallas_call | solution.py:50
  867.6 9.7 collective-permute-start.47
  879.2 10.0 %back_first_0.1.refs_4_ = bf16[640,2048]{1,0:T(8,128)(2,1)} custom-call(s32[11]{0:T(128)} %pad_add_fusion.refs_0_, bf16[2560,768]{1,0:T(8,128)(2,1)} %attend_back.2.refs_5_.refs_1_, bf16[2560,768]{1,0:T(8,128)(2,1)} %attend_back.3.refs_5_.refs_2_, bf16[2048,2048]{1,0:T(8,128)(2,1)} %get-tuple-element.140.refs_2_.refs_5_.refs_3_.refs_7_.refs_8_.refs_9_, ...), custom_call_target="tpu_custom_call" | custom-call | flops 999999995904 | bytes 1 | tf_op jit(solution)/shard_map/back_first_0/pallas_call | solution.py:50
  890.8 10.4 %first_back.1 = (f32[640,2048]{1,0:T(8,128)}, f32[8,2048]{1,0:T(8,128)}) custom-call(s32[11]{0:T(128)} %pad_add_fusion.refs_0_, bf16[640,2048]{1,0:T(8,128)(2,1)} %refs_1_.13, f32[2,2048]{1,0:T(2,128)} %get-tuple-element.113.refs_2_.refs_4_.refs_5_, f32[640,2048]{1,0:T(8,128)} %get-tuple-element.168.refs_6_.refs_3_, bf16[640,2048]{1,0:T(8,128)(2,1)} %back_first_0.1.refs_4_, ...), custom_call_target="tpu_custom_call" | custom-call | flops 999999995904 | bytes 1 | tf_op jit(solution)/shard_map/first_back/pallas_call | solution.py:50
  923.7 13.9 %collective-permute-start.51 = (f32[2,512]{1,0:T(2,128)}, f32[2,512]{1,0:T(2,128)}, u32[]{:S(2)}, u32[]{:S(2)}) collective-permute-start(f32[2,512]{1,0:T(2,128)} %get-tuple-element.212), channel_id=1, source_target_pairs={{0,24},{8,16},{16,8},{24,0},{1,25},{9,17},{17,9},{25,1},{2,26},{10... | collective-permute-start | bytes 12296 | tf_op jit(solution)/shard_map/ppermute | solution.py:34
  945.3 23.0 %collective-permute-done.47.refs_3_ = bf16[256,2048]{1,0:T(8,128)(2,1)} collective-permute-done((bf16[256,2048]{1,0:T(8,128)(2,1)}, bf16[256,2048]{1,0:T(8,128)(2,1)}, u32[]{:S(2)}, u32[]{:S(2)}) %collective-permute-start.47) | collective-permute-done | bytes 1048608 | tf_op jit(solution)/shard_map/ppermute | solution.py:1175
  968.4 8.7 outer_heads.1
  (174 shorter events, 201.2 us)
Async XLA Ops:
  7.2 156.5 %all-gather.5.cloned.1.call-start = ((), (), s32[]{:S(2)}) async-start(), calls=%async_computation.2 | async-start | bytes 2621440 | tf_op jit(solution)/shard_map/all_gather | solution.py:1035
  7.2 10.7 %collective-permute-start.2 = (f32[2,512]{1,0:T(2,128)}, f32[2,512]{1,0:T(2,128)}, u32[]{:S(2)}, u32[]{:S(2)}) collective-permute-start(f32[2,512]{1,0:T(2,128)} %refs_1_.8), channel_id=1, source_target_pairs={{0,24},{8,16},{16,8},{24,0},{1,25},{9,17},{17,9},{25,1},{2,26},{10... | collective-permute-start | bytes 12296 | tf_op jit(solution)/shard_map/ppermute | solution.py:34
  7.3 10.6 %collective-permute-start.1 = (f32[2,512]{1,0:T(2,128)}, f32[2,512]{1,0:T(2,128)}, u32[]{:S(2)}, u32[]{:S(2)}) collective-permute-start(f32[2,512]{1,0:T(2,128)} %refs_1_.8), channel_id=1, source_target_pairs={{0,16},{8,24},{16,0},{24,8},{1,17},{9,25},{17,1},{25,9},{2,18},{10... | collective-permute-start | bytes 12296 | tf_op jit(solution)/shard_map/ppermute | solution.py:34
  9.2 8.7 collective-permute-start
  16.2 31.6 %collective-permute-start.6 = (bf16[256,2048]{1,0:T(8,128)(2,1)}, bf16[256,2048]{1,0:T(8,128)(2,1)}, u32[]{:S(2)}, u32[]{:S(2)}) collective-permute-start(bf16[256,2048]{1,0:T(8,128)(2,1)} %cast_heads.1.refs_5_), channel_id=1, source_target_pairs={{0,8},{8,16},{16,24},{24,0},{1,9},{9,17},{17,25},{25,1},{2,10},{10... | collective-permute-start | bytes 3145736 | tf_op jit(solution)/shard_map/ppermute | solution.py:982
  16.3 24.4 %collective-permute-start.3 = (bf16[256,2048]{1,0:T(8,128)(2,1)}, bf16[256,2048]{1,0:T(8,128)(2,1)}, u32[]{:S(2)}, u32[]{:S(2)}) collective-permute-start(bf16[256,2048]{1,0:T(8,128)(2,1)} %cast_heads.1.refs_5_), channel_id=1, source_target_pairs={{0,4},{4,0},{1,5},{5,1},{2,6},{6,2},{3,7},{7,3},{8,12},{12,8},{9,1... | collective-permute-start | bytes 3145736 | tf_op jit(solution)/shard_map/ppermute | solution.py:34
  25.9 57.7 %collective-permute-start.5 = (bf16[640,2048]{1,0:T(8,128)(2,1)}, bf16[640,2048]{1,0:T(8,128)(2,1)}, u32[]{:S(2)}, u32[]{:S(2)}) collective-permute-start(bf16[640,2048]{1,0:T(8,128)(2,1)} %get-tuple-element.114.refs_2_.refs_1_), channel_id=1, source_target_pairs={{0,2},{1,3},{2,0},{3,1},{4,6},{5,7},{6,4},{7,5},{8,10},{9,11},{10,... | collective-permute-start | bytes 7864328 | tf_op jit(solution)/shard_map/ppermute | solution.py:34
  49.0 25.9 %collective-permute-start.8 = (bf16[256,2048]{1,0:T(8,128)(2,1)}, bf16[256,2048]{1,0:T(8,128)(2,1)}, u32[]{:S(2)}, u32[]{:S(2)}) collective-permute-start(bf16[256,2048]{1,0:T(8,128)(2,1)} %get-tuple-element.120.refs_7_), channel_id=1, source_target_pairs={{0,4},{4,0},{1,5},{5,1},{2,6},{6,2},{3,7},{7,3},{8,12},{12,8},{9,1... | collective-permute-start | bytes 3145736 | tf_op jit(solution)/shard_map/ppermute | solution.py:34
  50.6 25.6 %collective-permute-start.7 = (bf16[256,2048]{1,0:T(8,128)(2,1)}, bf16[256,2048]{1,0:T(8,128)(2,1)}, u32[]{:S(2)}, u32[]{:S(2)}) collective-permute-start(bf16[256,2048]{1,0:T(8,128)(2,1)} %get-tuple-element.120.refs_7_), channel_id=1, source_target_pairs={{0,8},{8,16},{16,24},{24,0},{1,9},{9,17},{17,25},{25,1},{2,10},{10... | collective-permute-start | bytes 3145736 | tf_op jit(solution)/shard_map/ppermute | solution.py:982
  78.0 29.6 %collective-permute-start.11 = (bf16[256,2048]{1,0:T(8,128)(2,1)}, bf16[256,2048]{1,0:T(8,128)(2,1)}, u32[]{:S(2)}, u32[]{:S(2)}) collective-permute-start(bf16[256,2048]{1,0:T(8,128)(2,1)} %get-tuple-element.123.refs_9_), channel_id=1, source_target_pairs={{0,8},{8,16},{16,24},{24,0},{1,9},{9,17},{17,25},{25,1},{2,10},{10... | collective-permute-start | bytes 3145736 | tf_op jit(solution)/shard_map/ppermute | solution.py:982
  81.2 24.5 %collective-permute-start.9 = (bf16[256,2048]{1,0:T(8,128)(2,1)}, bf16[256,2048]{1,0:T(8,128)(2,1)}, u32[]{:S(2)}, u32[]{:S(2)}) collective-permute-start(bf16[256,2048]{1,0:T(8,128)(2,1)} %get-tuple-element.123.refs_9_), channel_id=1, source_target_pairs={{0,4},{4,0},{1,5},{5,1},{2,6},{6,2},{3,7},{7,3},{8,12},{12,8},{9,1... | collective-permute-start | bytes 3145736 | tf_op jit(solution)/shard_map/ppermute | solution.py:34
  109.5 25.9 %collective-permute-start.12 = (bf16[256,2048]{1,0:T(8,128)(2,1)}, bf16[256,2048]{1,0:T(8,128)(2,1)}, u32[]{:S(2)}, u32[]{:S(2)}) collective-permute-start(bf16[256,2048]{1,0:T(8,128)(2,1)} %get-tuple-element.126.refs_11_), channel_id=1, source_target_pairs={{0,4},{4,0},{1,5},{5,1},{2,6},{6,2},{3,7},{7,3},{8,12},{12,8},{9,1... | collective-permute-start | bytes 3145736 | tf_op jit(solution)/shard_map/ppermute | solution.py:34
  114.7 92.8 %all-gather.7.cloned.1.call-start = ((), (), s32[]{:S(2)}) async-start(), calls=%async_computation.3 | async-start | bytes 2621440 | tf_op jit(solution)/shard_map/all_gather | solution.py:1035
  116.6 98.3 %collective-permute-start.13 = (bf16[640,2048]{1,0:T(8,128)(2,1)}, bf16[640,2048]{1,0:T(8,128)(2,1)}, u32[]{:S(2)}, u32[]{:S(2)}) collective-permute-start(bf16[640,2048]{1,0:T(8,128)(2,1)} %get-tuple-element.143.refs_1_.refs_4_), channel_id=1, source_target_pairs={{0,2},{1,3},{2,0},{3,1},{4,6},{5,7},{6,4},{7,5},{8,10},{9,11},{10,... | collective-permute-start | bytes 7864328 | tf_op jit(solution)/shard_map/ppermute | solution.py:34
  163.6 91.1 %all-gather.9.cloned.1.call-start = ((), (), s32[]{:S(2)}) async-start(), calls=%async_computation.4 | async-start | bytes 2621440 | tf_op jit(solution)/shard_map/all_gather | solution.py:1035
  165.5 47.6 %collective-permute-start.14 = (bf16[1024,1024]{1,0:T(8,128)(2,1)}, bf16[1024,1024]{1,0:T(8,128)(2,1)}, u32[]{:S(2)}, u32[]{:S(2)}) collective-permute-start(bf16[1024,1024]{1,0:T(8,128)(2,1)} %get-tuple-element.145.refs_5_), channel_id=1, source_target_pairs={{0,4},{4,0},{1,5},{5,1},{2,6},{6,2},{3,7},{7,3},{8,12},{12,8},{9,1... | collective-permute-start | bytes 6291464 | tf_op jit(solution)/shard_map/ppermute | solution.py:34
  201.5 114.2 %all-gather.11.cloned.1.call-start = ((), (), s32[]{:S(2)}) async-start(), calls=%async_computation.5 | async-start | bytes 2621440 | tf_op jit(solution)/shard_map/all_gather | solution.py:1035
  214.3 104.1 %collective-permute-start.24 = (bf16[1024,1024]{1,0:T(8,128)(2,1)}, bf16[1024,1024]{1,0:T(8,128)(2,1)}, u32[]{:S(2)}, u32[]{:S(2)}) collective-permute-start(bf16[1024,1024]{1,0:T(8,128)(2,1)} %get-tuple-element.158.refs_7_), channel_id=1, source_target_pairs={{0,4},{4,0},{1,5},{5,1},{2,6},{6,2},{3,7},{7,3},{8,12},{12,8},{9,1... | collective-permute-start | bytes 6291464 | tf_op jit(solution)/shard_map/ppermute | solution.py:34
  216.8 9.0 collective-permute-start.16
  219.2 527.8 %reduce-scatter.3.cloned.1.call-start = ((), (), s32[]{:S(2)}) async-start(), calls=%async_computation.6 | async-start | bytes 5242880 | tf_op jit(solution)/shard_map/reduce_scatter | solution.py:1121
  246.5 59.3 %collective-permute-start.19 = (bf16[640,2048]{1,0:T(8,128)(2,1)}, bf16[640,2048]{1,0:T(8,128)(2,1)}, u32[]{:S(2)}, u32[]{:S(2)}) collective-permute-start(bf16[640,2048]{1,0:T(8,128)(2,1)} %project_2.1.refs_4_), channel_id=1, source_target_pairs={{0,2},{1,3},{2,0},{3,1},{4,6},{5,7},{6,4},{7,5},{8,10},{9,11},{10,... | collective-permute-start | bytes 7864328 | tf_op jit(solution)/shard_map/ppermute | solution.py:34
  255.8 95.6 %collective-permute-start.22 = (bf16[1024,1024]{1,0:T(8,128)(2,1)}, bf16[1024,1024]{1,0:T(8,128)(2,1)}, u32[]{:S(2)}, u32[]{:S(2)}) collective-permute-start(bf16[1024,1024]{1,0:T(8,128)(2,1)} %get-tuple-element.155.refs_3_.refs_2_), channel_id=1, source_target_pairs={{0,4},{4,0},{1,5},{5,1},{2,6},{6,2},{3,7},{7,3},{8,12},{12,8},{9,1... | collective-permute-start | bytes 6291464 | tf_op jit(solution)/shard_map/ppermute | solution.py:34
  314.2 36.1 %collective-permute-start.21 = (bf16[640,2048]{1,0:T(8,128)(2,1)}, bf16[640,2048]{1,0:T(8,128)(2,1)}, u32[]{:S(2)}, u32[]{:S(2)}) collective-permute-start(bf16[640,2048]{1,0:T(8,128)(2,1)} %get-tuple-element.154.refs_1_), channel_id=1, source_target_pairs={{0,1},{1,0},{2,3},{3,2},{4,5},{5,4},{6,7},{7,6},{8,9},{9,8},{10,11... | collective-permute-start | bytes 7864328 | tf_op jit(solution)/shard_map/ppermute | solution.py:34
  314.2 80.8 %collective-permute-start.20 = (bf16[640,2048]{1,0:T(8,128)(2,1)}, bf16[640,2048]{1,0:T(8,128)(2,1)}, u32[]{:S(2)}, u32[]{:S(2)}) collective-permute-start(bf16[640,2048]{1,0:T(8,128)(2,1)} %get-tuple-element.154.refs_1_), channel_id=1, source_target_pairs={{0,2},{1,3},{2,0},{3,1},{4,6},{5,7},{6,4},{7,5},{8,10},{9,11},{10,... | collective-permute-start | bytes 7864328 | tf_op jit(solution)/shard_map/ppermute | solution.py:34
  316.9 48.1 %collective-permute-start.23 = (bf16[1024,1024]{1,0:T(8,128)(2,1)}, bf16[1024,1024]{1,0:T(8,128)(2,1)}, u32[]{:S(2)}, u32[]{:S(2)}) collective-permute-start(bf16[1024,1024]{1,0:T(8,128)(2,1)} %get-tuple-element.157.refs_5_.refs_4_), channel_id=1, source_target_pairs={{0,4},{4,0},{1,5},{5,1},{2,6},{6,2},{3,7},{7,3},{8,12},{12,8},{9,1... | collective-permute-start | bytes 6291464 | tf_op jit(solution)/shard_map/ppermute | solution.py:34
  448.9 177.6 %collective-permute-start.34 = (bf16[1024,2048]{1,0:T(8,128)(2,1)}, bf16[1024,2048]{1,0:T(8,128)(2,1)}, u32[]{:S(2)}, u32[]{:S(2)}) collective-permute-start(bf16[1024,2048]{1,0:T(8,128)(2,1)} %lower_far.1.refs_6_), channel_id=1, source_target_pairs={{0,4},{4,0},{1,5},{5,1},{2,6},{6,2},{3,7},{7,3},{8,12},{12,8},{9,1... | collective-permute-start | bytes 12582920 | tf_op jit(solution)/shard_map/ppermute | solution.py:34
  462.3 12.7 %collective-permute-start.27 = (bf16[640,2048]{1,0:T(8,128)(2,1)}, bf16[640,2048]{1,0:T(8,128)(2,1)}, u32[]{:S(2)}, u32[]{:S(2)}) collective-permute-start(bf16[640,2048]{1,0:T(8,128)(2,1)} %back_second_3.1.refs_6_), channel_id=1, source_target_pairs={{0,1},{1,0},{2,3},{3,2},{4,5},{5,4},{6,7},{7,6},{8,9},{9,8},{10,11... | collective-permute-start | bytes 7864328 | tf_op jit(solution)/shard_map/ppermute | solution.py:34
  474.4 13.6 %collective-permute-start.26 = (bf16[640,2048]{1,0:T(8,128)(2,1)}, bf16[640,2048]{1,0:T(8,128)(2,1)}, u32[]{:S(2)}, u32[]{:S(2)}) collective-permute-start(bf16[640,2048]{1,0:T(8,128)(2,1)} %back_second_1.1.refs_7_), channel_id=1, source_target_pairs={{0,1},{1,0},{2,3},{3,2},{4,5},{5,4},{6,7},{7,6},{8,9},{9,8},{10,11... | collective-permute-start | bytes 7864328 | tf_op jit(solution)/shard_map/ppermute | solution.py:34
  487.4 59.2 %collective-permute-start.28 = (bf16[640,2048]{1,0:T(8,128)(2,1)}, bf16[640,2048]{1,0:T(8,128)(2,1)}, u32[]{:S(2)}, u32[]{:S(2)}) collective-permute-start(bf16[640,2048]{1,0:T(8,128)(2,1)} %back_second_2.1.refs_7_), channel_id=1, source_target_pairs={{0,2},{1,3},{2,0},{3,1},{4,6},{5,7},{6,4},{7,5},{8,10},{9,11},{10,... | collective-permute-start | bytes 7864328 | tf_op jit(solution)/shard_map/ppermute | solution.py:34
  517.7 155.8 %collective-permute-start.36 = (bf16[1024,2048]{1,0:T(8,128)(2,1)}, bf16[1024,2048]{1,0:T(8,128)(2,1)}, u32[]{:S(2)}, u32[]{:S(2)}) collective-permute-start(bf16[1024,2048]{1,0:T(8,128)(2,1)} %raise_far.1.refs_6_), channel_id=1, source_target_pairs={{0,4},{4,0},{1,5},{5,1},{2,6},{6,2},{3,7},{7,3},{8,12},{12,8},{9,1... | collective-permute-start | bytes 12582920 | tf_op jit(solution)/shard_map/ppermute | solution.py:34
  557.7 88.4 %collective-permute-start.33 = (bf16[640,2048]{1,0:T(8,128)(2,1)}, bf16[640,2048]{1,0:T(8,128)(2,1)}, u32[]{:S(2)}, u32[]{:S(2)}) collective-permute-start(bf16[640,2048]{1,0:T(8,128)(2,1)} %get-tuple-element.169.refs_1_), channel_id=1, source_target_pairs={{0,2},{1,3},{2,0},{3,1},{4,6},{5,7},{6,4},{7,5},{8,10},{9,11},{10,... | collective-permute-start | bytes 7864328 | tf_op jit(solution)/shard_map/ppermute | solution.py:34
  558.3 17.1 %collective-permute-start.29 = (bf16[640,2048]{1,0:T(8,128)(2,1)}, bf16[640,2048]{1,0:T(8,128)(2,1)}, u32[]{:S(2)}, u32[]{:S(2)}) collective-permute-start(bf16[640,2048]{1,0:T(8,128)(2,1)} %get-tuple-element.169.refs_1_), channel_id=1, source_target_pairs={{0,1},{1,0},{2,3},{3,2},{4,5},{5,4},{6,7},{7,6},{8,9},{9,8},{10,11... | collective-permute-start | bytes 7864328 | tf_op jit(solution)/shard_map/ppermute | solution.py:34
  588.6 12.1 %collective-permute-start.31 = (bf16[640,2048]{1,0:T(8,128)(2,1)}, bf16[640,2048]{1,0:T(8,128)(2,1)}, u32[]{:S(2)}, u32[]{:S(2)}) collective-permute-start(bf16[640,2048]{1,0:T(8,128)(2,1)} %lower_3.1.refs_3_), channel_id=1, source_target_pairs={{0,1},{1,0},{2,3},{3,2},{4,5},{5,4},{6,7},{7,6},{8,9},{9,8},{10,11... | collective-permute-start | bytes 7864328 | tf_op jit(solution)/shard_map/ppermute | solution.py:34
  600.7 13.7 %collective-permute-start.30 = (bf16[640,2048]{1,0:T(8,128)(2,1)}, bf16[640,2048]{1,0:T(8,128)(2,1)}, u32[]{:S(2)}, u32[]{:S(2)}) collective-permute-start(bf16[640,2048]{1,0:T(8,128)(2,1)} %lower_1.1.refs_4_), channel_id=1, source_target_pairs={{0,1},{1,0},{2,3},{3,2},{4,5},{5,4},{6,7},{7,6},{8,9},{9,8},{10,11... | collective-permute-start | bytes 7864328 | tf_op jit(solution)/shard_map/ppermute | solution.py:34
  612.8 126.2 %collective-permute-start.32 = (bf16[640,2048]{1,0:T(8,128)(2,1)}, bf16[640,2048]{1,0:T(8,128)(2,1)}, u32[]{:S(2)}, u32[]{:S(2)}) collective-permute-start(bf16[640,2048]{1,0:T(8,128)(2,1)} %lower_2.1.refs_4_), channel_id=1, source_target_pairs={{0,2},{1,3},{2,0},{3,1},{4,6},{5,7},{6,4},{7,5},{8,10},{9,11},{10,... | collective-permute-start | bytes 7864328 | tf_op jit(solution)/shard_map/ppermute | solution.py:34
  646.0 291.6 %reduce-scatter.5.cloned.1.call-start = ((), (), s32[]{:S(2)}) async-start(), calls=%async_computation.7 | async-start | bytes 5242880 | tf_op jit(solution)/shard_map/reduce_scatter | solution.py:1121
  672.8 170.2 %collective-permute-start.41 = (bf16[1024,512]{1,0:T(8,128)(2,1)}, bf16[1024,512]{1,0:T(8,128)(2,1)}, u32[]{:S(2)}, u32[]{:S(2)}) collective-permute-start(bf16[1024,512]{1,0:T(8,128)(2,1)} %out_far.1.refs_9_), channel_id=1, source_target_pairs={{0,4},{4,0},{1,5},{5,1},{2,6},{6,2},{3,7},{7,3},{8,12},{12,8},{9,1... | collective-permute-start | bytes 3145736 | tf_op jit(solution)/shard_map/ppermute | solution.py:34
  729.9 113.2 %collective-permute-start.39 = (bf16[1024,768]{1,0:T(8,128)(2,1)}, bf16[1024,768]{1,0:T(8,128)(2,1)}, u32[]{:S(2)}, u32[]{:S(2)}) collective-permute-start(bf16[1024,768]{1,0:T(8,128)(2,1)} %in_far.2.refs_6_), channel_id=1, source_target_pairs={{0,4},{4,0},{1,5},{5,1},{2,6},{6,2},{3,7},{7,3},{8,12},{12,8},{9,1... | collective-permute-start | bytes 4718600 | tf_op jit(solution)/shard_map/ppermute | solution.py:34
  791.3 51.8 %collective-permute-start.40 = (bf16[1024,768]{1,0:T(8,128)(2,1)}, bf16[1024,768]{1,0:T(8,128)(2,1)}, u32[]{:S(2)}, u32[]{:S(2)}) collective-permute-start(bf16[1024,768]{1,0:T(8,128)(2,1)} %in_far.3.refs_4_), channel_id=1, source_target_pairs={{0,4},{4,0},{1,5},{5,1},{2,6},{6,2},{3,7},{7,3},{8,12},{12,8},{9,1... | collective-permute-start | bytes 4718600 | tf_op jit(solution)/shard_map/ppermute | solution.py:34
  810.4 11.3 %collective-permute-start.38 = (bf16[640,2048]{1,0:T(8,128)(2,1)}, bf16[640,2048]{1,0:T(8,128)(2,1)}, u32[]{:S(2)}, u32[]{:S(2)}) collective-permute-start(bf16[640,2048]{1,0:T(8,128)(2,1)} %back_first_3.1.refs_4_), channel_id=1, source_target_pairs={{0,1},{1,0},{2,3},{3,2},{4,5},{5,4},{6,7},{7,6},{8,9},{9,8},{10,11... | collective-permute-start | bytes 7864328 | tf_op jit(solution)/shard_map/ppermute | solution.py:34
  810.4 68.8 %collective-permute-start.37 = (bf16[640,2048]{1,0:T(8,128)(2,1)}, bf16[640,2048]{1,0:T(8,128)(2,1)}, u32[]{:S(2)}, u32[]{:S(2)}) collective-permute-start(bf16[640,2048]{1,0:T(8,128)(2,1)} %back_first_1.1.refs_6_), channel_id=1, source_target_pairs={{0,1},{1,0},{2,3},{3,2},{4,5},{5,4},{6,7},{7,6},{8,9},{9,8},{10,11... | collective-permute-start | bytes 7864328 | tf_op jit(solution)/shard_map/ppermute | solution.py:34
  831.6 59.2 %collective-permute-start.42 = (bf16[640,2048]{1,0:T(8,128)(2,1)}, bf16[640,2048]{1,0:T(8,128)(2,1)}, u32[]{:S(2)}, u32[]{:S(2)}) collective-permute-start(bf16[640,2048]{1,0:T(8,128)(2,1)} %back_first_2.1.refs_6_), channel_id=1, source_target_pairs={{0,2},{1,3},{2,0},{3,1},{4,6},{5,7},{6,4},{7,5},{8,10},{9,11},{10,... | collective-permute-start | bytes 7864328 | tf_op jit(solution)/shard_map/ppermute | solution.py:34
  864.8 80.4 %collective-permute-start.46 = (bf16[256,2048]{1,0:T(8,128)(2,1)}, bf16[256,2048]{1,0:T(8,128)(2,1)}, u32[]{:S(2)}, u32[]{:S(2)}) collective-permute-start(bf16[256,2048]{1,0:T(8,128)(2,1)} %get-tuple-element.185), channel_id=1, source_target_pairs={{0,8},{8,16},{16,24},{24,0},{1,9},{9,17},{17,25},{25,1},{2,10},{10... | collective-permute-start | bytes 3145736 | tf_op jit(solution)/shard_map/ppermute | solution.py:1175
  867.6 100.7 %collective-permute-start.47 = (bf16[256,2048]{1,0:T(8,128)(2,1)}, bf16[256,2048]{1,0:T(8,128)(2,1)}, u32[]{:S(2)}, u32[]{:S(2)}) collective-permute-start(bf16[256,2048]{1,0:T(8,128)(2,1)} %get-tuple-element.186), channel_id=1, source_target_pairs={{0,16},{8,24},{16,0},{24,8},{1,17},{9,25},{17,1},{25,9},{2,18},{10... | collective-permute-start | bytes 3145736 | tf_op jit(solution)/shard_map/ppermute | solution.py:1175
  877.3 91.1 %collective-permute-start.48 = (bf16[256,2048]{1,0:T(8,128)(2,1)}, bf16[256,2048]{1,0:T(8,128)(2,1)}, u32[]{:S(2)}, u32[]{:S(2)}) collective-permute-start(bf16[256,2048]{1,0:T(8,128)(2,1)} %get-tuple-element.187), channel_id=1, source_target_pairs={{0,24},{8,0},{16,8},{24,16},{1,25},{9,1},{17,9},{25,17},{2,26},{10... | collective-permute-start | bytes 3145736 | tf_op jit(solution)/shard_map/ppermute | solution.py:1175
  923.7 53.4 %collective-permute-start.49 = (f32[2,512]{1,0:T(2,128)}, f32[2,512]{1,0:T(2,128)}, u32[]{:S(2)}, u32[]{:S(2)}) collective-permute-start(f32[2,512]{1,0:T(2,128)} %get-tuple-element.211), channel_id=1, source_target_pairs={{0,8},{8,0},{16,24},{24,16},{1,9},{9,1},{17,25},{25,17},{2,10},{10... | collective-permute-start | bytes 12296 | tf_op jit(solution)/shard_map/ppermute | solution.py:34
  923.7 53.4 %collective-permute-start.51 = (f32[2,512]{1,0:T(2,128)}, f32[2,512]{1,0:T(2,128)}, u32[]{:S(2)}, u32[]{:S(2)}) collective-permute-start(f32[2,512]{1,0:T(2,128)} %get-tuple-element.212), channel_id=1, source_target_pairs={{0,24},{8,16},{16,8},{24,0},{1,25},{9,17},{17,9},{25,1},{2,26},{10... | collective-permute-start | bytes 12296 | tf_op jit(solution)/shard_map/ppermute | solution.py:34
  945.2 31.9 %collective-permute-start.50 = (f32[2,512]{1,0:T(2,128)}, f32[2,512]{1,0:T(2,128)}, u32[]{:S(2)}, u32[]{:S(2)}) collective-permute-start(f32[2,512]{1,0:T(2,128)} %get-tuple-element.213), channel_id=1, source_target_pairs={{0,16},{8,24},{16,0},{24,8},{1,17},{9,25},{17,1},{25,9},{2,18},{10... | collective-permute-start | bytes 12296 | tf_op jit(solution)/shard_map/ppermute | solution.py:34
  (17 other events, 86.3 us)
Sparse Core Ops, SparseCore 0:
  114.8 43.7 all-gather.4
  163.7 43.7 all-gather.6
  209.7 44.9 all-gather.8
  256.6 44.6 all-gather.10
  646.1 75.1 reduce-scatter.2
  731.3 79.6 reduce-scatter.4

commit v3 on v2

--- a/solution.py
+++ b/solution.py
@@ -148,27 +148,30 @@
             values[n, :, HEAD_DIM:] = jnp.ones((total, HEAD_DIM), BF16)
 
     first_row = index * block
-    here = pl.ds(pl.multiple_of(first_row, block), block)
     acc[...] = jnp.zeros_like(acc)
     top[...] = jnp.full_like(top, NEGATIVE)
     low_start = item_start(first_row, meta, items)
     high_start = item_start(first_row + block - 1, meta, items)
 
-    def tile(j, masked):
-        at = pl.ds(pl.multiple_of(j * block, block), block)
+    def tile(j, masked, keys=block, low=0, high=block):
+        at = pl.ds(pl.multiple_of(j * block, block), keys)
+        here = pl.ds(pl.multiple_of(first_row + low, math.gcd(block, low)), high - low)
+        own = slice(low, high)
         if masked:
-            q_place = first_row + lax.broadcasted_iota(jnp.int32, (block, 1), 0)
-            k_place = j * block + lax.broadcasted_iota(jnp.int32, (1, block), 1)
+            q_place = first_row + low + lax.broadcasted_iota(jnp.int32, (high - low, 1), 0)
+            k_place = j * block + lax.broadcasted_iota(jnp.int32, (1, keys), 1)
             live = (k_place <= q_place) & (k_place >= item_start(q_place, meta, items))
         scores = [dot_last(nat[here, head_columns(n, 0)], nat[at, head_columns(n, 1)]) for n in range(pairs)]
         for n in range(pairs):
             s = jnp.where(live, scores[n], NEGATIVE) if masked else scores[n]
-            old = top[n]
+            old = top[n, own, :]
             new = jnp.maximum(old, jnp.max(s, axis=1, keepdims=True))
-            p = jnp.exp2((s - jnp.concatenate([new] * (block // HEAD_DIM), axis=1)) * SCALE_LOG2)
+            p = jnp.exp2((s - jnp.concatenate([new] * (keys // HEAD_DIM), axis=1)) * SCALE_LOG2)
             keep = jnp.exp2((old - new) * SCALE_LOG2)
-            top[n] = new
-            acc[n] = acc[n] * jnp.concatenate([keep, keep], axis=1) + dot(p.astype(BF16), values[n, at, :])
+            top[n, own, :] = new
+            acc[n, own, :] = acc[n, own, :] * jnp.concatenate([keep, keep], axis=1) + dot(
+                p.astype(BF16), values[n, at, :]
+            )
 
     @pl.loop(low_start // block, index)
     def _(j):
@@ -182,7 +185,9 @@
         def _():
             tile(j, True)
 
-    tile(index, True)
+    middle = block // 2
+    tile(index, True, middle, 0, middle)
+    tile(index, True, block, middle, block)
     per = block // step
     for n in range(pairs):
         weight = acc[n, :, HEAD_DIM:]
@@ -246,22 +251,24 @@
     low_start = item_start(first_row, meta, items)
     high_start = item_start(first_row + block - 1, meta, items)
 
-    def tile(j, masked):
-        at = pl.ds(pl.multiple_of(j * block, block), block)
+    def tile(j, masked, low=0, high=block):
+        at = pl.ds(pl.multiple_of(j * block + low, math.gcd(block, low)), high - low)
+        here = pl.ds(pl.multiple_of(first_row + low, math.gcd(block, low)), block - low)
+        mine = slice(low, block)
         if masked:
-            k_place = j * block + lax.broadcasted_iota(jnp.int32, (block, 1), 0)
-            q_place = first_row + lax.broadcasted_iota(jnp.int32, (1, block), 1)
+            k_place = j * block + low + lax.broadcasted_iota(jnp.int32, (high - low, 1), 0)
+            q_place = first_row + mine.start + lax.broadcasted_iota(jnp.int32, (1, block - mine.start), 1)
             live = (k_place <= q_place) & (k_place >= item_start(q_place, meta, items))
         scores = [dot_last(nat[at, head_columns(n, 1)], nat[here, head_columns(n, 0)]) for n in range(pairs)]
         backs = [dot_last(nat[at, head_columns(n, 2)], nat_back[here, own[n]]) for n in range(pairs)]
         for n in range(pairs):
-            p = jnp.exp2(scores[n] * SCALE_LOG2 - logs[n, 0, 0:1, :])
+            p = jnp.exp2(scores[n] * SCALE_LOG2 - logs[n, 0, 0:1, mine])
             if masked:
                 p = jnp.where(live, p, 0.0)
-            s = (p * (backs[n] - row_terms[n])).astype(BF16)
+            s = (p * (backs[n] - row_terms[n][:, mine])).astype(BF16)
             dv[at, own[n]] += dot(p.astype(BF16), nat_back[here, own[n]])
             dk[at, own[n]] += dot(s, nat[here, head_columns(n, 0)])
-            dq[:, own[n]] += dot_first(s, nat[at, head_columns(n, 1)])
+            dq[mine, own[n]] += dot_first(s, nat[at, head_columns(n, 1)])
 
     @pl.loop(low_start // block, index)
     def _(j):
@@ -275,7 +282,9 @@
         def _():
             tile(j, True)
 
-    tile(index, True)
+    middle = block // 2
+    tile(index, True, 0, middle)
+    tile(index, True, middle, block)
     per = block // step
     for n in range(pairs):
         out = (dq[:, own[n]] * SCALE).astype(BF16)
@@ -328,7 +337,7 @@
 
 
 def tile_of(size):
-    return next(tile for tile in (min(TILE, size), 384, 256, 128) if size % tile == 0)
+    return next(tile for tile in (min(TILE, size), 256, 128) if size % tile == 0)
 
 
 def part_of(array, row=lambda m: 0, column=0, source_row=0, rows=None, source_column=0, columns=None):
@@ -337,9 +346,9 @@
 
 
 class Pieces:
-    def __init__(self, refs, places, dim, target, sems, meta):
+    def __init__(self, refs, places, dim, target, sems, meta, tile=None):
         self.refs, self.places, self.dim, self.target, self.sems, self.meta = refs, places, dim, target, sems, meta
-        self.tile = tile_of(target.shape[dim])
+        self.tile = tile or tile_of(target.shape[dim])
 
     def span(self, p):
         row, column, _, rows, _, columns = self.places[p]
@@ -607,14 +616,18 @@
         bit *= 2
 
 
-def weight_grad_kernel(rows_a, first, meta, *refs):
-    count = len(rows_a)
-    left, (right, out, slots, held, left_sems, right_sems) = refs[:count], refs[count:]
+def weight_grad_kernel(rows_a, columns, first, meta, *refs):
+    count, many = len(rows_a), len(columns)
+    left, right, (out, slots, held, left_sems, right_sems) = (
+        refs[:count], refs[count : count + many], refs[count + many :]
+    )
     i = pl.program_id(0)
     steps = pl.num_programs(0)
     wide = slots.shape[2]
-    parts = Pieces([right], [part_of(right)[1]], 1, held, right_sems, meta)
-    tile = parts.tile
+    places = [part_of(v, column=at)[1] for v, at in zip(right, columns)]
+    loads = tile_of(right[0].shape[1])
+    parts = Pieces(right, places, 1, held, right_sems, meta, loads)
+    tile = tile_of(held.shape[1])
 
     def fetch(step, slot):
         at = pl.ds(pl.multiple_of(first + step * wide, wide), wide)
@@ -641,7 +654,8 @@
     def _(n):
         @pl.when(i == 0)
         def _():
-            parts.wait(n)
+            for m in range(tile // loads):
+                parts.wait(n * (tile // loads) + m)
 
         at = pl.ds(pl.multiple_of(n * tile, tile), tile)
         out[:, at] = dot_first(slots[i % 2], held[:, at]).astype(BF16)
@@ -649,19 +663,23 @@
 
 def weight_grad(name, meta, left, right, first, half, after=()):
     wide = min(512, half)
-    total, n = right.shape
+    columns, n = [], 0
+    for v in right:
+        columns.append(n)
+        n += v.shape[1]
+    total = right[0].shape[0]
     return run(
-        functools.partial(weight_grad_kernel, [r for _, r in left], first),
+        functools.partial(weight_grad_kernel, [r for _, r in left], columns, first),
         name,
         (half // wide,),
         meta,
-        [(a, ANYWHERE) for a, _ in left] + [(right, ANYWHERE)],
+        [(a, ANYWHERE) for a, _ in left] + [(v, ANYWHERE) for v in right],
         [((half, n), BF16, pl.BlockSpec((wide, n), lambda i, m: (i, 0)))],
         [
             pltpu.VMEM((2, total, wide), BF16),
             pltpu.VMEM((total, n), BF16),
             pltpu.SemaphoreType.DMA((2, len(left))),
-            pltpu.SemaphoreType.DMA((1, tiles_of(n))),
+            pltpu.SemaphoreType.DMA((len(right), n // tile_of(right[0].shape[1]))),
         ],
         after,
     )[0]
@@ -1100,7 +1118,7 @@
     pieces = lambda values: [(v, k * rows_here) for k, v in enumerate(values)]
 
     def grad(name, left, right, first):
-        return weight_grad(name, meta, pieces(left), right, first, half)
+        return weight_grad(name, meta, pieces(left), right if type(right) is list else [right], first, half)
 
     grad_lower_far = across(grad("lower_far", all_back, hidden, half))
     keep, received = scatter("back_second", [back_before], raise_w)
@@ -1160,15 +1178,14 @@
     )
     far_send = near(product(3))
     far_keep = near(product(1))
-    grad_ins = [grad("in_own", all_one, back_triples[0], 0)]
     send = product(2, far_send)
-    grad_ins += [grad("in_own", all_one, v, 0) for v in back_triples[1:]]
+    grad_in = grad("in_own", all_one, back_triples, 0)
     in_wide, out_wide = pairs * 3 * HEAD_DIM, heads * HEAD_DIM
     moment_heads, square_heads, *deltas = adam(
         "adam_heads", meta, items, by_head,
-        [(v, in_wide, 0) for v in grad_ins] + [(grad_out, out_wide, 0)],
+        [(grad_in, calls * in_wide, 0), (grad_out, out_wide, 0)],
         [(v, in_wide, 0) for v in grad_in_fars] + [(grad_out_far, out_wide, 0)],
-        [(heads_all, in_wide, n) for n in range(calls)] + [(heads_all, out_wide, 3)],
+        [(heads_all, calls * in_wide, 0), (heads_all, out_wide, 3)],
         first_heads[:, None], second_heads[:, None], 0, groups,
     )
     heads_deltas = [deltas[0]] + [

time: 996 us -> 981 us (0.985)
  starting transfers between devices: 66.2 us -> 51.5 us
    pallas_call x81 -> x80, Pallas kernels: 698 us -> 692 us  [run(): pl.pallas_call(body, grid_spec=pltpu.PrefetchScalarGridSpec(num_scalar_pr...]
where the time goes in v3:
time: 981 us; the launch traced here: 970 us
  Pallas kernels  692 us (71%)
  waiting for transfers between devices  205 us (21%)
  starting transfers between devices  51.5 us (5%)
  between operations  15.1 us (2%)
    pallas_call x80, Pallas kernels, run(): pl.pallas_call(body, grid_spec=pltpu.PrefetchScalarGridSpec(num_scalar_pr...  692 us
    ppermute x46, waiting for transfers between devices, swap(): return lax.ppermute(value, axis, [(i, i ^ bit) for i in range(size)])  175 us
    ppermute x46, starting transfers between devices, swap(): return lax.ppermute(value, axis, [(i, i ^ bit) for i in range(size)])  40 us
    ppermute x3, waiting for transfers between devices, local(): lax.ppermute(deltas[k], 'group', [(i, (i + k) % groups) for i in range(gr...  26.2 us
  transfers between devices with their start and end apart: 58, of which 21 were waited for; matrix products, arithmetic and copies ran while one was open for 0% of the time, Pallas kernels for 66%

profile of v3, /device:TPU:24, one launch (start us, length us, event | category | flops | bytes accessed | tf_op | source)
XLA Modules:
  0.0 969.7 jit_solution(3076891146113004998)
XLA Ops:
  31.4 9.3 collective-permute-done.3.refs_3_.refs_6_
  53.8 21.2 %collective-permute-done.8.refs_3_.refs_8_ = bf16[256,2048]{1,0:T(8,128)(2,1)} collective-permute-done((bf16[256,2048]{1,0:T(8,128)(2,1)}, bf16[256,2048]{1,0:T(8,128)(2,1)}, u32[]{:S(2)}, u32[]{:S(2)}) %collective-permute-start.8) | collective-permute-done | bytes 1048608 | tf_op jit(solution)/shard_map/ppermute | solution.py:34
  83.6 22.1 %collective-permute-done.9.refs_3_.refs_10_ = bf16[256,2048]{1,0:T(8,128)(2,1)} collective-permute-done((bf16[256,2048]{1,0:T(8,128)(2,1)}, bf16[256,2048]{1,0:T(8,128)(2,1)}, u32[]{:S(2)}, u32[]{:S(2)}) %collective-permute-start.9) | collective-permute-done | bytes 1048608 | tf_op jit(solution)/shard_map/ppermute | solution.py:34
  118.2 17.2 %collective-permute-done.12.refs_12_ = bf16[256,2048]{1,0:T(8,128)(2,1)} collective-permute-done((bf16[256,2048]{1,0:T(8,128)(2,1)}, bf16[256,2048]{1,0:T(8,128)(2,1)}, u32[]{:S(2)}, u32[]{:S(2)}) %collective-permute-start.12) | collective-permute-done | bytes 1048608 | tf_op jit(solution)/shard_map/ppermute | solution.py:34
  135.4 27.0 %qkv.1 = (bf16[2560,1536]{1,0:T(8,128)(2,1)}, bf16[2048,2048]{1,0:T(8,128)(2,1)}) custom-call(s32[11]{0:T(128)} %pad_add_fusion.refs_0_, bf16[640,2048]{1,0:T(8,128)(2,1)} %get-tuple-element.114.refs_2_.refs_1_, bf16[640,2048]{1,0:T(8,128)(2,1)} %collective-permute-done.4.refs_3_.refs_2_, bf16[640,2048]{1,0:T(8,128)(2,1)} %get-tuple-element.124.refs_3_, ...), custom_call_target="tpu_custom_call" | custom-call | flops 999999995904 | bytes 1 | tf_op jit(solution)/shard_map/qkv/pallas_call | solution.py:50
  166.1 18.6 %attend.2 = (bf16[2560,512]{1,0:T(8,128)(2,1)}, f32[4,5,8,512]{3,2,1,0:T(8,128)}) custom-call(s32[11]{0:T(128)} %pad_add_fusion.refs_0_, bf16[2560,1536]{1,0:T(8,128)(2,1)} %get-tuple-element.130.refs_2_.refs_1_, s32[1]{0:T(128)} %get-tuple-element.134.refs_2_), custom_call_target="tpu_custom_call" | custom-call | flops 999999995904 | bytes 1 | tf_op jit(solution)/shard_map/attend/pallas_call | solution.py:50
  185.8 18.6 %attend.3 = (bf16[2560,512]{1,0:T(8,128)(2,1)}, f32[4,5,8,512]{3,2,1,0:T(8,128)}) custom-call(s32[11]{0:T(128)} %pad_add_fusion.refs_0_, bf16[2560,1536]{1,0:T(8,128)(2,1)} %get-tuple-element.130.refs_2_.refs_1_, bf16[2560,512]{1,0:T(8,128)(2,1)} %get-tuple-element.135.refs_2_, ...), custom_call_target="tpu_custom_call", output_to_operand_aliasing={{0}: (2, {}), {1}: (3, {})} | custom-call | flops 999999995904 | bytes 1 | tf_op jit(solution)/shard_map/attend/pallas_call | solution.py:50
  257.1 48.7 %collective-permute-done.19.refs_3_ = bf16[640,2048]{1,0:T(8,128)(2,1)} collective-permute-done((bf16[640,2048]{1,0:T(8,128)(2,1)}, bf16[640,2048]{1,0:T(8,128)(2,1)}, u32[]{:S(2)}, u32[]{:S(2)}) %collective-permute-start.19) | collective-permute-done | bytes 2621472 | tf_op jit(solution)/shard_map/ppermute | solution.py:34
  305.8 8.4 second_norm.1
  318.4 31.8 %back_hidden.1 = (bf16[2560,2048]{1,0:T(8,128)(2,1)}, bf16[2048,2048]{1,0:T(8,128)(2,1)}) custom-call(s32[11]{0:T(128)} %pad_add_fusion.refs_0_, bf16[640,2048]{1,0:T(8,128)(2,1)} %get-tuple-element.143.refs_1_.refs_4_, bf16[640,2048]{1,0:T(8,128)(2,1)} %collective-permute-done.15.refs_2_, bf16[640,2048]{1,0:T(8,128)(2,1)} %get-tuple-element.150.refs_3_, ...), custom_call_target="tpu_custom_call" | custom-call | flops 999999995904 | bytes 1 | tf_op jit(solution)/shard_map/back_hidden/pallas_call | solution.py:50
  351.5 13.6 %collective-permute-done.23.refs_6_.refs_5_ = bf16[1024,1024]{1,0:T(8,128)(2,1)} collective-permute-done((bf16[1024,1024]{1,0:T(8,128)(2,1)}, bf16[1024,1024]{1,0:T(8,128)(2,1)}, u32[]{:S(2)}, u32[]{:S(2)}) %collective-permute-start.23) | collective-permute-done | bytes 2097184 | tf_op jit(solution)/shard_map/ppermute | solution.py:34
  365.0 29.9 %raise.2 = (bf16[2560,2048]{1,0:T(8,128)(2,1)}, bf16[2560,2048]{1,0:T(8,128)(2,1)}) custom-call(s32[11]{0:T(128)} %pad_add_fusion.refs_0_, bf16[640,2048]{1,0:T(8,128)(2,1)} %get-tuple-element.154.refs_1_, bf16[640,2048]{1,0:T(8,128)(2,1)} %collective-permute-done.21.refs_2_, bf16[1024,1024]{1,0:T(8,128)(2,1)} %get-tuple-element.155.refs_3_.refs_2_, ...), custom_call_target="tpu_custom_call" | custom-call | flops 999999995904 | bytes 1 | tf_op jit(solution)/shard_map/raise/pallas_call | solution.py:50
  401.5 30.3 %raise.3 = (bf16[2560,2048]{1,0:T(8,128)(2,1)}, bf16[2560,2048]{1,0:T(8,128)(2,1)}) custom-call(s32[11]{0:T(128)} %pad_add_fusion.refs_0_, bf16[640,2048]{1,0:T(8,128)(2,1)} %get-tuple-element.162.refs_1_.refs_3_, bf16[640,2048]{1,0:T(8,128)(2,1)} %collective-permute-done.25.refs_2_.refs_4_, ...), custom_call_target="tpu_custom_call", output_to_operand_aliasing={{0}: (8, {}), {1}: (9, {})} | custom-call | flops 999999995904 | bytes 1 | tf_op jit(solution)/shard_map/raise/pallas_call | solution.py:50
  431.8 17.1 %lower_far.1.refs_6_ = bf16[1024,2048]{1,0:T(8,128)(2,1)} custom-call(s32[11]{0:T(128)} %pad_add_fusion.refs_0_, bf16[640,2048]{1,0:T(8,128)(2,1)} %get-tuple-element.143.refs_1_.refs_4_, bf16[640,2048]{1,0:T(8,128)(2,1)} %collective-permute-done.15.refs_2_, bf16[640,2048]{1,0:T(8,128)(2,1)} %get-tuple-element.150.refs_3_, ...), custom_call_target="tpu_custom_call" | custom-call | flops 999999995904 | bytes 1 | tf_op jit(solution)/shard_map/lower_far/pallas_call | solution.py:50
  450.4 11.9 %back_second_3.1.refs_6_ = bf16[640,2048]{1,0:T(8,128)(2,1)} custom-call(s32[11]{0:T(128)} %pad_add_fusion.refs_0_, bf16[2560,2048]{1,0:T(8,128)(2,1)} %get-tuple-element.167.refs_1_.refs_5_, bf16[1024,1024]{1,0:T(8,128)(2,1)} %get-tuple-element.155.refs_3_.refs_2_, bf16[1024,1024]{1,0:T(8,128)(2,1)} %collective-permute-done.22.refs_4_.refs_3_, ...), custom_call_target="tpu_custom_call" | custom-call | flops 999999995904 | bytes 1 | tf_op jit(solution)/shard_map/back_second_3/pallas_call | solution.py:50
  462.4 12.0 %back_second_1.1.refs_7_ = bf16[640,2048]{1,0:T(8,128)(2,1)} custom-call(s32[11]{0:T(128)} %pad_add_fusion.refs_0_, bf16[2560,2048]{1,0:T(8,128)(2,1)} %get-tuple-element.167.refs_1_.refs_5_, bf16[1024,1024]{1,0:T(8,128)(2,1)} %get-tuple-element.155.refs_3_.refs_2_, bf16[1024,1024]{1,0:T(8,128)(2,1)} %collective-permute-done.22.refs_4_.refs_3_, ...), custom_call_target="tpu_custom_call" | custom-call | flops 999999995904 | bytes 1 | tf_op jit(solution)/shard_map/back_second_1/pallas_call | solution.py:50
  475.0 12.5 %back_second_2.1.refs_7_ = bf16[640,2048]{1,0:T(8,128)(2,1)} custom-call(s32[11]{0:T(128)} %pad_add_fusion.refs_0_, bf16[2560,2048]{1,0:T(8,128)(2,1)} %get-tuple-element.167.refs_1_.refs_5_, bf16[1024,1024]{1,0:T(8,128)(2,1)} %get-tuple-element.155.refs_3_.refs_2_, bf16[1024,1024]{1,0:T(8,128)(2,1)} %collective-permute-done.22.refs_4_.refs_3_, ...), custom_call_target="tpu_custom_call" | custom-call | flops 999999995904 | bytes 1 | tf_op jit(solution)/shard_map/back_second_2/pallas_call | solution.py:50
  488.1 12.5 %back_second_0.1.refs_6_.refs_2_ = bf16[640,2048]{1,0:T(8,128)(2,1)} custom-call(s32[11]{0:T(128)} %pad_add_fusion.refs_0_, bf16[2560,2048]{1,0:T(8,128)(2,1)} %get-tuple-element.167.refs_1_.refs_5_, bf16[1024,1024]{1,0:T(8,128)(2,1)} %get-tuple-element.155.refs_3_.refs_2_, bf16[1024,1024]{1,0:T(8,128)(2,1)} %collective-permute-done.22.refs_4_.refs_3_, ...), custom_call_target="tpu_custom_call" | custom-call | flops 999999995904 | bytes 1 | tf_op jit(solution)/shard_map/back_second_0/pallas_call | solution.py:50
  500.6 17.1 %raise_far.1.refs_6_ = bf16[1024,2048]{1,0:T(8,128)(2,1)} custom-call(s32[11]{0:T(128)} %pad_add_fusion.refs_0_, bf16[640,2048]{1,0:T(8,128)(2,1)} %get-tuple-element.154.refs_1_, bf16[640,2048]{1,0:T(8,128)(2,1)} %collective-permute-done.21.refs_2_, bf16[640,2048]{1,0:T(8,128)(2,1)} %get-tuple-element.162.refs_1_.refs_3_, ...), custom_call_target="tpu_custom_call" | custom-call | flops 999999995904 | bytes 1 | tf_op jit(solution)/shard_map/raise_far/pallas_call | solution.py:50
  518.3 17.1 %lower_own.1.refs_6_.refs_1_ = bf16[1024,2048]{1,0:T(8,128)(2,1)} custom-call(s32[11]{0:T(128)} %pad_add_fusion.refs_0_, bf16[640,2048]{1,0:T(8,128)(2,1)} %get-tuple-element.143.refs_1_.refs_4_, bf16[640,2048]{1,0:T(8,128)(2,1)} %collective-permute-done.15.refs_2_, bf16[640,2048]{1,0:T(8,128)(2,1)} %get-tuple-element.150.refs_3_, ...), custom_call_target="tpu_custom_call" | custom-call | flops 999999995904 | bytes 1 | tf_op jit(solution)/shard_map/lower_own/pallas_call | solution.py:50
  535.4 11.2 %collective-permute-done.28.refs_3_ = bf16[640,2048]{1,0:T(8,128)(2,1)} collective-permute-done((bf16[640,2048]{1,0:T(8,128)(2,1)}, bf16[640,2048]{1,0:T(8,128)(2,1)}, u32[]{:S(2)}, u32[]{:S(2)}) %collective-permute-start.28) | collective-permute-done | bytes 2621472 | tf_op jit(solution)/shard_map/ppermute | solution.py:34
  546.6 11.0 %second_back.1 = (f32[640,2048]{1,0:T(8,128)}, f32[8,2048]{1,0:T(8,128)}, bf16[640,2048]{1,0:T(8,128)(2,1)}) custom-call(s32[11]{0:T(128)} %pad_add_fusion.refs_0_, f32[640,2048]{1,0:T(8,128)} %get-tuple-element.153.refs_2_.refs_1_, bf16[640,2048]{1,0:T(8,128)(2,1)} %back_second_0.1.refs_6_.refs_2_, bf16[640,2048]{1,0:T(8,128)(2,1)} %collective-permute-done.28.refs_3_, ...), custom_call_target="tpu_custom_call" | custom-call | flops 999999995904 | bytes 1 | tf_op jit(solution)/shard_map/second_back/pallas_call | solution.py:50
  558.2 17.1 %raise_own.1.refs_1_ = bf16[1024,2048]{1,0:T(8,128)(2,1)} custom-call(s32[11]{0:T(128)} %pad_add_fusion.refs_0_, bf16[640,2048]{1,0:T(8,128)(2,1)} %get-tuple-element.154.refs_1_, bf16[640,2048]{1,0:T(8,128)(2,1)} %collective-permute-done.21.refs_2_, bf16[640,2048]{1,0:T(8,128)(2,1)} %get-tuple-element.162.refs_1_.refs_3_, ...), custom_call_target="tpu_custom_call" | custom-call | flops 999999995904 | bytes 1 | tf_op jit(solution)/shard_map/raise_own/pallas_call | solution.py:50
  576.5 12.1 %lower_3.1.refs_3_ = bf16[640,2048]{1,0:T(8,128)(2,1)} custom-call(s32[11]{0:T(128)} %pad_add_fusion.refs_0_, bf16[2560,2048]{1,0:T(8,128)(2,1)} %get-tuple-element.165.refs_5_.refs_1_, bf16[2048,2048]{1,0:T(8,128)(2,1)} %get-tuple-element.166.refs_2_.refs_3_, s32[1]{0:T(128)} %pause.48.refs_3_), custom_call_target="tpu_custom_call" | custom-call | flops 999999995904 | bytes 1 | tf_op jit(solution)/shard_map/lower_3/pallas_call | solution.py:50
  589.1 11.4 %lower_1.1.refs_4_ = bf16[640,2048]{1,0:T(8,128)(2,1)} custom-call(s32[11]{0:T(128)} %pad_add_fusion.refs_0_, bf16[2560,2048]{1,0:T(8,128)(2,1)} %get-tuple-element.165.refs_5_.refs_1_, bf16[2048,2048]{1,0:T(8,128)(2,1)} %get-tuple-element.166.refs_2_.refs_3_, bf16[640,2048]{1,0:T(8,128)(2,1)} %lower_3.1.refs_3_), custom_call_target="tpu_custom_call" | custom-call | flops 999999995904 | bytes 1 | tf_op jit(solution)/shard_map/lower_1/pallas_call | solution.py:50
  600.7 12.0 %lower_2.1.refs_4_ = bf16[640,2048]{1,0:T(8,128)(2,1)} custom-call(s32[11]{0:T(128)} %pad_add_fusion.refs_0_, bf16[2560,2048]{1,0:T(8,128)(2,1)} %get-tuple-element.165.refs_5_.refs_1_, bf16[2048,2048]{1,0:T(8,128)(2,1)} %get-tuple-element.166.refs_2_.refs_3_, bf16[640,2048]{1,0:T(8,128)(2,1)} %collective-permute-done.31.refs_3_, ...), custom_call_target="tpu_custom_call" | custom-call | flops 999999995904 | bytes 1 | tf_op jit(solution)/shard_map/lower_2/pallas_call | solution.py:50
  614.3 12.1 %lower_0.1.refs_6_.refs_2_ = bf16[640,2048]{1,0:T(8,128)(2,1)} custom-call(s32[11]{0:T(128)} %pad_add_fusion.refs_0_, bf16[2560,2048]{1,0:T(8,128)(2,1)} %get-tuple-element.165.refs_5_.refs_1_, bf16[2048,2048]{1,0:T(8,128)(2,1)} %get-tuple-element.166.refs_2_.refs_3_, bf16[640,2048]{1,0:T(8,128)(2,1)} %collective-permute-done.30.refs_3_, ...), custom_call_target="tpu_custom_call" | custom-call | flops 999999995904 | bytes 1 | tf_op jit(solution)/shard_map/lower_0/pallas_call | solution.py:50
  626.3 19.5 %adam_lower.1 = (f32[1,2,1024,2048]{3,2,1,0:T(8,128)}, f32[1,2,1024,2048]{3,2,1,0:T(8,128)}, bf16[1024,2048]{1,0:T(8,128)(2,1)}) custom-call(s32[11]{0:T(128)} %pad_add_fusion.refs_0_, bf16[1024,2048]{1,0:T(8,128)(2,1)} %lower_own.1.refs_6_.refs_1_, bf16[1024,2048]{1,0:T(8,128)(2,1)} %collective-permute-done.34.refs_2_, ...), custom_call_target="tpu_custom_call" | custom-call | flops 999999995904 | bytes 1 | tf_op jit(solution)/shard_map/adam_lower/pallas_call | solution.py:50
  652.5 12.0 %back_mixed.1.refs_6_.refs_3_ = bf16[2560,512]{1,0:T(8,128)(2,1)} custom-call(s32[11]{0:T(128)} %pad_add_fusion.refs_0_, bf16[640,2048]{1,0:T(8,128)(2,1)} %get-tuple-element.169.refs_1_, bf16[640,2048]{1,0:T(8,128)(2,1)} %collective-permute-done.29.refs_2_, bf16[640,2048]{1,0:T(8,128)(2,1)} %get-tuple-element.171.refs_3_, ...), custom_call_target="tpu_custom_call" | custom-call | flops 999999995904 | bytes 1 | tf_op jit(solution)/shard_map/back_mixed/pallas_call | solution.py:50
  664.5 7.9 out_far.1.refs_9_
  673.1 19.6 %adam_raise.1 = (f32[1,2,1024,2048]{3,2,1,0:T(8,128)}, f32[1,2,1024,2048]{3,2,1,0:T(8,128)}, bf16[1024,2048]{1,0:T(8,128)(2,1)}) custom-call(s32[11]{0:T(128)} %pad_add_fusion.refs_0_, bf16[1024,2048]{1,0:T(8,128)(2,1)} %raise_own.1.refs_1_, bf16[1024,2048]{1,0:T(8,128)(2,1)} %collective-permute-done.36.refs_2_, ...), custom_call_target="tpu_custom_call", output_to_operand_aliasing={{0}: (7, {}), {1}: (8, {})} | custom-call | flops 999999995904 | bytes 1 | tf_op jit(solution)/shard_map/adam_raise/pallas_call | solution.py:50
  692.7 27.4 %attend_back.2.refs_5_.refs_1_ = bf16[2560,768]{1,0:T(8,128)(2,1)} custom-call(s32[11]{0:T(128)} %pad_add_fusion.refs_0_, bf16[2560,1536]{1,0:T(8,128)(2,1)} %get-tuple-element.130.refs_2_.refs_1_, bf16[2560,512]{1,0:T(8,128)(2,1)} %get-tuple-element.139.refs_2_.refs_1_.refs_5_, bf16[2560,512]{1,0:T(8,128)(2,1)} %back_mixed.1.refs_6_.refs_3_, ...), custom_call_target="tpu_custom_call" | custom-call | flops 999999995904 | bytes 1 | tf_op jit(solution)/shard_map/attend_back/pallas_call | solution.py:50
  720.1 9.4 in_far.2.refs_6_
  731.0 7.9 out_own.1.refs_4_.refs_2_
  738.8 6.6 output.1.refs_5_
  745.5 7.8 outer_lower.1
  753.2 27.4 %attend_back.3.refs_5_.refs_2_.refs_6_ = bf16[2560,768]{1,0:T(8,128)(2,1)} custom-call(s32[11]{0:T(128)} %pad_add_fusion.refs_0_, bf16[2560,1536]{1,0:T(8,128)(2,1)} %get-tuple-element.130.refs_2_.refs_1_, bf16[2560,512]{1,0:T(8,128)(2,1)} %get-tuple-element.139.refs_2_.refs_1_.refs_5_, bf16[2560,512]{1,0:T(8,128)(2,1)} %back_mixed.1.refs_6_.refs_3_, ...), custom_call_target="tpu_custom_call" | custom-call | flops 999999995904 | bytes 1 | tf_op jit(solution)/shard_map/attend_back/pallas_call | solution.py:50
  780.6 9.4 in_far.3.refs_4_
  790.8 9.4 back_first_3.1.refs_4_
  800.2 9.5 back_first_1.1.refs_5_
  810.2 10.1 %back_first_2.1.refs_7_ = bf16[640,2048]{1,0:T(8,128)(2,1)} custom-call(s32[11]{0:T(128)} %pad_add_fusion.refs_0_, bf16[2560,768]{1,0:T(8,128)(2,1)} %attend_back.2.refs_5_.refs_1_, bf16[2560,768]{1,0:T(8,128)(2,1)} %attend_back.3.refs_5_.refs_2_.refs_6_, bf16[2048,2048]{1,0:T(8,128)(2,1)} %get-tuple-element.140.refs_2_.refs_5_.refs_3_.refs_6_.refs_7_, ...), custom_call_target="tpu_custom_call" | custom-call | flops 999999995904 | bytes 1 | tf_op jit(solution)/shard_map/back_first_2/pallas_call | solution.py:50
  821.3 13.9 %in_own.1.refs_1_ = bf16[1024,1536]{1,0:T(8,128)(2,1)} custom-call(s32[11]{0:T(128)} %pad_add_fusion.refs_0_, bf16[640,2048]{1,0:T(8,128)(2,1)} %get-tuple-element.114.refs_2_.refs_1_, bf16[640,2048]{1,0:T(8,128)(2,1)} %collective-permute-done.4.refs_3_.refs_2_, bf16[640,2048]{1,0:T(8,128)(2,1)} %get-tuple-element.124.refs_3_, ...), custom_call_target="tpu_custom_call" | custom-call | flops 999999995904 | bytes 1 | tf_op jit(solution)/shard_map/in_own/pallas_call | solution.py:50
  835.2 21.8 %adam_heads.1 = (f32[1,1,1024,2048]{3,2,1,0:T(8,128)}, f32[1,1,1024,2048]{3,2,1,0:T(8,128)}, bf16[256,2048]{1,0:T(8,128)(2,1)}, bf16[256,2048]{1,0:T(8,128)(2,1)...) custom-call(s32[11]{0:T(128)} %pad_add_fusion.refs_0_, bf16[1024,1536]{1,0:T(8,128)(2,1)} %in_own.1.refs_1_, ...), custom_call_target="tpu_custom_call" | custom-call | flops 999999995904 | bytes 1 | tf_op jit(solution)/shard_map/adam_heads/pallas_call | solution.py:50
  863.4 10.0 %back_first_0.1.refs_4_ = bf16[640,2048]{1,0:T(8,128)(2,1)} custom-call(s32[11]{0:T(128)} %pad_add_fusion.refs_0_, bf16[2560,768]{1,0:T(8,128)(2,1)} %attend_back.2.refs_5_.refs_1_, bf16[2560,768]{1,0:T(8,128)(2,1)} %attend_back.3.refs_5_.refs_2_.refs_6_, bf16[2048,2048]{1,0:T(8,128)(2,1)} %get-tuple-element.140.refs_2_.refs_5_.refs_3_.refs_6_.refs_7_, ...), custom_call_target="tpu_custom_call" | custom-call | flops 999999995904 | bytes 1 | tf_op jit(solution)/shard_map/back_first_0/pallas_call | solution.py:50
  879.5 10.5 %first_back.1 = (f32[640,2048]{1,0:T(8,128)}, f32[8,2048]{1,0:T(8,128)}) custom-call(s32[11]{0:T(128)} %pad_add_fusion.refs_0_, bf16[640,2048]{1,0:T(8,128)(2,1)} %refs_1_.13, f32[2,2048]{1,0:T(2,128)} %get-tuple-element.113.refs_2_.refs_4_.refs_5_, f32[640,2048]{1,0:T(8,128)} %get-tuple-element.168.refs_6_.refs_3_, bf16[640,2048]{1,0:T(8,128)(2,1)} %back_first_0.1.refs_4_, ...), custom_call_target="tpu_custom_call" | custom-call | flops 999999995904 | bytes 1 | tf_op jit(solution)/shard_map/first_back/pallas_call | solution.py:50
  918.6 7.6 outer_raise.1
  926.4 26.2 %collective-permute-done.47.refs_3_ = bf16[256,2048]{1,0:T(8,128)(2,1)} collective-permute-done((bf16[256,2048]{1,0:T(8,128)(2,1)}, bf16[256,2048]{1,0:T(8,128)(2,1)}, u32[]{:S(2)}, u32[]{:S(2)}) %collective-permute-start.47) | collective-permute-done | bytes 1048608 | tf_op jit(solution)/shard_map/ppermute | solution.py:1192
  952.6 8.7 outer_heads.1
  (173 shorter events, 188.5 us)
Async XLA Ops:
  7.2 156.5 %all-gather.5.cloned.1.call-start = ((), (), s32[]{:S(2)}) async-start(), calls=%async_computation.2 | async-start | bytes 2621440 | tf_op jit(solution)/shard_map/all_gather | solution.py:1053
  7.2 10.7 %collective-permute-start.2 = (f32[2,512]{1,0:T(2,128)}, f32[2,512]{1,0:T(2,128)}, u32[]{:S(2)}, u32[]{:S(2)}) collective-permute-start(f32[2,512]{1,0:T(2,128)} %refs_1_.8), channel_id=1, source_target_pairs={{0,24},{8,16},{16,8},{24,0},{1,25},{9,17},{17,9},{25,1},{2,26},{10... | collective-permute-start | bytes 12296 | tf_op jit(solution)/shard_map/ppermute | solution.py:34
  7.3 10.6 %collective-permute-start.1 = (f32[2,512]{1,0:T(2,128)}, f32[2,512]{1,0:T(2,128)}, u32[]{:S(2)}, u32[]{:S(2)}) collective-permute-start(f32[2,512]{1,0:T(2,128)} %refs_1_.8), channel_id=1, source_target_pairs={{0,16},{8,24},{16,0},{24,8},{1,17},{9,25},{17,1},{25,9},{2,18},{10... | collective-permute-start | bytes 12296 | tf_op jit(solution)/shard_map/ppermute | solution.py:34
  9.2 8.7 collective-permute-start
  16.2 31.6 %collective-permute-start.6 = (bf16[256,2048]{1,0:T(8,128)(2,1)}, bf16[256,2048]{1,0:T(8,128)(2,1)}, u32[]{:S(2)}, u32[]{:S(2)}) collective-permute-start(bf16[256,2048]{1,0:T(8,128)(2,1)} %cast_heads.1.refs_5_), channel_id=1, source_target_pairs={{0,8},{8,16},{16,24},{24,0},{1,9},{9,17},{17,25},{25,1},{2,10},{10... | collective-permute-start | bytes 3145736 | tf_op jit(solution)/shard_map/ppermute | solution.py:1000
  16.3 24.4 %collective-permute-start.3 = (bf16[256,2048]{1,0:T(8,128)(2,1)}, bf16[256,2048]{1,0:T(8,128)(2,1)}, u32[]{:S(2)}, u32[]{:S(2)}) collective-permute-start(bf16[256,2048]{1,0:T(8,128)(2,1)} %cast_heads.1.refs_5_), channel_id=1, source_target_pairs={{0,4},{4,0},{1,5},{5,1},{2,6},{6,2},{3,7},{7,3},{8,12},{12,8},{9,1... | collective-permute-start | bytes 3145736 | tf_op jit(solution)/shard_map/ppermute | solution.py:34
  25.9 57.7 %collective-permute-start.5 = (bf16[640,2048]{1,0:T(8,128)(2,1)}, bf16[640,2048]{1,0:T(8,128)(2,1)}, u32[]{:S(2)}, u32[]{:S(2)}) collective-permute-start(bf16[640,2048]{1,0:T(8,128)(2,1)} %get-tuple-element.114.refs_2_.refs_1_), channel_id=1, source_target_pairs={{0,2},{1,3},{2,0},{3,1},{4,6},{5,7},{6,4},{7,5},{8,10},{9,11},{10,... | collective-permute-start | bytes 7864328 | tf_op jit(solution)/shard_map/ppermute | solution.py:34
  49.0 25.9 %collective-permute-start.8 = (bf16[256,2048]{1,0:T(8,128)(2,1)}, bf16[256,2048]{1,0:T(8,128)(2,1)}, u32[]{:S(2)}, u32[]{:S(2)}) collective-permute-start(bf16[256,2048]{1,0:T(8,128)(2,1)} %get-tuple-element.120.refs_7_), channel_id=1, source_target_pairs={{0,4},{4,0},{1,5},{5,1},{2,6},{6,2},{3,7},{7,3},{8,12},{12,8},{9,1... | collective-permute-start | bytes 3145736 | tf_op jit(solution)/shard_map/ppermute | solution.py:34
  50.6 25.6 %collective-permute-start.7 = (bf16[256,2048]{1,0:T(8,128)(2,1)}, bf16[256,2048]{1,0:T(8,128)(2,1)}, u32[]{:S(2)}, u32[]{:S(2)}) collective-permute-start(bf16[256,2048]{1,0:T(8,128)(2,1)} %get-tuple-element.120.refs_7_), channel_id=1, source_target_pairs={{0,8},{8,16},{16,24},{24,0},{1,9},{9,17},{17,25},{25,1},{2,10},{10... | collective-permute-start | bytes 3145736 | tf_op jit(solution)/shard_map/ppermute | solution.py:1000
  78.0 29.6 %collective-permute-start.11 = (bf16[256,2048]{1,0:T(8,128)(2,1)}, bf16[256,2048]{1,0:T(8,128)(2,1)}, u32[]{:S(2)}, u32[]{:S(2)}) collective-permute-start(bf16[256,2048]{1,0:T(8,128)(2,1)} %get-tuple-element.123.refs_9_), channel_id=1, source_target_pairs={{0,8},{8,16},{16,24},{24,0},{1,9},{9,17},{17,25},{25,1},{2,10},{10... | collective-permute-start | bytes 3145736 | tf_op jit(solution)/shard_map/ppermute | solution.py:1000
  81.2 24.5 %collective-permute-start.9 = (bf16[256,2048]{1,0:T(8,128)(2,1)}, bf16[256,2048]{1,0:T(8,128)(2,1)}, u32[]{:S(2)}, u32[]{:S(2)}) collective-permute-start(bf16[256,2048]{1,0:T(8,128)(2,1)} %get-tuple-element.123.refs_9_), channel_id=1, source_target_pairs={{0,4},{4,0},{1,5},{5,1},{2,6},{6,2},{3,7},{7,3},{8,12},{12,8},{9,1... | collective-permute-start | bytes 3145736 | tf_op jit(solution)/shard_map/ppermute | solution.py:34
  109.5 25.9 %collective-permute-start.12 = (bf16[256,2048]{1,0:T(8,128)(2,1)}, bf16[256,2048]{1,0:T(8,128)(2,1)}, u32[]{:S(2)}, u32[]{:S(2)}) collective-permute-start(bf16[256,2048]{1,0:T(8,128)(2,1)} %get-tuple-element.126.refs_11_), channel_id=1, source_target_pairs={{0,4},{4,0},{1,5},{5,1},{2,6},{6,2},{3,7},{7,3},{8,12},{12,8},{9,1... | collective-permute-start | bytes 3145736 | tf_op jit(solution)/shard_map/ppermute | solution.py:34
  114.7 92.8 %all-gather.7.cloned.1.call-start = ((), (), s32[]{:S(2)}) async-start(), calls=%async_computation.3 | async-start | bytes 2621440 | tf_op jit(solution)/shard_map/all_gather | solution.py:1053
  116.6 98.3 %collective-permute-start.13 = (bf16[640,2048]{1,0:T(8,128)(2,1)}, bf16[640,2048]{1,0:T(8,128)(2,1)}, u32[]{:S(2)}, u32[]{:S(2)}) collective-permute-start(bf16[640,2048]{1,0:T(8,128)(2,1)} %get-tuple-element.143.refs_1_.refs_4_), channel_id=1, source_target_pairs={{0,2},{1,3},{2,0},{3,1},{4,6},{5,7},{6,4},{7,5},{8,10},{9,11},{10,... | collective-permute-start | bytes 7864328 | tf_op jit(solution)/shard_map/ppermute | solution.py:34
  163.6 90.8 %all-gather.9.cloned.1.call-start = ((), (), s32[]{:S(2)}) async-start(), calls=%async_computation.4 | async-start | bytes 2621440 | tf_op jit(solution)/shard_map/all_gather | solution.py:1053
  165.5 47.6 %collective-permute-start.14 = (bf16[1024,1024]{1,0:T(8,128)(2,1)}, bf16[1024,1024]{1,0:T(8,128)(2,1)}, u32[]{:S(2)}, u32[]{:S(2)}) collective-permute-start(bf16[1024,1024]{1,0:T(8,128)(2,1)} %get-tuple-element.145.refs_5_), channel_id=1, source_target_pairs={{0,4},{4,0},{1,5},{5,1},{2,6},{6,2},{3,7},{7,3},{8,12},{12,8},{9,1... | collective-permute-start | bytes 6291464 | tf_op jit(solution)/shard_map/ppermute | solution.py:34
  204.4 111.3 %all-gather.11.cloned.1.call-start = ((), (), s32[]{:S(2)}) async-start(), calls=%async_computation.5 | async-start | bytes 2621440 | tf_op jit(solution)/shard_map/all_gather | solution.py:1053
  214.3 104.1 %collective-permute-start.24 = (bf16[1024,1024]{1,0:T(8,128)(2,1)}, bf16[1024,1024]{1,0:T(8,128)(2,1)}, u32[]{:S(2)}, u32[]{:S(2)}) collective-permute-start(bf16[1024,1024]{1,0:T(8,128)(2,1)} %get-tuple-element.158.refs_7_), channel_id=1, source_target_pairs={{0,4},{4,0},{1,5},{5,1},{2,6},{6,2},{3,7},{7,3},{8,12},{12,8},{9,1... | collective-permute-start | bytes 6291464 | tf_op jit(solution)/shard_map/ppermute | solution.py:34
  216.8 9.0 collective-permute-start.16
  219.2 526.3 %reduce-scatter.3.cloned.1.call-start = ((), (), s32[]{:S(2)}) async-start(), calls=%async_computation.6 | async-start | bytes 5242880 | tf_op jit(solution)/shard_map/reduce_scatter | solution.py:1139
  246.5 59.3 %collective-permute-start.19 = (bf16[640,2048]{1,0:T(8,128)(2,1)}, bf16[640,2048]{1,0:T(8,128)(2,1)}, u32[]{:S(2)}, u32[]{:S(2)}) collective-permute-start(bf16[640,2048]{1,0:T(8,128)(2,1)} %project_2.1.refs_4_), channel_id=1, source_target_pairs={{0,2},{1,3},{2,0},{3,1},{4,6},{5,7},{6,4},{7,5},{8,10},{9,11},{10,... | collective-permute-start | bytes 7864328 | tf_op jit(solution)/shard_map/ppermute | solution.py:34
  255.6 95.9 %collective-permute-start.22 = (bf16[1024,1024]{1,0:T(8,128)(2,1)}, bf16[1024,1024]{1,0:T(8,128)(2,1)}, u32[]{:S(2)}, u32[]{:S(2)}) collective-permute-start(bf16[1024,1024]{1,0:T(8,128)(2,1)} %get-tuple-element.155.refs_3_.refs_2_), channel_id=1, source_target_pairs={{0,4},{4,0},{1,5},{5,1},{2,6},{6,2},{3,7},{7,3},{8,12},{12,8},{9,1... | collective-permute-start | bytes 6291464 | tf_op jit(solution)/shard_map/ppermute | solution.py:34
  314.2 36.1 %collective-permute-start.21 = (bf16[640,2048]{1,0:T(8,128)(2,1)}, bf16[640,2048]{1,0:T(8,128)(2,1)}, u32[]{:S(2)}, u32[]{:S(2)}) collective-permute-start(bf16[640,2048]{1,0:T(8,128)(2,1)} %get-tuple-element.154.refs_1_), channel_id=1, source_target_pairs={{0,1},{1,0},{2,3},{3,2},{4,5},{5,4},{6,7},{7,6},{8,9},{9,8},{10,11... | collective-permute-start | bytes 7864328 | tf_op jit(solution)/shard_map/ppermute | solution.py:34
  314.2 80.8 %collective-permute-start.20 = (bf16[640,2048]{1,0:T(8,128)(2,1)}, bf16[640,2048]{1,0:T(8,128)(2,1)}, u32[]{:S(2)}, u32[]{:S(2)}) collective-permute-start(bf16[640,2048]{1,0:T(8,128)(2,1)} %get-tuple-element.154.refs_1_), channel_id=1, source_target_pairs={{0,2},{1,3},{2,0},{3,1},{4,6},{5,7},{6,4},{7,5},{8,10},{9,11},{10,... | collective-permute-start | bytes 7864328 | tf_op jit(solution)/shard_map/ppermute | solution.py:34
  316.9 48.1 %collective-permute-start.23 = (bf16[1024,1024]{1,0:T(8,128)(2,1)}, bf16[1024,1024]{1,0:T(8,128)(2,1)}, u32[]{:S(2)}, u32[]{:S(2)}) collective-permute-start(bf16[1024,1024]{1,0:T(8,128)(2,1)} %get-tuple-element.157.refs_5_.refs_4_), channel_id=1, source_target_pairs={{0,4},{4,0},{1,5},{5,1},{2,6},{6,2},{3,7},{7,3},{8,12},{12,8},{9,1... | collective-permute-start | bytes 6291464 | tf_op jit(solution)/shard_map/ppermute | solution.py:34
  448.9 177.4 %collective-permute-start.34 = (bf16[1024,2048]{1,0:T(8,128)(2,1)}, bf16[1024,2048]{1,0:T(8,128)(2,1)}, u32[]{:S(2)}, u32[]{:S(2)}) collective-permute-start(bf16[1024,2048]{1,0:T(8,128)(2,1)} %lower_far.1.refs_6_), channel_id=1, source_target_pairs={{0,4},{4,0},{1,5},{5,1},{2,6},{6,2},{3,7},{7,3},{8,12},{12,8},{9,1... | collective-permute-start | bytes 12582920 | tf_op jit(solution)/shard_map/ppermute | solution.py:34
  462.3 12.7 %collective-permute-start.27 = (bf16[640,2048]{1,0:T(8,128)(2,1)}, bf16[640,2048]{1,0:T(8,128)(2,1)}, u32[]{:S(2)}, u32[]{:S(2)}) collective-permute-start(bf16[640,2048]{1,0:T(8,128)(2,1)} %back_second_3.1.refs_6_), channel_id=1, source_target_pairs={{0,1},{1,0},{2,3},{3,2},{4,5},{5,4},{6,7},{7,6},{8,9},{9,8},{10,11... | collective-permute-start | bytes 7864328 | tf_op jit(solution)/shard_map/ppermute | solution.py:34
  474.4 13.6 %collective-permute-start.26 = (bf16[640,2048]{1,0:T(8,128)(2,1)}, bf16[640,2048]{1,0:T(8,128)(2,1)}, u32[]{:S(2)}, u32[]{:S(2)}) collective-permute-start(bf16[640,2048]{1,0:T(8,128)(2,1)} %back_second_1.1.refs_7_), channel_id=1, source_target_pairs={{0,1},{1,0},{2,3},{3,2},{4,5},{5,4},{6,7},{7,6},{8,9},{9,8},{10,11... | collective-permute-start | bytes 7864328 | tf_op jit(solution)/shard_map/ppermute | solution.py:34
  487.5 59.2 %collective-permute-start.28 = (bf16[640,2048]{1,0:T(8,128)(2,1)}, bf16[640,2048]{1,0:T(8,128)(2,1)}, u32[]{:S(2)}, u32[]{:S(2)}) collective-permute-start(bf16[640,2048]{1,0:T(8,128)(2,1)} %back_second_2.1.refs_7_), channel_id=1, source_target_pairs={{0,2},{1,3},{2,0},{3,1},{4,6},{5,7},{6,4},{7,5},{8,10},{9,11},{10,... | collective-permute-start | bytes 7864328 | tf_op jit(solution)/shard_map/ppermute | solution.py:34
  517.7 155.4 %collective-permute-start.36 = (bf16[1024,2048]{1,0:T(8,128)(2,1)}, bf16[1024,2048]{1,0:T(8,128)(2,1)}, u32[]{:S(2)}, u32[]{:S(2)}) collective-permute-start(bf16[1024,2048]{1,0:T(8,128)(2,1)} %raise_far.1.refs_6_), channel_id=1, source_target_pairs={{0,4},{4,0},{1,5},{5,1},{2,6},{6,2},{3,7},{7,3},{8,12},{12,8},{9,1... | collective-permute-start | bytes 12582920 | tf_op jit(solution)/shard_map/ppermute | solution.py:34
  557.6 88.3 %collective-permute-start.33 = (bf16[640,2048]{1,0:T(8,128)(2,1)}, bf16[640,2048]{1,0:T(8,128)(2,1)}, u32[]{:S(2)}, u32[]{:S(2)}) collective-permute-start(bf16[640,2048]{1,0:T(8,128)(2,1)} %get-tuple-element.169.refs_1_), channel_id=1, source_target_pairs={{0,2},{1,3},{2,0},{3,1},{4,6},{5,7},{6,4},{7,5},{8,10},{9,11},{10,... | collective-permute-start | bytes 7864328 | tf_op jit(solution)/shard_map/ppermute | solution.py:34
  558.2 17.1 %collective-permute-start.29 = (bf16[640,2048]{1,0:T(8,128)(2,1)}, bf16[640,2048]{1,0:T(8,128)(2,1)}, u32[]{:S(2)}, u32[]{:S(2)}) collective-permute-start(bf16[640,2048]{1,0:T(8,128)(2,1)} %get-tuple-element.169.refs_1_), channel_id=1, source_target_pairs={{0,1},{1,0},{2,3},{3,2},{4,5},{5,4},{6,7},{7,6},{8,9},{9,8},{10,11... | collective-permute-start | bytes 7864328 | tf_op jit(solution)/shard_map/ppermute | solution.py:34
  588.6 12.1 %collective-permute-start.31 = (bf16[640,2048]{1,0:T(8,128)(2,1)}, bf16[640,2048]{1,0:T(8,128)(2,1)}, u32[]{:S(2)}, u32[]{:S(2)}) collective-permute-start(bf16[640,2048]{1,0:T(8,128)(2,1)} %lower_3.1.refs_3_), channel_id=1, source_target_pairs={{0,1},{1,0},{2,3},{3,2},{4,5},{5,4},{6,7},{7,6},{8,9},{9,8},{10,11... | collective-permute-start | bytes 7864328 | tf_op jit(solution)/shard_map/ppermute | solution.py:34
  600.6 13.7 %collective-permute-start.30 = (bf16[640,2048]{1,0:T(8,128)(2,1)}, bf16[640,2048]{1,0:T(8,128)(2,1)}, u32[]{:S(2)}, u32[]{:S(2)}) collective-permute-start(bf16[640,2048]{1,0:T(8,128)(2,1)} %lower_1.1.refs_4_), channel_id=1, source_target_pairs={{0,1},{1,0},{2,3},{3,2},{4,5},{5,4},{6,7},{7,6},{8,9},{9,8},{10,11... | collective-permute-start | bytes 7864328 | tf_op jit(solution)/shard_map/ppermute | solution.py:34
  612.7 126.1 %collective-permute-start.32 = (bf16[640,2048]{1,0:T(8,128)(2,1)}, bf16[640,2048]{1,0:T(8,128)(2,1)}, u32[]{:S(2)}, u32[]{:S(2)}) collective-permute-start(bf16[640,2048]{1,0:T(8,128)(2,1)} %lower_2.1.refs_4_), channel_id=1, source_target_pairs={{0,2},{1,3},{2,0},{3,1},{4,6},{5,7},{6,4},{7,5},{8,10},{9,11},{10,... | collective-permute-start | bytes 7864328 | tf_op jit(solution)/shard_map/ppermute | solution.py:34
  645.9 272.8 %reduce-scatter.5.cloned.1.call-start = ((), (), s32[]{:S(2)}) async-start(), calls=%async_computation.7 | async-start | bytes 5242880 | tf_op jit(solution)/shard_map/reduce_scatter | solution.py:1139
  672.3 162.9 %collective-permute-start.41 = (bf16[1024,512]{1,0:T(8,128)(2,1)}, bf16[1024,512]{1,0:T(8,128)(2,1)}, u32[]{:S(2)}, u32[]{:S(2)}) collective-permute-start(bf16[1024,512]{1,0:T(8,128)(2,1)} %out_far.1.refs_9_), channel_id=1, source_target_pairs={{0,4},{4,0},{1,5},{5,1},{2,6},{6,2},{3,7},{7,3},{8,12},{12,8},{9,1... | collective-permute-start | bytes 3145736 | tf_op jit(solution)/shard_map/ppermute | solution.py:34
  729.5 105.7 %collective-permute-start.39 = (bf16[1024,768]{1,0:T(8,128)(2,1)}, bf16[1024,768]{1,0:T(8,128)(2,1)}, u32[]{:S(2)}, u32[]{:S(2)}) collective-permute-start(bf16[1024,768]{1,0:T(8,128)(2,1)} %in_far.2.refs_6_), channel_id=1, source_target_pairs={{0,4},{4,0},{1,5},{5,1},{2,6},{6,2},{3,7},{7,3},{8,12},{12,8},{9,1... | collective-permute-start | bytes 4718600 | tf_op jit(solution)/shard_map/ppermute | solution.py:34
  790.0 45.2 %collective-permute-start.40 = (bf16[1024,768]{1,0:T(8,128)(2,1)}, bf16[1024,768]{1,0:T(8,128)(2,1)}, u32[]{:S(2)}, u32[]{:S(2)}) collective-permute-start(bf16[1024,768]{1,0:T(8,128)(2,1)} %in_far.3.refs_4_), channel_id=1, source_target_pairs={{0,4},{4,0},{1,5},{5,1},{2,6},{6,2},{3,7},{7,3},{8,12},{12,8},{9,1... | collective-permute-start | bytes 4718600 | tf_op jit(solution)/shard_map/ppermute | solution.py:34
  800.1 10.1 %collective-permute-start.38 = (bf16[640,2048]{1,0:T(8,128)(2,1)}, bf16[640,2048]{1,0:T(8,128)(2,1)}, u32[]{:S(2)}, u32[]{:S(2)}) collective-permute-start(bf16[640,2048]{1,0:T(8,128)(2,1)} %back_first_3.1.refs_4_), channel_id=1, source_target_pairs={{0,1},{1,0},{2,3},{3,2},{4,5},{5,4},{6,7},{7,6},{8,9},{9,8},{10,11... | collective-permute-start | bytes 7864328 | tf_op jit(solution)/shard_map/ppermute | solution.py:34
  809.7 53.7 %collective-permute-start.37 = (bf16[640,2048]{1,0:T(8,128)(2,1)}, bf16[640,2048]{1,0:T(8,128)(2,1)}, u32[]{:S(2)}, u32[]{:S(2)}) collective-permute-start(bf16[640,2048]{1,0:T(8,128)(2,1)} %back_first_1.1.refs_5_), channel_id=1, source_target_pairs={{0,1},{1,0},{2,3},{3,2},{4,5},{5,4},{6,7},{7,6},{8,9},{9,8},{10,11... | collective-permute-start | bytes 7864328 | tf_op jit(solution)/shard_map/ppermute | solution.py:34
  820.3 59.2 %collective-permute-start.42 = (bf16[640,2048]{1,0:T(8,128)(2,1)}, bf16[640,2048]{1,0:T(8,128)(2,1)}, u32[]{:S(2)}, u32[]{:S(2)}) collective-permute-start(bf16[640,2048]{1,0:T(8,128)(2,1)} %back_first_2.1.refs_7_), channel_id=1, source_target_pairs={{0,2},{1,3},{2,0},{3,1},{4,6},{5,7},{6,4},{7,5},{8,10},{9,11},{10,... | collective-permute-start | bytes 7864328 | tf_op jit(solution)/shard_map/ppermute | solution.py:34
  857.0 69.2 %collective-permute-start.46 = (bf16[256,2048]{1,0:T(8,128)(2,1)}, bf16[256,2048]{1,0:T(8,128)(2,1)}, u32[]{:S(2)}, u32[]{:S(2)}) collective-permute-start(bf16[256,2048]{1,0:T(8,128)(2,1)} %get-tuple-element.185), channel_id=1, source_target_pairs={{0,8},{8,16},{16,24},{24,0},{1,9},{9,17},{17,25},{25,1},{2,10},{10... | collective-permute-start | bytes 3145736 | tf_op jit(solution)/shard_map/ppermute | solution.py:1192
  857.1 95.4 %collective-permute-start.47 = (bf16[256,2048]{1,0:T(8,128)(2,1)}, bf16[256,2048]{1,0:T(8,128)(2,1)}, u32[]{:S(2)}, u32[]{:S(2)}) collective-permute-start(bf16[256,2048]{1,0:T(8,128)(2,1)} %get-tuple-element.186), channel_id=1, source_target_pairs={{0,16},{8,24},{16,0},{24,8},{1,17},{9,25},{17,1},{25,9},{2,18},{10... | collective-permute-start | bytes 3145736 | tf_op jit(solution)/shard_map/ppermute | solution.py:1192
  861.5 91.1 %collective-permute-start.48 = (bf16[256,2048]{1,0:T(8,128)(2,1)}, bf16[256,2048]{1,0:T(8,128)(2,1)}, u32[]{:S(2)}, u32[]{:S(2)}) collective-permute-start(bf16[256,2048]{1,0:T(8,128)(2,1)} %get-tuple-element.187), channel_id=1, source_target_pairs={{0,24},{8,0},{16,8},{24,16},{1,25},{9,1},{17,9},{25,17},{2,26},{10... | collective-permute-start | bytes 3145736 | tf_op jit(solution)/shard_map/ppermute | solution.py:1192
  912.4 48.8 %collective-permute-start.49 = (f32[2,512]{1,0:T(2,128)}, f32[2,512]{1,0:T(2,128)}, u32[]{:S(2)}, u32[]{:S(2)}) collective-permute-start(f32[2,512]{1,0:T(2,128)} %get-tuple-element.211), channel_id=1, source_target_pairs={{0,8},{8,0},{16,24},{24,16},{1,9},{9,1},{17,25},{25,17},{2,10},{10... | collective-permute-start | bytes 12296 | tf_op jit(solution)/shard_map/ppermute | solution.py:34
  912.4 48.8 %collective-permute-start.51 = (f32[2,512]{1,0:T(2,128)}, f32[2,512]{1,0:T(2,128)}, u32[]{:S(2)}, u32[]{:S(2)}) collective-permute-start(f32[2,512]{1,0:T(2,128)} %get-tuple-element.212), channel_id=1, source_target_pairs={{0,24},{8,16},{16,8},{24,0},{1,25},{9,17},{17,9},{25,1},{2,26},{10... | collective-permute-start | bytes 12296 | tf_op jit(solution)/shard_map/ppermute | solution.py:34
  926.3 35.0 %collective-permute-start.50 = (f32[2,512]{1,0:T(2,128)}, f32[2,512]{1,0:T(2,128)}, u32[]{:S(2)}, u32[]{:S(2)}) collective-permute-start(f32[2,512]{1,0:T(2,128)} %get-tuple-element.213), channel_id=1, source_target_pairs={{0,16},{8,24},{16,0},{24,8},{1,17},{9,25},{17,1},{25,9},{2,18},{10... | collective-permute-start | bytes 12296 | tf_op jit(solution)/shard_map/ppermute | solution.py:34
  (17 other events, 86.4 us)
Sparse Core Ops, SparseCore 0:
  114.8 43.7 all-gather.4
  163.7 43.7 all-gather.6
  209.7 44.6 all-gather.8
  256.4 44.6 all-gather.10
  646.0 75.1 reduce-scatter.2
  731.1 76.1 reduce-scatter.4

commit v4 on v3

--- a/solution.py
+++ b/solution.py
@@ -471,14 +471,14 @@
 
 def rows_matmul(
     name, meta, pieces, weight, finish, extra, outs, use=None, rows=None, saved=False, staged=False, filled=(),
-    after=()
+    block_column=0, columns=None, after=()
 ):
     strips, places = zip(*weight)
     tall, depth = pieces[0].shape
     wide = max(place[1] + place[5] for place in places)
     use = use or wide
     count, parts = len(pieces), len(strips)
-    block = lambda index: pl.BlockSpec((tall, use), lambda i, m: (index(i), 0))
+    block = lambda index: pl.BlockSpec((tall, use), lambda i, m: (index(i), block_column))
     more = [((depth, wide), BF16, pl.BlockSpec((depth // count, wide), lambda i, m: (i, 0)))] if saved else []
     ins = [(p, ANYWHERE) for p in pieces] + [(p, ANYWHERE) for p in strips] + [(a, block(f)) for a, f in extra]
     return run(
@@ -487,7 +487,7 @@
         (count,),
         meta,
         ins + [(v, ANYWHERE) for v in filled],
-        [((rows or count * tall, use), d, block(f)) for d, f in outs] + more,
+        [((rows or count * tall, columns or use), d, block(f)) for d, f in outs] + more,
         [
             pltpu.VMEM((2, tall, depth), BF16),
             pltpu.VMEM((depth, wide), BF16),
@@ -986,11 +986,13 @@
     def gather_near(even, copy):
         return [near(copy)] + [near(v) for v in even[1:]]
 
-    def scatter(name, x, weight):
+    def scatter(name, x, weight, between=None):
         product = lambda n, received=None: term(
             f"{name}_{n}", meta, x, weight, rows_here, ranks, n, received
         )
         far_send = near(product(3))
+        if between:
+            between()
         far_keep = near(product(1))
         send = product(2, far_send)
         keep = product(0, far_keep)
@@ -1103,18 +1105,22 @@
     lower_w = [part_of(lower_all)]
     wait(after=[odd_first])
 
-    def feed(pieces, first, filled=()):
+    def feed(pieces, first, weight, filled=(), column=0):
         return rows_matmul(
-            "raise", meta, pieces, raise_w, store_gelu, [(back_hidden, lambda i: i + first)],
+            "raise", meta, pieces, weight, store_gelu, [(back_hidden, lambda i: i + first)],
             [(BF16, lambda i: i + first)] * 2, rows=total, staged=True, filled=filled,
+            block_column=column, columns=units,
         )
 
-    filled = feed([even_two[0], odd_first], 0)
+    filled = ()
+    for n in range(2):
+        unit_half = [part_of(raise_own[n]), part_of(raise_far[n], lambda m: half)]
+        filled = feed([even_two[0], odd_first], 0, unit_half, filled, n)
     even_two[1:] = wait(*even_two[1:])
     odd_two = [odd_first] + [near(v) for v in even_two[1:]]
     wait()
     all_two = ordered(even_two, odd_two)
-    hidden, back_before = feed(all_two[2:], 2, filled)
+    hidden, back_before = feed(all_two[2:], 2, raise_w, filled)
     pieces = lambda values: [(v, k * rows_here) for k, v in enumerate(values)]
 
     def grad(name, left, right, first):
@@ -1124,16 +1130,21 @@
     keep, received = scatter("back_second", [back_before], raise_w)
     grad_raise_far = across(grad("raise_far", all_two, back_before, half))
     grad_lower = grad("lower_own", all_back, hidden, 0)
-    back_middle, gain_second, back_low_middle = run(
-        lambda meta, *refs: second_back_kernel(*refs), "second_back", (steps,), meta,
-        [(v, row_block) for v in (middle, keep, received, back_low)] + [(gains, both)],
-        [(row_shape, F32, row_block), ((8, width), F32, gain_block), (row_shape, BF16, row_block)],
-    )
-    even_middle = gather_far(back_low_middle)
-    odd_first = near(back_low_middle)
-    grad_raise = grad("raise_own", all_two, back_before, 0)
-    wait(after=[odd_first])
-    out_keep, out_received = scatter("lower", [hidden], lower_w)
+    middle_back = []
+
+    def second_back():
+        middle_back.extend(run(
+            lambda meta, *refs: second_back_kernel(*refs), "second_back", (steps,), meta,
+            [(v, row_block) for v in (middle, keep, received, back_low)] + [(gains, both)],
+            [(row_shape, F32, row_block), ((8, width), F32, gain_block), (row_shape, BF16, row_block)],
+        ))
+        middle_back.append(gather_far(middle_back[2]))
+        middle_back.append(near(middle_back[2]))
+        middle_back.append(grad("raise_own", all_two, back_before, 0))
+        wait(after=middle_back[4:5])
+
+    out_keep, out_received = scatter("lower", [hidden], lower_w, second_back)
+    back_middle, gain_second, back_low_middle, even_middle, odd_first, grad_raise = middle_back
 
     def summed(delta):
         return lax.psum_scatter(delta, "group", scatter_dimension=0, tiled=True)

time: 981 us -> 962 us (0.981)
  waiting for transfers between devices: 205 us -> 176 us
  starting transfers between devices: 51.5 us -> 69.1 us
    ppermute x46, waiting for transfers between devices: 175 us -> 146 us  [swap(): return lax.ppermute(value, axis, [(i, i ^ bit) for i in range(size)])]
    ppermute x46, starting transfers between devices: 40 us -> 51 us  [swap(): return lax.ppermute(value, axis, [(i, i ^ bit) for i in range(size)])]
    pallas_call x80 -> x81, Pallas kernels: 692 us -> 687 us  [run(): pl.pallas_call(body, grid_spec=pltpu.PrefetchScalarGridSpec(num_scalar_pr...]
  transfers between devices with their start and end apart: 58 -> 58, of which waited for: 21 -> 18; matrix products, arithmetic and copies ran while one was open for 0% -> 0% of each run, Pallas kernels for 66% -> 67%
where the time goes in v4:
time: 962 us; the launch traced here: 952 us
  Pallas kernels  687 us (71%)
  waiting for transfers between devices  176 us (18%)
  starting transfers between devices  69.1 us (7%)
  between operations  15.1 us (2%)
    pallas_call x81, Pallas kernels, run(): pl.pallas_call(body, grid_spec=pltpu.PrefetchScalarGridSpec(num_scalar_pr...  687 us
    ppermute x46, waiting for transfers between devices, swap(): return lax.ppermute(value, axis, [(i, i ^ bit) for i in range(size)])  146 us
    ppermute x46, starting transfers between devices, swap(): return lax.ppermute(value, axis, [(i, i ^ bit) for i in range(size)])  51 us
    ppermute x3, waiting for transfers between devices, local(): lax.ppermute(deltas[k], 'group', [(i, (i + k) % groups) for i in range(gr...  21.9 us
  transfers between devices with their start and end apart: 58, of which 18 were waited for; matrix products, arithmetic and copies ran while one was open for 0% of the time, Pallas kernels for 67%

profile of v4, /device:TPU:24, one launch (start us, length us, event | category | flops | bytes accessed | tf_op | source)
XLA Modules:
  0.0 952.1 jit_solution(1770429350709636219)
XLA Ops:
  31.4 9.2 collective-permute-done.3.refs_3_.refs_6_
  53.8 21.2 %collective-permute-done.8.refs_3_.refs_8_ = bf16[256,2048]{1,0:T(8,128)(2,1)} collective-permute-done((bf16[256,2048]{1,0:T(8,128)(2,1)}, bf16[256,2048]{1,0:T(8,128)(2,1)}, u32[]{:S(2)}, u32[]{:S(2)}) %collective-permute-start.8) | collective-permute-done | bytes 1048608 | tf_op jit(solution)/shard_map/ppermute | solution.py:34
  83.6 22.1 %collective-permute-done.9.refs_3_.refs_10_ = bf16[256,2048]{1,0:T(8,128)(2,1)} collective-permute-done((bf16[256,2048]{1,0:T(8,128)(2,1)}, bf16[256,2048]{1,0:T(8,128)(2,1)}, u32[]{:S(2)}, u32[]{:S(2)}) %collective-permute-start.9) | collective-permute-done | bytes 1048608 | tf_op jit(solution)/shard_map/ppermute | solution.py:34
  118.2 17.2 %collective-permute-done.12.refs_12_ = bf16[256,2048]{1,0:T(8,128)(2,1)} collective-permute-done((bf16[256,2048]{1,0:T(8,128)(2,1)}, bf16[256,2048]{1,0:T(8,128)(2,1)}, u32[]{:S(2)}, u32[]{:S(2)}) %collective-permute-start.12) | collective-permute-done | bytes 1048608 | tf_op jit(solution)/shard_map/ppermute | solution.py:34
  135.4 27.0 %qkv.1 = (bf16[2560,1536]{1,0:T(8,128)(2,1)}, bf16[2048,2048]{1,0:T(8,128)(2,1)}) custom-call(s32[11]{0:T(128)} %pad_add_fusion.refs_0_, bf16[640,2048]{1,0:T(8,128)(2,1)} %get-tuple-element.116.refs_2_.refs_1_, bf16[640,2048]{1,0:T(8,128)(2,1)} %collective-permute-done.4.refs_3_.refs_2_, bf16[640,2048]{1,0:T(8,128)(2,1)} %get-tuple-element.126.refs_3_, ...), custom_call_target="tpu_custom_call" | custom-call | flops 999999995904 | bytes 1 | tf_op jit(solution)/shard_map/qkv/pallas_call | solution.py:50
  166.1 16.6 %attend.2 = (bf16[2560,512]{1,0:T(8,128)(2,1)}, f32[4,5,8,512]{3,2,1,0:T(8,128)}) custom-call(s32[11]{0:T(128)} %pad_add_fusion.refs_0_, bf16[2560,1536]{1,0:T(8,128)(2,1)} %get-tuple-element.132.refs_2_.refs_1_, s32[1]{0:T(128)} %get-tuple-element.136.refs_2_), custom_call_target="tpu_custom_call" | custom-call | flops 999999995904 | bytes 1 | tf_op jit(solution)/shard_map/attend/pallas_call | solution.py:50
  183.8 16.6 %attend.3 = (bf16[2560,512]{1,0:T(8,128)(2,1)}, f32[4,5,8,512]{3,2,1,0:T(8,128)}) custom-call(s32[11]{0:T(128)} %pad_add_fusion.refs_0_, bf16[2560,1536]{1,0:T(8,128)(2,1)} %get-tuple-element.132.refs_2_.refs_1_, bf16[2560,512]{1,0:T(8,128)(2,1)} %get-tuple-element.137.refs_2_, ...), custom_call_target="tpu_custom_call", output_to_operand_aliasing={{0}: (2, {}), {1}: (3, {})} | custom-call | flops 999999995904 | bytes 1 | tf_op jit(solution)/shard_map/attend/pallas_call | solution.py:50
  257.1 48.7 %collective-permute-done.19.refs_3_ = bf16[640,2048]{1,0:T(8,128)(2,1)} collective-permute-done((bf16[640,2048]{1,0:T(8,128)(2,1)}, bf16[640,2048]{1,0:T(8,128)(2,1)}, u32[]{:S(2)}, u32[]{:S(2)}) %collective-permute-start.19) | collective-permute-done | bytes 2621472 | tf_op jit(solution)/shard_map/ppermute | solution.py:34
  305.8 8.4 second_norm.1
  318.4 31.8 %back_hidden.1 = (bf16[2560,2048]{1,0:T(8,128)(2,1)}, bf16[2048,2048]{1,0:T(8,128)(2,1)}) custom-call(s32[11]{0:T(128)} %pad_add_fusion.refs_0_, bf16[640,2048]{1,0:T(8,128)(2,1)} %get-tuple-element.145.refs_1_.refs_4_, bf16[640,2048]{1,0:T(8,128)(2,1)} %collective-permute-done.15.refs_2_, bf16[640,2048]{1,0:T(8,128)(2,1)} %get-tuple-element.152.refs_3_, ...), custom_call_target="tpu_custom_call" | custom-call | flops 999999995904 | bytes 1 | tf_op jit(solution)/shard_map/back_hidden/pallas_call | solution.py:50
  351.5 17.5 %raise.3 = (bf16[2560,2048]{1,0:T(8,128)(2,1)}, bf16[2560,2048]{1,0:T(8,128)(2,1)}) custom-call(s32[11]{0:T(128)} %pad_add_fusion.refs_0_, bf16[640,2048]{1,0:T(8,128)(2,1)} %get-tuple-element.156.refs_1_, bf16[640,2048]{1,0:T(8,128)(2,1)} %collective-permute-done.21.refs_2_, bf16[1024,1024]{1,0:T(8,128)(2,1)} %get-tuple-element.162.refs_3_.refs_2_, ...), custom_call_target="tpu_custom_call" | custom-call | flops 999999995904 | bytes 1 | tf_op jit(solution)/shard_map/raise/pallas_call | solution.py:50
  368.9 16.8 %raise.4 = (bf16[2560,2048]{1,0:T(8,128)(2,1)}, bf16[2560,2048]{1,0:T(8,128)(2,1)}) custom-call(s32[11]{0:T(128)} %pad_add_fusion.refs_0_, bf16[640,2048]{1,0:T(8,128)(2,1)} %get-tuple-element.156.refs_1_, bf16[640,2048]{1,0:T(8,128)(2,1)} %collective-permute-done.21.refs_2_, ...), custom_call_target="tpu_custom_call", output_to_operand_aliasing={{0}: (6, {}), {1}: (7, {})} | custom-call | flops 999999995904 | bytes 1 | tf_op jit(solution)/shard_map/raise/pallas_call | solution.py:50
  392.2 30.3 %raise.5 = (bf16[2560,2048]{1,0:T(8,128)(2,1)}, bf16[2560,2048]{1,0:T(8,128)(2,1)}) custom-call(s32[11]{0:T(128)} %pad_add_fusion.refs_0_, bf16[640,2048]{1,0:T(8,128)(2,1)} %get-tuple-element.166.refs_1_.refs_3_, bf16[640,2048]{1,0:T(8,128)(2,1)} %collective-permute-done.25.refs_2_.refs_4_, ...), custom_call_target="tpu_custom_call", output_to_operand_aliasing={{0}: (8, {}), {1}: (9, {})} | custom-call | flops 999999995904 | bytes 1 | tf_op jit(solution)/shard_map/raise/pallas_call | solution.py:50
  422.5 17.1 %lower_far.1.refs_6_ = bf16[1024,2048]{1,0:T(8,128)(2,1)} custom-call(s32[11]{0:T(128)} %pad_add_fusion.refs_0_, bf16[640,2048]{1,0:T(8,128)(2,1)} %get-tuple-element.145.refs_1_.refs_4_, bf16[640,2048]{1,0:T(8,128)(2,1)} %collective-permute-done.15.refs_2_, bf16[640,2048]{1,0:T(8,128)(2,1)} %get-tuple-element.152.refs_3_, ...), custom_call_target="tpu_custom_call" | custom-call | flops 999999995904 | bytes 1 | tf_op jit(solution)/shard_map/lower_far/pallas_call | solution.py:50
  440.3 11.9 %back_second_3.1.refs_6_ = bf16[640,2048]{1,0:T(8,128)(2,1)} custom-call(s32[11]{0:T(128)} %pad_add_fusion.refs_0_, bf16[2560,2048]{1,0:T(8,128)(2,1)} %get-tuple-element.171.refs_1_.refs_5_, bf16[1024,1024]{1,0:T(8,128)(2,1)} %get-tuple-element.162.refs_3_.refs_2_, bf16[1024,1024]{1,0:T(8,128)(2,1)} %collective-permute-done.24.refs_4_.refs_3_, ...), custom_call_target="tpu_custom_call" | custom-call | flops 999999995904 | bytes 1 | tf_op jit(solution)/shard_map/back_second_3/pallas_call | solution.py:50
  452.2 12.0 %back_second_1.1.refs_7_ = bf16[640,2048]{1,0:T(8,128)(2,1)} custom-call(s32[11]{0:T(128)} %pad_add_fusion.refs_0_, bf16[2560,2048]{1,0:T(8,128)(2,1)} %get-tuple-element.171.refs_1_.refs_5_, bf16[1024,1024]{1,0:T(8,128)(2,1)} %get-tuple-element.162.refs_3_.refs_2_, bf16[1024,1024]{1,0:T(8,128)(2,1)} %collective-permute-done.24.refs_4_.refs_3_, ...), custom_call_target="tpu_custom_call" | custom-call | flops 999999995904 | bytes 1 | tf_op jit(solution)/shard_map/back_second_1/pallas_call | solution.py:50
  464.8 12.5 %back_second_2.1.refs_7_ = bf16[640,2048]{1,0:T(8,128)(2,1)} custom-call(s32[11]{0:T(128)} %pad_add_fusion.refs_0_, bf16[2560,2048]{1,0:T(8,128)(2,1)} %get-tuple-element.171.refs_1_.refs_5_, bf16[1024,1024]{1,0:T(8,128)(2,1)} %get-tuple-element.162.refs_3_.refs_2_, bf16[1024,1024]{1,0:T(8,128)(2,1)} %collective-permute-done.24.refs_4_.refs_3_, ...), custom_call_target="tpu_custom_call" | custom-call | flops 999999995904 | bytes 1 | tf_op jit(solution)/shard_map/back_second_2/pallas_call | solution.py:50
  477.9 12.5 %back_second_0.1.refs_6_.refs_2_ = bf16[640,2048]{1,0:T(8,128)(2,1)} custom-call(s32[11]{0:T(128)} %pad_add_fusion.refs_0_, bf16[2560,2048]{1,0:T(8,128)(2,1)} %get-tuple-element.171.refs_1_.refs_5_, bf16[1024,1024]{1,0:T(8,128)(2,1)} %get-tuple-element.162.refs_3_.refs_2_, bf16[1024,1024]{1,0:T(8,128)(2,1)} %collective-permute-done.24.refs_4_.refs_3_, ...), custom_call_target="tpu_custom_call" | custom-call | flops 999999995904 | bytes 1 | tf_op jit(solution)/shard_map/back_second_0/pallas_call | solution.py:50
  490.4 17.1 %raise_far.1.refs_6_ = bf16[1024,2048]{1,0:T(8,128)(2,1)} custom-call(s32[11]{0:T(128)} %pad_add_fusion.refs_0_, bf16[640,2048]{1,0:T(8,128)(2,1)} %get-tuple-element.156.refs_1_, bf16[640,2048]{1,0:T(8,128)(2,1)} %collective-permute-done.21.refs_2_, bf16[640,2048]{1,0:T(8,128)(2,1)} %get-tuple-element.166.refs_1_.refs_3_, ...), custom_call_target="tpu_custom_call" | custom-call | flops 999999995904 | bytes 1 | tf_op jit(solution)/shard_map/raise_far/pallas_call | solution.py:50
  509.1 17.1 %lower_own.1.refs_3_.refs_1_ = bf16[1024,2048]{1,0:T(8,128)(2,1)} custom-call(s32[11]{0:T(128)} %pad_add_fusion.refs_0_, bf16[640,2048]{1,0:T(8,128)(2,1)} %get-tuple-element.145.refs_1_.refs_4_, bf16[640,2048]{1,0:T(8,128)(2,1)} %collective-permute-done.15.refs_2_, bf16[640,2048]{1,0:T(8,128)(2,1)} %get-tuple-element.152.refs_3_, ...), custom_call_target="tpu_custom_call" | custom-call | flops 999999995904 | bytes 1 | tf_op jit(solution)/shard_map/lower_own/pallas_call | solution.py:50
  526.2 11.5 %lower_3.1.refs_6_ = bf16[640,2048]{1,0:T(8,128)(2,1)} custom-call(s32[11]{0:T(128)} %pad_add_fusion.refs_0_, bf16[2560,2048]{1,0:T(8,128)(2,1)} %get-tuple-element.169.refs_5_.refs_1_, bf16[2048,2048]{1,0:T(8,128)(2,1)} %get-tuple-element.170.refs_2_.refs_3_, bf16[1024,2048]{1,0:T(8,128)(2,1)} %lower_own.1.refs_3_.refs_1_), custom_call_target="tpu_custom_call" | custom-call | flops 999999995904 | bytes 1 | tf_op jit(solution)/shard_map/lower_3/pallas_call | solution.py:50
  537.8 11.0 %second_back.1 = (f32[640,2048]{1,0:T(8,128)}, f32[8,2048]{1,0:T(8,128)}, bf16[640,2048]{1,0:T(8,128)(2,1)}) custom-call(s32[11]{0:T(128)} %pad_add_fusion.refs_0_, f32[640,2048]{1,0:T(8,128)} %get-tuple-element.155.refs_2_.refs_1_, bf16[640,2048]{1,0:T(8,128)(2,1)} %back_second_0.1.refs_6_.refs_2_, bf16[640,2048]{1,0:T(8,128)(2,1)} %collective-permute-done.28.refs_3_, ...), custom_call_target="tpu_custom_call" | custom-call | flops 999999995904 | bytes 1 | tf_op jit(solution)/shard_map/second_back/pallas_call | solution.py:50
  550.5 17.1 %raise_own.1.refs_1_ = bf16[1024,2048]{1,0:T(8,128)(2,1)} custom-call(s32[11]{0:T(128)} %pad_add_fusion.refs_0_, bf16[640,2048]{1,0:T(8,128)(2,1)} %get-tuple-element.156.refs_1_, bf16[640,2048]{1,0:T(8,128)(2,1)} %collective-permute-done.21.refs_2_, bf16[640,2048]{1,0:T(8,128)(2,1)} %get-tuple-element.166.refs_1_.refs_3_, ...), custom_call_target="tpu_custom_call" | custom-call | flops 999999995904 | bytes 1 | tf_op jit(solution)/shard_map/raise_own/pallas_call | solution.py:50
  568.8 12.1 %lower_1.1.refs_4_ = bf16[640,2048]{1,0:T(8,128)(2,1)} custom-call(s32[11]{0:T(128)} %pad_add_fusion.refs_0_, bf16[2560,2048]{1,0:T(8,128)(2,1)} %get-tuple-element.169.refs_5_.refs_1_, bf16[2048,2048]{1,0:T(8,128)(2,1)} %get-tuple-element.170.refs_2_.refs_3_, s32[1]{0:T(128)} %pause.48.refs_3_), custom_call_target="tpu_custom_call" | custom-call | flops 999999995904 | bytes 1 | tf_op jit(solution)/shard_map/lower_1/pallas_call | solution.py:50
  581.2 12.1 %lower_2.1.refs_4_ = bf16[640,2048]{1,0:T(8,128)(2,1)} custom-call(s32[11]{0:T(128)} %pad_add_fusion.refs_0_, bf16[2560,2048]{1,0:T(8,128)(2,1)} %get-tuple-element.169.refs_5_.refs_1_, bf16[2048,2048]{1,0:T(8,128)(2,1)} %get-tuple-element.170.refs_2_.refs_3_, bf16[640,2048]{1,0:T(8,128)(2,1)} %collective-permute-done.31.refs_3_, ...), custom_call_target="tpu_custom_call" | custom-call | flops 999999995904 | bytes 1 | tf_op jit(solution)/shard_map/lower_2/pallas_call | solution.py:50
  593.9 12.1 %lower_0.1.refs_6_.refs_2_ = bf16[640,2048]{1,0:T(8,128)(2,1)} custom-call(s32[11]{0:T(128)} %pad_add_fusion.refs_0_, bf16[2560,2048]{1,0:T(8,128)(2,1)} %get-tuple-element.169.refs_5_.refs_1_, bf16[2048,2048]{1,0:T(8,128)(2,1)} %get-tuple-element.170.refs_2_.refs_3_, bf16[640,2048]{1,0:T(8,128)(2,1)} %collective-permute-done.30.refs_3_, ...), custom_call_target="tpu_custom_call" | custom-call | flops 999999995904 | bytes 1 | tf_op jit(solution)/shard_map/lower_0/pallas_call | solution.py:50
  606.0 19.5 %adam_lower.1 = (f32[1,2,1024,2048]{3,2,1,0:T(8,128)}, f32[1,2,1024,2048]{3,2,1,0:T(8,128)}, bf16[1024,2048]{1,0:T(8,128)(2,1)}) custom-call(s32[11]{0:T(128)} %pad_add_fusion.refs_0_, bf16[1024,2048]{1,0:T(8,128)(2,1)} %lower_own.1.refs_3_.refs_1_, bf16[1024,2048]{1,0:T(8,128)(2,1)} %collective-permute-done.34.refs_2_, ...), custom_call_target="tpu_custom_call" | custom-call | flops 999999995904 | bytes 1 | tf_op jit(solution)/shard_map/adam_lower/pallas_call | solution.py:50
  632.1 12.0 %back_mixed.1.refs_6_.refs_3_ = bf16[2560,512]{1,0:T(8,128)(2,1)} custom-call(s32[11]{0:T(128)} %pad_add_fusion.refs_0_, bf16[640,2048]{1,0:T(8,128)(2,1)} %get-tuple-element.173.refs_1_, bf16[640,2048]{1,0:T(8,128)(2,1)} %collective-permute-done.29.refs_2_, bf16[640,2048]{1,0:T(8,128)(2,1)} %get-tuple-element.175.refs_3_, ...), custom_call_target="tpu_custom_call" | custom-call | flops 999999995904 | bytes 1 | tf_op jit(solution)/shard_map/back_mixed/pallas_call | solution.py:50
  644.2 7.9 out_far.1.refs_9_
  652.8 19.6 %adam_raise.1 = (f32[1,2,1024,2048]{3,2,1,0:T(8,128)}, f32[1,2,1024,2048]{3,2,1,0:T(8,128)}, bf16[1024,2048]{1,0:T(8,128)(2,1)}) custom-call(s32[11]{0:T(128)} %pad_add_fusion.refs_0_, bf16[1024,2048]{1,0:T(8,128)(2,1)} %raise_own.1.refs_1_, bf16[1024,2048]{1,0:T(8,128)(2,1)} %collective-permute-done.36.refs_2_, ...), custom_call_target="tpu_custom_call", output_to_operand_aliasing={{0}: (7, {}), {1}: (8, {})} | custom-call | flops 999999995904 | bytes 1 | tf_op jit(solution)/shard_map/adam_raise/pallas_call | solution.py:50
  672.4 24.0 %attend_back.2.refs_5_.refs_1_ = bf16[2560,768]{1,0:T(8,128)(2,1)} custom-call(s32[11]{0:T(128)} %pad_add_fusion.refs_0_, bf16[2560,1536]{1,0:T(8,128)(2,1)} %get-tuple-element.132.refs_2_.refs_1_, bf16[2560,512]{1,0:T(8,128)(2,1)} %get-tuple-element.141.refs_2_.refs_1_.refs_5_, bf16[2560,512]{1,0:T(8,128)(2,1)} %back_mixed.1.refs_6_.refs_3_, ...), custom_call_target="tpu_custom_call" | custom-call | flops 999999995904 | bytes 1 | tf_op jit(solution)/shard_map/attend_back/pallas_call | solution.py:50
  696.5 9.4 in_far.2.refs_6_
  707.3 7.9 out_own.1.refs_4_.refs_2_
  722.1 7.8 outer_lower.1
  729.9 24.1 %attend_back.3.refs_5_.refs_2_.refs_6_ = bf16[2560,768]{1,0:T(8,128)(2,1)} custom-call(s32[11]{0:T(128)} %pad_add_fusion.refs_0_, bf16[2560,1536]{1,0:T(8,128)(2,1)} %get-tuple-element.132.refs_2_.refs_1_, bf16[2560,512]{1,0:T(8,128)(2,1)} %get-tuple-element.141.refs_2_.refs_1_.refs_5_, bf16[2560,512]{1,0:T(8,128)(2,1)} %back_mixed.1.refs_6_.refs_3_, ...), custom_call_target="tpu_custom_call" | custom-call | flops 999999995904 | bytes 1 | tf_op jit(solution)/shard_map/attend_back/pallas_call | solution.py:50
  754.0 9.4 in_far.3.refs_4_
  764.4 9.4 back_first_3.1.refs_4_
  773.8 9.5 back_first_1.1.refs_5_
  783.9 10.1 %back_first_2.1.refs_7_ = bf16[640,2048]{1,0:T(8,128)(2,1)} custom-call(s32[11]{0:T(128)} %pad_add_fusion.refs_0_, bf16[2560,768]{1,0:T(8,128)(2,1)} %attend_back.2.refs_5_.refs_1_, bf16[2560,768]{1,0:T(8,128)(2,1)} %attend_back.3.refs_5_.refs_2_.refs_6_, bf16[2048,2048]{1,0:T(8,128)(2,1)} %get-tuple-element.142.refs_2_.refs_5_.refs_3_.refs_6_.refs_7_, ...), custom_call_target="tpu_custom_call" | custom-call | flops 999999995904 | bytes 1 | tf_op jit(solution)/shard_map/back_first_2/pallas_call | solution.py:50
  795.5 13.9 %in_own.1.refs_1_ = bf16[1024,1536]{1,0:T(8,128)(2,1)} custom-call(s32[11]{0:T(128)} %pad_add_fusion.refs_0_, bf16[640,2048]{1,0:T(8,128)(2,1)} %get-tuple-element.116.refs_2_.refs_1_, bf16[640,2048]{1,0:T(8,128)(2,1)} %collective-permute-done.4.refs_3_.refs_2_, bf16[640,2048]{1,0:T(8,128)(2,1)} %get-tuple-element.126.refs_3_, ...), custom_call_target="tpu_custom_call" | custom-call | flops 999999995904 | bytes 1 | tf_op jit(solution)/shard_map/in_own/pallas_call | solution.py:50
  809.4 21.8 %adam_heads.1 = (f32[1,1,1024,2048]{3,2,1,0:T(8,128)}, f32[1,1,1024,2048]{3,2,1,0:T(8,128)}, bf16[256,2048]{1,0:T(8,128)(2,1)}, bf16[256,2048]{1,0:T(8,128)(2,1)...) custom-call(s32[11]{0:T(128)} %pad_add_fusion.refs_0_, bf16[1024,1536]{1,0:T(8,128)(2,1)} %in_own.1.refs_1_, ...), custom_call_target="tpu_custom_call" | custom-call | flops 999999995904 | bytes 1 | tf_op jit(solution)/shard_map/adam_heads/pallas_call | solution.py:50
  831.3 12.8 %collective-permute-start.47 = (bf16[256,2048]{1,0:T(8,128)(2,1)}, bf16[256,2048]{1,0:T(8,128)(2,1)}, u32[]{:S(2)}, u32[]{:S(2)}) collective-permute-start(bf16[256,2048]{1,0:T(8,128)(2,1)} %get-tuple-element.190), channel_id=1, source_target_pairs={{0,16},{8,24},{16,0},{24,8},{1,17},{9,25},{17,1},{25,9},{2,18},{10... | collective-permute-start | bytes 3145736 | tf_op jit(solution)/shard_map/ppermute | solution.py:1203
  844.1 10.0 %back_first_0.1.refs_4_ = bf16[640,2048]{1,0:T(8,128)(2,1)} custom-call(s32[11]{0:T(128)} %pad_add_fusion.refs_0_, bf16[2560,768]{1,0:T(8,128)(2,1)} %attend_back.2.refs_5_.refs_1_, bf16[2560,768]{1,0:T(8,128)(2,1)} %attend_back.3.refs_5_.refs_2_.refs_6_, bf16[2048,2048]{1,0:T(8,128)(2,1)} %get-tuple-element.142.refs_2_.refs_5_.refs_3_.refs_6_.refs_7_, ...), custom_call_target="tpu_custom_call" | custom-call | flops 999999995904 | bytes 1 | tf_op jit(solution)/shard_map/back_first_0/pallas_call | solution.py:50
  854.1 10.6 %first_back.1 = (f32[640,2048]{1,0:T(8,128)}, f32[8,2048]{1,0:T(8,128)}) custom-call(s32[11]{0:T(128)} %pad_add_fusion.refs_0_, bf16[640,2048]{1,0:T(8,128)(2,1)} %refs_1_.13, f32[2,2048]{1,0:T(2,128)} %get-tuple-element.115.refs_2_.refs_4_.refs_5_, f32[640,2048]{1,0:T(8,128)} %get-tuple-element.172.refs_6_.refs_3_, bf16[640,2048]{1,0:T(8,128)(2,1)} %back_first_0.1.refs_4_, ...), custom_call_target="tpu_custom_call" | custom-call | flops 999999995904 | bytes 1 | tf_op jit(solution)/shard_map/first_back/pallas_call | solution.py:50
  887.1 10.4 %collective-permute-start.49 = (f32[2,512]{1,0:T(2,128)}, f32[2,512]{1,0:T(2,128)}, u32[]{:S(2)}, u32[]{:S(2)}) collective-permute-start(f32[2,512]{1,0:T(2,128)} %get-tuple-element.215), channel_id=1, source_target_pairs={{0,8},{8,0},{16,24},{24,16},{1,9},{9,1},{17,25},{25,17},{2,10},{10... | collective-permute-start | bytes 12296 | tf_op jit(solution)/shard_map/ppermute | solution.py:34
  905.1 7.9 collective-permute-start.50
  913.0 21.9 %collective-permute-done.47.refs_3_ = bf16[256,2048]{1,0:T(8,128)(2,1)} collective-permute-done((bf16[256,2048]{1,0:T(8,128)(2,1)}, bf16[256,2048]{1,0:T(8,128)(2,1)}, u32[]{:S(2)}, u32[]{:S(2)}) %collective-permute-start.47) | collective-permute-done | bytes 1048608 | tf_op jit(solution)/shard_map/ppermute | solution.py:1203
  934.9 8.7 outer_heads.1
  (174 shorter events, 189.1 us)
Async XLA Ops:
  7.2 156.5 %all-gather.5.cloned.1.call-start = ((), (), s32[]{:S(2)}) async-start(), calls=%async_computation.2 | async-start | bytes 2621440 | tf_op jit(solution)/shard_map/all_gather | solution.py:1055
  7.2 10.7 %collective-permute-start.2 = (f32[2,512]{1,0:T(2,128)}, f32[2,512]{1,0:T(2,128)}, u32[]{:S(2)}, u32[]{:S(2)}) collective-permute-start(f32[2,512]{1,0:T(2,128)} %refs_1_.8), channel_id=1, source_target_pairs={{0,24},{8,16},{16,8},{24,0},{1,25},{9,17},{17,9},{25,1},{2,26},{10... | collective-permute-start | bytes 12296 | tf_op jit(solution)/shard_map/ppermute | solution.py:34
  7.3 10.6 %collective-permute-start.1 = (f32[2,512]{1,0:T(2,128)}, f32[2,512]{1,0:T(2,128)}, u32[]{:S(2)}, u32[]{:S(2)}) collective-permute-start(f32[2,512]{1,0:T(2,128)} %refs_1_.8), channel_id=1, source_target_pairs={{0,16},{8,24},{16,0},{24,8},{1,17},{9,25},{17,1},{25,9},{2,18},{10... | collective-permute-start | bytes 12296 | tf_op jit(solution)/shard_map/ppermute | solution.py:34
  9.2 8.7 collective-permute-start
  16.2 31.6 %collective-permute-start.6 = (bf16[256,2048]{1,0:T(8,128)(2,1)}, bf16[256,2048]{1,0:T(8,128)(2,1)}, u32[]{:S(2)}, u32[]{:S(2)}) collective-permute-start(bf16[256,2048]{1,0:T(8,128)(2,1)} %cast_heads.1.refs_5_), channel_id=1, source_target_pairs={{0,8},{8,16},{16,24},{24,0},{1,9},{9,17},{17,25},{25,1},{2,10},{10... | collective-permute-start | bytes 3145736 | tf_op jit(solution)/shard_map/ppermute | solution.py:1002
  16.3 24.4 %collective-permute-start.3 = (bf16[256,2048]{1,0:T(8,128)(2,1)}, bf16[256,2048]{1,0:T(8,128)(2,1)}, u32[]{:S(2)}, u32[]{:S(2)}) collective-permute-start(bf16[256,2048]{1,0:T(8,128)(2,1)} %cast_heads.1.refs_5_), channel_id=1, source_target_pairs={{0,4},{4,0},{1,5},{5,1},{2,6},{6,2},{3,7},{7,3},{8,12},{12,8},{9,1... | collective-permute-start | bytes 3145736 | tf_op jit(solution)/shard_map/ppermute | solution.py:34
  25.9 57.7 %collective-permute-start.5 = (bf16[640,2048]{1,0:T(8,128)(2,1)}, bf16[640,2048]{1,0:T(8,128)(2,1)}, u32[]{:S(2)}, u32[]{:S(2)}) collective-permute-start(bf16[640,2048]{1,0:T(8,128)(2,1)} %get-tuple-element.116.refs_2_.refs_1_), channel_id=1, source_target_pairs={{0,2},{1,3},{2,0},{3,1},{4,6},{5,7},{6,4},{7,5},{8,10},{9,11},{10,... | collective-permute-start | bytes 7864328 | tf_op jit(solution)/shard_map/ppermute | solution.py:34
  49.0 25.9 %collective-permute-start.8 = (bf16[256,2048]{1,0:T(8,128)(2,1)}, bf16[256,2048]{1,0:T(8,128)(2,1)}, u32[]{:S(2)}, u32[]{:S(2)}) collective-permute-start(bf16[256,2048]{1,0:T(8,128)(2,1)} %get-tuple-element.122.refs_7_), channel_id=1, source_target_pairs={{0,4},{4,0},{1,5},{5,1},{2,6},{6,2},{3,7},{7,3},{8,12},{12,8},{9,1... | collective-permute-start | bytes 3145736 | tf_op jit(solution)/shard_map/ppermute | solution.py:34
  50.6 25.6 %collective-permute-start.7 = (bf16[256,2048]{1,0:T(8,128)(2,1)}, bf16[256,2048]{1,0:T(8,128)(2,1)}, u32[]{:S(2)}, u32[]{:S(2)}) collective-permute-start(bf16[256,2048]{1,0:T(8,128)(2,1)} %get-tuple-element.122.refs_7_), channel_id=1, source_target_pairs={{0,8},{8,16},{16,24},{24,0},{1,9},{9,17},{17,25},{25,1},{2,10},{10... | collective-permute-start | bytes 3145736 | tf_op jit(solution)/shard_map/ppermute | solution.py:1002
  78.0 29.6 %collective-permute-start.11 = (bf16[256,2048]{1,0:T(8,128)(2,1)}, bf16[256,2048]{1,0:T(8,128)(2,1)}, u32[]{:S(2)}, u32[]{:S(2)}) collective-permute-start(bf16[256,2048]{1,0:T(8,128)(2,1)} %get-tuple-element.125.refs_9_), channel_id=1, source_target_pairs={{0,8},{8,16},{16,24},{24,0},{1,9},{9,17},{17,25},{25,1},{2,10},{10... | collective-permute-start | bytes 3145736 | tf_op jit(solution)/shard_map/ppermute | solution.py:1002
  81.2 24.5 %collective-permute-start.9 = (bf16[256,2048]{1,0:T(8,128)(2,1)}, bf16[256,2048]{1,0:T(8,128)(2,1)}, u32[]{:S(2)}, u32[]{:S(2)}) collective-permute-start(bf16[256,2048]{1,0:T(8,128)(2,1)} %get-tuple-element.125.refs_9_), channel_id=1, source_target_pairs={{0,4},{4,0},{1,5},{5,1},{2,6},{6,2},{3,7},{7,3},{8,12},{12,8},{9,1... | collective-permute-start | bytes 3145736 | tf_op jit(solution)/shard_map/ppermute | solution.py:34
  109.5 25.9 %collective-permute-start.12 = (bf16[256,2048]{1,0:T(8,128)(2,1)}, bf16[256,2048]{1,0:T(8,128)(2,1)}, u32[]{:S(2)}, u32[]{:S(2)}) collective-permute-start(bf16[256,2048]{1,0:T(8,128)(2,1)} %get-tuple-element.128.refs_11_), channel_id=1, source_target_pairs={{0,4},{4,0},{1,5},{5,1},{2,6},{6,2},{3,7},{7,3},{8,12},{12,8},{9,1... | collective-permute-start | bytes 3145736 | tf_op jit(solution)/shard_map/ppermute | solution.py:34
  114.7 92.8 %all-gather.7.cloned.1.call-start = ((), (), s32[]{:S(2)}) async-start(), calls=%async_computation.3 | async-start | bytes 2621440 | tf_op jit(solution)/shard_map/all_gather | solution.py:1055
  116.6 98.3 %collective-permute-start.13 = (bf16[640,2048]{1,0:T(8,128)(2,1)}, bf16[640,2048]{1,0:T(8,128)(2,1)}, u32[]{:S(2)}, u32[]{:S(2)}) collective-permute-start(bf16[640,2048]{1,0:T(8,128)(2,1)} %get-tuple-element.145.refs_1_.refs_4_), channel_id=1, source_target_pairs={{0,2},{1,3},{2,0},{3,1},{4,6},{5,7},{6,4},{7,5},{8,10},{9,11},{10,... | collective-permute-start | bytes 7864328 | tf_op jit(solution)/shard_map/ppermute | solution.py:34
  163.6 90.8 %all-gather.9.cloned.1.call-start = ((), (), s32[]{:S(2)}) async-start(), calls=%async_computation.4 | async-start | bytes 2621440 | tf_op jit(solution)/shard_map/all_gather | solution.py:1055
  165.5 47.6 %collective-permute-start.14 = (bf16[1024,1024]{1,0:T(8,128)(2,1)}, bf16[1024,1024]{1,0:T(8,128)(2,1)}, u32[]{:S(2)}, u32[]{:S(2)}) collective-permute-start(bf16[1024,1024]{1,0:T(8,128)(2,1)} %get-tuple-element.147.refs_5_), channel_id=1, source_target_pairs={{0,4},{4,0},{1,5},{5,1},{2,6},{6,2},{3,7},{7,3},{8,12},{12,8},{9,1... | collective-permute-start | bytes 6291464 | tf_op jit(solution)/shard_map/ppermute | solution.py:34
  200.5 115.2 %all-gather.11.cloned.1.call-start = ((), (), s32[]{:S(2)}) async-start(), calls=%async_computation.5 | async-start | bytes 2621440 | tf_op jit(solution)/shard_map/all_gather | solution.py:1055
  214.3 104.1 %collective-permute-start.23 = (bf16[1024,1024]{1,0:T(8,128)(2,1)}, bf16[1024,1024]{1,0:T(8,128)(2,1)}, u32[]{:S(2)}, u32[]{:S(2)}) collective-permute-start(bf16[1024,1024]{1,0:T(8,128)(2,1)} %get-tuple-element.159.refs_7_), channel_id=1, source_target_pairs={{0,4},{4,0},{1,5},{5,1},{2,6},{6,2},{3,7},{7,3},{8,12},{12,8},{9,1... | collective-permute-start | bytes 6291464 | tf_op jit(solution)/shard_map/ppermute | solution.py:34
  216.8 9.0 collective-permute-start.16
  219.2 503.0 %reduce-scatter.3.cloned.1.call-start = ((), (), s32[]{:S(2)}) async-start(), calls=%async_computation.6 | async-start | bytes 5242880 | tf_op jit(solution)/shard_map/reduce_scatter | solution.py:1150
  246.5 59.3 %collective-permute-start.19 = (bf16[640,2048]{1,0:T(8,128)(2,1)}, bf16[640,2048]{1,0:T(8,128)(2,1)}, u32[]{:S(2)}, u32[]{:S(2)}) collective-permute-start(bf16[640,2048]{1,0:T(8,128)(2,1)} %project_2.1.refs_4_), channel_id=1, source_target_pairs={{0,2},{1,3},{2,0},{3,1},{4,6},{5,7},{6,4},{7,5},{8,10},{9,11},{10,... | collective-permute-start | bytes 7864328 | tf_op jit(solution)/shard_map/ppermute | solution.py:34
  255.6 95.9 %collective-permute-start.24 = (bf16[1024,1024]{1,0:T(8,128)(2,1)}, bf16[1024,1024]{1,0:T(8,128)(2,1)}, u32[]{:S(2)}, u32[]{:S(2)}) collective-permute-start(bf16[1024,1024]{1,0:T(8,128)(2,1)} %get-tuple-element.162.refs_3_.refs_2_), channel_id=1, source_target_pairs={{0,4},{4,0},{1,5},{5,1},{2,6},{6,2},{3,7},{7,3},{8,12},{12,8},{9,1... | collective-permute-start | bytes 6291464 | tf_op jit(solution)/shard_map/ppermute | solution.py:34
  314.2 36.1 %collective-permute-start.21 = (bf16[640,2048]{1,0:T(8,128)(2,1)}, bf16[640,2048]{1,0:T(8,128)(2,1)}, u32[]{:S(2)}, u32[]{:S(2)}) collective-permute-start(bf16[640,2048]{1,0:T(8,128)(2,1)} %get-tuple-element.156.refs_1_), channel_id=1, source_target_pairs={{0,1},{1,0},{2,3},{3,2},{4,5},{5,4},{6,7},{7,6},{8,9},{9,8},{10,11... | collective-permute-start | bytes 7864328 | tf_op jit(solution)/shard_map/ppermute | solution.py:34
  314.2 71.5 %collective-permute-start.20 = (bf16[640,2048]{1,0:T(8,128)(2,1)}, bf16[640,2048]{1,0:T(8,128)(2,1)}, u32[]{:S(2)}, u32[]{:S(2)}) collective-permute-start(bf16[640,2048]{1,0:T(8,128)(2,1)} %get-tuple-element.156.refs_1_), channel_id=1, source_target_pairs={{0,2},{1,3},{2,0},{3,1},{4,6},{5,7},{6,4},{7,5},{8,10},{9,11},{10,... | collective-permute-start | bytes 7864328 | tf_op jit(solution)/shard_map/ppermute | solution.py:34
  316.9 52.0 %collective-permute-start.22 = (bf16[1024,1024]{1,0:T(8,128)(2,1)}, bf16[1024,1024]{1,0:T(8,128)(2,1)}, u32[]{:S(2)}, u32[]{:S(2)}) collective-permute-start(bf16[1024,1024]{1,0:T(8,128)(2,1)} %get-tuple-element.158.refs_3_.refs_5_.refs_4_), channel_id=1, source_target_pairs={{0,4},{4,0},{1,5},{5,1},{2,6},{6,2},{3,7},{7,3},{8,12},{12,8},{9,1... | collective-permute-start | bytes 6291464 | tf_op jit(solution)/shard_map/ppermute | solution.py:34
  439.6 166.4 %collective-permute-start.34 = (bf16[1024,2048]{1,0:T(8,128)(2,1)}, bf16[1024,2048]{1,0:T(8,128)(2,1)}, u32[]{:S(2)}, u32[]{:S(2)}) collective-permute-start(bf16[1024,2048]{1,0:T(8,128)(2,1)} %lower_far.1.refs_6_), channel_id=1, source_target_pairs={{0,4},{4,0},{1,5},{5,1},{2,6},{6,2},{3,7},{7,3},{8,12},{12,8},{9,1... | collective-permute-start | bytes 12582920 | tf_op jit(solution)/shard_map/ppermute | solution.py:34
  452.1 12.7 %collective-permute-start.27 = (bf16[640,2048]{1,0:T(8,128)(2,1)}, bf16[640,2048]{1,0:T(8,128)(2,1)}, u32[]{:S(2)}, u32[]{:S(2)}) collective-permute-start(bf16[640,2048]{1,0:T(8,128)(2,1)} %back_second_3.1.refs_6_), channel_id=1, source_target_pairs={{0,1},{1,0},{2,3},{3,2},{4,5},{5,4},{6,7},{7,6},{8,9},{9,8},{10,11... | collective-permute-start | bytes 7864328 | tf_op jit(solution)/shard_map/ppermute | solution.py:34
  464.3 13.6 %collective-permute-start.26 = (bf16[640,2048]{1,0:T(8,128)(2,1)}, bf16[640,2048]{1,0:T(8,128)(2,1)}, u32[]{:S(2)}, u32[]{:S(2)}) collective-permute-start(bf16[640,2048]{1,0:T(8,128)(2,1)} %back_second_1.1.refs_7_), channel_id=1, source_target_pairs={{0,1},{1,0},{2,3},{3,2},{4,5},{5,4},{6,7},{7,6},{8,9},{9,8},{10,11... | collective-permute-start | bytes 7864328 | tf_op jit(solution)/shard_map/ppermute | solution.py:34
  477.3 60.4 %collective-permute-start.28 = (bf16[640,2048]{1,0:T(8,128)(2,1)}, bf16[640,2048]{1,0:T(8,128)(2,1)}, u32[]{:S(2)}, u32[]{:S(2)}) collective-permute-start(bf16[640,2048]{1,0:T(8,128)(2,1)} %back_second_2.1.refs_7_), channel_id=1, source_target_pairs={{0,2},{1,3},{2,0},{3,1},{4,6},{5,7},{6,4},{7,5},{8,10},{9,11},{10,... | collective-permute-start | bytes 7864328 | tf_op jit(solution)/shard_map/ppermute | solution.py:34
  507.5 145.3 %collective-permute-start.36 = (bf16[1024,2048]{1,0:T(8,128)(2,1)}, bf16[1024,2048]{1,0:T(8,128)(2,1)}, u32[]{:S(2)}, u32[]{:S(2)}) collective-permute-start(bf16[1024,2048]{1,0:T(8,128)(2,1)} %raise_far.1.refs_6_), channel_id=1, source_target_pairs={{0,4},{4,0},{1,5},{5,1},{2,6},{6,2},{3,7},{7,3},{8,12},{12,8},{9,1... | collective-permute-start | bytes 12582920 | tf_op jit(solution)/shard_map/ppermute | solution.py:34
  537.7 43.5 %collective-permute-start.31 = (bf16[640,2048]{1,0:T(8,128)(2,1)}, bf16[640,2048]{1,0:T(8,128)(2,1)}, u32[]{:S(2)}, u32[]{:S(2)}) collective-permute-start(bf16[640,2048]{1,0:T(8,128)(2,1)} %lower_3.1.refs_6_), channel_id=1, source_target_pairs={{0,1},{1,0},{2,3},{3,2},{4,5},{5,4},{6,7},{7,6},{8,9},{9,8},{10,11... | collective-permute-start | bytes 7864328 | tf_op jit(solution)/shard_map/ppermute | solution.py:34
  548.8 76.8 %collective-permute-start.33 = (bf16[640,2048]{1,0:T(8,128)(2,1)}, bf16[640,2048]{1,0:T(8,128)(2,1)}, u32[]{:S(2)}, u32[]{:S(2)}) collective-permute-start(bf16[640,2048]{1,0:T(8,128)(2,1)} %get-tuple-element.173.refs_1_), channel_id=1, source_target_pairs={{0,2},{1,3},{2,0},{3,1},{4,6},{5,7},{6,4},{7,5},{8,10},{9,11},{10,... | collective-permute-start | bytes 7864328 | tf_op jit(solution)/shard_map/ppermute | solution.py:34
  550.3 17.3 %collective-permute-start.29 = (bf16[640,2048]{1,0:T(8,128)(2,1)}, bf16[640,2048]{1,0:T(8,128)(2,1)}, u32[]{:S(2)}, u32[]{:S(2)}) collective-permute-start(bf16[640,2048]{1,0:T(8,128)(2,1)} %get-tuple-element.173.refs_1_), channel_id=1, source_target_pairs={{0,1},{1,0},{2,3},{3,2},{4,5},{5,4},{6,7},{7,6},{8,9},{9,8},{10,11... | collective-permute-start | bytes 7864328 | tf_op jit(solution)/shard_map/ppermute | solution.py:34
  580.8 13.1 %collective-permute-start.30 = (bf16[640,2048]{1,0:T(8,128)(2,1)}, bf16[640,2048]{1,0:T(8,128)(2,1)}, u32[]{:S(2)}, u32[]{:S(2)}) collective-permute-start(bf16[640,2048]{1,0:T(8,128)(2,1)} %lower_1.1.refs_4_), channel_id=1, source_target_pairs={{0,1},{1,0},{2,3},{3,2},{4,5},{5,4},{6,7},{7,6},{8,9},{9,8},{10,11... | collective-permute-start | bytes 7864328 | tf_op jit(solution)/shard_map/ppermute | solution.py:34
  593.3 121.9 %collective-permute-start.32 = (bf16[640,2048]{1,0:T(8,128)(2,1)}, bf16[640,2048]{1,0:T(8,128)(2,1)}, u32[]{:S(2)}, u32[]{:S(2)}) collective-permute-start(bf16[640,2048]{1,0:T(8,128)(2,1)} %lower_2.1.refs_4_), channel_id=1, source_target_pairs={{0,2},{1,3},{2,0},{3,1},{4,6},{5,7},{6,4},{7,5},{8,10},{9,11},{10,... | collective-permute-start | bytes 7864328 | tf_op jit(solution)/shard_map/ppermute | solution.py:34
  625.6 271.9 %reduce-scatter.5.cloned.1.call-start = ((), (), s32[]{:S(2)}) async-start(), calls=%async_computation.7 | async-start | bytes 5242880 | tf_op jit(solution)/shard_map/reduce_scatter | solution.py:1150
  652.1 157.3 %collective-permute-start.41 = (bf16[1024,512]{1,0:T(8,128)(2,1)}, bf16[1024,512]{1,0:T(8,128)(2,1)}, u32[]{:S(2)}, u32[]{:S(2)}) collective-permute-start(bf16[1024,512]{1,0:T(8,128)(2,1)} %out_far.1.refs_9_), channel_id=1, source_target_pairs={{0,4},{4,0},{1,5},{5,1},{2,6},{6,2},{3,7},{7,3},{8,12},{12,8},{9,1... | collective-permute-start | bytes 3145736 | tf_op jit(solution)/shard_map/ppermute | solution.py:34
  705.9 103.6 %collective-permute-start.39 = (bf16[1024,768]{1,0:T(8,128)(2,1)}, bf16[1024,768]{1,0:T(8,128)(2,1)}, u32[]{:S(2)}, u32[]{:S(2)}) collective-permute-start(bf16[1024,768]{1,0:T(8,128)(2,1)} %in_far.2.refs_6_), channel_id=1, source_target_pairs={{0,4},{4,0},{1,5},{5,1},{2,6},{6,2},{3,7},{7,3},{8,12},{12,8},{9,1... | collective-permute-start | bytes 4718600 | tf_op jit(solution)/shard_map/ppermute | solution.py:34
  763.4 46.0 %collective-permute-start.40 = (bf16[1024,768]{1,0:T(8,128)(2,1)}, bf16[1024,768]{1,0:T(8,128)(2,1)}, u32[]{:S(2)}, u32[]{:S(2)}) collective-permute-start(bf16[1024,768]{1,0:T(8,128)(2,1)} %in_far.3.refs_4_), channel_id=1, source_target_pairs={{0,4},{4,0},{1,5},{5,1},{2,6},{6,2},{3,7},{7,3},{8,12},{12,8},{9,1... | collective-permute-start | bytes 4718600 | tf_op jit(solution)/shard_map/ppermute | solution.py:34
  773.8 10.1 %collective-permute-start.38 = (bf16[640,2048]{1,0:T(8,128)(2,1)}, bf16[640,2048]{1,0:T(8,128)(2,1)}, u32[]{:S(2)}, u32[]{:S(2)}) collective-permute-start(bf16[640,2048]{1,0:T(8,128)(2,1)} %back_first_3.1.refs_4_), channel_id=1, source_target_pairs={{0,1},{1,0},{2,3},{3,2},{4,5},{5,4},{6,7},{7,6},{8,9},{9,8},{10,11... | collective-permute-start | bytes 7864328 | tf_op jit(solution)/shard_map/ppermute | solution.py:34
  783.3 60.8 %collective-permute-start.37 = (bf16[640,2048]{1,0:T(8,128)(2,1)}, bf16[640,2048]{1,0:T(8,128)(2,1)}, u32[]{:S(2)}, u32[]{:S(2)}) collective-permute-start(bf16[640,2048]{1,0:T(8,128)(2,1)} %back_first_1.1.refs_5_), channel_id=1, source_target_pairs={{0,1},{1,0},{2,3},{3,2},{4,5},{5,4},{6,7},{7,6},{8,9},{9,8},{10,11... | collective-permute-start | bytes 7864328 | tf_op jit(solution)/shard_map/ppermute | solution.py:34
  794.0 60.2 %collective-permute-start.42 = (bf16[640,2048]{1,0:T(8,128)(2,1)}, bf16[640,2048]{1,0:T(8,128)(2,1)}, u32[]{:S(2)}, u32[]{:S(2)}) collective-permute-start(bf16[640,2048]{1,0:T(8,128)(2,1)} %back_first_2.1.refs_7_), channel_id=1, source_target_pairs={{0,2},{1,3},{2,0},{3,1},{4,6},{5,7},{6,4},{7,5},{8,10},{9,11},{10,... | collective-permute-start | bytes 7864328 | tf_op jit(solution)/shard_map/ppermute | solution.py:34
  831.2 73.9 %collective-permute-start.46 = (bf16[256,2048]{1,0:T(8,128)(2,1)}, bf16[256,2048]{1,0:T(8,128)(2,1)}, u32[]{:S(2)}, u32[]{:S(2)}) collective-permute-start(bf16[256,2048]{1,0:T(8,128)(2,1)} %get-tuple-element.189), channel_id=1, source_target_pairs={{0,8},{8,16},{16,24},{24,0},{1,9},{9,17},{17,25},{25,1},{2,10},{10... | collective-permute-start | bytes 3145736 | tf_op jit(solution)/shard_map/ppermute | solution.py:1203
  831.3 103.6 %collective-permute-start.47 = (bf16[256,2048]{1,0:T(8,128)(2,1)}, bf16[256,2048]{1,0:T(8,128)(2,1)}, u32[]{:S(2)}, u32[]{:S(2)}) collective-permute-start(bf16[256,2048]{1,0:T(8,128)(2,1)} %get-tuple-element.190), channel_id=1, source_target_pairs={{0,16},{8,24},{16,0},{24,8},{1,17},{9,25},{17,1},{25,9},{2,18},{10... | collective-permute-start | bytes 3145736 | tf_op jit(solution)/shard_map/ppermute | solution.py:1203
  844.1 90.8 %collective-permute-start.48 = (bf16[256,2048]{1,0:T(8,128)(2,1)}, bf16[256,2048]{1,0:T(8,128)(2,1)}, u32[]{:S(2)}, u32[]{:S(2)}) collective-permute-start(bf16[256,2048]{1,0:T(8,128)(2,1)} %get-tuple-element.191), channel_id=1, source_target_pairs={{0,24},{8,0},{16,8},{24,16},{1,25},{9,1},{17,9},{25,17},{2,26},{10... | collective-permute-start | bytes 3145736 | tf_op jit(solution)/shard_map/ppermute | solution.py:1203
  887.1 56.5 %collective-permute-start.49 = (f32[2,512]{1,0:T(2,128)}, f32[2,512]{1,0:T(2,128)}, u32[]{:S(2)}, u32[]{:S(2)}) collective-permute-start(f32[2,512]{1,0:T(2,128)} %get-tuple-element.215), channel_id=1, source_target_pairs={{0,8},{8,0},{16,24},{24,16},{1,9},{9,1},{17,25},{25,17},{2,10},{10... | collective-permute-start | bytes 12296 | tf_op jit(solution)/shard_map/ppermute | solution.py:34
  897.5 46.1 %collective-permute-start.51 = (f32[2,512]{1,0:T(2,128)}, f32[2,512]{1,0:T(2,128)}, u32[]{:S(2)}, u32[]{:S(2)}) collective-permute-start(f32[2,512]{1,0:T(2,128)} %get-tuple-element.216), channel_id=1, source_target_pairs={{0,24},{8,16},{16,8},{24,0},{1,25},{9,17},{17,9},{25,1},{2,26},{10... | collective-permute-start | bytes 12296 | tf_op jit(solution)/shard_map/ppermute | solution.py:34
  905.1 38.5 %collective-permute-start.50 = (f32[2,512]{1,0:T(2,128)}, f32[2,512]{1,0:T(2,128)}, u32[]{:S(2)}, u32[]{:S(2)}) collective-permute-start(f32[2,512]{1,0:T(2,128)} %get-tuple-element.217), channel_id=1, source_target_pairs={{0,16},{8,24},{16,0},{24,8},{1,17},{9,25},{17,1},{25,9},{2,18},{10... | collective-permute-start | bytes 12296 | tf_op jit(solution)/shard_map/ppermute | solution.py:34
  (17 other events, 86.4 us)
Sparse Core Ops, SparseCore 0:
  114.8 43.7 all-gather.4
  163.7 43.7 all-gather.6
  209.7 44.6 all-gather.8
  256.4 44.6 all-gather.10
  625.7 75.9 reduce-scatter.2
  707.4 80.4 reduce-scatter.4

commit v5 on v4

--- a/solution.py
+++ b/solution.py
@@ -1176,13 +1176,9 @@
         grad_in_fars.append(across(grad("in_far", all_one, back_triples[n], half)))
         if n == 0:
             grad_out = grad("out_own", all_middle, mixed, 0)
-            block_output = run(
-                functools.partial(output_kernel, items, half), "output", (steps,), meta,
-                [(v, row_block) for v in (middle, out_keep, out_received)],
-                [(row_shape, BF16, row_block)],
-            )[0]
             hidden_out = outer(
-                "outer_lower", meta, groups, [lower_delta], weight_hidden, momentum_hidden, average_hidden, 1
+                "outer_lower", meta, groups, [lower_delta], weight_hidden, momentum_hidden, average_hidden, 1,
+                after=[out_received],
             )
     product = lambda n, received=None: term(
         f"back_first_{n}", meta, back_triples, inward_w, rows_here, ranks, n, received
@@ -1205,6 +1201,11 @@
     ]
     keep = product(0, far_keep)
     keep, received = finish_sum(send, keep, rows_here, ranks)
+    block_output = run(
+        functools.partial(output_kernel, items, half), "output", (steps,), meta,
+        [(v, row_block) for v in (middle, out_keep, out_received)],
+        [(row_shape, BF16, row_block)],
+    )[0]
     input_grad, gain_first = run(
         functools.partial(first_back_kernel, items, half), "first_back", (steps,), meta,
         [(block_input, row_block), (gains, both)] + [(v, row_block) for v in (back_middle, keep, received)],

time: 962 us -> 956 us (level)
  transfers between devices with their start and end apart: 58 -> 58, of which waited for: 18 -> 18; matrix products, arithmetic and copies ran while one was open for 0% -> 0% of each run, Pallas kernels for 67% -> 68%
where the time goes in v5:
time: 956 us; the launch traced here: 944 us
  Pallas kernels  686 us (72%)
  waiting for transfers between devices  174 us (18%)
  starting transfers between devices  63.6 us (7%)
  between operations  15.1 us (2%)
    pallas_call x81, Pallas kernels, run(): pl.pallas_call(body, grid_spec=pltpu.PrefetchScalarGridSpec(num_scalar_pr...  686 us
    ppermute x46, waiting for transfers between devices, swap(): return lax.ppermute(value, axis, [(i, i ^ bit) for i in range(size)])  144 us
    ppermute x46, starting transfers between devices, swap(): return lax.ppermute(value, axis, [(i, i ^ bit) for i in range(size)])  46.2 us
    ppermute x3, waiting for transfers between devices, local(): lax.ppermute(deltas[k], 'group', [(i, (i + k) % groups) for i in range(gr...  21.9 us
  transfers between devices with their start and end apart: 58, of which 18 were waited for; matrix products, arithmetic and copies ran while one was open for 0% of the time, Pallas kernels for 68%

profile of v5, /device:TPU:24, one launch (start us, length us, event | category | flops | bytes accessed | tf_op | source)
XLA Modules:
  0.0 944.4 jit_solution(11602535344516967262)
XLA Ops:
  31.4 9.3 collective-permute-done.3.refs_3_.refs_6_
  53.8 21.2 %collective-permute-done.8.refs_3_.refs_8_ = bf16[256,2048]{1,0:T(8,128)(2,1)} collective-permute-done((bf16[256,2048]{1,0:T(8,128)(2,1)}, bf16[256,2048]{1,0:T(8,128)(2,1)}, u32[]{:S(2)}, u32[]{:S(2)}) %collective-permute-start.8) | collective-permute-done | bytes 1048608 | tf_op jit(solution)/shard_map/ppermute | solution.py:34
  83.6 22.1 %collective-permute-done.9.refs_3_.refs_10_ = bf16[256,2048]{1,0:T(8,128)(2,1)} collective-permute-done((bf16[256,2048]{1,0:T(8,128)(2,1)}, bf16[256,2048]{1,0:T(8,128)(2,1)}, u32[]{:S(2)}, u32[]{:S(2)}) %collective-permute-start.9) | collective-permute-done | bytes 1048608 | tf_op jit(solution)/shard_map/ppermute | solution.py:34
  118.2 17.2 %collective-permute-done.12.refs_12_ = bf16[256,2048]{1,0:T(8,128)(2,1)} collective-permute-done((bf16[256,2048]{1,0:T(8,128)(2,1)}, bf16[256,2048]{1,0:T(8,128)(2,1)}, u32[]{:S(2)}, u32[]{:S(2)}) %collective-permute-start.12) | collective-permute-done | bytes 1048608 | tf_op jit(solution)/shard_map/ppermute | solution.py:34
  135.4 27.0 %qkv.1 = (bf16[2560,1536]{1,0:T(8,128)(2,1)}, bf16[2048,2048]{1,0:T(8,128)(2,1)}) custom-call(s32[11]{0:T(128)} %pad_add_fusion.refs_0_, bf16[640,2048]{1,0:T(8,128)(2,1)} %get-tuple-element.116.refs_2_.refs_1_, bf16[640,2048]{1,0:T(8,128)(2,1)} %collective-permute-done.4.refs_3_.refs_2_, bf16[640,2048]{1,0:T(8,128)(2,1)} %get-tuple-element.126.refs_3_, ...), custom_call_target="tpu_custom_call" | custom-call | flops 999999995904 | bytes 1 | tf_op jit(solution)/shard_map/qkv/pallas_call | solution.py:50
  166.1 16.6 %attend.2 = (bf16[2560,512]{1,0:T(8,128)(2,1)}, f32[4,5,8,512]{3,2,1,0:T(8,128)}) custom-call(s32[11]{0:T(128)} %pad_add_fusion.refs_0_, bf16[2560,1536]{1,0:T(8,128)(2,1)} %get-tuple-element.132.refs_2_.refs_1_, s32[1]{0:T(128)} %get-tuple-element.136.refs_2_), custom_call_target="tpu_custom_call" | custom-call | flops 999999995904 | bytes 1 | tf_op jit(solution)/shard_map/attend/pallas_call | solution.py:50
  183.8 16.6 %attend.3 = (bf16[2560,512]{1,0:T(8,128)(2,1)}, f32[4,5,8,512]{3,2,1,0:T(8,128)}) custom-call(s32[11]{0:T(128)} %pad_add_fusion.refs_0_, bf16[2560,1536]{1,0:T(8,128)(2,1)} %get-tuple-element.132.refs_2_.refs_1_, bf16[2560,512]{1,0:T(8,128)(2,1)} %get-tuple-element.137.refs_2_, ...), custom_call_target="tpu_custom_call", output_to_operand_aliasing={{0}: (2, {}), {1}: (3, {})} | custom-call | flops 999999995904 | bytes 1 | tf_op jit(solution)/shard_map/attend/pallas_call | solution.py:50
  200.5 7.0 all-gather.7.cloned.1.call-done.refs_1_
  257.1 48.7 %collective-permute-done.19.refs_3_ = bf16[640,2048]{1,0:T(8,128)(2,1)} collective-permute-done((bf16[640,2048]{1,0:T(8,128)(2,1)}, bf16[640,2048]{1,0:T(8,128)(2,1)}, u32[]{:S(2)}, u32[]{:S(2)}) %collective-permute-start.19) | collective-permute-done | bytes 2621472 | tf_op jit(solution)/shard_map/ppermute | solution.py:34
  305.8 8.5 second_norm.1
  318.5 31.8 %back_hidden.1 = (bf16[2560,2048]{1,0:T(8,128)(2,1)}, bf16[2048,2048]{1,0:T(8,128)(2,1)}) custom-call(s32[11]{0:T(128)} %pad_add_fusion.refs_0_, bf16[640,2048]{1,0:T(8,128)(2,1)} %get-tuple-element.145.refs_1_.refs_4_, bf16[640,2048]{1,0:T(8,128)(2,1)} %collective-permute-done.15.refs_2_, bf16[640,2048]{1,0:T(8,128)(2,1)} %get-tuple-element.152.refs_3_, ...), custom_call_target="tpu_custom_call" | custom-call | flops 999999995904 | bytes 1 | tf_op jit(solution)/shard_map/back_hidden/pallas_call | solution.py:50
  351.5 17.4 %raise.3 = (bf16[2560,2048]{1,0:T(8,128)(2,1)}, bf16[2560,2048]{1,0:T(8,128)(2,1)}) custom-call(s32[11]{0:T(128)} %pad_add_fusion.refs_0_, bf16[640,2048]{1,0:T(8,128)(2,1)} %get-tuple-element.156.refs_1_, bf16[640,2048]{1,0:T(8,128)(2,1)} %collective-permute-done.21.refs_2_, bf16[1024,1024]{1,0:T(8,128)(2,1)} %get-tuple-element.162.refs_3_.refs_2_, ...), custom_call_target="tpu_custom_call" | custom-call | flops 999999995904 | bytes 1 | tf_op jit(solution)/shard_map/raise/pallas_call | solution.py:50
  368.9 16.8 %raise.4 = (bf16[2560,2048]{1,0:T(8,128)(2,1)}, bf16[2560,2048]{1,0:T(8,128)(2,1)}) custom-call(s32[11]{0:T(128)} %pad_add_fusion.refs_0_, bf16[640,2048]{1,0:T(8,128)(2,1)} %get-tuple-element.156.refs_1_, bf16[640,2048]{1,0:T(8,128)(2,1)} %collective-permute-done.21.refs_2_, ...), custom_call_target="tpu_custom_call", output_to_operand_aliasing={{0}: (6, {}), {1}: (7, {})} | custom-call | flops 999999995904 | bytes 1 | tf_op jit(solution)/shard_map/raise/pallas_call | solution.py:50
  392.3 30.3 %raise.5 = (bf16[2560,2048]{1,0:T(8,128)(2,1)}, bf16[2560,2048]{1,0:T(8,128)(2,1)}) custom-call(s32[11]{0:T(128)} %pad_add_fusion.refs_0_, bf16[640,2048]{1,0:T(8,128)(2,1)} %get-tuple-element.166.refs_1_.refs_3_, bf16[640,2048]{1,0:T(8,128)(2,1)} %collective-permute-done.25.refs_2_.refs_4_, ...), custom_call_target="tpu_custom_call", output_to_operand_aliasing={{0}: (8, {}), {1}: (9, {})} | custom-call | flops 999999995904 | bytes 1 | tf_op jit(solution)/shard_map/raise/pallas_call | solution.py:50
  422.5 17.1 %lower_far.1.refs_6_ = bf16[1024,2048]{1,0:T(8,128)(2,1)} custom-call(s32[11]{0:T(128)} %pad_add_fusion.refs_0_, bf16[640,2048]{1,0:T(8,128)(2,1)} %get-tuple-element.145.refs_1_.refs_4_, bf16[640,2048]{1,0:T(8,128)(2,1)} %collective-permute-done.15.refs_2_, bf16[640,2048]{1,0:T(8,128)(2,1)} %get-tuple-element.152.refs_3_, ...), custom_call_target="tpu_custom_call" | custom-call | flops 999999995904 | bytes 1 | tf_op jit(solution)/shard_map/lower_far/pallas_call | solution.py:50
  440.3 11.9 %back_second_3.1.refs_6_ = bf16[640,2048]{1,0:T(8,128)(2,1)} custom-call(s32[11]{0:T(128)} %pad_add_fusion.refs_0_, bf16[2560,2048]{1,0:T(8,128)(2,1)} %get-tuple-element.171.refs_1_.refs_5_, bf16[1024,1024]{1,0:T(8,128)(2,1)} %get-tuple-element.162.refs_3_.refs_2_, bf16[1024,1024]{1,0:T(8,128)(2,1)} %collective-permute-done.24.refs_4_.refs_3_, ...), custom_call_target="tpu_custom_call" | custom-call | flops 999999995904 | bytes 1 | tf_op jit(solution)/shard_map/back_second_3/pallas_call | solution.py:50
  452.2 12.0 %back_second_1.1.refs_7_ = bf16[640,2048]{1,0:T(8,128)(2,1)} custom-call(s32[11]{0:T(128)} %pad_add_fusion.refs_0_, bf16[2560,2048]{1,0:T(8,128)(2,1)} %get-tuple-element.171.refs_1_.refs_5_, bf16[1024,1024]{1,0:T(8,128)(2,1)} %get-tuple-element.162.refs_3_.refs_2_, bf16[1024,1024]{1,0:T(8,128)(2,1)} %collective-permute-done.24.refs_4_.refs_3_, ...), custom_call_target="tpu_custom_call" | custom-call | flops 999999995904 | bytes 1 | tf_op jit(solution)/shard_map/back_second_1/pallas_call | solution.py:50
  464.8 12.5 %back_second_2.1.refs_7_ = bf16[640,2048]{1,0:T(8,128)(2,1)} custom-call(s32[11]{0:T(128)} %pad_add_fusion.refs_0_, bf16[2560,2048]{1,0:T(8,128)(2,1)} %get-tuple-element.171.refs_1_.refs_5_, bf16[1024,1024]{1,0:T(8,128)(2,1)} %get-tuple-element.162.refs_3_.refs_2_, bf16[1024,1024]{1,0:T(8,128)(2,1)} %collective-permute-done.24.refs_4_.refs_3_, ...), custom_call_target="tpu_custom_call" | custom-call | flops 999999995904 | bytes 1 | tf_op jit(solution)/shard_map/back_second_2/pallas_call | solution.py:50
  477.9 12.5 %back_second_0.1.refs_6_.refs_2_ = bf16[640,2048]{1,0:T(8,128)(2,1)} custom-call(s32[11]{0:T(128)} %pad_add_fusion.refs_0_, bf16[2560,2048]{1,0:T(8,128)(2,1)} %get-tuple-element.171.refs_1_.refs_5_, bf16[1024,1024]{1,0:T(8,128)(2,1)} %get-tuple-element.162.refs_3_.refs_2_, bf16[1024,1024]{1,0:T(8,128)(2,1)} %collective-permute-done.24.refs_4_.refs_3_, ...), custom_call_target="tpu_custom_call" | custom-call | flops 999999995904 | bytes 1 | tf_op jit(solution)/shard_map/back_second_0/pallas_call | solution.py:50
  490.4 17.1 %raise_far.1.refs_6_ = bf16[1024,2048]{1,0:T(8,128)(2,1)} custom-call(s32[11]{0:T(128)} %pad_add_fusion.refs_0_, bf16[640,2048]{1,0:T(8,128)(2,1)} %get-tuple-element.156.refs_1_, bf16[640,2048]{1,0:T(8,128)(2,1)} %collective-permute-done.21.refs_2_, bf16[640,2048]{1,0:T(8,128)(2,1)} %get-tuple-element.166.refs_1_.refs_3_, ...), custom_call_target="tpu_custom_call" | custom-call | flops 999999995904 | bytes 1 | tf_op jit(solution)/shard_map/raise_far/pallas_call | solution.py:50
  509.1 17.1 %lower_own.1.refs_3_.refs_1_ = bf16[1024,2048]{1,0:T(8,128)(2,1)} custom-call(s32[11]{0:T(128)} %pad_add_fusion.refs_0_, bf16[640,2048]{1,0:T(8,128)(2,1)} %get-tuple-element.145.refs_1_.refs_4_, bf16[640,2048]{1,0:T(8,128)(2,1)} %collective-permute-done.15.refs_2_, bf16[640,2048]{1,0:T(8,128)(2,1)} %get-tuple-element.152.refs_3_, ...), custom_call_target="tpu_custom_call" | custom-call | flops 999999995904 | bytes 1 | tf_op jit(solution)/shard_map/lower_own/pallas_call | solution.py:50
  526.2 11.5 %lower_3.1.refs_6_ = bf16[640,2048]{1,0:T(8,128)(2,1)} custom-call(s32[11]{0:T(128)} %pad_add_fusion.refs_0_, bf16[2560,2048]{1,0:T(8,128)(2,1)} %get-tuple-element.169.refs_5_.refs_1_, bf16[2048,2048]{1,0:T(8,128)(2,1)} %get-tuple-element.170.refs_2_.refs_3_, bf16[1024,2048]{1,0:T(8,128)(2,1)} %lower_own.1.refs_3_.refs_1_), custom_call_target="tpu_custom_call" | custom-call | flops 999999995904 | bytes 1 | tf_op jit(solution)/shard_map/lower_3/pallas_call | solution.py:50
  537.8 11.0 %second_back.1 = (f32[640,2048]{1,0:T(8,128)}, f32[8,2048]{1,0:T(8,128)}, bf16[640,2048]{1,0:T(8,128)(2,1)}) custom-call(s32[11]{0:T(128)} %pad_add_fusion.refs_0_, f32[640,2048]{1,0:T(8,128)} %get-tuple-element.155.refs_2_.refs_1_, bf16[640,2048]{1,0:T(8,128)(2,1)} %back_second_0.1.refs_6_.refs_2_, bf16[640,2048]{1,0:T(8,128)(2,1)} %collective-permute-done.28.refs_3_, ...), custom_call_target="tpu_custom_call" | custom-call | flops 999999995904 | bytes 1 | tf_op jit(solution)/shard_map/second_back/pallas_call | solution.py:50
  550.4 17.1 %raise_own.1.refs_1_ = bf16[1024,2048]{1,0:T(8,128)(2,1)} custom-call(s32[11]{0:T(128)} %pad_add_fusion.refs_0_, bf16[640,2048]{1,0:T(8,128)(2,1)} %get-tuple-element.156.refs_1_, bf16[640,2048]{1,0:T(8,128)(2,1)} %collective-permute-done.21.refs_2_, bf16[640,2048]{1,0:T(8,128)(2,1)} %get-tuple-element.166.refs_1_.refs_3_, ...), custom_call_target="tpu_custom_call" | custom-call | flops 999999995904 | bytes 1 | tf_op jit(solution)/shard_map/raise_own/pallas_call | solution.py:50
  568.7 12.1 %lower_1.1.refs_4_ = bf16[640,2048]{1,0:T(8,128)(2,1)} custom-call(s32[11]{0:T(128)} %pad_add_fusion.refs_0_, bf16[2560,2048]{1,0:T(8,128)(2,1)} %get-tuple-element.169.refs_5_.refs_1_, bf16[2048,2048]{1,0:T(8,128)(2,1)} %get-tuple-element.170.refs_2_.refs_3_, s32[1]{0:T(128)} %pause.48.refs_3_), custom_call_target="tpu_custom_call" | custom-call | flops 999999995904 | bytes 1 | tf_op jit(solution)/shard_map/lower_1/pallas_call | solution.py:50
  581.2 12.1 %lower_2.1.refs_4_ = bf16[640,2048]{1,0:T(8,128)(2,1)} custom-call(s32[11]{0:T(128)} %pad_add_fusion.refs_0_, bf16[2560,2048]{1,0:T(8,128)(2,1)} %get-tuple-element.169.refs_5_.refs_1_, bf16[2048,2048]{1,0:T(8,128)(2,1)} %get-tuple-element.170.refs_2_.refs_3_, bf16[640,2048]{1,0:T(8,128)(2,1)} %collective-permute-done.31.refs_3_, ...), custom_call_target="tpu_custom_call" | custom-call | flops 999999995904 | bytes 1 | tf_op jit(solution)/shard_map/lower_2/pallas_call | solution.py:50
  593.9 12.0 %lower_0.1.refs_6_.refs_2_ = bf16[640,2048]{1,0:T(8,128)(2,1)} custom-call(s32[11]{0:T(128)} %pad_add_fusion.refs_0_, bf16[2560,2048]{1,0:T(8,128)(2,1)} %get-tuple-element.169.refs_5_.refs_1_, bf16[2048,2048]{1,0:T(8,128)(2,1)} %get-tuple-element.170.refs_2_.refs_3_, bf16[640,2048]{1,0:T(8,128)(2,1)} %collective-permute-done.30.refs_3_, ...), custom_call_target="tpu_custom_call" | custom-call | flops 999999995904 | bytes 1 | tf_op jit(solution)/shard_map/lower_0/pallas_call | solution.py:50
  606.0 19.5 %adam_lower.1 = (f32[1,2,1024,2048]{3,2,1,0:T(8,128)}, f32[1,2,1024,2048]{3,2,1,0:T(8,128)}, bf16[1024,2048]{1,0:T(8,128)(2,1)}) custom-call(s32[11]{0:T(128)} %pad_add_fusion.refs_0_, bf16[1024,2048]{1,0:T(8,128)(2,1)} %lower_own.1.refs_3_.refs_1_, bf16[1024,2048]{1,0:T(8,128)(2,1)} %collective-permute-done.34.refs_2_, ...), custom_call_target="tpu_custom_call" | custom-call | flops 999999995904 | bytes 1 | tf_op jit(solution)/shard_map/adam_lower/pallas_call | solution.py:50
  632.1 12.0 %back_mixed.1.refs_6_.refs_3_ = bf16[2560,512]{1,0:T(8,128)(2,1)} custom-call(s32[11]{0:T(128)} %pad_add_fusion.refs_0_, bf16[640,2048]{1,0:T(8,128)(2,1)} %get-tuple-element.173.refs_1_, bf16[640,2048]{1,0:T(8,128)(2,1)} %collective-permute-done.29.refs_2_, bf16[640,2048]{1,0:T(8,128)(2,1)} %get-tuple-element.175.refs_3_, ...), custom_call_target="tpu_custom_call" | custom-call | flops 999999995904 | bytes 1 | tf_op jit(solution)/shard_map/back_mixed/pallas_call | solution.py:50
  644.1 7.9 out_far.1.refs_9_
  652.8 19.6 %adam_raise.1 = (f32[1,2,1024,2048]{3,2,1,0:T(8,128)}, f32[1,2,1024,2048]{3,2,1,0:T(8,128)}, bf16[1024,2048]{1,0:T(8,128)(2,1)}) custom-call(s32[11]{0:T(128)} %pad_add_fusion.refs_0_, bf16[1024,2048]{1,0:T(8,128)(2,1)} %raise_own.1.refs_1_, bf16[1024,2048]{1,0:T(8,128)(2,1)} %collective-permute-done.36.refs_2_, ...), custom_call_target="tpu_custom_call", output_to_operand_aliasing={{0}: (7, {}), {1}: (8, {})} | custom-call | flops 999999995904 | bytes 1 | tf_op jit(solution)/shard_map/adam_raise/pallas_call | solution.py:50
  672.4 24.0 %attend_back.2.refs_5_.refs_1_ = bf16[2560,768]{1,0:T(8,128)(2,1)} custom-call(s32[11]{0:T(128)} %pad_add_fusion.refs_0_, bf16[2560,1536]{1,0:T(8,128)(2,1)} %get-tuple-element.132.refs_2_.refs_1_, bf16[2560,512]{1,0:T(8,128)(2,1)} %get-tuple-element.141.refs_2_.refs_1_.refs_5_, bf16[2560,512]{1,0:T(8,128)(2,1)} %back_mixed.1.refs_6_.refs_3_, ...), custom_call_target="tpu_custom_call" | custom-call | flops 999999995904 | bytes 1 | tf_op jit(solution)/shard_map/attend_back/pallas_call | solution.py:50
  696.4 9.5 %in_far.2.refs_6_ = bf16[1024,768]{1,0:T(8,128)(2,1)} custom-call(s32[11]{0:T(128)} %pad_add_fusion.refs_0_, bf16[640,2048]{1,0:T(8,128)(2,1)} %get-tuple-element.116.refs_2_.refs_1_, bf16[640,2048]{1,0:T(8,128)(2,1)} %collective-permute-done.4.refs_3_.refs_2_, bf16[640,2048]{1,0:T(8,128)(2,1)} %get-tuple-element.126.refs_3_, ...), custom_call_target="tpu_custom_call" | custom-call | flops 999999995904 | bytes 1 | tf_op jit(solution)/shard_map/in_far/pallas_call | solution.py:50
  707.4 7.9 out_own.1.refs_5_.refs_2_
  715.3 7.7 outer_lower.1
  723.0 24.2 %attend_back.3.refs_5_.refs_2_.refs_6_ = bf16[2560,768]{1,0:T(8,128)(2,1)} custom-call(s32[11]{0:T(128)} %pad_add_fusion.refs_0_, bf16[2560,1536]{1,0:T(8,128)(2,1)} %get-tuple-element.132.refs_2_.refs_1_, bf16[2560,512]{1,0:T(8,128)(2,1)} %get-tuple-element.141.refs_2_.refs_1_.refs_5_, bf16[2560,512]{1,0:T(8,128)(2,1)} %back_mixed.1.refs_6_.refs_3_, ...), custom_call_target="tpu_custom_call" | custom-call | flops 999999995904 | bytes 1 | tf_op jit(solution)/shard_map/attend_back/pallas_call | solution.py:50
  747.2 9.4 in_far.3.refs_4_
  757.3 9.5 %back_first_3.1.refs_4_ = bf16[640,2048]{1,0:T(8,128)(2,1)} custom-call(s32[11]{0:T(128)} %pad_add_fusion.refs_0_, bf16[2560,768]{1,0:T(8,128)(2,1)} %attend_back.2.refs_5_.refs_1_, bf16[2560,768]{1,0:T(8,128)(2,1)} %attend_back.3.refs_5_.refs_2_.refs_6_, bf16[2048,2048]{1,0:T(8,128)(2,1)} %get-tuple-element.142.refs_2_.refs_5_.refs_3_.refs_6_.refs_7_, ...), custom_call_target="tpu_custom_call" | custom-call | flops 999999995904 | bytes 1 | tf_op jit(solution)/shard_map/back_first_3/pallas_call | solution.py:50
  766.9 9.4 back_first_1.1.refs_5_
  776.9 10.0 %back_first_2.1.refs_7_ = bf16[640,2048]{1,0:T(8,128)(2,1)} custom-call(s32[11]{0:T(128)} %pad_add_fusion.refs_0_, bf16[2560,768]{1,0:T(8,128)(2,1)} %attend_back.2.refs_5_.refs_1_, bf16[2560,768]{1,0:T(8,128)(2,1)} %attend_back.3.refs_5_.refs_2_.refs_6_, bf16[2048,2048]{1,0:T(8,128)(2,1)} %get-tuple-element.142.refs_2_.refs_5_.refs_3_.refs_6_.refs_7_, ...), custom_call_target="tpu_custom_call" | custom-call | flops 999999995904 | bytes 1 | tf_op jit(solution)/shard_map/back_first_2/pallas_call | solution.py:50
  788.4 13.9 %in_own.1.refs_1_ = bf16[1024,1536]{1,0:T(8,128)(2,1)} custom-call(s32[11]{0:T(128)} %pad_add_fusion.refs_0_, bf16[640,2048]{1,0:T(8,128)(2,1)} %get-tuple-element.116.refs_2_.refs_1_, bf16[640,2048]{1,0:T(8,128)(2,1)} %collective-permute-done.4.refs_3_.refs_2_, bf16[640,2048]{1,0:T(8,128)(2,1)} %get-tuple-element.126.refs_3_, ...), custom_call_target="tpu_custom_call" | custom-call | flops 999999995904 | bytes 1 | tf_op jit(solution)/shard_map/in_own/pallas_call | solution.py:50
  802.4 21.8 %adam_heads.1 = (f32[1,1,1024,2048]{3,2,1,0:T(8,128)}, f32[1,1,1024,2048]{3,2,1,0:T(8,128)}, bf16[256,2048]{1,0:T(8,128)(2,1)}, bf16[256,2048]{1,0:T(8,128)(2,1)...) custom-call(s32[11]{0:T(128)} %pad_add_fusion.refs_0_, bf16[1024,1536]{1,0:T(8,128)(2,1)} %in_own.1.refs_1_, ...), custom_call_target="tpu_custom_call" | custom-call | flops 999999995904 | bytes 1 | tf_op jit(solution)/shard_map/adam_heads/pallas_call | solution.py:50
  836.4 10.0 %back_first_0.1.refs_4_ = bf16[640,2048]{1,0:T(8,128)(2,1)} custom-call(s32[11]{0:T(128)} %pad_add_fusion.refs_0_, bf16[2560,768]{1,0:T(8,128)(2,1)} %attend_back.2.refs_5_.refs_1_, bf16[2560,768]{1,0:T(8,128)(2,1)} %attend_back.3.refs_5_.refs_2_.refs_6_, bf16[2048,2048]{1,0:T(8,128)(2,1)} %get-tuple-element.142.refs_2_.refs_5_.refs_3_.refs_6_.refs_7_, ...), custom_call_target="tpu_custom_call" | custom-call | flops 999999995904 | bytes 1 | tf_op jit(solution)/shard_map/back_first_0/pallas_call | solution.py:50
  853.0 10.5 %first_back.1 = (f32[640,2048]{1,0:T(8,128)}, f32[8,2048]{1,0:T(8,128)}) custom-call(s32[11]{0:T(128)} %pad_add_fusion.refs_0_, bf16[640,2048]{1,0:T(8,128)(2,1)} %refs_1_.13, f32[2,2048]{1,0:T(2,128)} %get-tuple-element.115.refs_2_.refs_4_.refs_5_, f32[640,2048]{1,0:T(8,128)} %get-tuple-element.172.refs_6_.refs_3_, bf16[640,2048]{1,0:T(8,128)(2,1)} %back_first_0.1.refs_4_, ...), custom_call_target="tpu_custom_call" | custom-call | flops 999999995904 | bytes 1 | tf_op jit(solution)/shard_map/first_back/pallas_call | solution.py:50
  889.7 7.6 outer_raise.1
  897.3 8.0 collective-permute-start.50
  905.3 21.9 %collective-permute-done.47.refs_3_ = bf16[256,2048]{1,0:T(8,128)(2,1)} collective-permute-done((bf16[256,2048]{1,0:T(8,128)(2,1)}, bf16[256,2048]{1,0:T(8,128)(2,1)}, u32[]{:S(2)}, u32[]{:S(2)}) %collective-permute-start.47) | collective-permute-done | bytes 1048608 | tf_op jit(solution)/shard_map/ppermute | solution.py:1199
  927.2 8.7 outer_heads.1
  (174 shorter events, 190.0 us)
Async XLA Ops:
  7.2 156.5 %all-gather.5.cloned.1.call-start = ((), (), s32[]{:S(2)}) async-start(), calls=%async_computation.2 | async-start | bytes 2621440 | tf_op jit(solution)/shard_map/all_gather | solution.py:1055
  7.2 10.7 %collective-permute-start.2 = (f32[2,512]{1,0:T(2,128)}, f32[2,512]{1,0:T(2,128)}, u32[]{:S(2)}, u32[]{:S(2)}) collective-permute-start(f32[2,512]{1,0:T(2,128)} %refs_1_.8), channel_id=1, source_target_pairs={{0,24},{8,16},{16,8},{24,0},{1,25},{9,17},{17,9},{25,1},{2,26},{10... | collective-permute-start | bytes 12296 | tf_op jit(solution)/shard_map/ppermute | solution.py:34
  7.3 10.6 %collective-permute-start.1 = (f32[2,512]{1,0:T(2,128)}, f32[2,512]{1,0:T(2,128)}, u32[]{:S(2)}, u32[]{:S(2)}) collective-permute-start(f32[2,512]{1,0:T(2,128)} %refs_1_.8), channel_id=1, source_target_pairs={{0,16},{8,24},{16,0},{24,8},{1,17},{9,25},{17,1},{25,9},{2,18},{10... | collective-permute-start | bytes 12296 | tf_op jit(solution)/shard_map/ppermute | solution.py:34
  9.2 8.7 collective-permute-start
  16.2 31.6 %collective-permute-start.6 = (bf16[256,2048]{1,0:T(8,128)(2,1)}, bf16[256,2048]{1,0:T(8,128)(2,1)}, u32[]{:S(2)}, u32[]{:S(2)}) collective-permute-start(bf16[256,2048]{1,0:T(8,128)(2,1)} %cast_heads.1.refs_5_), channel_id=1, source_target_pairs={{0,8},{8,16},{16,24},{24,0},{1,9},{9,17},{17,25},{25,1},{2,10},{10... | collective-permute-start | bytes 3145736 | tf_op jit(solution)/shard_map/ppermute | solution.py:1002
  16.3 24.4 %collective-permute-start.3 = (bf16[256,2048]{1,0:T(8,128)(2,1)}, bf16[256,2048]{1,0:T(8,128)(2,1)}, u32[]{:S(2)}, u32[]{:S(2)}) collective-permute-start(bf16[256,2048]{1,0:T(8,128)(2,1)} %cast_heads.1.refs_5_), channel_id=1, source_target_pairs={{0,4},{4,0},{1,5},{5,1},{2,6},{6,2},{3,7},{7,3},{8,12},{12,8},{9,1... | collective-permute-start | bytes 3145736 | tf_op jit(solution)/shard_map/ppermute | solution.py:34
  25.9 57.7 %collective-permute-start.5 = (bf16[640,2048]{1,0:T(8,128)(2,1)}, bf16[640,2048]{1,0:T(8,128)(2,1)}, u32[]{:S(2)}, u32[]{:S(2)}) collective-permute-start(bf16[640,2048]{1,0:T(8,128)(2,1)} %get-tuple-element.116.refs_2_.refs_1_), channel_id=1, source_target_pairs={{0,2},{1,3},{2,0},{3,1},{4,6},{5,7},{6,4},{7,5},{8,10},{9,11},{10,... | collective-permute-start | bytes 7864328 | tf_op jit(solution)/shard_map/ppermute | solution.py:34
  49.0 25.9 %collective-permute-start.8 = (bf16[256,2048]{1,0:T(8,128)(2,1)}, bf16[256,2048]{1,0:T(8,128)(2,1)}, u32[]{:S(2)}, u32[]{:S(2)}) collective-permute-start(bf16[256,2048]{1,0:T(8,128)(2,1)} %get-tuple-element.122.refs_7_), channel_id=1, source_target_pairs={{0,4},{4,0},{1,5},{5,1},{2,6},{6,2},{3,7},{7,3},{8,12},{12,8},{9,1... | collective-permute-start | bytes 3145736 | tf_op jit(solution)/shard_map/ppermute | solution.py:34
  50.6 25.6 %collective-permute-start.7 = (bf16[256,2048]{1,0:T(8,128)(2,1)}, bf16[256,2048]{1,0:T(8,128)(2,1)}, u32[]{:S(2)}, u32[]{:S(2)}) collective-permute-start(bf16[256,2048]{1,0:T(8,128)(2,1)} %get-tuple-element.122.refs_7_), channel_id=1, source_target_pairs={{0,8},{8,16},{16,24},{24,0},{1,9},{9,17},{17,25},{25,1},{2,10},{10... | collective-permute-start | bytes 3145736 | tf_op jit(solution)/shard_map/ppermute | solution.py:1002
  78.0 29.6 %collective-permute-start.11 = (bf16[256,2048]{1,0:T(8,128)(2,1)}, bf16[256,2048]{1,0:T(8,128)(2,1)}, u32[]{:S(2)}, u32[]{:S(2)}) collective-permute-start(bf16[256,2048]{1,0:T(8,128)(2,1)} %get-tuple-element.125.refs_9_), channel_id=1, source_target_pairs={{0,8},{8,16},{16,24},{24,0},{1,9},{9,17},{17,25},{25,1},{2,10},{10... | collective-permute-start | bytes 3145736 | tf_op jit(solution)/shard_map/ppermute | solution.py:1002
  81.2 24.5 %collective-permute-start.9 = (bf16[256,2048]{1,0:T(8,128)(2,1)}, bf16[256,2048]{1,0:T(8,128)(2,1)}, u32[]{:S(2)}, u32[]{:S(2)}) collective-permute-start(bf16[256,2048]{1,0:T(8,128)(2,1)} %get-tuple-element.125.refs_9_), channel_id=1, source_target_pairs={{0,4},{4,0},{1,5},{5,1},{2,6},{6,2},{3,7},{7,3},{8,12},{12,8},{9,1... | collective-permute-start | bytes 3145736 | tf_op jit(solution)/shard_map/ppermute | solution.py:34
  109.5 25.9 %collective-permute-start.12 = (bf16[256,2048]{1,0:T(8,128)(2,1)}, bf16[256,2048]{1,0:T(8,128)(2,1)}, u32[]{:S(2)}, u32[]{:S(2)}) collective-permute-start(bf16[256,2048]{1,0:T(8,128)(2,1)} %get-tuple-element.128.refs_11_), channel_id=1, source_target_pairs={{0,4},{4,0},{1,5},{5,1},{2,6},{6,2},{3,7},{7,3},{8,12},{12,8},{9,1... | collective-permute-start | bytes 3145736 | tf_op jit(solution)/shard_map/ppermute | solution.py:34
  114.7 92.8 %all-gather.7.cloned.1.call-start = ((), (), s32[]{:S(2)}) async-start(), calls=%async_computation.3 | async-start | bytes 2621440 | tf_op jit(solution)/shard_map/all_gather | solution.py:1055
  116.6 98.3 %collective-permute-start.13 = (bf16[640,2048]{1,0:T(8,128)(2,1)}, bf16[640,2048]{1,0:T(8,128)(2,1)}, u32[]{:S(2)}, u32[]{:S(2)}) collective-permute-start(bf16[640,2048]{1,0:T(8,128)(2,1)} %get-tuple-element.145.refs_1_.refs_4_), channel_id=1, source_target_pairs={{0,2},{1,3},{2,0},{3,1},{4,6},{5,7},{6,4},{7,5},{8,10},{9,11},{10,... | collective-permute-start | bytes 7864328 | tf_op jit(solution)/shard_map/ppermute | solution.py:34
  163.6 90.8 %all-gather.9.cloned.1.call-start = ((), (), s32[]{:S(2)}) async-start(), calls=%async_computation.4 | async-start | bytes 2621440 | tf_op jit(solution)/shard_map/all_gather | solution.py:1055
  165.5 47.6 %collective-permute-start.14 = (bf16[1024,1024]{1,0:T(8,128)(2,1)}, bf16[1024,1024]{1,0:T(8,128)(2,1)}, u32[]{:S(2)}, u32[]{:S(2)}) collective-permute-start(bf16[1024,1024]{1,0:T(8,128)(2,1)} %get-tuple-element.147.refs_5_), channel_id=1, source_target_pairs={{0,4},{4,0},{1,5},{5,1},{2,6},{6,2},{3,7},{7,3},{8,12},{12,8},{9,1... | collective-permute-start | bytes 6291464 | tf_op jit(solution)/shard_map/ppermute | solution.py:34
  200.5 115.3 %all-gather.11.cloned.1.call-start = ((), (), s32[]{:S(2)}) async-start(), calls=%async_computation.5 | async-start | bytes 2621440 | tf_op jit(solution)/shard_map/all_gather | solution.py:1055
  214.3 104.2 %collective-permute-start.23 = (bf16[1024,1024]{1,0:T(8,128)(2,1)}, bf16[1024,1024]{1,0:T(8,128)(2,1)}, u32[]{:S(2)}, u32[]{:S(2)}) collective-permute-start(bf16[1024,1024]{1,0:T(8,128)(2,1)} %get-tuple-element.159.refs_7_), channel_id=1, source_target_pairs={{0,4},{4,0},{1,5},{5,1},{2,6},{6,2},{3,7},{7,3},{8,12},{12,8},{9,1... | collective-permute-start | bytes 6291464 | tf_op jit(solution)/shard_map/ppermute | solution.py:34
  216.8 9.0 collective-permute-start.16
  219.2 496.1 %reduce-scatter.3.cloned.1.call-start = ((), (), s32[]{:S(2)}) async-start(), calls=%async_computation.6 | async-start | bytes 5242880 | tf_op jit(solution)/shard_map/reduce_scatter | solution.py:1150
  246.5 59.3 %collective-permute-start.19 = (bf16[640,2048]{1,0:T(8,128)(2,1)}, bf16[640,2048]{1,0:T(8,128)(2,1)}, u32[]{:S(2)}, u32[]{:S(2)}) collective-permute-start(bf16[640,2048]{1,0:T(8,128)(2,1)} %project_2.1.refs_4_), channel_id=1, source_target_pairs={{0,2},{1,3},{2,0},{3,1},{4,6},{5,7},{6,4},{7,5},{8,10},{9,11},{10,... | collective-permute-start | bytes 7864328 | tf_op jit(solution)/shard_map/ppermute | solution.py:34
  255.6 95.9 %collective-permute-start.24 = (bf16[1024,1024]{1,0:T(8,128)(2,1)}, bf16[1024,1024]{1,0:T(8,128)(2,1)}, u32[]{:S(2)}, u32[]{:S(2)}) collective-permute-start(bf16[1024,1024]{1,0:T(8,128)(2,1)} %get-tuple-element.162.refs_3_.refs_2_), channel_id=1, source_target_pairs={{0,4},{4,0},{1,5},{5,1},{2,6},{6,2},{3,7},{7,3},{8,12},{12,8},{9,1... | collective-permute-start | bytes 6291464 | tf_op jit(solution)/shard_map/ppermute | solution.py:34
  314.3 36.0 %collective-permute-start.21 = (bf16[640,2048]{1,0:T(8,128)(2,1)}, bf16[640,2048]{1,0:T(8,128)(2,1)}, u32[]{:S(2)}, u32[]{:S(2)}) collective-permute-start(bf16[640,2048]{1,0:T(8,128)(2,1)} %get-tuple-element.156.refs_1_), channel_id=1, source_target_pairs={{0,1},{1,0},{2,3},{3,2},{4,5},{5,4},{6,7},{7,6},{8,9},{9,8},{10,11... | collective-permute-start | bytes 7864328 | tf_op jit(solution)/shard_map/ppermute | solution.py:34
  314.3 71.5 %collective-permute-start.20 = (bf16[640,2048]{1,0:T(8,128)(2,1)}, bf16[640,2048]{1,0:T(8,128)(2,1)}, u32[]{:S(2)}, u32[]{:S(2)}) collective-permute-start(bf16[640,2048]{1,0:T(8,128)(2,1)} %get-tuple-element.156.refs_1_), channel_id=1, source_target_pairs={{0,2},{1,3},{2,0},{3,1},{4,6},{5,7},{6,4},{7,5},{8,10},{9,11},{10,... | collective-permute-start | bytes 7864328 | tf_op jit(solution)/shard_map/ppermute | solution.py:34
  317.0 52.0 %collective-permute-start.22 = (bf16[1024,1024]{1,0:T(8,128)(2,1)}, bf16[1024,1024]{1,0:T(8,128)(2,1)}, u32[]{:S(2)}, u32[]{:S(2)}) collective-permute-start(bf16[1024,1024]{1,0:T(8,128)(2,1)} %get-tuple-element.158.refs_3_.refs_5_.refs_4_), channel_id=1, source_target_pairs={{0,4},{4,0},{1,5},{5,1},{2,6},{6,2},{3,7},{7,3},{8,12},{12,8},{9,1... | collective-permute-start | bytes 6291464 | tf_op jit(solution)/shard_map/ppermute | solution.py:34
  439.6 166.3 %collective-permute-start.34 = (bf16[1024,2048]{1,0:T(8,128)(2,1)}, bf16[1024,2048]{1,0:T(8,128)(2,1)}, u32[]{:S(2)}, u32[]{:S(2)}) collective-permute-start(bf16[1024,2048]{1,0:T(8,128)(2,1)} %lower_far.1.refs_6_), channel_id=1, source_target_pairs={{0,4},{4,0},{1,5},{5,1},{2,6},{6,2},{3,7},{7,3},{8,12},{12,8},{9,1... | collective-permute-start | bytes 12582920 | tf_op jit(solution)/shard_map/ppermute | solution.py:34
  452.2 12.7 %collective-permute-start.27 = (bf16[640,2048]{1,0:T(8,128)(2,1)}, bf16[640,2048]{1,0:T(8,128)(2,1)}, u32[]{:S(2)}, u32[]{:S(2)}) collective-permute-start(bf16[640,2048]{1,0:T(8,128)(2,1)} %back_second_3.1.refs_6_), channel_id=1, source_target_pairs={{0,1},{1,0},{2,3},{3,2},{4,5},{5,4},{6,7},{7,6},{8,9},{9,8},{10,11... | collective-permute-start | bytes 7864328 | tf_op jit(solution)/shard_map/ppermute | solution.py:34
  464.3 13.6 %collective-permute-start.26 = (bf16[640,2048]{1,0:T(8,128)(2,1)}, bf16[640,2048]{1,0:T(8,128)(2,1)}, u32[]{:S(2)}, u32[]{:S(2)}) collective-permute-start(bf16[640,2048]{1,0:T(8,128)(2,1)} %back_second_1.1.refs_7_), channel_id=1, source_target_pairs={{0,1},{1,0},{2,3},{3,2},{4,5},{5,4},{6,7},{7,6},{8,9},{9,8},{10,11... | collective-permute-start | bytes 7864328 | tf_op jit(solution)/shard_map/ppermute | solution.py:34
  477.3 60.4 %collective-permute-start.28 = (bf16[640,2048]{1,0:T(8,128)(2,1)}, bf16[640,2048]{1,0:T(8,128)(2,1)}, u32[]{:S(2)}, u32[]{:S(2)}) collective-permute-start(bf16[640,2048]{1,0:T(8,128)(2,1)} %back_second_2.1.refs_7_), channel_id=1, source_target_pairs={{0,2},{1,3},{2,0},{3,1},{4,6},{5,7},{6,4},{7,5},{8,10},{9,11},{10,... | collective-permute-start | bytes 7864328 | tf_op jit(solution)/shard_map/ppermute | solution.py:34
  507.5 145.2 %collective-permute-start.36 = (bf16[1024,2048]{1,0:T(8,128)(2,1)}, bf16[1024,2048]{1,0:T(8,128)(2,1)}, u32[]{:S(2)}, u32[]{:S(2)}) collective-permute-start(bf16[1024,2048]{1,0:T(8,128)(2,1)} %raise_far.1.refs_6_), channel_id=1, source_target_pairs={{0,4},{4,0},{1,5},{5,1},{2,6},{6,2},{3,7},{7,3},{8,12},{12,8},{9,1... | collective-permute-start | bytes 12582920 | tf_op jit(solution)/shard_map/ppermute | solution.py:34
  537.7 43.5 %collective-permute-start.31 = (bf16[640,2048]{1,0:T(8,128)(2,1)}, bf16[640,2048]{1,0:T(8,128)(2,1)}, u32[]{:S(2)}, u32[]{:S(2)}) collective-permute-start(bf16[640,2048]{1,0:T(8,128)(2,1)} %lower_3.1.refs_6_), channel_id=1, source_target_pairs={{0,1},{1,0},{2,3},{3,2},{4,5},{5,4},{6,7},{7,6},{8,9},{9,8},{10,11... | collective-permute-start | bytes 7864328 | tf_op jit(solution)/shard_map/ppermute | solution.py:34
  548.8 76.8 %collective-permute-start.33 = (bf16[640,2048]{1,0:T(8,128)(2,1)}, bf16[640,2048]{1,0:T(8,128)(2,1)}, u32[]{:S(2)}, u32[]{:S(2)}) collective-permute-start(bf16[640,2048]{1,0:T(8,128)(2,1)} %get-tuple-element.173.refs_1_), channel_id=1, source_target_pairs={{0,2},{1,3},{2,0},{3,1},{4,6},{5,7},{6,4},{7,5},{8,10},{9,11},{10,... | collective-permute-start | bytes 7864328 | tf_op jit(solution)/shard_map/ppermute | solution.py:34
  550.2 17.3 %collective-permute-start.29 = (bf16[640,2048]{1,0:T(8,128)(2,1)}, bf16[640,2048]{1,0:T(8,128)(2,1)}, u32[]{:S(2)}, u32[]{:S(2)}) collective-permute-start(bf16[640,2048]{1,0:T(8,128)(2,1)} %get-tuple-element.173.refs_1_), channel_id=1, source_target_pairs={{0,1},{1,0},{2,3},{3,2},{4,5},{5,4},{6,7},{7,6},{8,9},{9,8},{10,11... | collective-permute-start | bytes 7864328 | tf_op jit(solution)/shard_map/ppermute | solution.py:34
  580.8 13.1 %collective-permute-start.30 = (bf16[640,2048]{1,0:T(8,128)(2,1)}, bf16[640,2048]{1,0:T(8,128)(2,1)}, u32[]{:S(2)}, u32[]{:S(2)}) collective-permute-start(bf16[640,2048]{1,0:T(8,128)(2,1)} %lower_1.1.refs_4_), channel_id=1, source_target_pairs={{0,1},{1,0},{2,3},{3,2},{4,5},{5,4},{6,7},{7,6},{8,9},{9,8},{10,11... | collective-permute-start | bytes 7864328 | tf_op jit(solution)/shard_map/ppermute | solution.py:34
  593.3 122.0 %collective-permute-start.32 = (bf16[640,2048]{1,0:T(8,128)(2,1)}, bf16[640,2048]{1,0:T(8,128)(2,1)}, u32[]{:S(2)}, u32[]{:S(2)}) collective-permute-start(bf16[640,2048]{1,0:T(8,128)(2,1)} %lower_2.1.refs_4_), channel_id=1, source_target_pairs={{0,2},{1,3},{2,0},{3,1},{4,6},{5,7},{6,4},{7,5},{8,10},{9,11},{10,... | collective-permute-start | bytes 7864328 | tf_op jit(solution)/shard_map/ppermute | solution.py:34
  625.5 264.2 %reduce-scatter.5.cloned.1.call-start = ((), (), s32[]{:S(2)}) async-start(), calls=%async_computation.7 | async-start | bytes 5242880 | tf_op jit(solution)/shard_map/reduce_scatter | solution.py:1150
  652.0 150.3 %collective-permute-start.41 = (bf16[1024,512]{1,0:T(8,128)(2,1)}, bf16[1024,512]{1,0:T(8,128)(2,1)}, u32[]{:S(2)}, u32[]{:S(2)}) collective-permute-start(bf16[1024,512]{1,0:T(8,128)(2,1)} %out_far.1.refs_9_), channel_id=1, source_target_pairs={{0,4},{4,0},{1,5},{5,1},{2,6},{6,2},{3,7},{7,3},{8,12},{12,8},{9,1... | collective-permute-start | bytes 3145736 | tf_op jit(solution)/shard_map/ppermute | solution.py:34
  705.9 96.4 %collective-permute-start.39 = (bf16[1024,768]{1,0:T(8,128)(2,1)}, bf16[1024,768]{1,0:T(8,128)(2,1)}, u32[]{:S(2)}, u32[]{:S(2)}) collective-permute-start(bf16[1024,768]{1,0:T(8,128)(2,1)} %in_far.2.refs_6_), channel_id=1, source_target_pairs={{0,4},{4,0},{1,5},{5,1},{2,6},{6,2},{3,7},{7,3},{8,12},{12,8},{9,1... | collective-permute-start | bytes 4718600 | tf_op jit(solution)/shard_map/ppermute | solution.py:34
  756.6 45.8 %collective-permute-start.40 = (bf16[1024,768]{1,0:T(8,128)(2,1)}, bf16[1024,768]{1,0:T(8,128)(2,1)}, u32[]{:S(2)}, u32[]{:S(2)}) collective-permute-start(bf16[1024,768]{1,0:T(8,128)(2,1)} %in_far.3.refs_4_), channel_id=1, source_target_pairs={{0,4},{4,0},{1,5},{5,1},{2,6},{6,2},{3,7},{7,3},{8,12},{12,8},{9,1... | collective-permute-start | bytes 4718600 | tf_op jit(solution)/shard_map/ppermute | solution.py:34
  766.8 10.1 %collective-permute-start.38 = (bf16[640,2048]{1,0:T(8,128)(2,1)}, bf16[640,2048]{1,0:T(8,128)(2,1)}, u32[]{:S(2)}, u32[]{:S(2)}) collective-permute-start(bf16[640,2048]{1,0:T(8,128)(2,1)} %back_first_3.1.refs_4_), channel_id=1, source_target_pairs={{0,1},{1,0},{2,3},{3,2},{4,5},{5,4},{6,7},{7,6},{8,9},{9,8},{10,11... | collective-permute-start | bytes 7864328 | tf_op jit(solution)/shard_map/ppermute | solution.py:34
  776.3 60.1 %collective-permute-start.37 = (bf16[640,2048]{1,0:T(8,128)(2,1)}, bf16[640,2048]{1,0:T(8,128)(2,1)}, u32[]{:S(2)}, u32[]{:S(2)}) collective-permute-start(bf16[640,2048]{1,0:T(8,128)(2,1)} %back_first_1.1.refs_5_), channel_id=1, source_target_pairs={{0,1},{1,0},{2,3},{3,2},{4,5},{5,4},{6,7},{7,6},{8,9},{9,8},{10,11... | collective-permute-start | bytes 7864328 | tf_op jit(solution)/shard_map/ppermute | solution.py:34
  786.9 66.1 %collective-permute-start.42 = (bf16[640,2048]{1,0:T(8,128)(2,1)}, bf16[640,2048]{1,0:T(8,128)(2,1)}, u32[]{:S(2)}, u32[]{:S(2)}) collective-permute-start(bf16[640,2048]{1,0:T(8,128)(2,1)} %back_first_2.1.refs_7_), channel_id=1, source_target_pairs={{0,2},{1,3},{2,0},{3,1},{4,6},{5,7},{6,4},{7,5},{8,10},{9,11},{10,... | collective-permute-start | bytes 7864328 | tf_op jit(solution)/shard_map/ppermute | solution.py:34
  824.2 73.2 %collective-permute-start.46 = (bf16[256,2048]{1,0:T(8,128)(2,1)}, bf16[256,2048]{1,0:T(8,128)(2,1)}, u32[]{:S(2)}, u32[]{:S(2)}) collective-permute-start(bf16[256,2048]{1,0:T(8,128)(2,1)} %get-tuple-element.189), channel_id=1, source_target_pairs={{0,8},{8,16},{16,24},{24,0},{1,9},{9,17},{17,25},{25,1},{2,10},{10... | collective-permute-start | bytes 3145736 | tf_op jit(solution)/shard_map/ppermute | solution.py:1199
  831.1 96.1 %collective-permute-start.47 = (bf16[256,2048]{1,0:T(8,128)(2,1)}, bf16[256,2048]{1,0:T(8,128)(2,1)}, u32[]{:S(2)}, u32[]{:S(2)}) collective-permute-start(bf16[256,2048]{1,0:T(8,128)(2,1)} %get-tuple-element.190), channel_id=1, source_target_pairs={{0,16},{8,24},{16,0},{24,8},{1,17},{9,25},{17,1},{25,9},{2,18},{10... | collective-permute-start | bytes 3145736 | tf_op jit(solution)/shard_map/ppermute | solution.py:1199
  836.4 90.8 %collective-permute-start.48 = (bf16[256,2048]{1,0:T(8,128)(2,1)}, bf16[256,2048]{1,0:T(8,128)(2,1)}, u32[]{:S(2)}, u32[]{:S(2)}) collective-permute-start(bf16[256,2048]{1,0:T(8,128)(2,1)} %get-tuple-element.191), channel_id=1, source_target_pairs={{0,24},{8,0},{16,8},{24,16},{1,25},{9,1},{17,9},{25,17},{2,26},{10... | collective-permute-start | bytes 3145736 | tf_op jit(solution)/shard_map/ppermute | solution.py:1199
  885.8 50.1 %collective-permute-start.49 = (f32[2,512]{1,0:T(2,128)}, f32[2,512]{1,0:T(2,128)}, u32[]{:S(2)}, u32[]{:S(2)}) collective-permute-start(f32[2,512]{1,0:T(2,128)} %get-tuple-element.215), channel_id=1, source_target_pairs={{0,8},{8,0},{16,24},{24,16},{1,9},{9,1},{17,25},{25,17},{2,10},{10... | collective-permute-start | bytes 12296 | tf_op jit(solution)/shard_map/ppermute | solution.py:34
  889.6 46.3 %collective-permute-start.51 = (f32[2,512]{1,0:T(2,128)}, f32[2,512]{1,0:T(2,128)}, u32[]{:S(2)}, u32[]{:S(2)}) collective-permute-start(f32[2,512]{1,0:T(2,128)} %get-tuple-element.216), channel_id=1, source_target_pairs={{0,24},{8,16},{16,8},{24,0},{1,25},{9,17},{17,9},{25,1},{2,26},{10... | collective-permute-start | bytes 12296 | tf_op jit(solution)/shard_map/ppermute | solution.py:34
  897.3 38.6 %collective-permute-start.50 = (f32[2,512]{1,0:T(2,128)}, f32[2,512]{1,0:T(2,128)}, u32[]{:S(2)}, u32[]{:S(2)}) collective-permute-start(f32[2,512]{1,0:T(2,128)} %get-tuple-element.217), channel_id=1, source_target_pairs={{0,16},{8,24},{16,0},{24,8},{1,17},{9,25},{17,1},{25,9},{2,18},{10... | collective-permute-start | bytes 12296 | tf_op jit(solution)/shard_map/ppermute | solution.py:34
  (17 other events, 86.4 us)
Sparse Core Ops, SparseCore 0:
  114.8 43.7 all-gather.4
  163.7 43.7 all-gather.6
  209.7 44.6 all-gather.8
  256.4 44.6 all-gather.10
  625.6 75.9 reduce-scatter.2
  707.5 80.8 reduce-scatter.4
